TPU v7x, 32 devices: a whole 2x2x4 slice. The times are simulated.
32 devices in a mesh: gx: 8 (over y, x, core), gy: 4 (over z).
Axes of the slice: x: 2, y: 2, z: 4, core: 2. Of those that a mesh axis runs over, the one named last changes fastest.
Arguments:
- source: float32 [64, 64, 256], P('gx', 'gy'), may hold values from -6 to 6
- initial: float32 [64, 64, 256], P('gx', 'gy'), may hold values from -6 to 6
- absorption: float32 [64, 64, 256], P('gx', 'gy'), may hold values from 0.01 to 0.2
- beta_x: float32 [64, 64, 256], P('gx', 'gy'), may hold values from 0.4 to 2.5
- beta_y: float32 [64, 64, 256], P('gx', 'gy'), may hold values from 0.4 to 2.5
- beta_z: float32 [64, 64, 256], P('gx', 'gy'), may hold values from 0.4 to 2.5
Outputs:
- solution: float32 [64, 64, 256], P('gx', 'gy')
All inputs are finite; a program needn't handle non-finite values.
Results may differ from a plain program's by a relative error of at most 0.00002.
Values sent between devices are 32-bit elements; how exact they have to be, the bound alone decides.
No kernel may reach another device: no remote copies, remote signals or barrier semaphores. Data moves between devices by JAX's collectives and lax.ppermute only.
A program may use at most 64 MiB of HBM per device.

v0:
```python
import jax
import jax.numpy as jnp
from jax import lax
from jax.sharding import PartitionSpec as P

SWEEPS = 4
COARSE_SWEEPS = 8


def extended(block, sides, width):
    for axis, dim in sides:
        count = lax.axis_size(axis)
        forward = [(i, i + 1) for i in range(count - 1)]
        forward.append((count - 1, 0))
        backward = [(target, source) for source, target in forward]
        low = lax.ppermute(
            lax.slice_in_dim(block, block.shape[dim] - width, None, axis=dim), axis, forward
        )
        high = lax.ppermute(lax.slice_in_dim(block, 0, width, axis=dim), axis, backward)
        block = jnp.concatenate([low, block, high], axis=dim)
    return block


def passed_along(block, axis, distance):
    devices = range(lax.axis_size(axis))
    route = [((i - distance) % len(devices), i) for i in devices]
    return lax.ppermute(block, axis, route)


def restrict_cells(field):
    size_x, size_y, size_z = field.shape
    return field.reshape(size_x // 2, 2, size_y // 2, 2, size_z // 2, 2).mean(axis=(1, 3, 5))


def restrict_faces(face_x, face_y, face_z):
    lower_x = face_x[0::2]
    size_x, size_y, size_z = lower_x.shape
    coarse_x = lower_x.reshape(size_x, size_y // 2, 2, size_z // 2, 2).mean(axis=(2, 4))
    lower_y = face_y[:, 0::2]
    size_x, size_y, size_z = lower_y.shape
    coarse_y = lower_y.reshape(size_x // 2, 2, size_y, size_z // 2, 2).mean(axis=(1, 4))
    lower_z = face_z[:, :, 0::2]
    size_x, size_y, size_z = lower_z.shape
    coarse_z = lower_z.reshape(size_x // 2, 2, size_y // 2, 2, size_z).mean(axis=(1, 3))
    return (coarse_x, coarse_y, coarse_z)


def restrict_plane_x(plane):
    size_x, size_y, size_z = plane.shape
    return plane.reshape(1, size_y // 2, 2, size_z // 2, 2).mean(axis=(2, 4))


def restrict_plane_y(plane):
    size_x, size_y, size_z = plane.shape
    return plane.reshape(size_x // 2, 2, 1, size_z // 2, 2).mean(axis=(1, 4))


def prolong_cells(field):
    size_x, size_y, size_z = field.shape
    spread = jnp.broadcast_to(field[:, None, :, None, :, None], (size_x, 2, size_y, 2, size_z, 2))
    return spread.reshape(2 * size_x, 2 * size_y, 2 * size_z)


def level_coeffs(absorb, face_xl, face_yl, face_zl, next_x, next_y, stencil_scale):
    face_xh = jnp.concatenate([face_xl[1:], next_x], axis=0)
    face_yh = jnp.concatenate([face_yl[:, 1:], next_y], axis=1)
    face_zh = jnp.concatenate([face_zl[:, :, 1:], jnp.zeros_like(face_zl[:, :, :1])], axis=2)
    diagonal = absorb + stencil_scale * (face_xl + face_xh + face_yl + face_yh + face_zl + face_zh)
    return (absorb, face_xl, face_xh, face_yl, face_yh, face_zl, face_zh, diagonal, stencil_scale)


def split_padded(padded):
    return (padded[:-2, 1:-1], padded[2:, 1:-1], padded[1:-1, :-2], padded[1:-1, 2:])


def neighbours(field, level):
    if level == 0:
        padded = extended(field, (("gx", 0), ("gy", 1)), 1)
    else:
        padded = extended(field, (("gx", 0), ("gy", 1)), 1)
    return split_padded(padded)


def apply_operator(field, coeffs, lower_x, upper_x, lower_y, upper_y):
    absorb, face_xl, face_xh, face_yl, face_yh, face_zl, face_zh, diagonal, stencil_scale = coeffs
    zeros_plane = jnp.zeros_like(field[:, :, :1])
    lower_z = jnp.concatenate([zeros_plane, field[:, :, :-1]], axis=2)
    upper_z = jnp.concatenate([field[:, :, 1:], zeros_plane], axis=2)
    flux = (
        face_xl * (field - lower_x)
        + face_xh * (field - upper_x)
        + face_yl * (field - lower_y)
        + face_yh * (field - upper_y)
        + face_zl * (field - lower_z)
        + face_zh * (field - upper_z)
    )
    return absorb * field + stencil_scale * flux


def chebyshev_weights(sweeps):
    cheb_theta = 1.125
    cheb_delta = 0.875
    cheb_sigma = cheb_theta / cheb_delta
    rho_old = 1.0 / cheb_sigma
    weights = [(0.0, 1.0 / cheb_theta)]
    for sweep in range(1, sweeps):
        rho_new = 1.0 / (2.0 * cheb_sigma - rho_old)
        weights.append((rho_new * rho_old, 2.0 * rho_new / cheb_delta))
        rho_old = rho_new
    return weights


def chebyshev_smooth(iterate, target, coeffs, sweeps, zero_start, finder):
    update = jnp.zeros_like(target)
    for sweep, pair in enumerate(chebyshev_weights(sweeps)):
        if sweep == 0 and zero_start:
            remain = target
        else:
            remain = target - apply_operator(iterate, coeffs, *finder(iterate))
        update = pair[0] * update + pair[1] * remain / coeffs[7]
        iterate = iterate + update
    return iterate


def shrink_coeffs(coeffs):
    inner = tuple((part[1:-1, 1:-1] for part in coeffs[:8]))
    return inner + (coeffs[8],)


def rim_setup(absorb, face_x, face_y, face_z, target, stencil_scale):
    depth = absorb.shape[2]
    stacked = jnp.concatenate([absorb, face_x, face_y, face_z, target], axis=2)
    padded = extended(stacked, (("gx", 0), ("gy", 1)), 2)
    absorb_p = padded[:, :, 0:depth]
    face_xp = padded[:, :, depth : 2 * depth]
    face_yp = padded[:, :, 2 * depth : 3 * depth]
    face_zp = padded[:, :, 3 * depth : 4 * depth]
    target_p = padded[:, :, 4 * depth : 5 * depth]
    absorb_one = absorb_p[1:-1, 1:-1]
    face_xl = face_xp[1:-1, 1:-1]
    face_xh = face_xp[2:, 1:-1]
    face_yl = face_yp[1:-1, 1:-1]
    face_yh = face_yp[1:-1, 2:]
    face_zl = face_zp[1:-1, 1:-1]
    face_zh = jnp.concatenate([face_zl[:, :, 1:], jnp.zeros_like(face_zl[:, :, :1])], axis=2)
    diagonal = absorb_one + stencil_scale * (
        face_xl + face_xh + face_yl + face_yh + face_zl + face_zh
    )
    coeffs_one = (
        absorb_one,
        face_xl,
        face_xh,
        face_yl,
        face_yh,
        face_zl,
        face_zh,
        diagonal,
        stencil_scale,
    )
    coeffs_two = shrink_coeffs(coeffs_one)
    return (coeffs_one, target_p[1:-1, 1:-1], coeffs_two, target_p[2:-2, 2:-2])


def padded_operator(padded, coeffs):
    return apply_operator(padded[1:-1, 1:-1], coeffs, *split_padded(padded))


def deep_pair(iterate, update, rim, first, second, residual_after):
    coeffs_one, target_one, coeffs_two, target_two = rim
    depth = iterate.shape[2]
    stacked = jnp.concatenate([iterate, update], axis=2)
    padded = extended(stacked, (("gx", 0), ("gy", 1)), 2)
    iter_p = padded[:, :, :depth]
    update_p = padded[:, :, depth:]
    remain = target_one - padded_operator(iter_p, coeffs_one)
    update_one = first[0] * update_p[1:-1, 1:-1] + first[1] * remain / coeffs_one[7]
    iter_one = iter_p[1:-1, 1:-1] + update_one
    remain_two = target_two - padded_operator(iter_one, coeffs_two)
    if residual_after:
        return (iter_one[1:-1, 1:-1], remain_two)
    update_two = second[0] * update_one[1:-1, 1:-1] + second[1] * remain_two / coeffs_two[7]
    return (iter_one[1:-1, 1:-1] + update_two, update_two)


def local(source, initial, absorption, beta_x, beta_y, beta_z):
    next_x = passed_along(beta_x[0:1], "gx", -1)
    next_y = passed_along(beta_y[:, 0:1], "gy", -1)
    coeffs_fine = level_coeffs(absorption, beta_x, beta_y, beta_z, next_x, next_y, 1.0)
    absorb_mid = restrict_cells(absorption)
    face_mid = restrict_faces(beta_x, beta_y, beta_z)
    next_x_mid = restrict_plane_x(next_x)
    next_y_mid = restrict_plane_y(next_y)
    coeffs_mid = level_coeffs(
        absorb_mid, face_mid[0], face_mid[1], face_mid[2], next_x_mid, next_y_mid, 0.25
    )
    absorb_low = restrict_cells(absorb_mid)
    face_low = restrict_faces(face_mid[0], face_mid[1], face_mid[2])

    def fine_finder(field):
        return neighbours(field, 0)

    def low_finder(field):
        return neighbours(field, 2)

    fine_iter = chebyshev_smooth(initial, source, coeffs_fine, SWEEPS, False, fine_finder)
    fine_rest = source - apply_operator(fine_iter, coeffs_fine, *fine_finder(fine_iter))
    source_mid = restrict_cells(fine_rest)
    weights = chebyshev_weights(SWEEPS)
    rim = rim_setup(absorb_mid, face_mid[0], face_mid[1], face_mid[2], source_mid, 0.25)
    zeros_mid = jnp.zeros_like(source_mid)
    mid_update = weights[0][0] * zeros_mid + weights[0][1] * source_mid / coeffs_mid[7]
    mid_iter = mid_update
    sweep = 1
    while sweep + 1 < SWEEPS:
        mid_iter, mid_update = deep_pair(
            mid_iter, mid_update, rim, weights[sweep], weights[sweep + 1], False
        )
        sweep = sweep + 2
    mid_iter, mid_rest = deep_pair(mid_iter, mid_update, rim, weights[sweep], weights[sweep], True)
    source_low = restrict_cells(mid_rest)
    next_x_low = restrict_plane_x(next_x_mid)
    next_y_low = restrict_plane_y(next_y_mid)
    coeffs_low = level_coeffs(
        absorb_low, face_low[0], face_low[1], face_low[2], next_x_low, next_y_low, 0.0625
    )
    low_iter = chebyshev_smooth(
        jnp.zeros_like(source_low), source_low, coeffs_low, COARSE_SWEEPS, True, low_finder
    )
    mid_iter = mid_iter + prolong_cells(low_iter)
    mid_update = jnp.zeros_like(source_mid)
    sweep = 0
    while sweep + 1 < SWEEPS:
        mid_iter, mid_update = deep_pair(
            mid_iter, mid_update, rim, weights[sweep], weights[sweep + 1], False
        )
        sweep = sweep + 2
    fine_iter = fine_iter + prolong_cells(mid_iter)
    return chebyshev_smooth(fine_iter, source, coeffs_fine, SWEEPS, False, fine_finder)


def solution(mesh):
    return jax.shard_map(
        local,
        mesh=mesh,
        in_specs=(
            P("gx", "gy", None),
            P("gx", "gy", None),
            P("gx", "gy", None),
            P("gx", "gy", None),
            P("gx", "gy", None),
            P("gx", "gy", None),
        ),
        out_specs=P("gx", "gy", None),
        check_vma=False,
    )
```

profile of v0, /device:TPU:0, one launch (start us, length us, event | category | flops | bytes accessed | tf_op | source)
XLA Modules:
  0.0 270.3 jit_solution(9279728046487276656)
XLA Ops:
  1.3 3.3 %collective-permute-start.1 = (f32[1,16,256]{2,1,0:T(8,128)}, f32[1,16,256]{2,1,0:T(8,128)S(1)}, u32[]{:S(2)}, u32[]{:S(2)}) collective-permute-start(f32[1,16,256]{2,1,0:T(8,128)} %slice.985), channel_id=1, source_target_pairs={{4,0},{8,4},{12,8},{16,12},{20,16},{24,20},{28,24},{0,28},{5,1},{9... | collective-permute-start | bytes 49160 | tf_op jit(solution)/shard_map/ppermute | solution.py:27
  6.1 3.6 %collective-permute-start.4 = (f32[8,1,256]{2,1,0:T(1,128)}, f32[8,1,256]{2,1,0:T(1,128)S(1)}, u32[]{:S(2)}, u32[]{:S(2)}) collective-permute-start(f32[8,1,256]{2,1,0:T(1,128)} %slice.991), channel_id=1, source_target_pairs={{1,0},{2,1},{3,2},{0,3},{5,4},{6,5},{7,6},{4,7},{9,8},{10,9},{11,1... | collective-permute-start | bytes 24584 | tf_op jit(solution)/shard_map/ppermute | solution.py:27
  10.4 2.6 collective-permute-start.2
  16.6 10.5 %reshape.120 = f32[4,2,8,2,128,2]{5,4,3,2,1,0:T(8,128)} reshape(f32[8,16,256]{2,1,0:T(8,128)} %param.8) | data formatting | bytes 262144 | tf_op jit(solution)/shard_map/reshape | solution.py:32
  27.1 4.1 %reduce_sum.127 = f32[4,8,128]{2,1,0:T(8,128)S(1)} reduce(f32[4,2,8,2,128,2]{5,4,3,2,1,0:T(8,128)} %reshape.120, f32[]{:T(128)} %constant.20.clone.1), dimensions={1,3,5}, to_apply=%region_1.0 | reduce | flops 28672 | bytes 147460 | tf_op jit(solution)/shard_map/reduce_sum | solution.py:32
  31.9 2.8 %reduce_sum.128 = f32[4,8,128]{0,2,1:T(8,128)} reduce(f32[4,8,2,128,2]{0,4,3,2,1:T(2,128)S(1)} %bitcast.19, f32[]{:T(128)} %constant.20.clone.1), dimensions={2,4}, to_apply=%region_2.0 | reduce | flops 12288 | bytes 81924 | tf_op jit(solution)/shard_map/reduce_sum | solution.py:38
  39.7 3.8 %collective-permute-start.5 = (f32[10,1,256]{2,1,0:T(1,128)S(1)}, f32[10,1,256]{2,1,0:T(1,128)S(1)}, u32[]{:S(2)}, u32[]{:S(2)}) collective-permute-start(f32[10,1,256]{2,1,0:T(1,128)S(1)} %get-tuple-element.64), channel_id=1, source_target_pairs={{1,0},{2,1},{3,2},{0,3},{5,4},{6,5},{7,6},{4,7},{9,8},{10,9},{11,1... | collective-permute-start | bytes 30728 | tf_op jit(solution)/shard_map/ppermute | solution.py:19
  46.4 2.6 collective-permute-start.7
  50.5 3.9 %collective-permute-start.9 = (f32[10,1,256]{2,1,0:T(1,128)S(1)}, f32[10,1,256]{2,1,0:T(1,128)S(1)}, u32[]{:S(2)}, u32[]{:S(2)}) collective-permute-start(f32[10,1,256]{2,1,0:T(1,128)S(1)} %get-tuple-element.62), channel_id=1, source_target_pairs={{1,0},{2,1},{3,2},{0,3},{5,4},{6,5},{7,6},{4,7},{9,8},{10,9},{11,1... | collective-permute-start | bytes 30728 | tf_op jit(solution)/shard_map/ppermute | solution.py:19
  61.6 2.8 %collective-permute-start.13 = (f32[10,1,256]{2,1,0:T(1,128)S(1)}, f32[10,1,256]{2,1,0:T(1,128)S(1)}, u32[]{:S(2)}, u32[]{:S(2)}) collective-permute-start(f32[10,1,256]{2,1,0:T(1,128)S(1)} %get-tuple-element.60), channel_id=1, source_target_pairs={{1,0},{2,1},{3,2},{0,3},{5,4},{6,5},{7,6},{4,7},{9,8},{10,9},{11,1... | collective-permute-start | bytes 30728 | tf_op jit(solution)/shard_map/ppermute | solution.py:19
  66.3 2.6 collective-permute-start.15
  71.7 2.7 collective-permute-start.17
  76.3 2.6 collective-permute-start.19
  81.7 2.7 collective-permute-start.21
  86.1 9.8 %reshape.119 = f32[4,2,8,2,128,2]{5,4,3,2,1,0:T(8,128)} reshape(f32[8,16,256]{2,1,0:T(8,128)S(1)} %fusion.78) | data formatting | bytes 262144 | tf_op jit(solution)/shard_map/reshape | solution.py:32
  95.9 4.0 %reduce_sum.126 = f32[4,8,128]{2,1,0:T(8,128)S(1)} reduce(f32[4,2,8,2,128,2]{5,4,3,2,1,0:T(8,128)} %reshape.119, f32[]{:T(128)} %constant.20.clone.1), dimensions={1,3,5}, to_apply=%region_0.0 | reduce | flops 28672 | bytes 147460 | tf_op jit(solution)/shard_map/reduce_sum | solution.py:32
  100.0 2.6 collective-permute-start.23
  105.5 2.7 collective-permute-start.25
  108.2 2.6 collective-permute-start.27
  112.7 3.8 %collective-permute-start.29 = (f32[8,2,640]{2,0,1:T(8,128)S(1)}, f32[8,2,640]{2,0,1:T(8,128)S(1)}, u32[]{:S(2)}, u32[]{:S(2)}) collective-permute-start(f32[8,2,640]{2,0,1:T(8,128)S(1)} %copy.175), channel_id=1, source_target_pairs={{1,0},{2,1},{3,2},{0,3},{5,4},{6,5},{7,6},{4,7},{9,8},{10,9},{11,1... | collective-permute-start | bytes 122888 | tf_op jit(solution)/shard_map/ppermute | solution.py:19
  119.1 2.6 collective-permute-start.31
  123.2 3.8 %collective-permute-start.33 = (f32[8,2,256]{2,1,0:T(2,128)S(1)}, f32[8,2,256]{2,1,0:T(2,128)S(1)}, u32[]{:S(2)}, u32[]{:S(2)}) collective-permute-start(f32[8,2,256]{2,1,0:T(2,128)S(1)} %get-tuple-element.116), channel_id=1, source_target_pairs={{1,0},{2,1},{3,2},{0,3},{5,4},{6,5},{7,6},{4,7},{9,8},{10,9},{11,1... | collective-permute-start | bytes 49160 | tf_op jit(solution)/shard_map/ppermute | solution.py:19
  130.4 2.6 collective-permute-start.35
  135.5 2.8 %collective-permute-start.37 = (f32[4,1,64]{2,1,0:T(1,128)S(1)}, f32[4,1,64]{2,1,0:T(1,128)S(1)}, u32[]{:S(2)}, u32[]{:S(2)}) collective-permute-start(f32[4,1,64]{2,1,0:T(1,128)S(1)} %get-tuple-element.157), channel_id=1, source_target_pairs={{1,0},{2,1},{3,2},{0,3},{5,4},{6,5},{7,6},{4,7},{9,8},{10,9},{11,1... | collective-permute-start | bytes 3080 | tf_op jit(solution)/shard_map/ppermute | solution.py:19
  140.0 2.6 collective-permute-start.39
  145.2 2.7 collective-permute-start.41
  149.6 2.6 collective-permute-start.43
  154.8 2.7 collective-permute-start.45
  159.2 2.6 collective-permute-start.47
  164.4 2.7 collective-permute-start.49
  168.7 2.6 collective-permute-start.51
  174.0 2.7 collective-permute-start.53
  178.3 2.6 collective-permute-start.55
  183.6 2.7 collective-permute-start.57
  187.9 2.6 collective-permute-start.59
  193.2 2.7 collective-permute-start.61
  198.2 2.6 collective-permute-start.63
  203.6 2.9 %collective-permute-start.65 = (f32[8,2,256]{2,1,0:T(2,128)S(1)}, f32[8,2,256]{2,1,0:T(2,128)S(1)}, u32[]{:S(2)}, u32[]{:S(2)}) collective-permute-start(f32[8,2,256]{2,1,0:T(2,128)S(1)} %get-tuple-element.114), channel_id=1, source_target_pairs={{1,0},{2,1},{3,2},{0,3},{5,4},{6,5},{7,6},{4,7},{9,8},{10,9},{11,1... | collective-permute-start | bytes 49160 | tf_op jit(solution)/shard_map/ppermute | solution.py:19
  208.4 2.6 collective-permute-start.67
  213.8 2.9 %collective-permute-start.69 = (f32[8,2,256]{2,1,0:T(2,128)S(1)}, f32[8,2,256]{2,1,0:T(2,128)S(1)}, u32[]{:S(2)}, u32[]{:S(2)}) collective-permute-start(f32[8,2,256]{2,1,0:T(2,128)S(1)} %get-tuple-element.112), channel_id=1, source_target_pairs={{1,0},{2,1},{3,2},{0,3},{5,4},{6,5},{7,6},{4,7},{9,8},{10,9},{11,1... | collective-permute-start | bytes 49160 | tf_op jit(solution)/shard_map/ppermute | solution.py:19
  218.8 3.9 %broadcast_in_dim.5 = f32[4,2,8,2,128,2]{5,4,3,2,1,0:T(8,128)} broadcast(f32[4,8,128]{2,1,0:T(8,128)S(1)} %fusion.241), dimensions={0,2,4} | broadcast | bytes 147456 | tf_op jit(solution)/shard_map/broadcast_in_dim | solution.py:60
  222.7 6.9 %reshape.131 = f32[8,16,256]{2,1,0:T(8,128)S(1)} reshape(f32[4,2,8,2,128,2]{5,4,3,2,1,0:T(8,128)} %broadcast_in_dim.5) | data formatting | bytes 262144 | tf_op jit(solution)/shard_map/reshape | solution.py:61
  229.8 2.6 collective-permute-start.71
  235.0 2.8 %collective-permute-start.73 = (f32[10,1,256]{2,1,0:T(1,128)S(1)}, f32[10,1,256]{2,1,0:T(1,128)S(1)}, u32[]{:S(2)}, u32[]{:S(2)}) collective-permute-start(f32[10,1,256]{2,1,0:T(1,128)S(1)} %get-tuple-element.52), channel_id=1, source_target_pairs={{1,0},{2,1},{3,2},{0,3},{5,4},{6,5},{7,6},{4,7},{9,8},{10,9},{11,1... | collective-permute-start | bytes 30728 | tf_op jit(solution)/shard_map/ppermute | solution.py:19
  239.7 2.6 collective-permute-start.75
  245.2 2.7 collective-permute-start.77
  255.2 2.7 collective-permute-start.81
  265.1 2.7 collective-permute-start.85
  (306 shorter events, 111.4 us)
Async XLA Ops:
  1.3 42.7 %collective-permute-start.1 = (f32[1,16,256]{2,1,0:T(8,128)}, f32[1,16,256]{2,1,0:T(8,128)S(1)}, u32[]{:S(2)}, u32[]{:S(2)}) collective-permute-start(f32[1,16,256]{2,1,0:T(8,128)} %slice.985), channel_id=1, source_target_pairs={{4,0},{8,4},{12,8},{16,12},{20,16},{24,20},{28,24},{0,28},{5,1},{9... | collective-permute-start | bytes 49160 | tf_op jit(solution)/shard_map/ppermute | solution.py:27
  6.1 37.9 %collective-permute-start.4 = (f32[8,1,256]{2,1,0:T(1,128)}, f32[8,1,256]{2,1,0:T(1,128)S(1)}, u32[]{:S(2)}, u32[]{:S(2)}) collective-permute-start(f32[8,1,256]{2,1,0:T(1,128)} %slice.991), channel_id=1, source_target_pairs={{1,0},{2,1},{3,2},{0,3},{5,4},{6,5},{7,6},{4,7},{9,8},{10,9},{11,1... | collective-permute-start | bytes 24584 | tf_op jit(solution)/shard_map/ppermute | solution.py:27
  10.4 29.1 %collective-permute-start = (f32[1,16,256]{2,1,0:T(8,128)S(1)}, f32[1,16,256]{2,1,0:T(8,128)S(1)}, u32[]{:S(2)}, u32[]{:S(2)}) collective-permute-start(f32[1,16,256]{2,1,0:T(8,128)S(1)} %get-tuple-element.106), channel_id=1, source_target_pairs={{0,4},{4,8},{8,12},{12,16},{16,20},{20,24},{24,28},{28,0},{1,5},{5... | collective-permute-start | bytes 49160 | tf_op jit(solution)/shard_map/ppermute | solution.py:16
  10.4 29.2 %collective-permute-start.2 = (f32[1,16,256]{2,1,0:T(8,128)S(1)}, f32[1,16,256]{2,1,0:T(8,128)S(1)}, u32[]{:S(2)}, u32[]{:S(2)}) collective-permute-start(f32[1,16,256]{2,1,0:T(8,128)S(1)} %get-tuple-element.105), channel_id=1, source_target_pairs={{4,0},{8,4},{12,8},{16,12},{20,16},{24,20},{28,24},{0,28},{5,1},{9... | collective-permute-start | bytes 49160 | tf_op jit(solution)/shard_map/ppermute | solution.py:19
  39.6 5.5 %collective-permute-start.3 = (f32[10,1,256]{2,1,0:T(1,128)S(1)}, f32[10,1,256]{2,1,0:T(1,128)S(1)}, u32[]{:S(2)}, u32[]{:S(2)}) collective-permute-start(f32[10,1,256]{2,1,0:T(1,128)S(1)} %get-tuple-element.63), channel_id=1, source_target_pairs={{0,1},{1,2},{2,3},{3,0},{4,5},{5,6},{6,7},{7,4},{8,9},{9,10},{10,1... | collective-permute-start | bytes 30728 | tf_op jit(solution)/shard_map/ppermute | solution.py:16
  39.7 5.5 %collective-permute-start.5 = (f32[10,1,256]{2,1,0:T(1,128)S(1)}, f32[10,1,256]{2,1,0:T(1,128)S(1)}, u32[]{:S(2)}, u32[]{:S(2)}) collective-permute-start(f32[10,1,256]{2,1,0:T(1,128)S(1)} %get-tuple-element.64), channel_id=1, source_target_pairs={{1,0},{2,1},{3,2},{0,3},{5,4},{6,5},{7,6},{4,7},{9,8},{10,9},{11,1... | collective-permute-start | bytes 30728 | tf_op jit(solution)/shard_map/ppermute | solution.py:19
  50.5 5.5 %collective-permute-start.8 = (f32[10,1,256]{2,1,0:T(1,128)S(1)}, f32[10,1,256]{2,1,0:T(1,128)S(1)}, u32[]{:S(2)}, u32[]{:S(2)}) collective-permute-start(f32[10,1,256]{2,1,0:T(1,128)S(1)} %get-tuple-element.61), channel_id=1, source_target_pairs={{0,1},{1,2},{2,3},{3,0},{4,5},{5,6},{6,7},{7,4},{8,9},{9,10},{10,1... | collective-permute-start | bytes 30728 | tf_op jit(solution)/shard_map/ppermute | solution.py:16
  50.5 5.5 %collective-permute-start.9 = (f32[10,1,256]{2,1,0:T(1,128)S(1)}, f32[10,1,256]{2,1,0:T(1,128)S(1)}, u32[]{:S(2)}, u32[]{:S(2)}) collective-permute-start(f32[10,1,256]{2,1,0:T(1,128)S(1)} %get-tuple-element.62), channel_id=1, source_target_pairs={{1,0},{2,1},{3,2},{0,3},{5,4},{6,5},{7,6},{4,7},{9,8},{10,9},{11,1... | collective-permute-start | bytes 30728 | tf_op jit(solution)/shard_map/ppermute | solution.py:19
  60.4 5.6 %collective-permute-start.12 = (f32[10,1,256]{2,1,0:T(1,128)S(1)}, f32[10,1,256]{2,1,0:T(1,128)S(1)}, u32[]{:S(2)}, u32[]{:S(2)}) collective-permute-start(f32[10,1,256]{2,1,0:T(1,128)S(1)} %get-tuple-element.59), channel_id=1, source_target_pairs={{0,1},{1,2},{2,3},{3,0},{4,5},{5,6},{6,7},{7,4},{8,9},{9,10},{10,1... | collective-permute-start | bytes 30728 | tf_op jit(solution)/shard_map/ppermute | solution.py:16
  61.6 4.4 %collective-permute-start.13 = (f32[10,1,256]{2,1,0:T(1,128)S(1)}, f32[10,1,256]{2,1,0:T(1,128)S(1)}, u32[]{:S(2)}, u32[]{:S(2)}) collective-permute-start(f32[10,1,256]{2,1,0:T(1,128)S(1)} %get-tuple-element.60), channel_id=1, source_target_pairs={{1,0},{2,1},{3,2},{0,3},{5,4},{6,5},{7,6},{4,7},{9,8},{10,9},{11,1... | collective-permute-start | bytes 30728 | tf_op jit(solution)/shard_map/ppermute | solution.py:19
  70.4 5.6 %collective-permute-start.16 = (f32[10,1,256]{2,1,0:T(1,128)S(1)}, f32[10,1,256]{2,1,0:T(1,128)S(1)}, u32[]{:S(2)}, u32[]{:S(2)}) collective-permute-start(f32[10,1,256]{2,1,0:T(1,128)S(1)} %get-tuple-element.57), channel_id=1, source_target_pairs={{0,1},{1,2},{2,3},{3,0},{4,5},{5,6},{6,7},{7,4},{8,9},{9,10},{10,1... | collective-permute-start | bytes 30728 | tf_op jit(solution)/shard_map/ppermute | solution.py:16
  71.7 4.3 %collective-permute-start.17 = (f32[10,1,256]{2,1,0:T(1,128)S(1)}, f32[10,1,256]{2,1,0:T(1,128)S(1)}, u32[]{:S(2)}, u32[]{:S(2)}) collective-permute-start(f32[10,1,256]{2,1,0:T(1,128)S(1)} %get-tuple-element.58), channel_id=1, source_target_pairs={{1,0},{2,1},{3,2},{0,3},{5,4},{6,5},{7,6},{4,7},{9,8},{10,9},{11,1... | collective-permute-start | bytes 30728 | tf_op jit(solution)/shard_map/ppermute | solution.py:19
  80.4 5.6 %collective-permute-start.20 = (f32[10,1,256]{2,1,0:T(1,128)S(1)}, f32[10,1,256]{2,1,0:T(1,128)S(1)}, u32[]{:S(2)}, u32[]{:S(2)}) collective-permute-start(f32[10,1,256]{2,1,0:T(1,128)S(1)} %get-tuple-element.55), channel_id=1, source_target_pairs={{0,1},{1,2},{2,3},{3,0},{4,5},{5,6},{6,7},{7,4},{8,9},{9,10},{10,1... | collective-permute-start | bytes 30728 | tf_op jit(solution)/shard_map/ppermute | solution.py:16
  81.7 4.3 %collective-permute-start.21 = (f32[10,1,256]{2,1,0:T(1,128)S(1)}, f32[10,1,256]{2,1,0:T(1,128)S(1)}, u32[]{:S(2)}, u32[]{:S(2)}) collective-permute-start(f32[10,1,256]{2,1,0:T(1,128)S(1)} %get-tuple-element.56), channel_id=1, source_target_pairs={{1,0},{2,1},{3,2},{0,3},{5,4},{6,5},{7,6},{4,7},{9,8},{10,9},{11,1... | collective-permute-start | bytes 30728 | tf_op jit(solution)/shard_map/ppermute | solution.py:19
  104.1 6.7 %collective-permute-start.24 = (f32[8,2,256]{2,1,0:T(2,128)S(1)}, f32[8,2,256]{2,1,0:T(2,128)S(1)}, u32[]{:S(2)}, u32[]{:S(2)}) collective-permute-start(f32[8,2,256]{2,1,0:T(2,128)S(1)} %get-tuple-element.125), channel_id=1, source_target_pairs={{0,1},{1,2},{2,3},{3,0},{4,5},{5,6},{6,7},{7,4},{8,9},{9,10},{10,1... | collective-permute-start | bytes 49160 | tf_op jit(solution)/shard_map/ppermute | solution.py:16
  105.5 5.3 %collective-permute-start.25 = (f32[8,2,256]{2,1,0:T(2,128)S(1)}, f32[8,2,256]{2,1,0:T(2,128)S(1)}, u32[]{:S(2)}, u32[]{:S(2)}) collective-permute-start(f32[8,2,256]{2,1,0:T(2,128)S(1)} %get-tuple-element.126), channel_id=1, source_target_pairs={{1,0},{2,1},{3,2},{0,3},{5,4},{6,5},{7,6},{4,7},{9,8},{10,9},{11,1... | collective-permute-start | bytes 49160 | tf_op jit(solution)/shard_map/ppermute | solution.py:19
  108.1 4.5 %collective-permute-start.26 = (f32[2,8,640]{2,1,0:T(8,128)S(1)}, f32[2,8,640]{2,1,0:T(8,128)S(1)}, u32[]{:S(2)}, u32[]{:S(2)}) collective-permute-start(f32[2,8,640]{2,1,0:T(8,128)S(1)} %get-tuple-element.109), channel_id=1, source_target_pairs={{0,4},{4,8},{8,12},{12,16},{16,20},{20,24},{24,28},{28,0},{1,5},{5... | collective-permute-start | bytes 122888 | tf_op jit(solution)/shard_map/ppermute | solution.py:16
  108.2 4.5 %collective-permute-start.27 = (f32[2,8,640]{2,1,0:T(8,128)S(1)}, f32[2,8,640]{2,1,0:T(8,128)S(1)}, u32[]{:S(2)}, u32[]{:S(2)}) collective-permute-start(f32[2,8,640]{2,1,0:T(8,128)S(1)} %get-tuple-element.110), channel_id=1, source_target_pairs={{4,0},{8,4},{12,8},{16,12},{20,16},{24,20},{28,24},{0,28},{5,1},{9... | collective-permute-start | bytes 122888 | tf_op jit(solution)/shard_map/ppermute | solution.py:19
  112.7 5.9 %collective-permute-start.28 = (f32[8,2,640]{2,0,1:T(8,128)S(1)}, f32[8,2,640]{2,0,1:T(8,128)S(1)}, u32[]{:S(2)}, u32[]{:S(2)}) collective-permute-start(f32[8,2,640]{2,0,1:T(8,128)S(1)} %copy.174), channel_id=1, source_target_pairs={{0,1},{1,2},{2,3},{3,0},{4,5},{5,6},{6,7},{7,4},{8,9},{9,10},{10,1... | collective-permute-start | bytes 122888 | tf_op jit(solution)/shard_map/ppermute | solution.py:16
  112.7 5.8 %collective-permute-start.29 = (f32[8,2,640]{2,0,1:T(8,128)S(1)}, f32[8,2,640]{2,0,1:T(8,128)S(1)}, u32[]{:S(2)}, u32[]{:S(2)}) collective-permute-start(f32[8,2,640]{2,0,1:T(8,128)S(1)} %copy.175), channel_id=1, source_target_pairs={{1,0},{2,1},{3,2},{0,3},{5,4},{6,5},{7,6},{4,7},{9,8},{10,9},{11,1... | collective-permute-start | bytes 122888 | tf_op jit(solution)/shard_map/ppermute | solution.py:19
  123.2 5.6 %collective-permute-start.32 = (f32[8,2,256]{2,1,0:T(2,128)S(1)}, f32[8,2,256]{2,1,0:T(2,128)S(1)}, u32[]{:S(2)}, u32[]{:S(2)}) collective-permute-start(f32[8,2,256]{2,1,0:T(2,128)S(1)} %get-tuple-element.115), channel_id=1, source_target_pairs={{0,1},{1,2},{2,3},{3,0},{4,5},{5,6},{6,7},{7,4},{8,9},{9,10},{10,1... | collective-permute-start | bytes 49160 | tf_op jit(solution)/shard_map/ppermute | solution.py:16
  123.2 5.5 %collective-permute-start.33 = (f32[8,2,256]{2,1,0:T(2,128)S(1)}, f32[8,2,256]{2,1,0:T(2,128)S(1)}, u32[]{:S(2)}, u32[]{:S(2)}) collective-permute-start(f32[8,2,256]{2,1,0:T(2,128)S(1)} %get-tuple-element.116), channel_id=1, source_target_pairs={{1,0},{2,1},{3,2},{0,3},{5,4},{6,5},{7,6},{4,7},{9,8},{10,9},{11,1... | collective-permute-start | bytes 49160 | tf_op jit(solution)/shard_map/ppermute | solution.py:19
  134.4 5.5 %collective-permute-start.36 = (f32[4,1,64]{2,1,0:T(1,128)S(1)}, f32[4,1,64]{2,1,0:T(1,128)S(1)}, u32[]{:S(2)}, u32[]{:S(2)}) collective-permute-start(f32[4,1,64]{2,1,0:T(1,128)S(1)} %get-tuple-element.156), channel_id=1, source_target_pairs={{0,1},{1,2},{2,3},{3,0},{4,5},{5,6},{6,7},{7,4},{8,9},{9,10},{10,1... | collective-permute-start | bytes 3080 | tf_op jit(solution)/shard_map/ppermute | solution.py:16
  135.5 4.3 %collective-permute-start.37 = (f32[4,1,64]{2,1,0:T(1,128)S(1)}, f32[4,1,64]{2,1,0:T(1,128)S(1)}, u32[]{:S(2)}, u32[]{:S(2)}) collective-permute-start(f32[4,1,64]{2,1,0:T(1,128)S(1)} %get-tuple-element.157), channel_id=1, source_target_pairs={{1,0},{2,1},{3,2},{0,3},{5,4},{6,5},{7,6},{4,7},{9,8},{10,9},{11,1... | collective-permute-start | bytes 3080 | tf_op jit(solution)/shard_map/ppermute | solution.py:19
  143.9 5.5 %collective-permute-start.40 = (f32[4,1,64]{2,1,0:T(1,128)S(1)}, f32[4,1,64]{2,1,0:T(1,128)S(1)}, u32[]{:S(2)}, u32[]{:S(2)}) collective-permute-start(f32[4,1,64]{2,1,0:T(1,128)S(1)} %get-tuple-element.154), channel_id=1, source_target_pairs={{0,1},{1,2},{2,3},{3,0},{4,5},{5,6},{6,7},{7,4},{8,9},{9,10},{10,1... | collective-permute-start | bytes 3080 | tf_op jit(solution)/shard_map/ppermute | solution.py:16
  145.2 4.2 %collective-permute-start.41 = (f32[4,1,64]{2,1,0:T(1,128)S(1)}, f32[4,1,64]{2,1,0:T(1,128)S(1)}, u32[]{:S(2)}, u32[]{:S(2)}) collective-permute-start(f32[4,1,64]{2,1,0:T(1,128)S(1)} %get-tuple-element.155), channel_id=1, source_target_pairs={{1,0},{2,1},{3,2},{0,3},{5,4},{6,5},{7,6},{4,7},{9,8},{10,9},{11,1... | collective-permute-start | bytes 3080 | tf_op jit(solution)/shard_map/ppermute | solution.py:19
  153.5 5.5 %collective-permute-start.44 = (f32[4,1,64]{2,1,0:T(1,128)S(1)}, f32[4,1,64]{2,1,0:T(1,128)S(1)}, u32[]{:S(2)}, u32[]{:S(2)}) collective-permute-start(f32[4,1,64]{2,1,0:T(1,128)S(1)} %get-tuple-element.152), channel_id=1, source_target_pairs={{0,1},{1,2},{2,3},{3,0},{4,5},{5,6},{6,7},{7,4},{8,9},{9,10},{10,1... | collective-permute-start | bytes 3080 | tf_op jit(solution)/shard_map/ppermute | solution.py:16
  154.8 4.2 %collective-permute-start.45 = (f32[4,1,64]{2,1,0:T(1,128)S(1)}, f32[4,1,64]{2,1,0:T(1,128)S(1)}, u32[]{:S(2)}, u32[]{:S(2)}) collective-permute-start(f32[4,1,64]{2,1,0:T(1,128)S(1)} %get-tuple-element.153), channel_id=1, source_target_pairs={{1,0},{2,1},{3,2},{0,3},{5,4},{6,5},{7,6},{4,7},{9,8},{10,9},{11,1... | collective-permute-start | bytes 3080 | tf_op jit(solution)/shard_map/ppermute | solution.py:19
  163.1 5.5 %collective-permute-start.48 = (f32[4,1,64]{2,1,0:T(1,128)S(1)}, f32[4,1,64]{2,1,0:T(1,128)S(1)}, u32[]{:S(2)}, u32[]{:S(2)}) collective-permute-start(f32[4,1,64]{2,1,0:T(1,128)S(1)} %get-tuple-element.150), channel_id=1, source_target_pairs={{0,1},{1,2},{2,3},{3,0},{4,5},{5,6},{6,7},{7,4},{8,9},{9,10},{10,1... | collective-permute-start | bytes 3080 | tf_op jit(solution)/shard_map/ppermute | solution.py:16
  164.4 4.2 %collective-permute-start.49 = (f32[4,1,64]{2,1,0:T(1,128)S(1)}, f32[4,1,64]{2,1,0:T(1,128)S(1)}, u32[]{:S(2)}, u32[]{:S(2)}) collective-permute-start(f32[4,1,64]{2,1,0:T(1,128)S(1)} %get-tuple-element.151), channel_id=1, source_target_pairs={{1,0},{2,1},{3,2},{0,3},{5,4},{6,5},{7,6},{4,7},{9,8},{10,9},{11,1... | collective-permute-start | bytes 3080 | tf_op jit(solution)/shard_map/ppermute | solution.py:19
  172.7 5.5 %collective-permute-start.52 = (f32[4,1,64]{2,1,0:T(1,128)S(1)}, f32[4,1,64]{2,1,0:T(1,128)S(1)}, u32[]{:S(2)}, u32[]{:S(2)}) collective-permute-start(f32[4,1,64]{2,1,0:T(1,128)S(1)} %get-tuple-element.148), channel_id=1, source_target_pairs={{0,1},{1,2},{2,3},{3,0},{4,5},{5,6},{6,7},{7,4},{8,9},{9,10},{10,1... | collective-permute-start | bytes 3080 | tf_op jit(solution)/shard_map/ppermute | solution.py:16
  174.0 4.2 %collective-permute-start.53 = (f32[4,1,64]{2,1,0:T(1,128)S(1)}, f32[4,1,64]{2,1,0:T(1,128)S(1)}, u32[]{:S(2)}, u32[]{:S(2)}) collective-permute-start(f32[4,1,64]{2,1,0:T(1,128)S(1)} %get-tuple-element.149), channel_id=1, source_target_pairs={{1,0},{2,1},{3,2},{0,3},{5,4},{6,5},{7,6},{4,7},{9,8},{10,9},{11,1... | collective-permute-start | bytes 3080 | tf_op jit(solution)/shard_map/ppermute | solution.py:19
  182.3 5.5 %collective-permute-start.56 = (f32[4,1,64]{2,1,0:T(1,128)S(1)}, f32[4,1,64]{2,1,0:T(1,128)S(1)}, u32[]{:S(2)}, u32[]{:S(2)}) collective-permute-start(f32[4,1,64]{2,1,0:T(1,128)S(1)} %get-tuple-element.146), channel_id=1, source_target_pairs={{0,1},{1,2},{2,3},{3,0},{4,5},{5,6},{6,7},{7,4},{8,9},{9,10},{10,1... | collective-permute-start | bytes 3080 | tf_op jit(solution)/shard_map/ppermute | solution.py:16
  183.6 4.2 %collective-permute-start.57 = (f32[4,1,64]{2,1,0:T(1,128)S(1)}, f32[4,1,64]{2,1,0:T(1,128)S(1)}, u32[]{:S(2)}, u32[]{:S(2)}) collective-permute-start(f32[4,1,64]{2,1,0:T(1,128)S(1)} %get-tuple-element.147), channel_id=1, source_target_pairs={{1,0},{2,1},{3,2},{0,3},{5,4},{6,5},{7,6},{4,7},{9,8},{10,9},{11,1... | collective-permute-start | bytes 3080 | tf_op jit(solution)/shard_map/ppermute | solution.py:19
  191.9 5.5 %collective-permute-start.60 = (f32[4,1,64]{2,1,0:T(1,128)S(1)}, f32[4,1,64]{2,1,0:T(1,128)S(1)}, u32[]{:S(2)}, u32[]{:S(2)}) collective-permute-start(f32[4,1,64]{2,1,0:T(1,128)S(1)} %get-tuple-element.144), channel_id=1, source_target_pairs={{0,1},{1,2},{2,3},{3,0},{4,5},{5,6},{6,7},{7,4},{8,9},{9,10},{10,1... | collective-permute-start | bytes 3080 | tf_op jit(solution)/shard_map/ppermute | solution.py:16
  193.2 4.2 %collective-permute-start.61 = (f32[4,1,64]{2,1,0:T(1,128)S(1)}, f32[4,1,64]{2,1,0:T(1,128)S(1)}, u32[]{:S(2)}, u32[]{:S(2)}) collective-permute-start(f32[4,1,64]{2,1,0:T(1,128)S(1)} %get-tuple-element.145), channel_id=1, source_target_pairs={{1,0},{2,1},{3,2},{0,3},{5,4},{6,5},{7,6},{4,7},{9,8},{10,9},{11,1... | collective-permute-start | bytes 3080 | tf_op jit(solution)/shard_map/ppermute | solution.py:19
  202.3 5.7 %collective-permute-start.64 = (f32[8,2,256]{2,1,0:T(2,128)S(1)}, f32[8,2,256]{2,1,0:T(2,128)S(1)}, u32[]{:S(2)}, u32[]{:S(2)}) collective-permute-start(f32[8,2,256]{2,1,0:T(2,128)S(1)} %get-tuple-element.113), channel_id=1, source_target_pairs={{0,1},{1,2},{2,3},{3,0},{4,5},{5,6},{6,7},{7,4},{8,9},{9,10},{10,1... | collective-permute-start | bytes 49160 | tf_op jit(solution)/shard_map/ppermute | solution.py:16
  203.6 4.3 %collective-permute-start.65 = (f32[8,2,256]{2,1,0:T(2,128)S(1)}, f32[8,2,256]{2,1,0:T(2,128)S(1)}, u32[]{:S(2)}, u32[]{:S(2)}) collective-permute-start(f32[8,2,256]{2,1,0:T(2,128)S(1)} %get-tuple-element.114), channel_id=1, source_target_pairs={{1,0},{2,1},{3,2},{0,3},{5,4},{6,5},{7,6},{4,7},{9,8},{10,9},{11,1... | collective-permute-start | bytes 49160 | tf_op jit(solution)/shard_map/ppermute | solution.py:19
  212.5 5.9 %collective-permute-start.68 = (f32[8,2,256]{2,1,0:T(2,128)S(1)}, f32[8,2,256]{2,1,0:T(2,128)S(1)}, u32[]{:S(2)}, u32[]{:S(2)}) collective-permute-start(f32[8,2,256]{2,1,0:T(2,128)S(1)} %get-tuple-element.111), channel_id=1, source_target_pairs={{0,1},{1,2},{2,3},{3,0},{4,5},{5,6},{6,7},{7,4},{8,9},{9,10},{10,1... | collective-permute-start | bytes 49160 | tf_op jit(solution)/shard_map/ppermute | solution.py:16
  213.8 4.5 %collective-permute-start.69 = (f32[8,2,256]{2,1,0:T(2,128)S(1)}, f32[8,2,256]{2,1,0:T(2,128)S(1)}, u32[]{:S(2)}, u32[]{:S(2)}) collective-permute-start(f32[8,2,256]{2,1,0:T(2,128)S(1)} %get-tuple-element.112), channel_id=1, source_target_pairs={{1,0},{2,1},{3,2},{0,3},{5,4},{6,5},{7,6},{4,7},{9,8},{10,9},{11,1... | collective-permute-start | bytes 49160 | tf_op jit(solution)/shard_map/ppermute | solution.py:19
  233.9 5.6 %collective-permute-start.72 = (f32[10,1,256]{2,1,0:T(1,128)S(1)}, f32[10,1,256]{2,1,0:T(1,128)S(1)}, u32[]{:S(2)}, u32[]{:S(2)}) collective-permute-start(f32[10,1,256]{2,1,0:T(1,128)S(1)} %get-tuple-element.51), channel_id=1, source_target_pairs={{0,1},{1,2},{2,3},{3,0},{4,5},{5,6},{6,7},{7,4},{8,9},{9,10},{10,1... | collective-permute-start | bytes 30728 | tf_op jit(solution)/shard_map/ppermute | solution.py:16
  235.0 4.4 %collective-permute-start.73 = (f32[10,1,256]{2,1,0:T(1,128)S(1)}, f32[10,1,256]{2,1,0:T(1,128)S(1)}, u32[]{:S(2)}, u32[]{:S(2)}) collective-permute-start(f32[10,1,256]{2,1,0:T(1,128)S(1)} %get-tuple-element.52), channel_id=1, source_target_pairs={{1,0},{2,1},{3,2},{0,3},{5,4},{6,5},{7,6},{4,7},{9,8},{10,9},{11,1... | collective-permute-start | bytes 30728 | tf_op jit(solution)/shard_map/ppermute | solution.py:19
  243.8 5.6 %collective-permute-start.76 = (f32[10,1,256]{2,1,0:T(1,128)S(1)}, f32[10,1,256]{2,1,0:T(1,128)S(1)}, u32[]{:S(2)}, u32[]{:S(2)}) collective-permute-start(f32[10,1,256]{2,1,0:T(1,128)S(1)} %get-tuple-element.49), channel_id=1, source_target_pairs={{0,1},{1,2},{2,3},{3,0},{4,5},{5,6},{6,7},{7,4},{8,9},{9,10},{10,1... | collective-permute-start | bytes 30728 | tf_op jit(solution)/shard_map/ppermute | solution.py:16
  245.2 4.3 %collective-permute-start.77 = (f32[10,1,256]{2,1,0:T(1,128)S(1)}, f32[10,1,256]{2,1,0:T(1,128)S(1)}, u32[]{:S(2)}, u32[]{:S(2)}) collective-permute-start(f32[10,1,256]{2,1,0:T(1,128)S(1)} %get-tuple-element.50), channel_id=1, source_target_pairs={{1,0},{2,1},{3,2},{0,3},{5,4},{6,5},{7,6},{4,7},{9,8},{10,9},{11,1... | collective-permute-start | bytes 30728 | tf_op jit(solution)/shard_map/ppermute | solution.py:19
  253.8 5.6 %collective-permute-start.80 = (f32[10,1,256]{2,1,0:T(1,128)S(1)}, f32[10,1,256]{2,1,0:T(1,128)S(1)}, u32[]{:S(2)}, u32[]{:S(2)}) collective-permute-start(f32[10,1,256]{2,1,0:T(1,128)S(1)} %get-tuple-element.47), channel_id=1, source_target_pairs={{0,1},{1,2},{2,3},{3,0},{4,5},{5,6},{6,7},{7,4},{8,9},{9,10},{10,1... | collective-permute-start | bytes 30728 | tf_op jit(solution)/shard_map/ppermute | solution.py:16
  255.2 4.3 %collective-permute-start.81 = (f32[10,1,256]{2,1,0:T(1,128)S(1)}, f32[10,1,256]{2,1,0:T(1,128)S(1)}, u32[]{:S(2)}, u32[]{:S(2)}) collective-permute-start(f32[10,1,256]{2,1,0:T(1,128)S(1)} %get-tuple-element.48), channel_id=1, source_target_pairs={{1,0},{2,1},{3,2},{0,3},{5,4},{6,5},{7,6},{4,7},{9,8},{10,9},{11,1... | collective-permute-start | bytes 30728 | tf_op jit(solution)/shard_map/ppermute | solution.py:19
  263.8 5.6 %collective-permute-start.84 = (f32[10,1,256]{2,1,0:T(1,128)S(1)}, f32[10,1,256]{2,1,0:T(1,128)S(1)}, u32[]{:S(2)}, u32[]{:S(2)}) collective-permute-start(f32[10,1,256]{2,1,0:T(1,128)S(1)} %get-tuple-element.45), channel_id=1, source_target_pairs={{0,1},{1,2},{2,3},{3,0},{4,5},{5,6},{6,7},{7,4},{8,9},{9,10},{10,1... | collective-permute-start | bytes 30728 | tf_op jit(solution)/shard_map/ppermute | solution.py:16
  265.1 4.3 %collective-permute-start.85 = (f32[10,1,256]{2,1,0:T(1,128)S(1)}, f32[10,1,256]{2,1,0:T(1,128)S(1)}, u32[]{:S(2)}, u32[]{:S(2)}) collective-permute-start(f32[10,1,256]{2,1,0:T(1,128)S(1)} %get-tuple-element.46), channel_id=1, source_target_pairs={{1,0},{2,1},{3,2},{0,3},{5,4},{6,5},{7,6},{4,7},{9,8},{10,9},{11,1... | collective-permute-start | bytes 30728 | tf_op jit(solution)/shard_map/ppermute | solution.py:19
  (44 other events, 245.3 us)
where the time goes:
time: 271 us; the launch traced here: 270 us
  starting transfers between devices  147 us (54%)
  waiting for transfers between devices  53.1 us (20%)
  local copies, waits for them, and re-layouts  50.5 us (19%)
  other arithmetic  18.6 us (7%)
    ppermute x42, starting transfers between devices, extended(): lax.ppermute(lax.slice_in_dim(block, 0, width, axis=dim), axis, backward)  117 us
    ppermute x42, waiting for transfers between devices, extended(): lax.ppermute(lax.slice_in_dim(block, block.shape[dim] - width, None, axis...  52.4 us
    ppermute x42, starting transfers between devices, extended(): lax.ppermute(lax.slice_in_dim(block, block.shape[dim] - width, None, axis...  23.3 us
    reshape x3, local copies, waits for them, and re-layouts, restrict_cells(): field.reshape(size_x // 2, 2, size_y // 2, 2, size_z // 2, 2)  21.3 us
    reduce_sum x4, other arithmetic, restrict_cells(): field.reshape(size_x // 2, 2, size_y // 2, 2, size_z // 2, 2)  8.43 us
    reshape x2, local copies, waits for them, and re-layouts, prolong_cells(): return spread.reshape(2 * size_x, 2 * size_y, 2 * size_z)  7.41 us
    ppermute x2, starting transfers between devices, passed_along(): return lax.ppermute(block, axis, route)  6.94 us
  transfers between devices with their start and end apart: 86, of which 40 were waited for; matrix products, arithmetic and copies ran while one was open for 13% of the time, Pallas kernels for 0%

commit v1 on v0

v1 whole, which is shorter than its diff:
```python
import functools

import jax
import jax.numpy as jnp
from jax import lax
from jax.experimental import pallas as pl
from jax.experimental.pallas import tpu as pltpu
from jax.sharding import PartitionSpec as P

SWEEPS = 4
COARSE_SWEEPS = 8
F32 = jnp.float32
TILE = (8, 128)
PAD = 8
FINE = 5
MID = 6


def chebyshev_weights(sweeps):
    cheb_theta = 1.125
    cheb_delta = 0.875
    cheb_sigma = cheb_theta / cheb_delta
    rho_old = 1.0 / cheb_sigma
    weights = [(0.0, 1.0 / cheb_theta)]
    for sweep in range(1, sweeps):
        rho_new = 1.0 / (2.0 * cheb_sigma - rho_old)
        weights.append((rho_new * rho_old, 2.0 * rho_new / cheb_delta))
        rho_old = rho_new
    return weights


def iota(shape, axis):
    return lax.broadcasted_iota(jnp.int32, shape, axis)


def selector(rows, columns, hit):
    return jnp.where(hit(iota((rows, columns), 0), iota((rows, columns), 1)), 1.0, 0.0).astype(F32)


def pair_sum(size):
    return selector(size, size // 2, lambda k, m: k // 2 == m)


def pair_copy(size):
    return selector(size, 2 * size, lambda k, m: k == m // 2)


def dot(left, right):
    return lax.dot(left, right, precision=lax.Precision.HIGHEST, preferred_element_type=F32)


def roll(value, shift, axis):
    return pltpu.roll(value, shift % value.shape[axis], axis)


class Writer:
    def __init__(self, ref):
        self.ref, self.at = ref, 0

    def put(self, value):
        rows, columns = value.shape
        for r in range(0, rows, TILE[0]):
            for c in range(0, columns, TILE[1]):
                self.ref[self.at] = value[r : r + TILE[0], c : c + TILE[1]]
                self.at += 1


class Reader:
    def __init__(self, ref, at=0):
        self.ref, self.at = ref, at

    def get(self, rows, columns):
        lines = []
        for _ in range(rows // TILE[0]):
            parts = []
            for _ in range(columns // TILE[1]):
                parts.append(self.ref[self.at])
                self.at += 1
            lines.append(parts[0] if len(parts) == 1 else jnp.concatenate(parts, axis=1))
        return lines[0] if len(lines) == 1 else jnp.concatenate(lines, axis=0)


UP_PLANES = (5, 4, 4, 4, 4, 4)
DOWN_PLANES = (5, 4, 4, 5, 4, 4)
UP_CORNER = (4, 3, 3, 3, 4, 3)
DOWN_CORNER = (4, 3, 3, 4, 4, 3)


def tiles_of(rows, columns):
    return (rows // TILE[0]) * (columns // TILE[1])


def is_upper(width):
    return iota((TILE[0], width), 0) < TILE[0] // 2


def shifted(value, axis, step):
    count = lax.axis_size(axis)
    return lax.ppermute(value, axis, [(i, (i + step) % count) for i in range(count)])


def pack_kernel(
    ini, src, absorb, face_x, face_y, face_z, up_x, down_x, up_y, down_y, mid, low, rows_mid
):
    fields = (ini, src, absorb, face_x, face_y, face_z)
    size_x, size_y, size_z = ini.shape
    half = size_y // 2
    blocks = range(0, size_x, 2)

    def both_planes(ref):
        return [ref[plane] + ref[plane + 1] for plane in blocks]

    stacked = both_planes(absorb) + [face_x[plane] for plane in blocks] + both_planes(face_y)
    summed = dot(jnp.concatenate(stacked, axis=0), pair_sum(size_z))
    picked = dot(
        jnp.concatenate(both_planes(face_z), axis=0),
        selector(size_z, size_z // 2, lambda k, m: k == 2 * m),
    )
    count = summed.shape[0]
    rows_mid[:count] = summed
    rows_mid[count:] = picked
    out = Writer(mid)
    for array, (factor, sides) in enumerate(((0.125, 2), (0.25, 2), (0.25, 1), (0.25, 2))):
        lines = (size_x // 2) * half
        start = 2 * array * lines
        total = rows_mid[pl.ds(start, lines, 2), :]
        if sides == 2:
            total = total + rows_mid[pl.ds(start + 1, lines, 2), :]
        out.put(total * factor)

    mid_x, mid_z = size_x // 2, size_z // 2
    both = (0, 1)
    low_z = mid_z // 2

    def coarser(array, planes, sides):
        lines = []
        for block in range(mid_x // 2):
            total = None
            for plane in planes:
                for side in sides:
                    at = array * mid_x + 2 * block + plane
                    part = mid[at, pl.ds(side, half // 2, 2), :]
                    total = part if total is None else total + part
            lines.append(total)
        return jnp.concatenate(lines, axis=0)

    left = selector(mid_z, mid_z, lambda k, m: k // 2 == m)
    right = selector(mid_z, mid_z, lambda k, m: k // 2 == m - low_z)
    evens = selector(mid_z, mid_z, lambda k, m: k == 2 * m)
    low[0] = dot(coarser(0, both, both) * 0.125, right)
    low[1] = dot(coarser(1, (0,), both) * 0.25, left) + dot(coarser(2, both, (0,)) * 0.25, right)
    low[2] = dot(coarser(3, both, both) * 0.25, evens)

    tops, bottoms = Writer(up_x), Writer(down_x)
    for ref, count in zip(fields, UP_PLANES):
        for plane in range(size_x - count, size_x):
            tops.put(ref[plane])
    for ref, count in zip(fields, DOWN_PLANES):
        for plane in range(count):
            bottoms.put(ref[plane])

    upper = is_upper(size_z)
    tops_y, bottoms_y = Writer(up_y), Writer(down_y)
    for ref in fields:
        for pair in range(0, size_x, 2):
            one, two = ref[pair], ref[pair + 1]
            tops_y.put(jnp.where(upper, roll(one[size_y - 8 :], 4, 0), two[size_y - 8 :]))
            bottoms_y.put(jnp.where(upper, one[:8], roll(two[:8], 4, 0)))
    tops_y.put(ini[:, size_y - 5, :])
    bottoms_y.put(ini[:, 4, :])
    bottoms_y.put(face_y[:, 4, :])
    for writer in (tops, bottoms, tops_y, bottoms_y):
        for tile in range(mid.shape[0]):
            writer.put(mid[tile])


def corner_of(low_y, high_y, plane, upper, first_tile=0):
    width = upper.shape[1]
    at = first_tile + (plane // 2) * tiles_of(8, width)
    low = Reader(low_y, at).get(8, width)
    high = Reader(high_y, at).get(8, width)
    if plane % 2 == 0:
        return jnp.where(upper, low, roll(high, 4, 0))
    return jnp.where(upper, roll(low, 4, 0), high)


def corner_kernel(size_x, size_z, low_y, high_y, up, down):
    upper = is_upper(size_z)
    per_field = (size_x // 2) * tiles_of(8, size_z)
    tops, bottoms = Writer(up), Writer(down)
    for field in range(6):
        for plane in range(size_x - UP_CORNER[field], size_x):
            tops.put(corner_of(low_y, high_y, plane, upper, field * per_field))
        for plane in range(DOWN_CORNER[field]):
            bottoms.put(corner_of(low_y, high_y, plane, upper, field * per_field))
    mid_tiles = 4 * (size_x // 2)
    for writer in (tops, bottoms):
        for ref in (low_y, high_y):
            for tile in range(ref.shape[0] - mid_tiles, ref.shape[0]):
                writer.put(ref[tile])


def scale_coeffs(scale, absorb, face_x, face_y, face_z, coeffs, diagonal, planes):
    rows, lanes = absorb.shape[1:]
    lane = iota((rows, lanes), 1)

    def body(i, carry):
        xl, xh = face_x[i], face_x[i + 1]
        yl, zl = face_y[i], face_z[i]
        yh = roll(yl, -1, 0)
        zh = jnp.where(lane == lanes - 1, 0.0, roll(zl, -1, 1))
        diag = absorb[i] + scale * (xl + xh + yl + yh + zl + zh)
        inverse = 1.0 / diag
        scaled = scale * inverse
        coeffs[0, i] = scaled * xl
        coeffs[1, i] = scaled * xh
        coeffs[2, i] = scaled * yl
        coeffs[3, i] = scaled * yh
        coeffs[4, i] = jnp.where(lane == 0, 0.0, scaled * zl)
        coeffs[5, i] = scaled * zh
        coeffs[6, i] = inverse
        if diagonal is not None:
            diagonal[i] = diag
        return carry

    lax.fori_loop(*planes, body, 0)


def scaled_remain(coeffs, target, i, below, here, above):
    total = target[i] - here
    total = total + coeffs[0, i] * below + coeffs[1, i] * above
    total = total + coeffs[2, i] * roll(here, 1, 0) + coeffs[3, i] * roll(here, -1, 0)
    return total + coeffs[4, i] * roll(here, 1, 1) + coeffs[5, i] * roll(here, -1, 1)


def sweep_window(iterate, update, coeffs, target, planes, pair, first, unroll=1):
    start, stop = planes

    def body(i, carry):
        below, here = carry
        above = iterate[i + 1]
        step = pair[1] * scaled_remain(coeffs, target, i, below, here, above)
        if not first:
            step = step + pair[0] * update[i]
        update[i] = step
        iterate[i] = here + step
        return here, above

    lax.fori_loop(start, stop, body, (iterate[start - 1], iterate[start]), unroll=unroll)


def assemble_fine(window, own, low_x, high_x, low_y, high_y, low_c, high_c, up, down, up_c, down_c, starts):
    size_x, size_y, size_z = own.shape
    for plane in range(size_x):
        window[FINE + plane, PAD : PAD + size_y] = own[plane]
    reader = Reader(low_x, starts[0])
    for plane in range(up):
        window[FINE - up + plane, PAD : PAD + size_y] = reader.get(size_y, size_z)
    reader = Reader(high_x, starts[1])
    for plane in range(down):
        window[FINE + size_x + plane, PAD : PAD + size_y] = reader.get(size_y, size_z)
    high = PAD + size_y
    low_reader, high_reader = Reader(low_y, starts[2]), Reader(high_y, starts[3])
    for pair in range(0, size_x, 2):
        tile = low_reader.get(8, size_z)
        window[FINE + pair, 0:8] = roll(tile, 4, 0)
        window[FINE + pair + 1, 0:8] = tile
        tile = high_reader.get(8, size_z)
        window[FINE + pair, high : high + 8] = tile
        window[FINE + pair + 1, high : high + 8] = roll(tile, 4, 0)
    for ref, start, first, count in (
        (low_c, starts[4], FINE - up_c, up_c),
        (high_c, starts[5], FINE + size_x, down_c),
    ):
        reader = Reader(ref, start)
        for plane in range(count):
            tile = roll(reader.get(8, size_z), 4, 0)
            window[first + plane, 0:8] = tile
            window[first + plane, high : high + 8] = tile


def fine_kernel(
    ini, src, absorb, face_x, face_y, face_z, low_x, high_x, low_y, high_y, low_c, high_c,
    iterate_out, coeffs, target, mid_target, up_x, down_x, up_y, down_y,
    windows, update, diagonal, rest,
):
    own = (ini, src, absorb, face_x, face_y, face_z)
    size_x, size_y, size_z = ini.shape
    plane_tiles, strip_tiles = tiles_of(size_y, size_z), tiles_of(8, size_z)
    starts = [0] * 6
    for field in range(6):
        assemble_fine(
            windows.at[field], own[field], low_x, high_x, low_y, high_y, low_c, high_c,
            UP_PLANES[field], DOWN_PLANES[field], UP_CORNER[field], DOWN_CORNER[field], tuple(starts),
        )
        starts[0] += UP_PLANES[field] * plane_tiles
        starts[1] += DOWN_PLANES[field] * plane_tiles
        starts[2] += (size_x // 2) * strip_tiles
        starts[3] += (size_x // 2) * strip_tiles
        starts[4] += UP_CORNER[field] * strip_tiles
        starts[5] += DOWN_CORNER[field] * strip_tiles
    low_line = Reader(low_y, starts[2]).get(8, size_z)
    high_reader = Reader(high_y, starts[3])
    high_line = high_reader.get(8, size_z)
    face_line = high_reader.get(8, size_z)
    high = PAD + size_y
    for plane in range(size_x):
        windows[0, FINE + plane, 3:4] = low_line[plane : plane + 1]
        windows[0, FINE + plane, high + 4 : high + 5] = high_line[plane : plane + 1]
        windows[4, FINE + plane, high + 4 : high + 5] = face_line[plane : plane + 1]

    iterate = windows.at[0]
    last = size_x + 2 * FINE - 1
    scale_coeffs(1.0, windows.at[2], windows.at[3], windows.at[4], windows.at[5], coeffs, diagonal, (1, last))

    def scale_target(i, carry):
        target[i] = windows[1, i] * coeffs[6, i]
        return carry

    lax.fori_loop(1, last, scale_target, 0)
    for sweep, pair in enumerate(chebyshev_weights(SWEEPS)):
        sweep_window(
            iterate, update, coeffs, target, (1 + sweep, last - sweep), pair, sweep == 0
        )
    mid_x, mid_y = size_x // 2, size_y // 2
    lines = []
    for block in range(mid_x):
        total = None
        for plane in (FINE + 2 * block, FINE + 2 * block + 1):
            remain = scaled_remain(coeffs, target, plane, iterate[plane - 1], iterate[plane], iterate[plane + 1])
            remain = (remain * diagonal[plane])[PAD : PAD + size_y]
            total = remain if total is None else total + remain
        lines.append(total)
    rest[...] = dot(jnp.concatenate(lines, axis=0), pair_sum(size_z))
    count = mid_x * mid_y
    coarse = (rest[pl.ds(0, count, 2), :] + rest[pl.ds(1, count, 2), :]) * 0.125
    for block in range(mid_x):
        mid_target[block] = coarse[block * mid_y : (block + 1) * mid_y]
    for plane in range(size_x):
        iterate_out[plane] = iterate[FINE + plane, PAD : PAD + size_y]

    tops, bottoms = Writer(up_x), Writer(down_x)
    for plane in range(size_x - 4, size_x):
        tops.put(iterate_out[plane])
    for plane in range(4):
        bottoms.put(iterate_out[plane])
    upper = is_upper(size_z)
    tops_y, bottoms_y = Writer(up_y), Writer(down_y)
    for pair in range(0, size_x, 2):
        one, two = iterate_out[pair], iterate_out[pair + 1]
        tops_y.put(jnp.where(upper, roll(one[size_y - 8 :], 4, 0), two[size_y - 8 :]))
        bottoms_y.put(jnp.where(upper, one[:8], roll(two[:8], 4, 0)))
    for writer in (tops, bottoms, tops_y, bottoms_y):
        writer.put(coarse)
    mids = 4 * mid_x
    near_low = [(low_c, low_c.shape[0] - 2 * mids), (low_x, low_x.shape[0] - mids), (low_c, low_c.shape[0] - mids)]
    near_high = [(high_c, high_c.shape[0] - 2 * mids), (high_x, high_x.shape[0] - mids), (high_c, high_c.shape[0] - mids)]
    for array in range(4):
        for ref, start in near_low:
            tops.put(ref[start + array * mid_x + mid_x - 1])
        for ref, start in near_high:
            bottoms.put(ref[start + array * mid_x])
    for ref, start in near_high:
        bottoms.put(ref[start + mid_x + 1])


def corner_two_kernel(size_x, size_z, low_y, high_y, up, down):
    upper = is_upper(size_z)
    tops, bottoms = Writer(up), Writer(down)
    for plane in range(size_x - 3, size_x):
        tops.put(corner_of(low_y, high_y, plane, upper))
    for plane in range(3):
        bottoms.put(corner_of(low_y, high_y, plane, upper))
    for writer in (tops, bottoms):
        for ref in (low_y, high_y):
            for tile in range(ref.shape[0] - size_x // 2, ref.shape[0]):
                writer.put(ref[tile])


def mid_kernel(
    count_x, count_y, mid, low, low_x, high_x, low_y, high_y, low_c, high_c,
    mid_target, low_x2, high_x2, low_y2, high_y2, low_c2, high_c2,
    window, target, slots,
    coeffs, diagonal, scaled, iterate, update, rest,
):
    mid_x, mid_y, mid_z = mid_target.shape
    mids = 4 * mid_x
    first = MID - mid_x
    blocks = {
        (0, 0): (low_c, low_c.shape[0] - 2 * mids), (0, 1): (low_x, low_x.shape[0] - mids),
        (0, 2): (low_c, low_c.shape[0] - mids), (1, 0): (low_y, low_y.shape[0] - mids),
        (1, 1): (mid, 0), (1, 2): (high_y, high_y.shape[0] - mids),
        (2, 0): (high_c, high_c.shape[0] - 2 * mids), (2, 1): (high_x, high_x.shape[0] - mids),
        (2, 2): (high_c, high_c.shape[0] - mids),
    }
    for (bx, by), (ref, start) in blocks.items():
        for array in range(4):
            for plane in range(mid_x):
                window[array, first + bx * mid_x + plane, by * mid_y : (by + 1) * mid_y] = ref[
                    start + array * mid_x + plane
                ]
    far = 3 * mid_x + first
    fine_tiles = 4 * tiles_of(2 * mid_y, 2 * mid_z)
    own_planes = fine_tiles + mid_x
    for array in range(4):
        for by in range(3):
            rows = slice(by * mid_y, (by + 1) * mid_y)
            window[array, first - 1, rows] = low_x2[own_planes + 3 * array + by]
            window[array, far, rows] = high_x2[own_planes + 3 * array + by]
    for by in range(3):
        window[1, far + 1, by * mid_y : (by + 1) * mid_y] = high_x2[own_planes + 12 + by]

    blocks = {
        (0, 0): (low_c2, low_c2.shape[0] - 2 * mid_x), (0, 1): (low_x2, fine_tiles),
        (0, 2): (low_c2, low_c2.shape[0] - mid_x), (1, 0): (low_y2, low_y2.shape[0] - mid_x),
        (1, 2): (high_y2, high_y2.shape[0] - mid_x),
        (2, 0): (high_c2, high_c2.shape[0] - 2 * mid_x), (2, 1): (high_x2, fine_tiles),
        (2, 2): (high_c2, high_c2.shape[0] - mid_x),
    }
    for plane in range(mid_x):
        target[MID + plane, mid_y : 2 * mid_y] = mid_target[plane]
    for (bx, by), (ref, start) in blocks.items():
        for plane in range(mid_x):
            target[first + bx * mid_x + plane, by * mid_y : (by + 1) * mid_y] = ref[start + plane]

    scale_coeffs(0.25, window.at[0], window.at[1], window.at[2], window.at[3], coeffs, diagonal, (first, far))
    weights = chebyshev_weights(SWEEPS)

    def start_sweep(i, carry):
        goal = target[i] * coeffs[6, i]
        scaled[i] = goal
        update[i] = weights[0][1] * goal
        iterate[i] = weights[0][1] * goal
        return carry

    lax.fori_loop(first, far, start_sweep, 0)
    for sweep in range(1, SWEEPS):
        sweep_window(iterate, update, coeffs, scaled, (first + sweep, far - sweep), weights[sweep], False)
    low_x_size = mid_x // 2
    for block in range(low_x_size):
        total = None
        for plane in (MID + 2 * block, MID + 2 * block + 1):
            remain = scaled_remain(coeffs, scaled, plane, iterate[plane - 1], iterate[plane], iterate[plane + 1])
            remain = (remain * diagonal[plane])[mid_y : 2 * mid_y]
            total = remain if total is None else total + remain
        rest[block * mid_y : (block + 1) * mid_y] = total
    count = low_x_size * mid_y // 2
    summed = rest[pl.ds(0, count, 2), :] + rest[pl.ds(1, count, 2), :]
    coarse = dot(summed * 0.125, selector(mid_z, mid_z, lambda k, m: k // 2 == m))
    halves = (
        [coarse + low[0], low[1], low[2], mid_target[0], mid_target[mid_x - 1]],
        [iterate[MID + plane, mid_y : 2 * mid_y] for plane in range(mid_x)],
    )

    def fill(i, carry):
        for side in range(2):
            for j in range(count_y):
                for tile, value in enumerate(halves[side]):
                    slots[(2 * i + side) * count_y + j, tile] = value
        return carry

    lax.fori_loop(0, count_x // 2, fill, 0)


def solve_low(count_x, count_y, half, fields, coeffs, target, iterate, update):
    size_x, size_y, lanes = target.shape
    low_x, low_y = size_x // count_x, size_y // count_y
    low_z = lanes // 2

    def place(i, carry):
        for j in range(count_y):
            for kind in range(3):
                tile = half(0, i * count_y + j, kind)
                for plane in range(low_x):
                    fields[kind, i * low_x + plane, j * low_y : (j + 1) * low_y] = tile[
                        plane * low_y : (plane + 1) * low_y
                    ]
        return carry

    lax.fori_loop(0, count_x, place, 0)
    lane = iota((size_y, lanes), 1)
    inside = lane < low_z
    scale = 0.0625
    weights = chebyshev_weights(COARSE_SWEEPS)

    def prepare(i, carry):
        after = jnp.where(i == size_x - 1, 0, i + 1)
        first, second, third = fields[0, i], fields[1, i], fields[2, i]
        xl, xh = second, fields[1, after]
        yl = roll(second, low_z, 1)
        yh = roll(yl, -1, 0)
        zl = third
        zh = jnp.where(lane == low_z - 1, 0.0, roll(third, -1, 1))
        diag = roll(first, low_z, 1) + scale * (xl + xh + yl + yh + zl + zh)
        inverse = jnp.where(inside, 1.0 / diag, 0.0)
        scaled = scale * inverse
        coeffs[0, i] = scaled * xl
        coeffs[1, i] = scaled * xh
        coeffs[2, i] = scaled * yl
        coeffs[3, i] = scaled * yh
        coeffs[4, i] = jnp.where(lane == 0, 0.0, scaled * zl)
        coeffs[5, i] = scaled * zh
        goal = first * inverse
        target[i] = goal
        update[i] = weights[0][1] * goal
        iterate[i] = weights[0][1] * goal
        return carry

    lax.fori_loop(0, size_x, prepare, 0)
    for pair in weights[1:]:
        start = iterate[0]

        def body(i, carry, pair=pair, start=start):
            below, here = carry
            after = jnp.where(i == size_x - 1, 0, i + 1)
            above = jnp.where(i == size_x - 1, start, iterate[after])
            step = pair[1] * scaled_remain(coeffs, target, i, below, here, above) + pair[0] * update[i]
            update[i] = step
            iterate[i] = here + step
            return here, above

        lax.fori_loop(0, size_x, body, (iterate[size_x - 1], start), unroll=4)


def last_kernel(
    count_x, count_y, place, own_half, other_half, window, mid_target, coeffs, target, iterate_own,
    low_x2, high_x2, low_y2, high_y2, low_c2, high_c2,
    out,
    low_fields, low_coeffs, low_target, low_iterate, low_update,
    mid_coeffs, mid_scaled, mid_iterate, mid_update, spread_mid,
    iterate, update, spread,
):
    size_x, size_y, size_z = iterate_own.shape
    mid_x, mid_y, mid_z = size_x // 2, size_y // 2, size_z // 2
    me_x, me_y = place[0], place[1]
    even = me_x % 2 == 0

    def half(which, device, tile):
        one, two = own_half[device, tile], other_half[device, tile]
        return jnp.where(even, one, two) if which == 0 else jnp.where(even, two, one)

    solve_low(count_x, count_y, half, low_fields, low_coeffs, low_target, low_iterate, low_update)

    def device(dx, dy):
        return lax.rem(me_x + dx + count_x, count_x) * count_y + lax.rem(me_y + dy + count_y, count_y)

    first, far = MID - mid_x, MID + 2 * mid_x
    for dy in (-1, 0, 1):
        rows = slice((dy + 1) * mid_y, (dy + 2) * mid_y)
        for dx in (-1, 0, 1):
            for plane in range(mid_x):
                mid_iterate[MID + dx * mid_x + plane, rows] = half(1, device(dx, dy), plane)
        for plane in range(first):
            mid_iterate[plane, rows] = half(1, device(-2, dy), mid_x - first + plane)
            mid_iterate[far + plane, rows] = half(1, device(2, dy), plane)
    low_size_x, low_size_y = low_target.shape[:2]
    low_planes, low_rows = (mid_x + 2 * MID) // 2, 16
    low_y = mid_y // 2
    turn = lax.rem(low_size_y - me_y * low_y + low_y, low_size_y)
    picked = []
    for plane in range(low_planes):
        at = lax.rem(me_x * (mid_x // 2) - MID // 2 + plane + low_size_x, low_size_x)
        picked.append(pltpu.roll(low_iterate[at], turn, 0)[:low_rows])
    wide = dot(jnp.concatenate(picked, axis=0), selector(mid_z, mid_z, lambda k, m: k == m // 2))
    count = low_planes * low_rows
    spread_mid[pl.ds(0, count, 2), :] = wide
    spread_mid[pl.ds(1, count, 2), :] = wide
    for plane in range(low_planes):
        part = spread_mid[plane * 2 * low_rows : plane * 2 * low_rows + 3 * mid_y]
        mid_iterate[2 * plane] += part
        mid_iterate[2 * plane + 1] += part

    scale_coeffs(0.25, window.at[0], window.at[1], window.at[2], window.at[3], mid_coeffs, None, (first - 1, far + 1))

    def scale_target(i, carry):
        mid_scaled[i] = mid_target[i] * mid_coeffs[6, i]
        return carry

    lax.fori_loop(first, far, scale_target, 0)
    for dy in (-1, 0, 1):
        rows = slice((dy + 1) * mid_y, (dy + 2) * mid_y)
        mid_scaled[first - 1, rows] = half(0, device(-2, dy), 4) * mid_coeffs[6, first - 1, rows]
        mid_scaled[far, rows] = half(0, device(2, dy), 3) * mid_coeffs[6, far, rows]
    for sweep, pair in enumerate(chebyshev_weights(SWEEPS)):
        sweep_window(
            mid_iterate, mid_update, mid_coeffs, mid_scaled, (first - 1 + sweep, far + 1 - sweep), pair, sweep == 0
        )

    fine_low = FINE - 4
    assemble_fine(
        iterate, iterate_own, low_x2, high_x2, low_y2, high_y2, low_c2, high_c2, 4, 4, 3, 3, (0,) * 6
    )
    planes = mid_x + 4
    rows = mid_y + 8
    picked = [roll(mid_iterate[MID - 2 + plane], -4, 0)[:rows] for plane in range(planes)]
    wide = dot(jnp.concatenate(picked, axis=0), pair_copy(mid_z))
    count = planes * rows
    for side in range(2):
        lanes = slice(side * mid_z, (side + 1) * mid_z)
        spread[side, pl.ds(0, count, 2), :] = wide[:, lanes]
        spread[side, pl.ds(1, count, 2), :] = wide[:, lanes]
    for plane in range(planes):
        lines = slice(plane * 2 * rows, (plane + 1) * 2 * rows)
        part = jnp.concatenate([spread[0, lines], spread[1, lines]], axis=1)
        iterate[fine_low + 2 * plane] += part
        iterate[fine_low + 2 * plane + 1] += part
    last = size_x + 2 * FINE - 2
    for sweep, pair in enumerate(chebyshev_weights(SWEEPS)):
        sweep_window(
            iterate, update, coeffs, target, (2 + sweep, last - sweep), pair, sweep == 0
        )
    for plane in range(size_x):
        out[plane] = iterate[FINE + plane, PAD : PAD + size_y]


def call(kernel, inputs, outs, scratch=(), scalars=0):
    spaces = [pltpu.SMEM] * scalars + [pltpu.VMEM] * (len(inputs) - scalars)
    return pl.pallas_call(
        kernel,
        out_shape=[jax.ShapeDtypeStruct(shape, F32) for shape in outs],
        in_specs=[pl.BlockSpec(memory_space=space) for space in spaces],
        out_specs=[pl.BlockSpec(memory_space=pltpu.VMEM)] * len(outs),
        scratch_shapes=[pltpu.VMEM(shape, F32) for shape in scratch],
        compiler_params=pltpu.CompilerParams(vmem_limit_bytes=60 * 1024 * 1024),
    )(*inputs)


def local(source, initial, absorption, beta_x, beta_y, beta_z):
    size_x, size_y, size_z = source.shape
    mid_x, mid_y, mid_z = size_x // 2, size_y // 2, size_z // 2
    low_x, low_y = mid_x // 2, mid_y // 2
    count_x, count_y = lax.axis_size("gx"), lax.axis_size("gy")
    devices = count_x * count_y
    plane, strip = tiles_of(size_y, size_z), tiles_of(8, size_z)
    mids = 4 * mid_x

    def tiles(count):
        return (count,) + TILE

    own = (initial, source, absorption, beta_x, beta_y, beta_z)
    pairs = size_x // 2
    up_x, down_x, up_y, down_y, mid, low = call(
        pack_kernel,
        own,
        [
            tiles(sum(UP_PLANES) * plane + mids),
            tiles(sum(DOWN_PLANES) * plane + mids),
            tiles((6 * pairs + 1) * strip + mids),
            tiles((6 * pairs + 2) * strip + mids),
            tiles(mids),
            tiles(3),
        ],
        [(4 * mid_x * size_y, mid_z)],
    )
    low_x1, high_x1 = shifted(up_x, "gx", 1), shifted(down_x, "gx", -1)
    low_y1, high_y1 = shifted(up_y, "gy", 1), shifted(down_y, "gy", -1)
    up_c, down_c = call(
        functools.partial(corner_kernel, size_x, size_z),
        (low_y1, high_y1),
        [tiles(sum(UP_CORNER) * strip + 2 * mids), tiles(sum(DOWN_CORNER) * strip + 2 * mids)],
    )
    low_c1, high_c1 = shifted(up_c, "gx", 1), shifted(down_c, "gx", -1)

    wide = (size_x + 2 * FINE, size_y + 2 * PAD, size_z)
    iterate, coeffs, target, mid_target, up_x, down_x, up_y, down_y = call(
        fine_kernel,
        own + (low_x1, high_x1, low_y1, high_y1, low_c1, high_c1),
        [
            source.shape,
            (7,) + wide,
            wide,
            (mid_x, mid_y, mid_z),
            tiles(4 * plane + mid_x + 12),
            tiles(4 * plane + mid_x + 15),
            tiles(pairs * strip + mid_x),
            tiles(pairs * strip + mid_x),
        ],
        [(6,) + wide, wide, wide, (mid_x * size_y, mid_z)],
    )
    low_x2, high_x2 = shifted(up_x, "gx", 1), shifted(down_x, "gx", -1)
    low_y2, high_y2 = shifted(up_y, "gy", 1), shifted(down_y, "gy", -1)
    up_c, down_c = call(
        functools.partial(corner_two_kernel, size_x, size_z),
        (low_y2, high_y2),
        [tiles(3 * strip + 2 * mid_x)] * 2,
    )
    low_c2, high_c2 = shifted(up_c, "gx", 1), shifted(down_c, "gx", -1)

    mid_wide = (mid_x + 2 * MID, 3 * mid_y, mid_z)
    window, mid_goal, slots = call(
        functools.partial(mid_kernel, count_x, count_y),
        (mid, low, low_x1, high_x1, low_y1, high_y1, low_c1, high_c1)
        + (mid_target, low_x2, high_x2, low_y2, high_y2, low_c2, high_c2),
        [(4,) + mid_wide, mid_wide, (devices, 5) + TILE],
        [(7,) + mid_wide] + [mid_wide] * 4 + [(low_x * mid_y, mid_z)],
    )
    own_half = lax.all_to_all(slots, ("gx", "gy"), 0, 0)
    other_half = lax.ppermute(own_half, "gx", [(i, i ^ 1) for i in range(count_x)])

    place = jnp.stack([lax.axis_index("gx"), lax.axis_index("gy")]).astype(jnp.int32)
    low_wide = (low_x * count_x, low_y * count_y, mid_z)
    low_planes = mid_wide[0] // 2
    (result,) = call(
        functools.partial(last_kernel, count_x, count_y),
        (place, own_half, other_half, window, mid_goal, coeffs, target, iterate)
        + (low_x2, high_x2, low_y2, high_y2, low_c2, high_c2),
        [source.shape],
        [(3,) + low_wide, (6,) + low_wide, low_wide, low_wide, low_wide]
        + [(7,) + mid_wide, mid_wide, mid_wide, mid_wide, (low_planes * 32, mid_z)]
        + [wide, wide, (2, (mid_x + 4) * 2 * (mid_y + 8), mid_z)],
        scalars=1,
    )
    return result


def solution(mesh):
    spec = P("gx", "gy", None)
    return jax.shard_map(
        local, mesh=mesh, in_specs=(spec,) * 6, out_specs=spec, check_vma=False
    )
```

time: 271 us -> 114 us (0.42)
  starting transfers between devices: 147 us -> 16.1 us
  local copies, waits for them, and re-layouts: 50.5 us -> 5.47 us
  Pallas kernels: 0 us -> 42.7 us
  waiting for transfers between devices: 53.1 us -> 27.1 us
  blocking collectives: 0 us -> 21.9 us
  other arithmetic: 18.6 us -> 0.63 us
    ppermute x86 -> x13, starting transfers between devices: 147 us -> 16.1 us  [the longest x12 14.7 us: shifted(): lax.ppermute(value, axis, [(i, (i + step) % count) for i in range(count)])]
    pallas_call x0 -> x6, Pallas kernels: none -> 42.7 us  [call(): pl.pallas_call(kernel, out_shape=[jax.ShapeDtypeStruct(shape, F32) for sh...]
    reshape x8 -> x0, local copies, waits for them, and re-layouts: 30.6 us -> none  [the longest x3 21.3 us: restrict_cells(): field.reshape(size_x // 2, 2, size_y // 2, 2, size_z // 2, 2)]
    ppermute x86 -> x13, waiting for transfers between devices: 53.1 us -> 27.1 us  [the longest x12 26 us: shifted(): lax.ppermute(value, axis, [(i, (i + step) % count) for i in range(count)])]
    all_to_all x0 -> x1, blocking collectives: none -> 21.9 us  [local(): own_half = lax.all_to_all(slots, ('gx', 'gy'), 0, 0)]
    reduce_sum x14 -> x0, other arithmetic: 13.1 us -> none  [the longest x4 8.43 us: restrict_cells(): field.reshape(size_x // 2, 2, size_y // 2, 2, size_z // 2, 2)]
    slice x64 -> x0, local copies, waits for them, and re-layouts: 13 us -> none  [the longest x24 3.56 us: apply_operator(): lower_z = jnp.concatenate([zeros_plane, field[:, :, :-1]], axis=2)]
    unnamed x16 -> x28, local copies, waits for them, and re-layouts: 0.05 us -> 5.47 us
  transfers between devices with their start and end apart: 86 -> 13, of which waited for: 40 -> 6; matrix products, arithmetic and copies ran while one was open for 13% -> 1% of each run, Pallas kernels for 0% -> 3%
where the time goes in v1:
time: 114 us
  Pallas kernels  42.7 us (37%)
  waiting for transfers between devices  27.1 us (24%)
  blocking collectives  21.9 us (19%)
  starting transfers between devices  16.1 us (14%)
  local copies, waits for them, and re-layouts  5.47 us (5%)
    pallas_call x6, Pallas kernels, call(): pl.pallas_call(kernel, out_shape=[jax.ShapeDtypeStruct(shape, F32) for sh...  42.7 us
    ppermute x12, waiting for transfers between devices, shifted(): lax.ppermute(value, axis, [(i, (i + step) % count) for i in range(count)])  26 us
    all_to_all x1, blocking collectives, local(): own_half = lax.all_to_all(slots, ('gx', 'gy'), 0, 0)  21.9 us
    ppermute x12, starting transfers between devices, shifted(): lax.ppermute(value, axis, [(i, (i + step) % count) for i in range(count)])  14.7 us
    unnamed x28, local copies, waits for them, and re-layouts  5.47 us
  transfers between devices with their start and end apart: 13, of which 6 were waited for; matrix products, arithmetic and copies ran while one was open for 1% of the time, Pallas kernels for 3%

profile of v1, /device:TPU:0, one launch (start us, length us, event | category | flops | bytes accessed | tf_op | source)
XLA Modules:
  0.0 114.0 jit_solution(7845829911364402577)
XLA Ops:
  0.0 3.2 %shard_map.64 = (f32[116,8,128]{2,1,0:T(8,128)}, f32[120,8,128]{2,1,0:T(8,128)}, f32[66,8,128]{2,1,0:T(8,128)}, f32[68,8,128]{2,1,0:T(8,128)}, f32[16,8,128]{2,1,0:T(8,128)}, /*index=5*/f32[3,8,128]{2,1,0:T(8,128)}) custom-call(f32[8,16,256]{2,1,0:T(8,128)} %ini.3, f32[8,16,256]{2,1,0:T(8,128)} %src.3, f32[8,16,256]{2,1,0:T(8,128)} %absorb.3, ...), custom_call_target="tpu_custom_call" | custom-call | tf_op jit(solution)/shard_map/pallas_call | solution.py:618
  3.2 5.0 %collective-permute-start.3 = (f32[68,8,128]{2,1,0:T(8,128)}, f32[68,8,128]{2,1,0:T(8,128)S(1)}, u32[]{:S(2)}, u32[]{:S(2)}) collective-permute-start(f32[68,8,128]{2,1,0:T(8,128)} %get-tuple-element.31), channel_id=1, source_target_pairs={{0,3},{1,0},{2,1},{3,2},{4,7},{5,4},{6,5},{7,6},{8,11},{9,8},{10,9... | collective-permute-start | bytes 835592 | tf_op jit(solution)/shard_map/ppermute | solution.py:99
  8.2 0.0 collective-permute-start.2
  8.2 1.6 %collective-permute-start.1 = (f32[120,8,128]{2,1,0:T(8,128)}, f32[120,8,128]{2,1,0:T(8,128)S(1)}, u32[]{:S(2)}, u32[]{:S(2)}) collective-permute-start(f32[120,8,128]{2,1,0:T(8,128)} %get-tuple-element.29), channel_id=1, source_target_pairs={{0,28},{4,0},{8,4},{12,8},{16,12},{20,16},{24,20},{28,24},{1,29},{... | collective-permute-start | bytes 1474568 | tf_op jit(solution)/shard_map/ppermute | solution.py:99
  9.8 0.0 collective-permute-start
  9.8 11.2 %collective-permute-done.2.low_y = f32[66,8,128]{2,1,0:T(8,128)S(1)} collective-permute-done((f32[66,8,128]{2,1,0:T(8,128)}, f32[66,8,128]{2,1,0:T(8,128)S(1)}, u32[]{:S(2)}, u32[]{:S(2)}) %collective-permute-start.2) | collective-permute-done | bytes 270368 | tf_op jit(solution)/shard_map/ppermute | solution.py:99
  21.1 0.0 collective-permute-done.3.high_y
  21.1 0.7 copy-done.2
  21.8 0.7 copy-done.1
  22.5 1.9 %shard_map.65 = (f32[72,8,128]{2,1,0:T(8,128)}, f32[74,8,128]{2,1,0:T(8,128)}) custom-call(f32[66,8,128]{2,1,0:T(8,128)} %copy-done.2, f32[68,8,128]{2,1,0:T(8,128)} %copy-done.1), custom_call_target="tpu_custom_call" | custom-call | tf_op jit(solution)/shard_map/pallas_call | solution.py:618
  24.4 1.0 collective-permute-start.5
  25.4 0.0 collective-permute-start.4
  25.4 0.0 collective-permute-done.low_x
  25.5 0.0 collective-permute-done.1.high_x
  25.5 0.0 copy-start.3
  25.5 9.6 %collective-permute-done.4.low_c = f32[72,8,128]{2,1,0:T(8,128)S(1)} collective-permute-done((f32[72,8,128]{2,1,0:T(8,128)}, f32[72,8,128]{2,1,0:T(8,128)S(1)}, u32[]{:S(2)}, u32[]{:S(2)}) %collective-permute-start.4) | collective-permute-done | bytes 294944 | tf_op jit(solution)/shard_map/ppermute | solution.py:99
  35.0 0.0 collective-permute-done.5.high_c
  35.0 0.0 copy-done.4
  35.1 0.7 copy-done.6
  35.8 0.7 copy-done.5
  36.5 10.6 %shard_map.66 = (f32[8,16,256]{2,1,0:T(8,128)}, f32[7,18,32,256]{3,2,1,0:T(8,128)}, f32[18,32,256]{2,1,0:T(8,128)}, f32[4,8,128]{2,1,0:T(8,128)}, f32[32,8,128]{...) custom-call(f32[8,16,256]{2,1,0:T(8,128)} %ini.3, f32[8,16,256]{2,1,0:T(8,128)} %src.3, ...), custom_call_target="tpu_custom_call" | custom-call | tf_op jit(solution)/shard_map/pallas_call | solution.py:618
  47.1 0.1 collective-permute-start.7
  47.3 0.4 collective-permute-start.6
  47.7 1.6 %collective-permute-start.8 = (f32[12,8,128]{2,1,0:T(8,128)}, f32[12,8,128]{2,1,0:T(8,128)S(1)}, u32[]{:S(2)}, u32[]{:S(2)}) collective-permute-start(f32[12,8,128]{2,1,0:T(8,128)} %get-tuple-element.37), channel_id=1, source_target_pairs={{0,1},{1,2},{2,3},{3,0},{4,5},{5,6},{6,7},{7,4},{8,9},{9,10},{10,1... | collective-permute-start | bytes 147464 | tf_op jit(solution)/shard_map/ppermute | solution.py:99
  49.3 2.2 %collective-permute-start.9 = (f32[12,8,128]{2,1,0:T(8,128)}, f32[12,8,128]{2,1,0:T(8,128)S(1)}, u32[]{:S(2)}, u32[]{:S(2)}) collective-permute-start(f32[12,8,128]{2,1,0:T(8,128)} %get-tuple-element.38), channel_id=1, source_target_pairs={{0,3},{1,0},{2,1},{3,2},{4,7},{5,4},{6,5},{7,6},{8,11},{9,8},{10,9... | collective-permute-start | bytes 147464 | tf_op jit(solution)/shard_map/ppermute | solution.py:99
  51.5 2.4 %collective-permute-done.8.low_y.low_y2 = f32[12,8,128]{2,1,0:T(8,128)S(1)} collective-permute-done((f32[12,8,128]{2,1,0:T(8,128)}, f32[12,8,128]{2,1,0:T(8,128)S(1)}, u32[]{:S(2)}, u32[]{:S(2)}) %collective-permute-start.8) | collective-permute-done | bytes 49184 | tf_op jit(solution)/shard_map/ppermute | solution.py:99
  53.9 0.2 collective-permute-done.9.high_y.high_y2
  54.1 0.4 copy-done.10
  54.5 0.6 copy-done.11
  55.1 1.5 %shard_map.67 = (f32[14,8,128]{2,1,0:T(8,128)}, f32[14,8,128]{2,1,0:T(8,128)}) custom-call(f32[12,8,128]{2,1,0:T(8,128)} %copy-done.10, f32[12,8,128]{2,1,0:T(8,128)} %copy-done.11), custom_call_target="tpu_custom_call" | custom-call | tf_op jit(solution)/shard_map/pallas_call | solution.py:618
  56.6 0.0 collective-permute-start.10
  56.6 2.6 %collective-permute-start.11 = (f32[14,8,128]{2,1,0:T(8,128)}, f32[14,8,128]{2,1,0:T(8,128)S(1)}, u32[]{:S(2)}, u32[]{:S(2)}) collective-permute-start(f32[14,8,128]{2,1,0:T(8,128)} %get-tuple-element.40), channel_id=1, source_target_pairs={{0,28},{4,0},{8,4},{12,8},{16,12},{20,16},{24,20},{28,24},{1,29},{... | collective-permute-start | bytes 172040 | tf_op jit(solution)/shard_map/ppermute | solution.py:99
  59.3 2.6 %collective-permute-done.10.low_c2 = f32[14,8,128]{2,1,0:T(8,128)S(1)} collective-permute-done((f32[14,8,128]{2,1,0:T(8,128)}, f32[14,8,128]{2,1,0:T(8,128)S(1)}, u32[]{:S(2)}, u32[]{:S(2)}) %collective-permute-start.10) | collective-permute-done | bytes 57376 | tf_op jit(solution)/shard_map/ppermute | solution.py:99
  61.9 0.0 collective-permute-done.11.high_c2
  61.9 0.0 collective-permute-done.6.low_x2
  61.9 0.0 copy-start.9
  61.9 0.0 collective-permute-done.7.high_x2
  61.9 0.6 copy-done.12
  62.5 0.0 copy-done.13
  62.5 0.0 copy-done.9
  62.6 0.1 copy-done.8
  62.7 6.2 %shard_map.68 = (f32[4,16,24,128]{3,2,1,0:T(8,128)}, f32[16,24,128]{2,1,0:T(8,128)}, f32[32,5,8,128]{3,2,1,0:T(8,128)}) custom-call(f32[16,8,128]{2,1,0:T(8,128)} %get-tuple-element.26.mid, f32[3,8,128]{2,1,0:T(8,128)} %get-tuple-element.27.low, f32[116,8,128]{2,1,0:T(8,128)} %copy-done.4, f32[120,8,128]{2,1,0:T(8,128)} %copy-done.3, ...), custom_call_target="tpu_custom_call" | custom-call | tf_op jit(solution)/shard_map/pallas_call | solution.py:618
  68.9 21.9 %all_to_all.5.own_half = f32[32,5,8,128]{3,2,1,0:T(8,128)S(1)} all-to-all(f32[32,5,8,128]{3,2,1,0:T(8,128)} %get-tuple-element.41), channel_id=1, replica_groups=mesh['gx'=8,'gy'=4] {'gx','gy'}, dimensions={0} | all-to-all | bytes 1310720 | tf_op jit(solution)/shard_map/all_to_all | solution.py:697
  90.8 1.4 %collective-permute-start.12 = (f32[32,5,8,128]{3,2,1,0:T(8,128)S(1)}, f32[32,5,8,128]{3,2,1,0:T(8,128)S(1)}, u32[]{:S(2)}, u32[]{:S(2)}) collective-permute-start(f32[32,5,8,128]{3,2,1,0:T(8,128)S(1)} %all_to_all.5.own_half), channel_id=1, source_target_pairs={{0,4},{4,0},{8,12},{12,8},{16,20},{20,16},{24,28},{28,24},{1,5},{5... | collective-permute-start | bytes 1966088 | tf_op jit(solution)/shard_map/ppermute | solution.py:698
  92.2 0.6 pad_add_fusion.place
  92.8 1.1 collective-permute-done.12.other_half
  93.9 0.8 copy-done.7
  94.7 19.3 %shard_map.69 = f32[8,16,256]{2,1,0:T(8,128)} custom-call(s32[2]{0:T(128)} %pad_add_fusion.place, f32[32,5,8,128]{3,2,1,0:T(8,128)} %copy-done, f32[32,5,8,128]{3,2,1,0:T(8,128)} %copy-done.7, f32[4,16,24,128]{3,2,1,0:T(8,128)} %get-tuple-element.42.window, f32[16,24,128]{2,1,0:T(8,128)} %get-tuple-element.43.mid_target, ...), custom_call_target="tpu_custom_call" | custom-call | tf_op jit(solution)/shard_map/pallas_call | solution.py:618
  (14 shorter events, 0.0 us)
Async XLA Ops:
  3.2 17.9 %collective-permute-start.3 = (f32[68,8,128]{2,1,0:T(8,128)}, f32[68,8,128]{2,1,0:T(8,128)S(1)}, u32[]{:S(2)}, u32[]{:S(2)}) collective-permute-start(f32[68,8,128]{2,1,0:T(8,128)} %get-tuple-element.31), channel_id=1, source_target_pairs={{0,3},{1,0},{2,1},{3,2},{4,7},{5,4},{6,5},{7,6},{8,11},{9,8},{10,9... | collective-permute-start | bytes 835592 | tf_op jit(solution)/shard_map/ppermute | solution.py:99
  8.2 12.8 %collective-permute-start.2 = (f32[66,8,128]{2,1,0:T(8,128)}, f32[66,8,128]{2,1,0:T(8,128)S(1)}, u32[]{:S(2)}, u32[]{:S(2)}) collective-permute-start(f32[66,8,128]{2,1,0:T(8,128)} %get-tuple-element.30), channel_id=1, source_target_pairs={{0,1},{1,2},{2,3},{3,0},{4,5},{5,6},{6,7},{7,4},{8,9},{9,10},{10,1... | collective-permute-start | bytes 811016 | tf_op jit(solution)/shard_map/ppermute | solution.py:99
  8.2 17.2 %collective-permute-start.1 = (f32[120,8,128]{2,1,0:T(8,128)}, f32[120,8,128]{2,1,0:T(8,128)S(1)}, u32[]{:S(2)}, u32[]{:S(2)}) collective-permute-start(f32[120,8,128]{2,1,0:T(8,128)} %get-tuple-element.29), channel_id=1, source_target_pairs={{0,28},{4,0},{8,4},{12,8},{16,12},{20,16},{24,20},{28,24},{1,29},{... | collective-permute-start | bytes 1474568 | tf_op jit(solution)/shard_map/ppermute | solution.py:99
  9.8 15.6 %collective-permute-start = (f32[116,8,128]{2,1,0:T(8,128)}, f32[116,8,128]{2,1,0:T(8,128)S(1)}, u32[]{:S(2)}, u32[]{:S(2)}) collective-permute-start(f32[116,8,128]{2,1,0:T(8,128)} %get-tuple-element.28), channel_id=1, source_target_pairs={{0,4},{4,8},{8,12},{12,16},{16,20},{20,24},{24,28},{28,0},{1,5},{5... | collective-permute-start | bytes 1425416 | tf_op jit(solution)/shard_map/ppermute | solution.py:99
  21.1 0.7 copy-start.2
  21.8 0.7 copy-start.1
  24.4 10.6 %collective-permute-start.5 = (f32[74,8,128]{2,1,0:T(8,128)}, f32[74,8,128]{2,1,0:T(8,128)S(1)}, u32[]{:S(2)}, u32[]{:S(2)}) collective-permute-start(f32[74,8,128]{2,1,0:T(8,128)} %get-tuple-element.33), channel_id=1, source_target_pairs={{0,28},{4,0},{8,4},{12,8},{16,12},{20,16},{24,20},{28,24},{1,29},{... | collective-permute-start | bytes 909320 | tf_op jit(solution)/shard_map/ppermute | solution.py:99
  25.4 9.6 %collective-permute-start.4 = (f32[72,8,128]{2,1,0:T(8,128)}, f32[72,8,128]{2,1,0:T(8,128)S(1)}, u32[]{:S(2)}, u32[]{:S(2)}) collective-permute-start(f32[72,8,128]{2,1,0:T(8,128)} %get-tuple-element.32), channel_id=1, source_target_pairs={{0,4},{4,8},{8,12},{12,16},{16,20},{20,24},{24,28},{28,0},{1,5},{5... | collective-permute-start | bytes 884744 | tf_op jit(solution)/shard_map/ppermute | solution.py:99
  25.5 9.6 %copy-start.4 = (f32[116,8,128]{2,1,0:T(8,128)}, f32[116,8,128]{2,1,0:T(8,128)S(1)}, u32[]{:S(2)}) copy-start(f32[116,8,128]{2,1,0:T(8,128)S(1)} %collective-permute-done.low_x) | copy-start | bytes 1425412
  25.5 9.6 %copy-start.3 = (f32[120,8,128]{2,1,0:T(8,128)}, f32[120,8,128]{2,1,0:T(8,128)S(1)}, u32[]{:S(2)}) copy-start(f32[120,8,128]{2,1,0:T(8,128)S(1)} %collective-permute-done.1.high_x) | copy-start | bytes 1474564
  35.0 0.7 copy-start.6
  35.8 0.7 copy-start.5
  47.1 14.8 %collective-permute-start.7 = (f32[35,8,128]{2,1,0:T(8,128)}, f32[35,8,128]{2,1,0:T(8,128)S(1)}, u32[]{:S(2)}, u32[]{:S(2)}) collective-permute-start(f32[35,8,128]{2,1,0:T(8,128)} %get-tuple-element.36), channel_id=1, source_target_pairs={{0,28},{4,0},{8,4},{12,8},{16,12},{20,16},{24,20},{28,24},{1,29},{... | collective-permute-start | bytes 430088 | tf_op jit(solution)/shard_map/ppermute | solution.py:99
  47.3 14.6 %collective-permute-start.6 = (f32[32,8,128]{2,1,0:T(8,128)}, f32[32,8,128]{2,1,0:T(8,128)S(1)}, u32[]{:S(2)}, u32[]{:S(2)}) collective-permute-start(f32[32,8,128]{2,1,0:T(8,128)} %get-tuple-element.35), channel_id=1, source_target_pairs={{0,4},{4,8},{8,12},{12,16},{16,20},{20,24},{24,28},{28,0},{1,5},{5... | collective-permute-start | bytes 393224 | tf_op jit(solution)/shard_map/ppermute | solution.py:99
  47.7 6.2 %collective-permute-start.8 = (f32[12,8,128]{2,1,0:T(8,128)}, f32[12,8,128]{2,1,0:T(8,128)S(1)}, u32[]{:S(2)}, u32[]{:S(2)}) collective-permute-start(f32[12,8,128]{2,1,0:T(8,128)} %get-tuple-element.37), channel_id=1, source_target_pairs={{0,1},{1,2},{2,3},{3,0},{4,5},{5,6},{6,7},{7,4},{8,9},{9,10},{10,1... | collective-permute-start | bytes 147464 | tf_op jit(solution)/shard_map/ppermute | solution.py:99
  49.3 4.8 %collective-permute-start.9 = (f32[12,8,128]{2,1,0:T(8,128)}, f32[12,8,128]{2,1,0:T(8,128)S(1)}, u32[]{:S(2)}, u32[]{:S(2)}) collective-permute-start(f32[12,8,128]{2,1,0:T(8,128)} %get-tuple-element.38), channel_id=1, source_target_pairs={{0,3},{1,0},{2,1},{3,2},{4,7},{5,4},{6,5},{7,6},{8,11},{9,8},{10,9... | collective-permute-start | bytes 147464 | tf_op jit(solution)/shard_map/ppermute | solution.py:99
  53.9 0.6 copy-start.10
  54.5 0.6 copy-start.11
  56.6 5.2 %collective-permute-start.10 = (f32[14,8,128]{2,1,0:T(8,128)}, f32[14,8,128]{2,1,0:T(8,128)S(1)}, u32[]{:S(2)}, u32[]{:S(2)}) collective-permute-start(f32[14,8,128]{2,1,0:T(8,128)} %get-tuple-element.39), channel_id=1, source_target_pairs={{0,4},{4,8},{8,12},{12,16},{16,20},{20,24},{24,28},{28,0},{1,5},{5... | collective-permute-start | bytes 172040 | tf_op jit(solution)/shard_map/ppermute | solution.py:99
  56.6 5.2 %collective-permute-start.11 = (f32[14,8,128]{2,1,0:T(8,128)}, f32[14,8,128]{2,1,0:T(8,128)S(1)}, u32[]{:S(2)}, u32[]{:S(2)}) collective-permute-start(f32[14,8,128]{2,1,0:T(8,128)} %get-tuple-element.40), channel_id=1, source_target_pairs={{0,28},{4,0},{8,4},{12,8},{16,12},{20,16},{24,20},{28,24},{1,29},{... | collective-permute-start | bytes 172040 | tf_op jit(solution)/shard_map/ppermute | solution.py:99
  61.9 0.6 copy-start.12
  61.9 0.6 copy-start.13
  61.9 0.7 copy-start.9
  61.9 0.8 copy-start.8
  90.8 3.1 %copy-start = (f32[32,5,8,128]{3,2,1,0:T(8,128)}, f32[32,5,8,128]{3,2,1,0:T(8,128)S(1)}, u32[]{:S(2)}) copy-start(f32[32,5,8,128]{3,2,1,0:T(8,128)S(1)} %all_to_all.5.own_half) | copy-start | bytes 1966084
  90.8 3.1 %collective-permute-start.12 = (f32[32,5,8,128]{3,2,1,0:T(8,128)S(1)}, f32[32,5,8,128]{3,2,1,0:T(8,128)S(1)}, u32[]{:S(2)}, u32[]{:S(2)}) collective-permute-start(f32[32,5,8,128]{3,2,1,0:T(8,128)S(1)} %all_to_all.5.own_half), channel_id=1, source_target_pairs={{0,4},{4,0},{8,12},{12,8},{16,20},{20,16},{24,28},{28,24},{1,5},{5... | collective-permute-start | bytes 1966088 | tf_op jit(solution)/shard_map/ppermute | solution.py:698
  93.9 0.8 copy-start.7

commit v2 on v1

--- a/solution.py
+++ b/solution.py
@@ -1,4 +1,5 @@
 import functools
+import math
 
 import jax
 import jax.numpy as jnp
@@ -53,6 +54,14 @@
     return pltpu.roll(value, shift % value.shape[axis], axis)
 
 
+def each(start, stop, body, carry=0):
+    if stop - start > 20:
+        return lax.fori_loop(start, stop, body, carry, unroll=2)
+    for i in range(start, stop):
+        carry = body(i, carry)
+    return carry
+
+
 class Writer:
     def __init__(self, ref):
         self.ref, self.at = ref, 0
@@ -100,9 +109,17 @@
 
 
 def pack_kernel(
-    ini, src, absorb, face_x, face_y, face_z, up_x, down_x, up_y, down_y, mid, low, rows_mid
+    ini_in, src_in, absorb_in, face_x_in, face_y_in, face_z_in,
+    up_x, down_x, up_y, down_y, mid, low, own, rows_mid, sems,
 ):
-    fields = (ini, src, absorb, face_x, face_y, face_z)
+    copies = []
+    for field, ref in enumerate((ini_in, src_in, absorb_in, face_x_in, face_y_in, face_z_in)):
+        copies.append(pltpu.make_async_copy(ref, own.at[field], sems.at[field]))
+        copies[-1].start()
+    for copy in copies:
+        copy.wait()
+    fields = tuple(own.at[field] for field in range(6))
+    ini, src, absorb, face_x, face_y, face_z = fields
     size_x, size_y, size_z = ini.shape
     half = size_y // 2
     blocks = range(0, size_x, 2)
@@ -193,11 +210,29 @@
             tops.put(corner_of(low_y, high_y, plane, upper, field * per_field))
         for plane in range(DOWN_CORNER[field]):
             bottoms.put(corner_of(low_y, high_y, plane, upper, field * per_field))
-    mid_tiles = 4 * (size_x // 2)
-    for writer in (tops, bottoms):
-        for ref in (low_y, high_y):
-            for tile in range(ref.shape[0] - mid_tiles, ref.shape[0]):
-                writer.put(ref[tile])
+    mid_x = size_x // 2
+    sides = [(ref, ref.shape[0] - 4 * mid_x) for ref in (low_y, high_y)]
+    upper = is_upper(TILE[1])
+    for writer, first, step in ((tops, mid_x - 1, -1), (bottoms, 0, 1)):
+        for array in range(4):
+            for q in range(2):
+                for ref, start in sides:
+                    writer.put(ref[start + array * mid_x + first + q * step])
+        for array in range(4):
+            for q in range(2, 4):
+                one, two = (roll(ref[start + array * mid_x + first + q * step], 4, 0) for ref, start in sides)
+                writer.put(jnp.where(upper, one, two))
+
+
+MID_CORNER = 24
+
+
+def whole_corner(ref, array, q, side):
+    return ref[ref.shape[0] - MID_CORNER + (array * 2 + q) * 2 + side]
+
+
+def part_corner(ref, array, q):
+    return ref[ref.shape[0] - MID_CORNER + 16 + array * 2 + q - 2]
 
 
 def scale_coeffs(scale, absorb, face_x, face_y, face_z, coeffs, diagonal, planes):
@@ -218,35 +253,35 @@
         coeffs[3, i] = scaled * yh
         coeffs[4, i] = jnp.where(lane == 0, 0.0, scaled * zl)
         coeffs[5, i] = scaled * zh
-        coeffs[6, i] = inverse
+        coeffs[7, i] = inverse
         if diagonal is not None:
             diagonal[i] = diag
         return carry
 
-    lax.fori_loop(*planes, body, 0)
-
-
-def scaled_remain(coeffs, target, i, below, here, above):
-    total = target[i] - here
+    each(*planes, body)
+
+
+def scaled_remain(coeffs, i, below, here, above):
+    total = coeffs[6, i] - here
     total = total + coeffs[0, i] * below + coeffs[1, i] * above
     total = total + coeffs[2, i] * roll(here, 1, 0) + coeffs[3, i] * roll(here, -1, 0)
     return total + coeffs[4, i] * roll(here, 1, 1) + coeffs[5, i] * roll(here, -1, 1)
 
 
-def sweep_window(iterate, update, coeffs, target, planes, pair, first, unroll=1):
+def sweep_window(iterate, update, coeffs, planes, pair, first):
     start, stop = planes
 
     def body(i, carry):
         below, here = carry
         above = iterate[i + 1]
-        step = pair[1] * scaled_remain(coeffs, target, i, below, here, above)
+        step = pair[1] * scaled_remain(coeffs, i, below, here, above)
         if not first:
             step = step + pair[0] * update[i]
         update[i] = step
         iterate[i] = here + step
         return here, above
 
-    lax.fori_loop(start, stop, body, (iterate[start - 1], iterate[start]), unroll=unroll)
+    each(start, stop, body, (iterate[start - 1], iterate[start]))
 
 
 def assemble_fine(window, own, low_x, high_x, low_y, high_y, low_c, high_c, up, down, up_c, down_c, starts):
@@ -280,17 +315,16 @@
 
 
 def fine_kernel(
-    ini, src, absorb, face_x, face_y, face_z, low_x, high_x, low_y, high_y, low_c, high_c,
-    iterate_out, coeffs, target, mid_target, up_x, down_x, up_y, down_y,
-    windows, update, diagonal, rest,
+    own, low_x, high_x, low_y, high_y, low_c, high_c,
+    iterate_out, coeffs_out, mid_target, up_x, down_x, up_y, down_y,
+    windows, coeffs, update, diagonal, rest, sem,
 ):
-    own = (ini, src, absorb, face_x, face_y, face_z)
-    size_x, size_y, size_z = ini.shape
+    size_x, size_y, size_z = own.shape[1:]
     plane_tiles, strip_tiles = tiles_of(size_y, size_z), tiles_of(8, size_z)
     starts = [0] * 6
     for field in range(6):
         assemble_fine(
-            windows.at[field], own[field], low_x, high_x, low_y, high_y, low_c, high_c,
+            windows.at[field], own.at[field], low_x, high_x, low_y, high_y, low_c, high_c,
             UP_PLANES[field], DOWN_PLANES[field], UP_CORNER[field], DOWN_CORNER[field], tuple(starts),
         )
         starts[0] += UP_PLANES[field] * plane_tiles
@@ -313,21 +347,20 @@
     last = size_x + 2 * FINE - 1
     scale_coeffs(1.0, windows.at[2], windows.at[3], windows.at[4], windows.at[5], coeffs, diagonal, (1, last))
 
-    def scale_target(i, carry):
-        target[i] = windows[1, i] * coeffs[6, i]
-        return carry
-
-    lax.fori_loop(1, last, scale_target, 0)
+    for plane in range(1, last):
+        coeffs[6, plane] = windows[1, plane] * coeffs[7, plane]
+    keep = pltpu.make_async_copy(coeffs.at[:7, 2 : last - 1], coeffs_out, sem)
+    keep.start()
     for sweep, pair in enumerate(chebyshev_weights(SWEEPS)):
         sweep_window(
-            iterate, update, coeffs, target, (1 + sweep, last - sweep), pair, sweep == 0
+            iterate, update, coeffs, (1 + sweep, last - sweep), pair, sweep == 0
         )
     mid_x, mid_y = size_x // 2, size_y // 2
     lines = []
     for block in range(mid_x):
         total = None
         for plane in (FINE + 2 * block, FINE + 2 * block + 1):
-            remain = scaled_remain(coeffs, target, plane, iterate[plane - 1], iterate[plane], iterate[plane + 1])
+            remain = scaled_remain(coeffs, plane, iterate[plane - 1], iterate[plane], iterate[plane + 1])
             remain = (remain * diagonal[plane])[PAD : PAD + size_y]
             total = remain if total is None else total + remain
         lines.append(total)
@@ -352,16 +385,18 @@
         bottoms_y.put(jnp.where(upper, one[:8], roll(two[:8], 4, 0)))
     for writer in (tops, bottoms, tops_y, bottoms_y):
         writer.put(coarse)
-    mids = 4 * mid_x
-    near_low = [(low_c, low_c.shape[0] - 2 * mids), (low_x, low_x.shape[0] - mids), (low_c, low_c.shape[0] - mids)]
-    near_high = [(high_c, high_c.shape[0] - 2 * mids), (high_x, high_x.shape[0] - mids), (high_c, high_c.shape[0] - mids)]
+    low_start, high_start = (ref.shape[0] - 4 * mid_x for ref in (low_x, high_x))
     for array in range(4):
-        for ref, start in near_low:
-            tops.put(ref[start + array * mid_x + mid_x - 1])
-        for ref, start in near_high:
-            bottoms.put(ref[start + array * mid_x])
-    for ref, start in near_high:
-        bottoms.put(ref[start + mid_x + 1])
+        tops.put(whole_corner(low_c, array, 0, 0))
+        tops.put(low_x[low_start + array * mid_x + mid_x - 1])
+        tops.put(whole_corner(low_c, array, 0, 1))
+        bottoms.put(whole_corner(high_c, array, 0, 0))
+        bottoms.put(high_x[high_start + array * mid_x])
+        bottoms.put(whole_corner(high_c, array, 0, 1))
+    bottoms.put(whole_corner(high_c, 1, 1, 0))
+    bottoms.put(high_x[high_start + mid_x + 1])
+    bottoms.put(whole_corner(high_c, 1, 1, 1))
+    keep.wait()
 
 
 def corner_two_kernel(size_x, size_z, low_y, high_y, up, down):
@@ -378,20 +413,18 @@
 
 
 def mid_kernel(
-    count_x, count_y, mid, low, low_x, high_x, low_y, high_y, low_c, high_c,
+    count_x, count_y, place, mid, low, low_x, high_x, low_y, high_y, low_c, high_c,
     mid_target, low_x2, high_x2, low_y2, high_y2, low_c2, high_c2,
     window, target, slots,
-    coeffs, diagonal, scaled, iterate, update, rest,
+    coeffs, diagonal, iterate, update, rest,
 ):
     mid_x, mid_y, mid_z = mid_target.shape
     mids = 4 * mid_x
     first = MID - mid_x
     blocks = {
-        (0, 0): (low_c, low_c.shape[0] - 2 * mids), (0, 1): (low_x, low_x.shape[0] - mids),
-        (0, 2): (low_c, low_c.shape[0] - mids), (1, 0): (low_y, low_y.shape[0] - mids),
+        (0, 1): (low_x, low_x.shape[0] - mids), (1, 0): (low_y, low_y.shape[0] - mids),
         (1, 1): (mid, 0), (1, 2): (high_y, high_y.shape[0] - mids),
-        (2, 0): (high_c, high_c.shape[0] - 2 * mids), (2, 1): (high_x, high_x.shape[0] - mids),
-        (2, 2): (high_c, high_c.shape[0] - mids),
+        (2, 1): (high_x, high_x.shape[0] - mids),
     }
     for (bx, by), (ref, start) in blocks.items():
         for array in range(4):
@@ -399,6 +432,15 @@
                 window[array, first + bx * mid_x + plane, by * mid_y : (by + 1) * mid_y] = ref[
                     start + array * mid_x + plane
                 ]
+    for ref, start, step in ((low_c, MID - 1, -1), (high_c, MID + mid_x, 1)):
+        for array in range(4):
+            for q in range(mid_x):
+                if q < 2:
+                    one, two = whole_corner(ref, array, q, 0), whole_corner(ref, array, q, 1)
+                else:
+                    one = two = roll(part_corner(ref, array, q), 4, 0)
+                window[array, start + q * step, :mid_y] = one
+                window[array, start + q * step, 2 * mid_y :] = two
     far = 3 * mid_x + first
     fine_tiles = 4 * tiles_of(2 * mid_y, 2 * mid_z)
     own_planes = fine_tiles + mid_x
@@ -427,43 +469,45 @@
     weights = chebyshev_weights(SWEEPS)
 
     def start_sweep(i, carry):
-        goal = target[i] * coeffs[6, i]
-        scaled[i] = goal
+        goal = target[i] * coeffs[7, i]
+        coeffs[6, i] = goal
         update[i] = weights[0][1] * goal
         iterate[i] = weights[0][1] * goal
         return carry
 
-    lax.fori_loop(first, far, start_sweep, 0)
+    each(first, far, start_sweep)
     for sweep in range(1, SWEEPS):
-        sweep_window(iterate, update, coeffs, scaled, (first + sweep, far - sweep), weights[sweep], False)
+        sweep_window(iterate, update, coeffs, (first + sweep, far - sweep), weights[sweep], False)
     low_x_size = mid_x // 2
     for block in range(low_x_size):
         total = None
         for plane in (MID + 2 * block, MID + 2 * block + 1):
-            remain = scaled_remain(coeffs, scaled, plane, iterate[plane - 1], iterate[plane], iterate[plane + 1])
+            remain = scaled_remain(coeffs, plane, iterate[plane - 1], iterate[plane], iterate[plane + 1])
             remain = (remain * diagonal[plane])[mid_y : 2 * mid_y]
             total = remain if total is None else total + remain
         rest[block * mid_y : (block + 1) * mid_y] = total
     count = low_x_size * mid_y // 2
     summed = rest[pl.ds(0, count, 2), :] + rest[pl.ds(1, count, 2), :]
     coarse = dot(summed * 0.125, selector(mid_z, mid_z, lambda k, m: k // 2 == m))
-    halves = (
-        [coarse + low[0], low[1], low[2], mid_target[0], mid_target[mid_x - 1]],
-        [iterate[MID + plane, mid_y : 2 * mid_y] for plane in range(mid_x)],
-    )
+    low_tiles = (coarse + low[0], low[1], low[2])
+    iterates = [iterate[MID + plane, mid_y : 2 * mid_y] for plane in range(mid_x)]
+    pairs = count_x // 2
+    following = lax.rem(place[0] // 2 + 1, pairs)
 
     def fill(i, carry):
-        for side in range(2):
-            for j in range(count_y):
-                for tile, value in enumerate(halves[side]):
-                    slots[(2 * i + side) * count_y + j, tile] = value
+        edge = jnp.where(i == following, mid_target[mid_x - 1], mid_target[0])
+        for j in range(count_y):
+            for tile, value in enumerate(low_tiles + (edge,)):
+                slots[2 * i * count_y + j, tile] = value
+            for tile, value in enumerate(iterates):
+                slots[(2 * i + 1) * count_y + j, tile] = value
         return carry
 
-    lax.fori_loop(0, count_x // 2, fill, 0)
-
-
-def solve_low(count_x, count_y, half, fields, coeffs, target, iterate, update):
-    size_x, size_y, lanes = target.shape
+    each(0, pairs, fill)
+
+
+def solve_low(count_x, count_y, half, fields, coeffs, iterate, update):
+    size_x, size_y, lanes = iterate.shape
     low_x, low_y = size_x // count_x, size_y // count_y
     low_z = lanes // 2
 
@@ -477,16 +521,20 @@
                     ]
         return carry
 
-    lax.fori_loop(0, count_x, place, 0)
+    each(0, count_x, place)
     lane = iota((size_y, lanes), 1)
     inside = lane < low_z
     scale = 0.0625
     weights = chebyshev_weights(COARSE_SWEEPS)
 
+    def following(i):
+        if isinstance(i, int):
+            return (i + 1) % size_x
+        return jnp.where(i == size_x - 1, 0, i + 1)
+
     def prepare(i, carry):
-        after = jnp.where(i == size_x - 1, 0, i + 1)
         first, second, third = fields[0, i], fields[1, i], fields[2, i]
-        xl, xh = second, fields[1, after]
+        xl, xh = second, fields[1, following(i)]
         yl = roll(second, low_z, 1)
         yh = roll(yl, -1, 0)
         zl = third
@@ -501,37 +549,42 @@
         coeffs[4, i] = jnp.where(lane == 0, 0.0, scaled * zl)
         coeffs[5, i] = scaled * zh
         goal = first * inverse
-        target[i] = goal
+        coeffs[6, i] = goal
         update[i] = weights[0][1] * goal
         iterate[i] = weights[0][1] * goal
         return carry
 
-    lax.fori_loop(0, size_x, prepare, 0)
+    each(0, size_x, prepare)
     for pair in weights[1:]:
         start = iterate[0]
 
         def body(i, carry, pair=pair, start=start):
             below, here = carry
-            after = jnp.where(i == size_x - 1, 0, i + 1)
-            above = jnp.where(i == size_x - 1, start, iterate[after])
-            step = pair[1] * scaled_remain(coeffs, target, i, below, here, above) + pair[0] * update[i]
+            if isinstance(i, int):
+                above = start if i == size_x - 1 else iterate[i + 1]
+            else:
+                above = jnp.where(i == size_x - 1, start, iterate[following(i)])
+            step = pair[1] * scaled_remain(coeffs, i, below, here, above) + pair[0] * update[i]
             update[i] = step
             iterate[i] = here + step
             return here, above
 
-        lax.fori_loop(0, size_x, body, (iterate[size_x - 1], start), unroll=4)
+        each(0, size_x, body, (iterate[size_x - 1], start))
 
 
 def last_kernel(
-    count_x, count_y, place, own_half, other_half, window, mid_target, coeffs, target, iterate_own,
+    count_x, count_y, place, own_half, other_half, window, mid_target, coeffs_in, iterate_own,
     low_x2, high_x2, low_y2, high_y2, low_c2, high_c2,
     out,
-    low_fields, low_coeffs, low_target, low_iterate, low_update,
-    mid_coeffs, mid_scaled, mid_iterate, mid_update, spread_mid,
-    iterate, update, spread,
+    low_fields, low_coeffs, low_iterate, low_update,
+    mid_coeffs, mid_iterate, mid_update, spread_mid,
+    coeffs, iterate, update, spread, sem,
 ):
     size_x, size_y, size_z = iterate_own.shape
     mid_x, mid_y, mid_z = size_x // 2, size_y // 2, size_z // 2
+    last = size_x + 2 * FINE - 2
+    fetch = pltpu.make_async_copy(coeffs_in, coeffs.at[:, 2:last], sem)
+    fetch.start()
     me_x, me_y = place[0], place[1]
     even = me_x % 2 == 0
 
@@ -539,7 +592,7 @@
         one, two = own_half[device, tile], other_half[device, tile]
         return jnp.where(even, one, two) if which == 0 else jnp.where(even, two, one)
 
-    solve_low(count_x, count_y, half, low_fields, low_coeffs, low_target, low_iterate, low_update)
+    solve_low(count_x, count_y, half, low_fields, low_coeffs, low_iterate, low_update)
 
     def device(dx, dy):
         return lax.rem(me_x + dx + count_x, count_x) * count_y + lax.rem(me_y + dy + count_y, count_y)
@@ -553,7 +606,7 @@
         for plane in range(first):
             mid_iterate[plane, rows] = half(1, device(-2, dy), mid_x - first + plane)
             mid_iterate[far + plane, rows] = half(1, device(2, dy), plane)
-    low_size_x, low_size_y = low_target.shape[:2]
+    low_size_x, low_size_y = low_iterate.shape[:2]
     low_planes, low_rows = (mid_x + 2 * MID) // 2, 16
     low_y = mid_y // 2
     turn = lax.rem(low_size_y - me_y * low_y + low_y, low_size_y)
@@ -572,18 +625,15 @@
 
     scale_coeffs(0.25, window.at[0], window.at[1], window.at[2], window.at[3], mid_coeffs, None, (first - 1, far + 1))
 
-    def scale_target(i, carry):
-        mid_scaled[i] = mid_target[i] * mid_coeffs[6, i]
-        return carry
-
-    lax.fori_loop(first, far, scale_target, 0)
+    for plane in range(first, far):
+        mid_coeffs[6, plane] = mid_target[plane] * mid_coeffs[7, plane]
     for dy in (-1, 0, 1):
         rows = slice((dy + 1) * mid_y, (dy + 2) * mid_y)
-        mid_scaled[first - 1, rows] = half(0, device(-2, dy), 4) * mid_coeffs[6, first - 1, rows]
-        mid_scaled[far, rows] = half(0, device(2, dy), 3) * mid_coeffs[6, far, rows]
+        for plane, dx in ((first - 1, -2), (far, 2)):
+            mid_coeffs[6, plane, rows] = half(0, device(dx, dy), 3) * mid_coeffs[7, plane, rows]
     for sweep, pair in enumerate(chebyshev_weights(SWEEPS)):
         sweep_window(
-            mid_iterate, mid_update, mid_coeffs, mid_scaled, (first - 1 + sweep, far + 1 - sweep), pair, sweep == 0
+            mid_iterate, mid_update, mid_coeffs, (first - 1 + sweep, far + 1 - sweep), pair, sweep == 0
         )
 
     fine_low = FINE - 4
@@ -604,24 +654,37 @@
         part = jnp.concatenate([spread[0, lines], spread[1, lines]], axis=1)
         iterate[fine_low + 2 * plane] += part
         iterate[fine_low + 2 * plane + 1] += part
-    last = size_x + 2 * FINE - 2
+    fetch.wait()
     for sweep, pair in enumerate(chebyshev_weights(SWEEPS)):
         sweep_window(
-            iterate, update, coeffs, target, (2 + sweep, last - sweep), pair, sweep == 0
+            iterate, update, coeffs, (2 + sweep, last - sweep), pair, sweep == 0
         )
     for plane in range(size_x):
         out[plane] = iterate[FINE + plane, PAD : PAD + size_y]
 
 
-def call(kernel, inputs, outs, scratch=(), scalars=0):
-    spaces = [pltpu.SMEM] * scalars + [pltpu.VMEM] * (len(inputs) - scalars)
+def call(kernel, inputs, outs, scratch=(), scalars=0, far_in=(), far_out=(), sems=0):
+    def place(i):
+        return pltpu.SMEM if i < scalars else pltpu.HBM if i in far_in else pltpu.VMEM
+
+    near = [x.shape for i, x in enumerate(inputs) if i >= scalars and i not in far_in]
+    near += [shape for i, shape in enumerate(outs) if i not in far_out] + list(scratch)
+    used = 4 * sum(math.prod(shape) for shape in near)
+    inputs = [pltpu.with_memory_space_constraint(x, pltpu.HBM) if i in far_in else x for i, x in enumerate(inputs)]
     return pl.pallas_call(
         kernel,
-        out_shape=[jax.ShapeDtypeStruct(shape, F32) for shape in outs],
-        in_specs=[pl.BlockSpec(memory_space=space) for space in spaces],
-        out_specs=[pl.BlockSpec(memory_space=pltpu.VMEM)] * len(outs),
-        scratch_shapes=[pltpu.VMEM(shape, F32) for shape in scratch],
-        compiler_params=pltpu.CompilerParams(vmem_limit_bytes=60 * 1024 * 1024),
+        out_shape=[
+            pltpu.HBM(shape, F32) if i in far_out else jax.ShapeDtypeStruct(shape, F32)
+            for i, shape in enumerate(outs)
+        ],
+        in_specs=[pl.BlockSpec(memory_space=place(i)) for i in range(len(inputs))],
+        out_specs=[
+            pl.BlockSpec(memory_space=pltpu.HBM if i in far_out else pltpu.VMEM) for i in range(len(outs))
+        ],
+        scratch_shapes=[pltpu.VMEM(shape, F32) for shape in scratch]
+        + ([pltpu.SemaphoreType.DMA((sems,))] if sems > 1 else [pltpu.SemaphoreType.DMA] * sems),
+        cost_estimate=pl.CostEstimate(flops=1000, bytes_accessed=1000, transcendentals=0),
+        compiler_params=pltpu.CompilerParams(vmem_limit_bytes=used + used // 4 + 2 * 1024 * 1024),
     )(*inputs)
 
 
@@ -637,11 +700,11 @@
     def tiles(count):
         return (count,) + TILE
 
-    own = (initial, source, absorption, beta_x, beta_y, beta_z)
+    place = jnp.stack([lax.axis_index("gx"), lax.axis_index("gy")]).astype(jnp.int32)
     pairs = size_x // 2
-    up_x, down_x, up_y, down_y, mid, low = call(
+    up_x, down_x, up_y, down_y, mid, low, own = call(
         pack_kernel,
-        own,
+        (initial, source, absorption, beta_x, beta_y, beta_z),
         [
             tiles(sum(UP_PLANES) * plane + mids),
             tiles(sum(DOWN_PLANES) * plane + mids),
@@ -649,33 +712,37 @@
             tiles((6 * pairs + 2) * strip + mids),
             tiles(mids),
             tiles(3),
+            (6,) + source.shape,
         ],
         [(4 * mid_x * size_y, mid_z)],
+        far_in=range(6),
+        sems=6,
     )
     low_x1, high_x1 = shifted(up_x, "gx", 1), shifted(down_x, "gx", -1)
     low_y1, high_y1 = shifted(up_y, "gy", 1), shifted(down_y, "gy", -1)
     up_c, down_c = call(
         functools.partial(corner_kernel, size_x, size_z),
         (low_y1, high_y1),
-        [tiles(sum(UP_CORNER) * strip + 2 * mids), tiles(sum(DOWN_CORNER) * strip + 2 * mids)],
+        [tiles(sum(UP_CORNER) * strip + MID_CORNER), tiles(sum(DOWN_CORNER) * strip + MID_CORNER)],
     )
     low_c1, high_c1 = shifted(up_c, "gx", 1), shifted(down_c, "gx", -1)
 
     wide = (size_x + 2 * FINE, size_y + 2 * PAD, size_z)
-    iterate, coeffs, target, mid_target, up_x, down_x, up_y, down_y = call(
+    iterate, coeffs, mid_target, up_x, down_x, up_y, down_y = call(
         fine_kernel,
-        own + (low_x1, high_x1, low_y1, high_y1, low_c1, high_c1),
+        (own, low_x1, high_x1, low_y1, high_y1, low_c1, high_c1),
         [
             source.shape,
-            (7,) + wide,
-            wide,
+            (7, wide[0] - 4) + wide[1:],
             (mid_x, mid_y, mid_z),
             tiles(4 * plane + mid_x + 12),
             tiles(4 * plane + mid_x + 15),
             tiles(pairs * strip + mid_x),
             tiles(pairs * strip + mid_x),
         ],
-        [(6,) + wide, wide, wide, (mid_x * size_y, mid_z)],
+        [(6,) + wide, (8,) + wide, wide, wide, (mid_x * size_y, mid_z)],
+        far_out=(1,),
+        sems=1,
     )
     low_x2, high_x2 = shifted(up_x, "gx", 1), shifted(down_x, "gx", -1)
     low_y2, high_y2 = shifted(up_y, "gy", 1), shifted(down_y, "gy", -1)
@@ -689,26 +756,28 @@
     mid_wide = (mid_x + 2 * MID, 3 * mid_y, mid_z)
     window, mid_goal, slots = call(
         functools.partial(mid_kernel, count_x, count_y),
-        (mid, low, low_x1, high_x1, low_y1, high_y1, low_c1, high_c1)
+        (place, mid, low, low_x1, high_x1, low_y1, high_y1, low_c1, high_c1)
         + (mid_target, low_x2, high_x2, low_y2, high_y2, low_c2, high_c2),
-        [(4,) + mid_wide, mid_wide, (devices, 5) + TILE],
-        [(7,) + mid_wide] + [mid_wide] * 4 + [(low_x * mid_y, mid_z)],
+        [(4,) + mid_wide, mid_wide, (devices, 4) + TILE],
+        [(8,) + mid_wide] + [mid_wide] * 3 + [(low_x * mid_y, mid_z)],
+        scalars=1,
     )
     own_half = lax.all_to_all(slots, ("gx", "gy"), 0, 0)
     other_half = lax.ppermute(own_half, "gx", [(i, i ^ 1) for i in range(count_x)])
 
-    place = jnp.stack([lax.axis_index("gx"), lax.axis_index("gy")]).astype(jnp.int32)
     low_wide = (low_x * count_x, low_y * count_y, mid_z)
     low_planes = mid_wide[0] // 2
     (result,) = call(
         functools.partial(last_kernel, count_x, count_y),
-        (place, own_half, other_half, window, mid_goal, coeffs, target, iterate)
+        (place, own_half, other_half, window, mid_goal, coeffs, iterate)
         + (low_x2, high_x2, low_y2, high_y2, low_c2, high_c2),
         [source.shape],
-        [(3,) + low_wide, (6,) + low_wide, low_wide, low_wide, low_wide]
-        + [(7,) + mid_wide, mid_wide, mid_wide, mid_wide, (low_planes * 32, mid_z)]
-        + [wide, wide, (2, (mid_x + 4) * 2 * (mid_y + 8), mid_z)],
+        [(3,) + low_wide, (7,) + low_wide, low_wide, low_wide]
+        + [(8,) + mid_wide, mid_wide, mid_wide, (low_planes * 32, mid_z)]
+        + [(7,) + wide, wide, wide, (2, (mid_x + 4) * 2 * (mid_y + 8), mid_z)],
         scalars=1,
+        far_in=(5,),
+        sems=1,
     )
     return result
 

time: 114 us -> 74 us (0.65)
  Pallas kernels: 42.7 us -> 12.7 us
  local copies, waits for them, and re-layouts: 5.47 us -> 0 us
  blocking collectives: 21.9 us -> 19.9 us
  waiting for transfers between devices: 27.1 us -> 25.1 us
    pallas_call x6, Pallas kernels: 42.7 us -> 12.7 us  [call(): pl.pallas_call(kernel, out_shape=[pltpu.HBM(shape, F32) if i in far_out e...]
    unnamed x28 -> x0, local copies, waits for them, and re-layouts: 5.47 us -> none
    ppermute x12, waiting for transfers between devices: 26 us -> 23.6 us  [shifted(): lax.ppermute(value, axis, [(i, (i + step) % count) for i in range(count)])]
    all_to_all x1, blocking collectives: 21.9 us -> 19.9 us  [local(): own_half = lax.all_to_all(slots, ('gx', 'gy'), 0, 0)]
  transfers between devices with their start and end apart: 13 -> 13, of which waited for: 6 -> 7; matrix products, arithmetic and copies ran while one was open for 1% -> 0% of each run, Pallas kernels for 3% -> 0%
where the time goes in v2:
time: 74 us; the launch traced here: 73.8 us
  waiting for transfers between devices  25.1 us (34%)
  blocking collectives  19.9 us (27%)
  starting transfers between devices  16 us (22%)
  Pallas kernels  12.7 us (17%)
    ppermute x12, waiting for transfers between devices, shifted(): lax.ppermute(value, axis, [(i, (i + step) % count) for i in range(count)])  23.6 us
    all_to_all x1, blocking collectives, local(): own_half = lax.all_to_all(slots, ('gx', 'gy'), 0, 0)  19.9 us
    ppermute x12, starting transfers between devices, shifted(): lax.ppermute(value, axis, [(i, (i + step) % count) for i in range(count)])  14.9 us
    pallas_call x6, Pallas kernels, call(): pl.pallas_call(kernel, out_shape=[pltpu.HBM(shape, F32) if i in far_out e...  12.7 us
    ppermute x1, waiting for transfers between devices, local(): lax.ppermute(own_half, 'gx', [(i, i ^ 1) for i in range(count_x)])  1.54 us
  transfers between devices with their start and end apart: 13, of which 7 were waited for; matrix products, arithmetic and copies ran while one was open for 0% of the time, Pallas kernels for 0%

profile of v2, /device:TPU:0, one launch (start us, length us, event | category | flops | bytes accessed | tf_op | source)
XLA Modules:
  0.0 73.8 jit_solution(8939662676090570966)
XLA Ops:
  0.0 2.2 %shard_map.64 = (f32[116,8,128]{2,1,0:T(8,128)S(1)}, f32[120,8,128]{2,1,0:T(8,128)S(1)}, f32[66,8,128]{2,1,0:T(8,128)S(1)}, f32[68,8,128]{2,1,0:T(8,128)S(1)}, f...) custom-call(f32[8,16,256]{2,1,0:T(8,128)} %ini_in.1, f32[8,16,256]{2,1,0:T(8,128)} %src_in.1, ...), custom_call_target="tpu_custom_call" | custom-call | flops 1000 | bytes 1000 | tf_op jit(solution)/shard_map/pallas_call | solution.py:674
  2.2 5.1 %collective-permute-start.3 = (f32[68,8,128]{2,1,0:T(8,128)S(1)}, f32[68,8,128]{2,1,0:T(8,128)S(1)}, u32[]{:S(2)}, u32[]{:S(2)}) collective-permute-start(f32[68,8,128]{2,1,0:T(8,128)S(1)} %get-tuple-element.31), channel_id=1, source_target_pairs={{0,3},{1,0},{2,1},{3,2},{4,7},{5,4},{6,5},{7,6},{8,11},{9,8},{10,9... | collective-permute-start | bytes 835592 | tf_op jit(solution)/shard_map/ppermute | solution.py:108
  7.3 0.0 collective-permute-start.2
  7.3 1.6 %collective-permute-start.1 = (f32[120,8,128]{2,1,0:T(8,128)S(1)}, f32[120,8,128]{2,1,0:T(8,128)S(1)}, u32[]{:S(2)}, u32[]{:S(2)}) collective-permute-start(f32[120,8,128]{2,1,0:T(8,128)S(1)} %get-tuple-element.29), channel_id=1, source_target_pairs={{0,28},{4,0},{8,4},{12,8},{16,12},{20,16},{24,20},{28,24},{1,29},{... | collective-permute-start | bytes 1474568 | tf_op jit(solution)/shard_map/ppermute | solution.py:108
  8.9 0.0 collective-permute-start
  8.9 11.0 %collective-permute-done.2.low_y = f32[66,8,128]{2,1,0:T(8,128)S(1)} collective-permute-done((f32[66,8,128]{2,1,0:T(8,128)S(1)}, f32[66,8,128]{2,1,0:T(8,128)S(1)}, u32[]{:S(2)}, u32[]{:S(2)}) %collective-permute-start.2) | collective-permute-done | bytes 270368 | tf_op jit(solution)/shard_map/ppermute | solution.py:108
  19.9 0.0 collective-permute-done.3.high_y
  20.0 1.1 %collective-permute-start.5 = (f32[66,8,128]{2,1,0:T(8,128)S(1)}, f32[66,8,128]{2,1,0:T(8,128)S(1)}, u32[]{:S(2)}, u32[]{:S(2)}) collective-permute-start(f32[66,8,128]{2,1,0:T(8,128)S(1)} %get-tuple-element.33), channel_id=1, source_target_pairs={{0,28},{4,0},{8,4},{12,8},{16,12},{20,16},{24,20},{28,24},{1,29},{... | collective-permute-start | bytes 811016 | tf_op jit(solution)/shard_map/ppermute | solution.py:108
  21.1 0.0 collective-permute-start.4
  21.1 0.6 collective-permute-done.low_x
  21.7 0.0 collective-permute-done.1.high_x
  21.7 8.1 %collective-permute-done.4.low_c = f32[64,8,128]{2,1,0:T(8,128)S(1)} collective-permute-done((f32[64,8,128]{2,1,0:T(8,128)S(1)}, f32[64,8,128]{2,1,0:T(8,128)S(1)}, u32[]{:S(2)}, u32[]{:S(2)}) %collective-permute-start.4) | collective-permute-done | bytes 262176 | tf_op jit(solution)/shard_map/ppermute | solution.py:108
  29.7 0.0 collective-permute-done.5.high_c
  29.7 3.5 %shard_map.66 = (f32[8,16,256]{2,1,0:T(8,128)S(1)}, f32[7,14,32,256]{3,2,1,0:T(8,128)}, f32[4,8,128]{2,1,0:T(8,128)S(1)}, f32[32,8,128]{2,1,0:T(8,128)S(1)}, f32...) custom-call(f32[6,8,16,256]{3,2,1,0:T(8,128)S(1)} %get-tuple-element.34.own, ...), custom_call_target="tpu_custom_call" | custom-call | flops 1000 | bytes 1000 | tf_op jit(solution)/shard_map/pallas_call | solution.py:674
  33.3 1.7 %collective-permute-start.8 = (f32[12,8,128]{2,1,0:T(8,128)S(1)}, f32[12,8,128]{2,1,0:T(8,128)S(1)}, u32[]{:S(2)}, u32[]{:S(2)}) collective-permute-start(f32[12,8,128]{2,1,0:T(8,128)S(1)} %get-tuple-element.38), channel_id=1, source_target_pairs={{0,1},{1,2},{2,3},{3,0},{4,5},{5,6},{6,7},{7,4},{8,9},{9,10},{10,1... | collective-permute-start | bytes 147464 | tf_op jit(solution)/shard_map/ppermute | solution.py:108
  35.0 2.2 %collective-permute-start.9 = (f32[12,8,128]{2,1,0:T(8,128)S(1)}, f32[12,8,128]{2,1,0:T(8,128)S(1)}, u32[]{:S(2)}, u32[]{:S(2)}) collective-permute-start(f32[12,8,128]{2,1,0:T(8,128)S(1)} %get-tuple-element.39), channel_id=1, source_target_pairs={{0,3},{1,0},{2,1},{3,2},{4,7},{5,4},{6,5},{7,6},{8,11},{9,8},{10,9... | collective-permute-start | bytes 147464 | tf_op jit(solution)/shard_map/ppermute | solution.py:108
  37.2 0.3 collective-permute-start.7
  37.5 0.2 collective-permute-start.6
  37.7 1.7 %collective-permute-done.8.low_y.low_y2 = f32[12,8,128]{2,1,0:T(8,128)S(1)} collective-permute-done((f32[12,8,128]{2,1,0:T(8,128)S(1)}, f32[12,8,128]{2,1,0:T(8,128)S(1)}, u32[]{:S(2)}, u32[]{:S(2)}) %collective-permute-start.8) | collective-permute-done | bytes 49184 | tf_op jit(solution)/shard_map/ppermute | solution.py:108
  39.3 0.2 collective-permute-done.9.high_y.high_y2
  39.6 0.1 collective-permute-start.10
  39.7 2.6 %collective-permute-start.11 = (f32[14,8,128]{2,1,0:T(8,128)S(1)}, f32[14,8,128]{2,1,0:T(8,128)S(1)}, u32[]{:S(2)}, u32[]{:S(2)}) collective-permute-start(f32[14,8,128]{2,1,0:T(8,128)S(1)} %get-tuple-element.41), channel_id=1, source_target_pairs={{0,28},{4,0},{8,4},{12,8},{16,12},{20,16},{24,20},{28,24},{1,29},{... | collective-permute-start | bytes 172040 | tf_op jit(solution)/shard_map/ppermute | solution.py:108
  42.3 0.1 pad_add_fusion.place
  42.4 2.0 %collective-permute-done.10.low_c2 = f32[14,8,128]{2,1,0:T(8,128)S(1)} collective-permute-done((f32[14,8,128]{2,1,0:T(8,128)S(1)}, f32[14,8,128]{2,1,0:T(8,128)S(1)}, u32[]{:S(2)}, u32[]{:S(2)}) %collective-permute-start.10) | collective-permute-done | bytes 57376 | tf_op jit(solution)/shard_map/ppermute | solution.py:108
  44.3 0.0 collective-permute-done.11.high_c2
  44.3 0.0 collective-permute-done.6.low_x2
  44.4 0.0 collective-permute-done.7.high_x2
  44.4 1.2 %shard_map.68 = (f32[4,16,24,128]{3,2,1,0:T(8,128)S(1)}, f32[16,24,128]{2,1,0:T(8,128)S(1)}, f32[32,4,8,128]{3,2,1,0:T(8,128)S(1)}) custom-call(s32[2]{0:T(128)S(1)} %pad_add_fusion.place, f32[16,8,128]{2,1,0:T(8,128)S(1)} %get-tuple-element.26.mid, f32[3,8,128]{2,1,0:T(8,128)S(1)} %get-tuple-element.27.low, f32[116,8,128]{2,1,0:T(8,128)S(1)} %collective-permute-done.low_x, ...), custom_call_target="tpu_custom_call" | custom-call | flops 1000 | bytes 1000 | tf_op jit(solution)/shard_map/pallas_call | solution.py:674
  45.5 19.9 %all_to_all.5.own_half = f32[32,4,8,128]{3,2,1,0:T(8,128)S(1)} all-to-all(f32[32,4,8,128]{3,2,1,0:T(8,128)S(1)} %get-tuple-element.42), channel_id=1, replica_groups=mesh['gx'=8,'gy'=4] {'gx','gy'}, dimensions={0} | all-to-all | bytes 1048576 | tf_op jit(solution)/shard_map/all_to_all | solution.py:765
  65.4 1.2 %collective-permute-start.12 = (f32[32,4,8,128]{3,2,1,0:T(8,128)S(1)}, f32[32,4,8,128]{3,2,1,0:T(8,128)S(1)}, u32[]{:S(2)}, u32[]{:S(2)}) collective-permute-start(f32[32,4,8,128]{3,2,1,0:T(8,128)S(1)} %all_to_all.5.own_half), channel_id=1, source_target_pairs={{0,4},{4,0},{8,12},{12,8},{16,20},{20,16},{24,28},{28,24},{1,5},{5... | collective-permute-start | bytes 1572872 | tf_op jit(solution)/shard_map/ppermute | solution.py:766
  66.6 1.5 %collective-permute-done.12.other_half = f32[32,4,8,128]{3,2,1,0:T(8,128)S(1)} collective-permute-done((f32[32,4,8,128]{3,2,1,0:T(8,128)S(1)}, f32[32,4,8,128]{3,2,1,0:T(8,128)S(1)}, u32[]{:S(2)}, u32[]{:S(2)}) %collective-permute-start.12) | collective-permute-done | bytes 524320 | tf_op jit(solution)/shard_map/ppermute | solution.py:766
  68.1 5.7 %shard_map.69 = f32[8,16,256]{2,1,0:T(8,128)} custom-call(s32[2]{0:T(128)S(1)} %pad_add_fusion.place, f32[32,4,8,128]{3,2,1,0:T(8,128)S(1)} %all_to_all.5.own_half, f32[32,4,8,128]{3,2,1,0:T(8,128)S(1)} %collective-permute-done.12.other_half, f32[4,16,24,128]{3,2,1,0:T(8,128)S(1)} %get-tuple-element.43.window, ...), custom_call_target="tpu_custom_call" | custom-call | flops 1000 | bytes 1000 | tf_op jit(solution)/shard_map/pallas_call | solution.py:674
  (2 shorter events, 0.1 us)
Async XLA Ops:
  2.2 17.7 %collective-permute-start.3 = (f32[68,8,128]{2,1,0:T(8,128)S(1)}, f32[68,8,128]{2,1,0:T(8,128)S(1)}, u32[]{:S(2)}, u32[]{:S(2)}) collective-permute-start(f32[68,8,128]{2,1,0:T(8,128)S(1)} %get-tuple-element.31), channel_id=1, source_target_pairs={{0,3},{1,0},{2,1},{3,2},{4,7},{5,4},{6,5},{7,6},{8,11},{9,8},{10,9... | collective-permute-start | bytes 835592 | tf_op jit(solution)/shard_map/ppermute | solution.py:108
  7.3 12.6 %collective-permute-start.2 = (f32[66,8,128]{2,1,0:T(8,128)S(1)}, f32[66,8,128]{2,1,0:T(8,128)S(1)}, u32[]{:S(2)}, u32[]{:S(2)}) collective-permute-start(f32[66,8,128]{2,1,0:T(8,128)S(1)} %get-tuple-element.30), channel_id=1, source_target_pairs={{0,1},{1,2},{2,3},{3,0},{4,5},{5,6},{6,7},{7,4},{8,9},{9,10},{10,1... | collective-permute-start | bytes 811016 | tf_op jit(solution)/shard_map/ppermute | solution.py:108
  7.3 14.3 %collective-permute-start.1 = (f32[120,8,128]{2,1,0:T(8,128)S(1)}, f32[120,8,128]{2,1,0:T(8,128)S(1)}, u32[]{:S(2)}, u32[]{:S(2)}) collective-permute-start(f32[120,8,128]{2,1,0:T(8,128)S(1)} %get-tuple-element.29), channel_id=1, source_target_pairs={{0,28},{4,0},{8,4},{12,8},{16,12},{20,16},{24,20},{28,24},{1,29},{... | collective-permute-start | bytes 1474568 | tf_op jit(solution)/shard_map/ppermute | solution.py:108
  8.9 12.7 %collective-permute-start = (f32[116,8,128]{2,1,0:T(8,128)S(1)}, f32[116,8,128]{2,1,0:T(8,128)S(1)}, u32[]{:S(2)}, u32[]{:S(2)}) collective-permute-start(f32[116,8,128]{2,1,0:T(8,128)S(1)} %get-tuple-element.28), channel_id=1, source_target_pairs={{0,4},{4,8},{8,12},{12,16},{16,20},{20,24},{24,28},{28,0},{1,5},{5... | collective-permute-start | bytes 1425416 | tf_op jit(solution)/shard_map/ppermute | solution.py:108
  20.0 9.8 %collective-permute-start.5 = (f32[66,8,128]{2,1,0:T(8,128)S(1)}, f32[66,8,128]{2,1,0:T(8,128)S(1)}, u32[]{:S(2)}, u32[]{:S(2)}) collective-permute-start(f32[66,8,128]{2,1,0:T(8,128)S(1)} %get-tuple-element.33), channel_id=1, source_target_pairs={{0,28},{4,0},{8,4},{12,8},{16,12},{20,16},{24,20},{28,24},{1,29},{... | collective-permute-start | bytes 811016 | tf_op jit(solution)/shard_map/ppermute | solution.py:108
  21.1 8.7 %collective-permute-start.4 = (f32[64,8,128]{2,1,0:T(8,128)S(1)}, f32[64,8,128]{2,1,0:T(8,128)S(1)}, u32[]{:S(2)}, u32[]{:S(2)}) collective-permute-start(f32[64,8,128]{2,1,0:T(8,128)S(1)} %get-tuple-element.32), channel_id=1, source_target_pairs={{0,4},{4,8},{8,12},{12,16},{16,20},{20,24},{24,28},{28,0},{1,5},{5... | collective-permute-start | bytes 786440 | tf_op jit(solution)/shard_map/ppermute | solution.py:108
  33.3 6.0 %collective-permute-start.8 = (f32[12,8,128]{2,1,0:T(8,128)S(1)}, f32[12,8,128]{2,1,0:T(8,128)S(1)}, u32[]{:S(2)}, u32[]{:S(2)}) collective-permute-start(f32[12,8,128]{2,1,0:T(8,128)S(1)} %get-tuple-element.38), channel_id=1, source_target_pairs={{0,1},{1,2},{2,3},{3,0},{4,5},{5,6},{6,7},{7,4},{8,9},{9,10},{10,1... | collective-permute-start | bytes 147464 | tf_op jit(solution)/shard_map/ppermute | solution.py:108
  35.0 4.6 %collective-permute-start.9 = (f32[12,8,128]{2,1,0:T(8,128)S(1)}, f32[12,8,128]{2,1,0:T(8,128)S(1)}, u32[]{:S(2)}, u32[]{:S(2)}) collective-permute-start(f32[12,8,128]{2,1,0:T(8,128)S(1)} %get-tuple-element.39), channel_id=1, source_target_pairs={{0,3},{1,0},{2,1},{3,2},{4,7},{5,4},{6,5},{7,6},{8,11},{9,8},{10,9... | collective-permute-start | bytes 147464 | tf_op jit(solution)/shard_map/ppermute | solution.py:108
  37.2 7.2 %collective-permute-start.7 = (f32[35,8,128]{2,1,0:T(8,128)S(1)}, f32[35,8,128]{2,1,0:T(8,128)S(1)}, u32[]{:S(2)}, u32[]{:S(2)}) collective-permute-start(f32[35,8,128]{2,1,0:T(8,128)S(1)} %get-tuple-element.37), channel_id=1, source_target_pairs={{0,28},{4,0},{8,4},{12,8},{16,12},{20,16},{24,20},{28,24},{1,29},{... | collective-permute-start | bytes 430088 | tf_op jit(solution)/shard_map/ppermute | solution.py:108
  37.5 6.9 %collective-permute-start.6 = (f32[32,8,128]{2,1,0:T(8,128)S(1)}, f32[32,8,128]{2,1,0:T(8,128)S(1)}, u32[]{:S(2)}, u32[]{:S(2)}) collective-permute-start(f32[32,8,128]{2,1,0:T(8,128)S(1)} %get-tuple-element.36), channel_id=1, source_target_pairs={{0,4},{4,8},{8,12},{12,16},{16,20},{20,24},{24,28},{28,0},{1,5},{5... | collective-permute-start | bytes 393224 | tf_op jit(solution)/shard_map/ppermute | solution.py:108
  39.6 4.8 %collective-permute-start.10 = (f32[14,8,128]{2,1,0:T(8,128)S(1)}, f32[14,8,128]{2,1,0:T(8,128)S(1)}, u32[]{:S(2)}, u32[]{:S(2)}) collective-permute-start(f32[14,8,128]{2,1,0:T(8,128)S(1)} %get-tuple-element.40), channel_id=1, source_target_pairs={{0,4},{4,8},{8,12},{12,16},{16,20},{20,24},{24,28},{28,0},{1,5},{5... | collective-permute-start | bytes 172040 | tf_op jit(solution)/shard_map/ppermute | solution.py:108
  39.7 4.7 %collective-permute-start.11 = (f32[14,8,128]{2,1,0:T(8,128)S(1)}, f32[14,8,128]{2,1,0:T(8,128)S(1)}, u32[]{:S(2)}, u32[]{:S(2)}) collective-permute-start(f32[14,8,128]{2,1,0:T(8,128)S(1)} %get-tuple-element.41), channel_id=1, source_target_pairs={{0,28},{4,0},{8,4},{12,8},{16,12},{20,16},{24,20},{28,24},{1,29},{... | collective-permute-start | bytes 172040 | tf_op jit(solution)/shard_map/ppermute | solution.py:108
  65.4 2.7 %collective-permute-start.12 = (f32[32,4,8,128]{3,2,1,0:T(8,128)S(1)}, f32[32,4,8,128]{3,2,1,0:T(8,128)S(1)}, u32[]{:S(2)}, u32[]{:S(2)}) collective-permute-start(f32[32,4,8,128]{3,2,1,0:T(8,128)S(1)} %all_to_all.5.own_half), channel_id=1, source_target_pairs={{0,4},{4,0},{8,12},{12,8},{16,20},{20,16},{24,28},{28,24},{1,5},{5... | collective-permute-start | bytes 1572872 | tf_op jit(solution)/shard_map/ppermute | solution.py:766

commit v3 on v2

--- a/solution.py
+++ b/solution.py
@@ -235,8 +235,39 @@
     return ref[ref.shape[0] - MID_CORNER + 16 + array * 2 + q - 2]
 
 
-def scale_coeffs(scale, absorb, face_x, face_y, face_z, coeffs, diagonal, planes):
-    rows, lanes = absorb.shape[1:]
+class Planes:
+    def __init__(self, *parts):
+        self.parts = parts
+        self.shape = parts[0][2].shape
+
+    def find(self, i):
+        for start, stop, ref, offset, lead in self.parts:
+            if start <= i < stop:
+                return ref, lead + (i - start + offset,)
+        raise IndexError(i)
+
+    def __getitem__(self, i):
+        ref, index = self.find(i)
+        return ref[index]
+
+
+class Stack:
+    def __init__(self, *parts):
+        self.parts = parts
+
+    def of(self, kind):
+        return Planes(*((a, b, ref, offset, (kind,)) for a, b, ref, offset in self.parts))
+
+    def __getitem__(self, index):
+        return self.of(index[0])[index[1]]
+
+    def __setitem__(self, index, value):
+        ref, place = self.of(index[0]).find(index[1])
+        ref[place] = value
+
+
+def scale_coeffs(scale, absorb, face_x, face_y, face_z, coeffs, planes, target=None, diagonal=None):
+    rows, lanes = absorb.shape[-2:]
     lane = iota((rows, lanes), 1)
 
     def body(i, carry):
@@ -253,107 +284,135 @@
         coeffs[3, i] = scaled * yh
         coeffs[4, i] = jnp.where(lane == 0, 0.0, scaled * zl)
         coeffs[5, i] = scaled * zh
-        coeffs[7, i] = inverse
+        if target is not None:
+            coeffs[6, i] = target[i] * inverse
+        else:
+            coeffs[6, i] = inverse
         if diagonal is not None:
-            diagonal[i] = diag
+            coeffs[7, i] = diag
         return carry
 
     each(*planes, body)
 
 
-def scaled_remain(coeffs, i, below, here, above):
-    total = coeffs[6, i] - here
+def scaled_remain(coeffs, i, below, here, above, goal=None):
+    total = (coeffs[6, i] if goal is None else goal[i]) - here
     total = total + coeffs[0, i] * below + coeffs[1, i] * above
     total = total + coeffs[2, i] * roll(here, 1, 0) + coeffs[3, i] * roll(here, -1, 0)
     return total + coeffs[4, i] * roll(here, 1, 1) + coeffs[5, i] * roll(here, -1, 1)
 
 
-def sweep_window(iterate, update, coeffs, planes, pair, first):
+def sweep_window(iterate, update, coeffs, planes, pair, first, goal=None, source=None):
     start, stop = planes
+    source = iterate if source is None else source
 
     def body(i, carry):
         below, here = carry
-        above = iterate[i + 1]
-        step = pair[1] * scaled_remain(coeffs, i, below, here, above)
+        above = source[i + 1]
+        step = pair[1] * scaled_remain(coeffs, i, below, here, above, goal)
         if not first:
             step = step + pair[0] * update[i]
         update[i] = step
         iterate[i] = here + step
         return here, above
 
-    each(start, stop, body, (iterate[start - 1], iterate[start]))
-
-
-def assemble_fine(window, own, low_x, high_x, low_y, high_y, low_c, high_c, up, down, up_c, down_c, starts):
+    each(start, stop, body, (source[start - 1], source[start]))
+
+
+def assemble_own(window, own, low_y, high_y, low_start, high_start):
     size_x, size_y, size_z = own.shape
-    for plane in range(size_x):
-        window[FINE + plane, PAD : PAD + size_y] = own[plane]
-    reader = Reader(low_x, starts[0])
-    for plane in range(up):
-        window[FINE - up + plane, PAD : PAD + size_y] = reader.get(size_y, size_z)
-    reader = Reader(high_x, starts[1])
-    for plane in range(down):
-        window[FINE + size_x + plane, PAD : PAD + size_y] = reader.get(size_y, size_z)
     high = PAD + size_y
-    low_reader, high_reader = Reader(low_y, starts[2]), Reader(high_y, starts[3])
+    low_reader, high_reader = Reader(low_y, low_start), Reader(high_y, high_start)
     for pair in range(0, size_x, 2):
+        window[pair, PAD:high] = own[pair]
+        window[pair + 1, PAD:high] = own[pair + 1]
         tile = low_reader.get(8, size_z)
-        window[FINE + pair, 0:8] = roll(tile, 4, 0)
-        window[FINE + pair + 1, 0:8] = tile
+        window[pair, 0:8] = roll(tile, 4, 0)
+        window[pair + 1, 0:8] = tile
         tile = high_reader.get(8, size_z)
-        window[FINE + pair, high : high + 8] = tile
-        window[FINE + pair + 1, high : high + 8] = roll(tile, 4, 0)
-    for ref, start, first, count in (
-        (low_c, starts[4], FINE - up_c, up_c),
-        (high_c, starts[5], FINE + size_x, down_c),
-    ):
-        reader = Reader(ref, start)
-        for plane in range(count):
-            tile = roll(reader.get(8, size_z), 4, 0)
-            window[first + plane, 0:8] = tile
-            window[first + plane, high : high + 8] = tile
-
-
-def fine_kernel(
-    own, low_x, high_x, low_y, high_y, low_c, high_c,
-    iterate_out, coeffs_out, mid_target, up_x, down_x, up_y, down_y,
-    windows, coeffs, update, diagonal, rest, sem,
-):
+        window[pair, high : high + 8] = tile
+        window[pair + 1, high : high + 8] = roll(tile, 4, 0)
+
+
+def assemble_side(window, first, count, rows, planes, plane_start, corners, corner_start, corner_count, from_end):
+    size_y, size_z = rows
+    high = PAD + size_y
+    reader = Reader(planes, plane_start)
+    for plane in range(count):
+        window[first + plane, PAD:high] = reader.get(size_y, size_z)
+    reader = Reader(corners, corner_start)
+    first += count - corner_count if from_end else 0
+    for plane in range(corner_count):
+        tile = roll(reader.get(8, size_z), 4, 0)
+        window[first + plane, 0:8] = tile
+        window[first + plane, high : high + 8] = tile
+
+
+def assemble_owns(windows, own, low_y, high_y):
     size_x, size_y, size_z = own.shape[1:]
-    plane_tiles, strip_tiles = tiles_of(size_y, size_z), tiles_of(8, size_z)
-    starts = [0] * 6
+    per_field = (size_x // 2) * tiles_of(8, size_z)
     for field in range(6):
-        assemble_fine(
-            windows.at[field], own.at[field], low_x, high_x, low_y, high_y, low_c, high_c,
-            UP_PLANES[field], DOWN_PLANES[field], UP_CORNER[field], DOWN_CORNER[field], tuple(starts),
-        )
-        starts[0] += UP_PLANES[field] * plane_tiles
-        starts[1] += DOWN_PLANES[field] * plane_tiles
-        starts[2] += (size_x // 2) * strip_tiles
-        starts[3] += (size_x // 2) * strip_tiles
-        starts[4] += UP_CORNER[field] * strip_tiles
-        starts[5] += DOWN_CORNER[field] * strip_tiles
-    low_line = Reader(low_y, starts[2]).get(8, size_z)
-    high_reader = Reader(high_y, starts[3])
+        assemble_own(windows.at[field], own.at[field], low_y, high_y, field * per_field, field * per_field)
+    low_line = Reader(low_y, 6 * per_field).get(8, size_z)
+    high_reader = Reader(high_y, 6 * per_field)
     high_line = high_reader.get(8, size_z)
     face_line = high_reader.get(8, size_z)
     high = PAD + size_y
     for plane in range(size_x):
-        windows[0, FINE + plane, 3:4] = low_line[plane : plane + 1]
-        windows[0, FINE + plane, high + 4 : high + 5] = high_line[plane : plane + 1]
-        windows[4, FINE + plane, high + 4 : high + 5] = face_line[plane : plane + 1]
-
-    iterate = windows.at[0]
-    last = size_x + 2 * FINE - 1
-    scale_coeffs(1.0, windows.at[2], windows.at[3], windows.at[4], windows.at[5], coeffs, diagonal, (1, last))
-
-    for plane in range(1, last):
-        coeffs[6, plane] = windows[1, plane] * coeffs[7, plane]
-    keep = pltpu.make_async_copy(coeffs.at[:7, 2 : last - 1], coeffs_out, sem)
-    keep.start()
+        windows[0, plane, 3:4] = low_line[plane : plane + 1]
+        windows[0, plane, high + 4 : high + 5] = high_line[plane : plane + 1]
+        windows[4, plane, high + 4 : high + 5] = face_line[plane : plane + 1]
+
+
+def assemble_sides(side_windows, rows, low_x, high_x, low_c, high_c):
+    plane_tiles, strip_tiles = tiles_of(*rows), tiles_of(8, rows[1])
+    starts = [0] * 4
+    for field in range(6):
+        up, down, up_c, down_c = (
+            kinds[field] for kinds in (UP_PLANES, DOWN_PLANES, UP_CORNER, DOWN_CORNER)
+        )
+        window = side_windows.at[field]
+        assemble_side(
+            window, FINE - up, up, rows, low_x, starts[0], low_c, starts[2], up_c, True
+        )
+        assemble_side(
+            window, FINE, down, rows, high_x, starts[1], high_c, starts[3], down_c, False
+        )
+        starts[0] += up * plane_tiles
+        starts[1] += down * plane_tiles
+        starts[2] += up_c * strip_tiles
+        starts[3] += down_c * strip_tiles
+
+
+def own_kernel(own, low_y, high_y, windows, coeffs):
+    assemble_owns(windows, own, low_y, high_y)
+    fields = [windows.at[field] for field in range(6)]
+    scale_coeffs(1.0, *fields[2:], coeffs, (0, own.shape[1] - 1), fields[1], True)
+
+
+def fine_kernel(
+    own_windows, own_coeffs, low_x, high_x, low_c, high_c,
+    iterate_out, mid_target, up_x, down_x, up_y, down_y,
+    side_windows, side_coeffs, iterate, update, rest,
+):
+    size_x, size_z = own_windows.shape[1], own_windows.shape[3]
+    size_y = own_windows.shape[2] - 2 * PAD
+    assemble_sides(side_windows, (size_y, size_z), low_x, high_x, low_c, high_c)
+    end = FINE + size_x
+    last = end + FINE - 1
+    windows = Stack(
+        (0, FINE, side_windows, 0), (FINE, end, own_windows, 0), (end, last + 1, side_windows, FINE)
+    )
+    coeffs = Stack(
+        (0, FINE, side_coeffs, 0), (FINE, end - 1, own_coeffs, 0), (end - 1, last + 1, side_coeffs, FINE)
+    )
+    fields = [windows.of(field) for field in range(6)]
+    scale_coeffs(1.0, *fields[2:], coeffs, (1, FINE), fields[1], True)
+    scale_coeffs(1.0, *fields[2:], coeffs, (end - 1, last), fields[1], True)
     for sweep, pair in enumerate(chebyshev_weights(SWEEPS)):
         sweep_window(
-            iterate, update, coeffs, (1 + sweep, last - sweep), pair, sweep == 0
+            iterate, update, coeffs, (1 + sweep, last - sweep), pair, sweep == 0,
+            source=fields[0] if sweep == 0 else None,
         )
     mid_x, mid_y = size_x // 2, size_y // 2
     lines = []
@@ -361,7 +420,7 @@
         total = None
         for plane in (FINE + 2 * block, FINE + 2 * block + 1):
             remain = scaled_remain(coeffs, plane, iterate[plane - 1], iterate[plane], iterate[plane + 1])
-            remain = (remain * diagonal[plane])[PAD : PAD + size_y]
+            remain = (remain * coeffs[7, plane])[PAD : PAD + size_y]
             total = remain if total is None else total + remain
         lines.append(total)
     rest[...] = dot(jnp.concatenate(lines, axis=0), pair_sum(size_z))
@@ -396,7 +455,6 @@
     bottoms.put(whole_corner(high_c, 1, 1, 0))
     bottoms.put(high_x[high_start + mid_x + 1])
     bottoms.put(whole_corner(high_c, 1, 1, 1))
-    keep.wait()
 
 
 def corner_two_kernel(size_x, size_z, low_y, high_y, up, down):
@@ -412,13 +470,9 @@
                 writer.put(ref[tile])
 
 
-def mid_kernel(
-    count_x, count_y, place, mid, low, low_x, high_x, low_y, high_y, low_c, high_c,
-    mid_target, low_x2, high_x2, low_y2, high_y2, low_c2, high_c2,
-    window, target, slots,
-    coeffs, diagonal, iterate, update, rest,
-):
-    mid_x, mid_y, mid_z = mid_target.shape
+def mid_coeffs_kernel(mid, low_x, high_x, low_y, high_y, low_c, high_c, low_x2, high_x2, coeffs, window):
+    mid_y, mid_z = mid.shape[1:]
+    mid_x = mid.shape[0] // 4
     mids = 4 * mid_x
     first = MID - mid_x
     blocks = {
@@ -452,6 +506,17 @@
     for by in range(3):
         window[1, far + 1, by * mid_y : (by + 1) * mid_y] = high_x2[own_planes + 12 + by]
 
+    scale_coeffs(0.25, *(window.at[array] for array in range(4)), coeffs, (first - 1, far + 1), None, True)
+
+
+def mid_kernel(
+    count_x, count_y, place, low, mid_target, coeffs, low_x2, high_x2, low_y2, high_y2, low_c2, high_c2,
+    goal, slots, target, iterate, update, rest,
+):
+    mid_x, mid_y, mid_z = mid_target.shape
+    first = MID - mid_x
+    far = 3 * mid_x + first
+    fine_tiles = 4 * tiles_of(2 * mid_y, 2 * mid_z)
     blocks = {
         (0, 0): (low_c2, low_c2.shape[0] - 2 * mid_x), (0, 1): (low_x2, fine_tiles),
         (0, 2): (low_c2, low_c2.shape[0] - mid_x), (1, 0): (low_y2, low_y2.shape[0] - mid_x),
@@ -465,25 +530,24 @@
         for plane in range(mid_x):
             target[first + bx * mid_x + plane, by * mid_y : (by + 1) * mid_y] = ref[start + plane]
 
-    scale_coeffs(0.25, window.at[0], window.at[1], window.at[2], window.at[3], coeffs, diagonal, (first, far))
     weights = chebyshev_weights(SWEEPS)
 
     def start_sweep(i, carry):
-        goal = target[i] * coeffs[7, i]
-        coeffs[6, i] = goal
-        update[i] = weights[0][1] * goal
-        iterate[i] = weights[0][1] * goal
+        value = target[i] * coeffs[6, i]
+        goal[i] = value
+        update[i] = weights[0][1] * value
+        iterate[i] = weights[0][1] * value
         return carry
 
     each(first, far, start_sweep)
     for sweep in range(1, SWEEPS):
-        sweep_window(iterate, update, coeffs, (first + sweep, far - sweep), weights[sweep], False)
+        sweep_window(iterate, update, coeffs, (first + sweep, far - sweep), weights[sweep], False, goal)
     low_x_size = mid_x // 2
     for block in range(low_x_size):
         total = None
         for plane in (MID + 2 * block, MID + 2 * block + 1):
-            remain = scaled_remain(coeffs, plane, iterate[plane - 1], iterate[plane], iterate[plane + 1])
-            remain = (remain * diagonal[plane])[mid_y : 2 * mid_y]
+            remain = scaled_remain(coeffs, plane, iterate[plane - 1], iterate[plane], iterate[plane + 1], goal)
+            remain = (remain * coeffs[7, plane])[mid_y : 2 * mid_y]
             total = remain if total is None else total + remain
         rest[block * mid_y : (block + 1) * mid_y] = total
     count = low_x_size * mid_y // 2
@@ -572,19 +636,36 @@
         each(0, size_x, body, (iterate[size_x - 1], start))
 
 
+def window_kernel(
+    fields_own, low_x1, high_x1, low_y1, high_y1, low_c1, high_c1,
+    own, low_x, high_x, low_y, high_y, low_c, high_c,
+    window, coeffs, own_windows, side_windows,
+):
+    size_x, size_y, size_z = own.shape
+    assemble_owns(own_windows, fields_own, low_y1, high_y1)
+    assemble_sides(side_windows, (size_y, size_z), low_x1, high_x1, low_c1, high_c1)
+    end = FINE + size_x
+    windows = Stack(
+        (0, FINE, side_windows, 0), (FINE, end, own_windows, 0), (end, end + FINE, side_windows, FINE)
+    )
+    fields = [windows.of(field) for field in range(6)]
+    scale_coeffs(1.0, *fields[2:], Stack((2, end + 3, coeffs, 0)), (2, end + 3), fields[1])
+    assemble_own(window.at[FINE : FINE + size_x], own, low_y, high_y, 0, 0)
+    assemble_side(window, FINE - 4, 4, (size_y, size_z), low_x, 0, low_c, 0, 3, True)
+    assemble_side(window, FINE + size_x, 4, (size_y, size_z), high_x, 0, high_c, 0, 3, False)
+
+
 def last_kernel(
-    count_x, count_y, place, own_half, other_half, window, mid_target, coeffs_in, iterate_own,
-    low_x2, high_x2, low_y2, high_y2, low_c2, high_c2,
+    count_x, count_y, place, own_half, other_half, mid_coeffs, goal_in, fine_coeffs, window,
     out,
     low_fields, low_coeffs, low_iterate, low_update,
-    mid_coeffs, mid_iterate, mid_update, spread_mid,
-    coeffs, iterate, update, spread, sem,
+    goal, mid_iterate, mid_update, spread_mid,
+    iterate, update, spread,
 ):
-    size_x, size_y, size_z = iterate_own.shape
+    size_x, size_y, size_z = out.shape
     mid_x, mid_y, mid_z = size_x // 2, size_y // 2, size_z // 2
     last = size_x + 2 * FINE - 2
-    fetch = pltpu.make_async_copy(coeffs_in, coeffs.at[:, 2:last], sem)
-    fetch.start()
+    coeffs = Stack((2, last, fine_coeffs, 0))
     me_x, me_y = place[0], place[1]
     even = me_x % 2 == 0
 
@@ -623,23 +704,18 @@
         mid_iterate[2 * plane] += part
         mid_iterate[2 * plane + 1] += part
 
-    scale_coeffs(0.25, window.at[0], window.at[1], window.at[2], window.at[3], mid_coeffs, None, (first - 1, far + 1))
-
     for plane in range(first, far):
-        mid_coeffs[6, plane] = mid_target[plane] * mid_coeffs[7, plane]
+        goal[plane] = goal_in[plane]
     for dy in (-1, 0, 1):
         rows = slice((dy + 1) * mid_y, (dy + 2) * mid_y)
         for plane, dx in ((first - 1, -2), (far, 2)):
-            mid_coeffs[6, plane, rows] = half(0, device(dx, dy), 3) * mid_coeffs[7, plane, rows]
+            goal[plane, rows] = half(0, device(dx, dy), 3) * mid_coeffs[6, plane, rows]
     for sweep, pair in enumerate(chebyshev_weights(SWEEPS)):
         sweep_window(
-            mid_iterate, mid_update, mid_coeffs, (first - 1 + sweep, far + 1 - sweep), pair, sweep == 0
+            mid_iterate, mid_update, mid_coeffs, (first - 1 + sweep, far + 1 - sweep), pair, sweep == 0, goal
         )
 
     fine_low = FINE - 4
-    assemble_fine(
-        iterate, iterate_own, low_x2, high_x2, low_y2, high_y2, low_c2, high_c2, 4, 4, 3, 3, (0,) * 6
-    )
     planes = mid_x + 4
     rows = mid_y + 8
     picked = [roll(mid_iterate[MID - 2 + plane], -4, 0)[:rows] for plane in range(planes)]
@@ -652,9 +728,8 @@
     for plane in range(planes):
         lines = slice(plane * 2 * rows, (plane + 1) * 2 * rows)
         part = jnp.concatenate([spread[0, lines], spread[1, lines]], axis=1)
-        iterate[fine_low + 2 * plane] += part
-        iterate[fine_low + 2 * plane + 1] += part
-    fetch.wait()
+        for at in (fine_low + 2 * plane, fine_low + 2 * plane + 1):
+            iterate[at] = window[at] + part
     for sweep, pair in enumerate(chebyshev_weights(SWEEPS)):
         sweep_window(
             iterate, update, coeffs, (2 + sweep, last - sweep), pair, sweep == 0
@@ -727,22 +802,23 @@
     )
     low_c1, high_c1 = shifted(up_c, "gx", 1), shifted(down_c, "gx", -1)
 
-    wide = (size_x + 2 * FINE, size_y + 2 * PAD, size_z)
-    iterate, coeffs, mid_target, up_x, down_x, up_y, down_y = call(
+    tall = (size_y + 2 * PAD, size_z)
+    wide = (size_x + 2 * FINE,) + tall
+    own_windows, own_coeffs = call(
+        own_kernel, (own, low_y1, high_y1), [(6, size_x) + tall, (8, size_x - 1) + tall]
+    )
+    iterate, mid_target, up_x, down_x, up_y, down_y = call(
         fine_kernel,
-        (own, low_x1, high_x1, low_y1, high_y1, low_c1, high_c1),
+        (own_windows, own_coeffs, low_x1, high_x1, low_c1, high_c1),
         [
             source.shape,
-            (7, wide[0] - 4) + wide[1:],
             (mid_x, mid_y, mid_z),
             tiles(4 * plane + mid_x + 12),
             tiles(4 * plane + mid_x + 15),
             tiles(pairs * strip + mid_x),
             tiles(pairs * strip + mid_x),
         ],
-        [(6,) + wide, (8,) + wide, wide, wide, (mid_x * size_y, mid_z)],
-        far_out=(1,),
-        sems=1,
+        [(6, 2 * FINE) + tall, (8, 2 * FINE + 1) + tall, wide, wide, (mid_x * size_y, mid_z)],
     )
     low_x2, high_x2 = shifted(up_x, "gx", 1), shifted(down_x, "gx", -1)
     low_y2, high_y2 = shifted(up_y, "gy", 1), shifted(down_y, "gy", -1)
@@ -754,30 +830,39 @@
     low_c2, high_c2 = shifted(up_c, "gx", 1), shifted(down_c, "gx", -1)
 
     mid_wide = (mid_x + 2 * MID, 3 * mid_y, mid_z)
-    window, mid_goal, slots = call(
+    (mid_coeffs,) = call(
+        mid_coeffs_kernel,
+        (mid, low_x1, high_x1, low_y1, high_y1, low_c1, high_c1, low_x2, high_x2),
+        [(8,) + mid_wide],
+        [(4,) + mid_wide],
+    )
+    goal, slots = call(
         functools.partial(mid_kernel, count_x, count_y),
-        (place, mid, low, low_x1, high_x1, low_y1, high_y1, low_c1, high_c1)
-        + (mid_target, low_x2, high_x2, low_y2, high_y2, low_c2, high_c2),
-        [(4,) + mid_wide, mid_wide, (devices, 4) + TILE],
-        [(8,) + mid_wide] + [mid_wide] * 3 + [(low_x * mid_y, mid_z)],
+        (place, low, mid_target, mid_coeffs, low_x2, high_x2, low_y2, high_y2, low_c2, high_c2),
+        [mid_wide, (devices, 4) + TILE],
+        [mid_wide] * 3 + [(low_x * mid_y, mid_z)],
         scalars=1,
     )
     own_half = lax.all_to_all(slots, ("gx", "gy"), 0, 0)
     other_half = lax.ppermute(own_half, "gx", [(i, i ^ 1) for i in range(count_x)])
 
+    window, coeffs = call(
+        window_kernel,
+        (own, low_x1, high_x1, low_y1, high_y1, low_c1, high_c1)
+        + (iterate, low_x2, high_x2, low_y2, high_y2, low_c2, high_c2),
+        [wide, (7, wide[0] - 4) + tall],
+        [(6, size_x) + tall, (6, 2 * FINE) + tall],
+    )
     low_wide = (low_x * count_x, low_y * count_y, mid_z)
     low_planes = mid_wide[0] // 2
     (result,) = call(
         functools.partial(last_kernel, count_x, count_y),
-        (place, own_half, other_half, window, mid_goal, coeffs, iterate)
-        + (low_x2, high_x2, low_y2, high_y2, low_c2, high_c2),
+        (place, own_half, other_half, mid_coeffs, goal, coeffs, window),
         [source.shape],
         [(3,) + low_wide, (7,) + low_wide, low_wide, low_wide]
-        + [(8,) + mid_wide, mid_wide, mid_wide, (low_planes * 32, mid_z)]
-        + [(7,) + wide, wide, wide, (2, (mid_x + 4) * 2 * (mid_y + 8), mid_z)],
+        + [mid_wide, mid_wide, mid_wide, (low_planes * 32, mid_z)]
+        + [wide, wide, (2, (mid_x + 4) * 2 * (mid_y + 8), mid_z)],
         scalars=1,
-        far_in=(5,),
-        sems=1,
     )
     return result
 

time: 74 us -> 71.3 us (0.964)
  Pallas kernels: 12.7 us -> 11.1 us
  waiting for transfers between devices: 25.1 us -> 24.1 us
    pallas_call x6 -> x9, Pallas kernels: 12.7 us -> 11.1 us  [call(): pl.pallas_call(kernel, out_shape=[pltpu.HBM(shape, F32) if i in far_out e...]
  transfers between devices with their start and end apart: 13 -> 13, of which waited for: 7 -> 8; matrix products, arithmetic and copies ran while one was open for 0% -> 0% of each run, Pallas kernels for 0% -> 1%
where the time goes in v3:
time: 71.3 us; the launch traced here: 71.2 us
  waiting for transfers between devices  24.1 us (34%)
  blocking collectives  19.9 us (28%)
  starting transfers between devices  16 us (22%)
  Pallas kernels  11.1 us (16%)
    ppermute x12, waiting for transfers between devices, shifted(): lax.ppermute(value, axis, [(i, (i + step) % count) for i in range(count)])  23.1 us
    all_to_all x1, blocking collectives, local(): own_half = lax.all_to_all(slots, ('gx', 'gy'), 0, 0)  19.9 us
    ppermute x12, starting transfers between devices, shifted(): lax.ppermute(value, axis, [(i, (i + step) % count) for i in range(count)])  14.8 us
    pallas_call x9, Pallas kernels, call(): pl.pallas_call(kernel, out_shape=[pltpu.HBM(shape, F32) if i in far_out e...  11.1 us
  transfers between devices with their start and end apart: 13, of which 8 were waited for; matrix products, arithmetic and copies ran while one was open for 0% of the time, Pallas kernels for 1%

profile of v3, /device:TPU:0, one launch (start us, length us, event | category | flops | bytes accessed | tf_op | source)
XLA Modules:
  0.0 71.2 jit_solution(17488060404117216858)
XLA Ops:
  0.0 2.2 %shard_map.64 = (f32[116,8,128]{2,1,0:T(8,128)S(1)}, f32[120,8,128]{2,1,0:T(8,128)S(1)}, f32[66,8,128]{2,1,0:T(8,128)S(1)}, f32[68,8,128]{2,1,0:T(8,128)S(1)}, f...) custom-call(f32[8,16,256]{2,1,0:T(8,128)} %ini_in.1, f32[8,16,256]{2,1,0:T(8,128)} %src_in.1, ...), custom_call_target="tpu_custom_call" | custom-call | flops 1000 | bytes 1000 | tf_op jit(solution)/shard_map/pallas_call | solution.py:749
  2.2 5.1 %collective-permute-start.1 = (f32[68,8,128]{2,1,0:T(8,128)S(1)}, f32[68,8,128]{2,1,0:T(8,128)S(1)}, u32[]{:S(2)}, u32[]{:S(2)}) collective-permute-start(f32[68,8,128]{2,1,0:T(8,128)S(1)} %get-tuple-element.31), channel_id=1, source_target_pairs={{0,3},{1,0},{2,1},{3,2},{4,7},{5,4},{6,5},{7,6},{8,11},{9,8},{10,9... | collective-permute-start | bytes 835592 | tf_op jit(solution)/shard_map/ppermute | solution.py:108
  7.3 0.0 collective-permute-start
  7.3 1.6 %collective-permute-start.3 = (f32[120,8,128]{2,1,0:T(8,128)S(1)}, f32[120,8,128]{2,1,0:T(8,128)S(1)}, u32[]{:S(2)}, u32[]{:S(2)}) collective-permute-start(f32[120,8,128]{2,1,0:T(8,128)S(1)} %get-tuple-element.35), channel_id=1, source_target_pairs={{0,28},{4,0},{8,4},{12,8},{16,12},{20,16},{24,20},{28,24},{1,29},{... | collective-permute-start | bytes 1474568 | tf_op jit(solution)/shard_map/ppermute | solution.py:108
  8.9 0.0 collective-permute-start.2
  8.9 11.0 %collective-permute-done.low_y.low_y1 = f32[66,8,128]{2,1,0:T(8,128)S(1)} collective-permute-done((f32[66,8,128]{2,1,0:T(8,128)S(1)}, f32[66,8,128]{2,1,0:T(8,128)S(1)}, u32[]{:S(2)}, u32[]{:S(2)}) %collective-permute-start) | collective-permute-done | bytes 270368 | tf_op jit(solution)/shard_map/ppermute | solution.py:108
  19.9 0.0 collective-permute-done.1.high_y.high_y1
  20.0 1.1 %collective-permute-start.5 = (f32[66,8,128]{2,1,0:T(8,128)S(1)}, f32[66,8,128]{2,1,0:T(8,128)S(1)}, u32[]{:S(2)}, u32[]{:S(2)}) collective-permute-start(f32[66,8,128]{2,1,0:T(8,128)S(1)} %get-tuple-element.37), channel_id=1, source_target_pairs={{0,28},{4,0},{8,4},{12,8},{16,12},{20,16},{24,20},{28,24},{1,29},{... | collective-permute-start | bytes 811016 | tf_op jit(solution)/shard_map/ppermute | solution.py:108
  21.1 0.0 collective-permute-start.4
  21.1 0.3 shard_map.65
  21.4 0.3 collective-permute-done.2.low_x.low_x1
  21.7 0.0 collective-permute-done.3.high_x.high_x1
  21.7 8.1 %collective-permute-done.4.low_c.low_c1 = f32[64,8,128]{2,1,0:T(8,128)S(1)} collective-permute-done((f32[64,8,128]{2,1,0:T(8,128)S(1)}, f32[64,8,128]{2,1,0:T(8,128)S(1)}, u32[]{:S(2)}, u32[]{:S(2)}) %collective-permute-start.4) | collective-permute-done | bytes 262176 | tf_op jit(solution)/shard_map/ppermute | solution.py:108
  29.7 0.0 collective-permute-done.5.high_c.high_c1
  29.7 2.6 %shard_map.67 = (f32[8,16,256]{2,1,0:T(8,128)S(1)}, f32[4,8,128]{2,1,0:T(8,128)S(1)}, f32[32,8,128]{2,1,0:T(8,128)}, f32[35,8,128]{2,1,0:T(8,128)}, f32[12,8,128...) custom-call(f32[6,8,32,256]{3,2,1,0:T(8,128)S(1)} %get-tuple-element.32.own_windows, ...), custom_call_target="tpu_custom_call" | custom-call | flops 1000 | bytes 1000 | tf_op jit(solution)/shard_map/pallas_call | solution.py:749
  32.4 1.6 %collective-permute-start.8 = (f32[12,8,128]{2,1,0:T(8,128)S(1)}, f32[12,8,128]{2,1,0:T(8,128)S(1)}, u32[]{:S(2)}, u32[]{:S(2)}) collective-permute-start(f32[12,8,128]{2,1,0:T(8,128)S(1)} %get-tuple-element.42), channel_id=1, source_target_pairs={{0,1},{1,2},{2,3},{3,0},{4,5},{5,6},{6,7},{7,4},{8,9},{9,10},{10,1... | collective-permute-start | bytes 147464 | tf_op jit(solution)/shard_map/ppermute | solution.py:108
  34.0 2.2 %collective-permute-start.9 = (f32[12,8,128]{2,1,0:T(8,128)S(1)}, f32[12,8,128]{2,1,0:T(8,128)S(1)}, u32[]{:S(2)}, u32[]{:S(2)}) collective-permute-start(f32[12,8,128]{2,1,0:T(8,128)S(1)} %get-tuple-element.43), channel_id=1, source_target_pairs={{0,3},{1,0},{2,1},{3,2},{4,7},{5,4},{6,5},{7,6},{8,11},{9,8},{10,9... | collective-permute-start | bytes 147464 | tf_op jit(solution)/shard_map/ppermute | solution.py:108
  36.2 0.3 collective-permute-start.7
  36.5 0.2 collective-permute-start.6
  36.7 1.7 %collective-permute-done.8.low_y.low_y2 = f32[12,8,128]{2,1,0:T(8,128)S(1)} collective-permute-done((f32[12,8,128]{2,1,0:T(8,128)S(1)}, f32[12,8,128]{2,1,0:T(8,128)S(1)}, u32[]{:S(2)}, u32[]{:S(2)}) %collective-permute-start.8) | collective-permute-done | bytes 49184 | tf_op jit(solution)/shard_map/ppermute | solution.py:108
  38.4 0.2 collective-permute-done.9.high_y.high_y2
  38.6 0.1 collective-permute-start.10
  38.7 2.6 %collective-permute-start.11 = (f32[14,8,128]{2,1,0:T(8,128)S(1)}, f32[14,8,128]{2,1,0:T(8,128)S(1)}, u32[]{:S(2)}, u32[]{:S(2)}) collective-permute-start(f32[14,8,128]{2,1,0:T(8,128)S(1)} %get-tuple-element.45), channel_id=1, source_target_pairs={{0,28},{4,0},{8,4},{12,8},{16,12},{20,16},{24,20},{28,24},{1,29},{... | collective-permute-start | bytes 172040 | tf_op jit(solution)/shard_map/ppermute | solution.py:108
  41.3 0.1 pad_add_fusion.place
  41.4 0.6 collective-permute-done.6.low_x2.low_x
  42.0 0.0 collective-permute-done.7.high_x2.high_x
  42.0 0.2 shard_map.68.coeffs.mid_coeffs
  42.2 1.2 %collective-permute-done.10.low_c2.low_c = f32[14,8,128]{2,1,0:T(8,128)S(1)} collective-permute-done((f32[14,8,128]{2,1,0:T(8,128)S(1)}, f32[14,8,128]{2,1,0:T(8,128)S(1)}, u32[]{:S(2)}, u32[]{:S(2)}) %collective-permute-start.10) | collective-permute-done | bytes 57376 | tf_op jit(solution)/shard_map/ppermute | solution.py:108
  43.4 0.0 collective-permute-done.11.high_c2.high_c
  43.4 1.0 %shard_map.70 = (f32[16,24,128]{2,1,0:T(8,128)S(1)}, f32[32,4,8,128]{3,2,1,0:T(8,128)S(1)}) custom-call(s32[2]{0:T(128)S(1)} %pad_add_fusion.place, f32[3,8,128]{2,1,0:T(8,128)S(1)} %get-tuple-element.28.low, f32[4,8,128]{2,1,0:T(8,128)S(1)} %get-tuple-element.38.mid_target, f32[8,16,24,128]{3,2,1,0:T(8,128)S(1)} %shard_map.68.coeffs.mid_coeffs, ...), custom_call_target="tpu_custom_call" | custom-call | flops 1000 | bytes 1000 | tf_op jit(solution)/shard_map/pallas_call | solution.py:749
  44.4 19.9 %all_to_all.5.own_half = f32[32,4,8,128]{3,2,1,0:T(8,128)S(1)} all-to-all(f32[32,4,8,128]{3,2,1,0:T(8,128)S(1)} %get-tuple-element.46), channel_id=1, replica_groups=mesh['gx'=8,'gy'=4] {'gx','gy'}, dimensions={0} | all-to-all | bytes 1048576 | tf_op jit(solution)/shard_map/all_to_all | solution.py:846
  64.3 1.2 %collective-permute-start.12 = (f32[32,4,8,128]{3,2,1,0:T(8,128)S(1)}, f32[32,4,8,128]{3,2,1,0:T(8,128)S(1)}, u32[]{:S(2)}, u32[]{:S(2)}) collective-permute-start(f32[32,4,8,128]{3,2,1,0:T(8,128)S(1)} %all_to_all.5.own_half), channel_id=1, source_target_pairs={{0,4},{4,0},{8,12},{12,8},{16,20},{20,16},{24,28},{28,24},{1,5},{5... | collective-permute-start | bytes 1572872 | tf_op jit(solution)/shard_map/ppermute | solution.py:847
  65.5 0.5 shard_map.71
  66.0 1.0 %collective-permute-done.12.other_half = f32[32,4,8,128]{3,2,1,0:T(8,128)S(1)} collective-permute-done((f32[32,4,8,128]{3,2,1,0:T(8,128)S(1)}, f32[32,4,8,128]{3,2,1,0:T(8,128)S(1)}, u32[]{:S(2)}, u32[]{:S(2)}) %collective-permute-start.12) | collective-permute-done | bytes 524320 | tf_op jit(solution)/shard_map/ppermute | solution.py:847
  67.0 4.1 %shard_map.72 = f32[8,16,256]{2,1,0:T(8,128)} custom-call(s32[2]{0:T(128)S(1)} %pad_add_fusion.place, f32[32,4,8,128]{3,2,1,0:T(8,128)S(1)} %all_to_all.5.own_half, f32[32,4,8,128]{3,2,1,0:T(8,128)S(1)} %collective-permute-done.12.other_half, f32[8,16,24,128]{3,2,1,0:T(8,128)S(1)} %shard_map.68.coeffs.mid_coeffs, ...), custom_call_target="tpu_custom_call" | custom-call | flops 1000 | bytes 1000 | tf_op jit(solution)/shard_map/pallas_call | solution.py:749
  (2 shorter events, 0.1 us)
Async XLA Ops:
  2.2 17.7 %collective-permute-start.1 = (f32[68,8,128]{2,1,0:T(8,128)S(1)}, f32[68,8,128]{2,1,0:T(8,128)S(1)}, u32[]{:S(2)}, u32[]{:S(2)}) collective-permute-start(f32[68,8,128]{2,1,0:T(8,128)S(1)} %get-tuple-element.31), channel_id=1, source_target_pairs={{0,3},{1,0},{2,1},{3,2},{4,7},{5,4},{6,5},{7,6},{8,11},{9,8},{10,9... | collective-permute-start | bytes 835592 | tf_op jit(solution)/shard_map/ppermute | solution.py:108
  7.3 12.6 %collective-permute-start = (f32[66,8,128]{2,1,0:T(8,128)S(1)}, f32[66,8,128]{2,1,0:T(8,128)S(1)}, u32[]{:S(2)}, u32[]{:S(2)}) collective-permute-start(f32[66,8,128]{2,1,0:T(8,128)S(1)} %get-tuple-element.30), channel_id=1, source_target_pairs={{0,1},{1,2},{2,3},{3,0},{4,5},{5,6},{6,7},{7,4},{8,9},{9,10},{10,1... | collective-permute-start | bytes 811016 | tf_op jit(solution)/shard_map/ppermute | solution.py:108
  7.3 14.3 %collective-permute-start.3 = (f32[120,8,128]{2,1,0:T(8,128)S(1)}, f32[120,8,128]{2,1,0:T(8,128)S(1)}, u32[]{:S(2)}, u32[]{:S(2)}) collective-permute-start(f32[120,8,128]{2,1,0:T(8,128)S(1)} %get-tuple-element.35), channel_id=1, source_target_pairs={{0,28},{4,0},{8,4},{12,8},{16,12},{20,16},{24,20},{28,24},{1,29},{... | collective-permute-start | bytes 1474568 | tf_op jit(solution)/shard_map/ppermute | solution.py:108
  8.9 12.7 %collective-permute-start.2 = (f32[116,8,128]{2,1,0:T(8,128)S(1)}, f32[116,8,128]{2,1,0:T(8,128)S(1)}, u32[]{:S(2)}, u32[]{:S(2)}) collective-permute-start(f32[116,8,128]{2,1,0:T(8,128)S(1)} %get-tuple-element.34), channel_id=1, source_target_pairs={{0,4},{4,8},{8,12},{12,16},{16,20},{20,24},{24,28},{28,0},{1,5},{5... | collective-permute-start | bytes 1425416 | tf_op jit(solution)/shard_map/ppermute | solution.py:108
  20.0 9.8 %collective-permute-start.5 = (f32[66,8,128]{2,1,0:T(8,128)S(1)}, f32[66,8,128]{2,1,0:T(8,128)S(1)}, u32[]{:S(2)}, u32[]{:S(2)}) collective-permute-start(f32[66,8,128]{2,1,0:T(8,128)S(1)} %get-tuple-element.37), channel_id=1, source_target_pairs={{0,28},{4,0},{8,4},{12,8},{16,12},{20,16},{24,20},{28,24},{1,29},{... | collective-permute-start | bytes 811016 | tf_op jit(solution)/shard_map/ppermute | solution.py:108
  21.1 8.7 %collective-permute-start.4 = (f32[64,8,128]{2,1,0:T(8,128)S(1)}, f32[64,8,128]{2,1,0:T(8,128)S(1)}, u32[]{:S(2)}, u32[]{:S(2)}) collective-permute-start(f32[64,8,128]{2,1,0:T(8,128)S(1)} %get-tuple-element.36), channel_id=1, source_target_pairs={{0,4},{4,8},{8,12},{12,16},{16,20},{20,24},{24,28},{28,0},{1,5},{5... | collective-permute-start | bytes 786440 | tf_op jit(solution)/shard_map/ppermute | solution.py:108
  32.4 6.0 %collective-permute-start.8 = (f32[12,8,128]{2,1,0:T(8,128)S(1)}, f32[12,8,128]{2,1,0:T(8,128)S(1)}, u32[]{:S(2)}, u32[]{:S(2)}) collective-permute-start(f32[12,8,128]{2,1,0:T(8,128)S(1)} %get-tuple-element.42), channel_id=1, source_target_pairs={{0,1},{1,2},{2,3},{3,0},{4,5},{5,6},{6,7},{7,4},{8,9},{9,10},{10,1... | collective-permute-start | bytes 147464 | tf_op jit(solution)/shard_map/ppermute | solution.py:108
  34.0 4.6 %collective-permute-start.9 = (f32[12,8,128]{2,1,0:T(8,128)S(1)}, f32[12,8,128]{2,1,0:T(8,128)S(1)}, u32[]{:S(2)}, u32[]{:S(2)}) collective-permute-start(f32[12,8,128]{2,1,0:T(8,128)S(1)} %get-tuple-element.43), channel_id=1, source_target_pairs={{0,3},{1,0},{2,1},{3,2},{4,7},{5,4},{6,5},{7,6},{8,11},{9,8},{10,9... | collective-permute-start | bytes 147464 | tf_op jit(solution)/shard_map/ppermute | solution.py:108
  36.2 5.8 %collective-permute-start.7 = (f32[35,8,128]{2,1,0:T(8,128)}, f32[35,8,128]{2,1,0:T(8,128)S(1)}, u32[]{:S(2)}, u32[]{:S(2)}) collective-permute-start(f32[35,8,128]{2,1,0:T(8,128)} %get-tuple-element.41), channel_id=1, source_target_pairs={{0,28},{4,0},{8,4},{12,8},{16,12},{20,16},{24,20},{28,24},{1,29},{... | collective-permute-start | bytes 430088 | tf_op jit(solution)/shard_map/ppermute | solution.py:108
  36.5 5.5 %collective-permute-start.6 = (f32[32,8,128]{2,1,0:T(8,128)}, f32[32,8,128]{2,1,0:T(8,128)S(1)}, u32[]{:S(2)}, u32[]{:S(2)}) collective-permute-start(f32[32,8,128]{2,1,0:T(8,128)} %get-tuple-element.40), channel_id=1, source_target_pairs={{0,4},{4,8},{8,12},{12,16},{16,20},{20,24},{24,28},{28,0},{1,5},{5... | collective-permute-start | bytes 393224 | tf_op jit(solution)/shard_map/ppermute | solution.py:108
  38.6 4.8 %collective-permute-start.10 = (f32[14,8,128]{2,1,0:T(8,128)S(1)}, f32[14,8,128]{2,1,0:T(8,128)S(1)}, u32[]{:S(2)}, u32[]{:S(2)}) collective-permute-start(f32[14,8,128]{2,1,0:T(8,128)S(1)} %get-tuple-element.44), channel_id=1, source_target_pairs={{0,4},{4,8},{8,12},{12,16},{16,20},{20,24},{24,28},{28,0},{1,5},{5... | collective-permute-start | bytes 172040 | tf_op jit(solution)/shard_map/ppermute | solution.py:108
  38.7 4.7 %collective-permute-start.11 = (f32[14,8,128]{2,1,0:T(8,128)S(1)}, f32[14,8,128]{2,1,0:T(8,128)S(1)}, u32[]{:S(2)}, u32[]{:S(2)}) collective-permute-start(f32[14,8,128]{2,1,0:T(8,128)S(1)} %get-tuple-element.45), channel_id=1, source_target_pairs={{0,28},{4,0},{8,4},{12,8},{16,12},{20,16},{24,20},{28,24},{1,29},{... | collective-permute-start | bytes 172040 | tf_op jit(solution)/shard_map/ppermute | solution.py:108
  64.3 2.7 %collective-permute-start.12 = (f32[32,4,8,128]{3,2,1,0:T(8,128)S(1)}, f32[32,4,8,128]{3,2,1,0:T(8,128)S(1)}, u32[]{:S(2)}, u32[]{:S(2)}) collective-permute-start(f32[32,4,8,128]{3,2,1,0:T(8,128)S(1)} %all_to_all.5.own_half), channel_id=1, source_target_pairs={{0,4},{4,0},{8,12},{12,8},{16,20},{20,16},{24,28},{28,24},{1,5},{5... | collective-permute-start | bytes 1572872 | tf_op jit(solution)/shard_map/ppermute | solution.py:847

commit v4 on v3

--- a/solution.py
+++ b/solution.py
@@ -93,6 +93,11 @@
 DOWN_PLANES = (5, 4, 4, 5, 4, 4)
 UP_CORNER = (4, 3, 3, 3, 4, 3)
 DOWN_CORNER = (4, 3, 3, 4, 4, 3)
+STRIP = 3
+
+
+def corner_tiles(counts):
+    return sum(count - 1 for count in counts)
 
 
 def tiles_of(rows, columns):
@@ -186,9 +191,22 @@
     tops_y.put(ini[:, size_y - 5, :])
     bottoms_y.put(ini[:, 4, :])
     bottoms_y.put(face_y[:, 4, :])
-    for writer in (tops, bottoms, tops_y, bottoms_y):
-        for tile in range(mid.shape[0]):
-            writer.put(mid[tile])
+    for writer in (tops_y, bottoms_y):
+        for tile in (1, 2):
+            writer.put(low[tile])
+    row, upper = iota(TILE, 0), is_upper(TILE[1])
+    for array in range(4):
+        parts = [mid[array * mid_x + plane] for plane in range(mid_x)]
+        for pair in range(0, mid_x, 2):
+            one, two = parts[pair], parts[pair + 1]
+            tops_y.put(jnp.where(upper, roll(one, 4, 0), two))
+            bottoms_y.put(jnp.where(upper, one, roll(two, 4, 0)))
+        far_low, far_high = roll(parts[0], -2, 0), roll(parts[0], -4, 0)
+        for plane in range(1, mid_x):
+            far_low = jnp.where(row < 2 * plane, far_low, roll(parts[plane], 2 * plane - 2, 0))
+            far_high = jnp.where(row < 2 * plane, far_high, roll(parts[plane], 2 * plane - 4, 0))
+        tops_y.put(far_low)
+        bottoms_y.put(far_high)
 
 
 def corner_of(low_y, high_y, plane, upper, first_tile=0):
@@ -201,38 +219,56 @@
     return jnp.where(upper, roll(low, 4, 0), high)
 
 
-def corner_kernel(size_x, size_z, low_y, high_y, up, down):
+def mix(near, far):
+    row = iota(near.shape, 0)
+    return jnp.where((row >= 2) & (row < 6), near, roll(far, 3, 0))
+
+
+def put_corners(writer, low_y, high_y, planes, upper, first_tile):
+    parts = [corner_of(low_y, high_y, plane, upper, first_tile) for plane in planes]
+    for part in parts[:-2]:
+        writer.put(part)
+    writer.put(mix(*parts[-2:]))
+
+
+def mid_strip(ref, array, plane, low):
+    start = ref.shape[0] - 4 * STRIP + array * STRIP
+    near, far, row = ref[start + plane // 2], ref[start + 2], iota(TILE, 0)
+    if (plane % 2 == 0) == low:
+        near = roll(near, 4, 0)
+    far = roll(far, (2 if low else 4) - 2 * plane, 0)
+    return jnp.where(row >= 4, near, far) if low else jnp.where(row < 4, near, far)
+
+
+def corner_kernel(size_x, size_z, low_y, high_y, mid, low_faces, up, down):
     upper = is_upper(size_z)
     per_field = (size_x // 2) * tiles_of(8, size_z)
     tops, bottoms = Writer(up), Writer(down)
     for field in range(6):
-        for plane in range(size_x - UP_CORNER[field], size_x):
-            tops.put(corner_of(low_y, high_y, plane, upper, field * per_field))
-        for plane in range(DOWN_CORNER[field]):
-            bottoms.put(corner_of(low_y, high_y, plane, upper, field * per_field))
+        start = field * per_field
+        planes = [size_x - 1 - plane for plane in range(UP_CORNER[field])]
+        put_corners(tops, low_y, high_y, planes, upper, start)
+        put_corners(bottoms, low_y, high_y, range(DOWN_CORNER[field]), upper, start)
     mid_x = size_x // 2
-    sides = [(ref, ref.shape[0] - 4 * mid_x) for ref in (low_y, high_y)]
     upper = is_upper(TILE[1])
-    for writer, first, step in ((tops, mid_x - 1, -1), (bottoms, 0, 1)):
-        for array in range(4):
-            for q in range(2):
-                for ref, start in sides:
-                    writer.put(ref[start + array * mid_x + first + q * step])
-        for array in range(4):
-            for q in range(2, 4):
-                one, two = (roll(ref[start + array * mid_x + first + q * step], 4, 0) for ref, start in sides)
-                writer.put(jnp.where(upper, one, two))
-
-
-MID_CORNER = 24
-
-
-def whole_corner(ref, array, q, side):
-    return ref[ref.shape[0] - MID_CORNER + (array * 2 + q) * 2 + side]
-
-
-def part_corner(ref, array, q):
-    return ref[ref.shape[0] - MID_CORNER + 16 + array * 2 + q - 2]
+    for writer, wanted in (
+        (tops, [(array, mid_x - 1) for array in range(4)]),
+        (bottoms, [(array, 0) for array in range(4)] + [(1, 1)]),
+    ):
+        for array, plane in wanted:
+            writer.put(
+                jnp.where(upper, mid_strip(high_y, array, plane, False), mid_strip(low_y, array, plane, True))
+            )
+        for array, plane in wanted:
+            writer.put(mid[array * mid_x + plane])
+        for tiles in ((low_faces[1], low_faces[2]), low_tiles_of(low_y), low_tiles_of(high_y)):
+            for tile in tiles:
+                writer.put(tile)
+
+
+def low_tiles_of(ref):
+    end = ref.shape[0] - 4 * STRIP
+    return ref[end - 2], ref[end - 1]
 
 
 class Planes:
@@ -341,11 +377,12 @@
     for plane in range(count):
         window[first + plane, PAD:high] = reader.get(size_y, size_z)
     reader = Reader(corners, corner_start)
-    first += count - corner_count if from_end else 0
-    for plane in range(corner_count):
-        tile = roll(reader.get(8, size_z), 4, 0)
-        window[first + plane, 0:8] = tile
-        window[first + plane, high : high + 8] = tile
+    tiles = [roll(reader.get(8, size_z), 4, 0) for _ in range(corner_count - 1)]
+    tiles.append(roll(tiles[-1], -3, 0))
+    for plane, tile in enumerate(tiles):
+        at = first + count - 1 - plane if from_end else first + plane
+        window[at, 0:8] = tile
+        window[at, high : high + 8] = tile
 
 
 def assemble_owns(windows, own, low_y, high_y):
@@ -380,18 +417,31 @@
         )
         starts[0] += up * plane_tiles
         starts[1] += down * plane_tiles
-        starts[2] += up_c * strip_tiles
-        starts[3] += down_c * strip_tiles
-
-
-def own_kernel(own, low_y, high_y, windows, coeffs):
+        starts[2] += (up_c - 1) * strip_tiles
+        starts[3] += (down_c - 1) * strip_tiles
+
+
+def own_kernel(own, low_y, high_y, windows, coeffs, up_corner, down_corner):
     assemble_owns(windows, own, low_y, high_y)
     fields = [windows.at[field] for field in range(6)]
     scale_coeffs(1.0, *fields[2:], coeffs, (0, own.shape[1] - 1), fields[1], True)
+    mid_x = own.shape[1] // 2
+    tops, bottoms = Writer(up_corner), Writer(down_corner)
+    upper = is_upper(TILE[1])
+    sides = ((low_y, True), (high_y, False))
+    for writer, first, step in ((tops, mid_x - 1, -1), (bottoms, 0, 1)):
+        for array in range(4):
+            for q in range(2):
+                for ref, low in sides:
+                    writer.put(mid_strip(ref, array, first + q * step, low))
+        for array in range(4):
+            for q in range(2, 4):
+                one, two = (roll(mid_strip(ref, array, first + q * step, low), 4, 0) for ref, low in sides)
+                writer.put(jnp.where(upper, one, two))
 
 
 def fine_kernel(
-    own_windows, own_coeffs, low_x, high_x, low_c, high_c,
+    own_windows, own_coeffs, up_corner, down_corner, mid, low_x, high_x, low_c, high_c,
     iterate_out, mid_target, up_x, down_x, up_y, down_y,
     side_windows, side_coeffs, iterate, update, rest,
 ):
@@ -444,68 +494,74 @@
         bottoms_y.put(jnp.where(upper, one[:8], roll(two[:8], 4, 0)))
     for writer in (tops, bottoms, tops_y, bottoms_y):
         writer.put(coarse)
-    low_start, high_start = (ref.shape[0] - 4 * mid_x for ref in (low_x, high_x))
-    for array in range(4):
-        tops.put(whole_corner(low_c, array, 0, 0))
-        tops.put(low_x[low_start + array * mid_x + mid_x - 1])
-        tops.put(whole_corner(low_c, array, 0, 1))
-        bottoms.put(whole_corner(high_c, array, 0, 0))
-        bottoms.put(high_x[high_start + array * mid_x])
-        bottoms.put(whole_corner(high_c, array, 0, 1))
-    bottoms.put(whole_corner(high_c, 1, 1, 0))
-    bottoms.put(high_x[high_start + mid_x + 1])
-    bottoms.put(whole_corner(high_c, 1, 1, 1))
+    for writer, ref in ((tops, up_corner), (bottoms, down_corner)):
+        for tile in range(MID_CORNER):
+            writer.put(ref[tile])
+    for writer in (tops, bottoms):
+        for tile in range(mid.shape[0]):
+            writer.put(mid[tile])
+    for writer, corners, extra in ((tops, low_c, 4), (bottoms, high_c, 5)):
+        start = corners.shape[0] - PASSED - 2 * extra
+        for tile in range(start, corners.shape[0]):
+            writer.put(corners[tile])
+
+
+MID_CORNER = 24
+PASSED = 6
+
+
+def whole_corner(ref, start, array, q, side):
+    return ref[start + (array * 2 + q) * 2 + side]
+
+
+def part_corner(ref, start, array, q):
+    return ref[start + 16 + array * 2 + q - 2]
 
 
 def corner_two_kernel(size_x, size_z, low_y, high_y, up, down):
     upper = is_upper(size_z)
     tops, bottoms = Writer(up), Writer(down)
-    for plane in range(size_x - 3, size_x):
-        tops.put(corner_of(low_y, high_y, plane, upper))
-    for plane in range(3):
-        bottoms.put(corner_of(low_y, high_y, plane, upper))
+    put_corners(tops, low_y, high_y, [size_x - 1, size_x - 2, size_x - 3], upper, 0)
+    put_corners(bottoms, low_y, high_y, range(3), upper, 0)
     for writer in (tops, bottoms):
         for ref in (low_y, high_y):
             for tile in range(ref.shape[0] - size_x // 2, ref.shape[0]):
                 writer.put(ref[tile])
 
 
-def mid_coeffs_kernel(mid, low_x, high_x, low_y, high_y, low_c, high_c, low_x2, high_x2, coeffs, window):
+def mid_coeffs_kernel(mid, low_y, high_y, low_x2, high_x2, coeffs, window):
     mid_y, mid_z = mid.shape[1:]
     mid_x = mid.shape[0] // 4
     mids = 4 * mid_x
     first = MID - mid_x
-    blocks = {
-        (0, 1): (low_x, low_x.shape[0] - mids), (1, 0): (low_y, low_y.shape[0] - mids),
-        (1, 1): (mid, 0), (1, 2): (high_y, high_y.shape[0] - mids),
-        (2, 1): (high_x, high_x.shape[0] - mids),
-    }
-    for (bx, by), (ref, start) in blocks.items():
+    corner = 4 * tiles_of(2 * mid_y, 2 * mid_z) + mid_x
+    passed = corner + MID_CORNER
+    for ref, start, block in ((low_x2, passed, 0), (mid, 0, 1), (high_x2, passed, 2)):
         for array in range(4):
             for plane in range(mid_x):
-                window[array, first + bx * mid_x + plane, by * mid_y : (by + 1) * mid_y] = ref[
-                    start + array * mid_x + plane
-                ]
-    for ref, start, step in ((low_c, MID - 1, -1), (high_c, MID + mid_x, 1)):
+                window[array, first + block * mid_x + plane, mid_y : 2 * mid_y] = ref[start + array * mid_x + plane]
+    for array in range(4):
+        for plane in range(mid_x):
+            window[array, MID + plane, :mid_y] = mid_strip(low_y, array, plane, True)
+            window[array, MID + plane, 2 * mid_y :] = mid_strip(high_y, array, plane, False)
+    passed += mids
+    far = 3 * mid_x + first
+    for ref, start, step, end, extra in (
+        (low_x2, MID - 1, -1, first - 1, 4), (high_x2, MID + mid_x, 1, far, 5)
+    ):
         for array in range(4):
             for q in range(mid_x):
                 if q < 2:
-                    one, two = whole_corner(ref, array, q, 0), whole_corner(ref, array, q, 1)
+                    one, two = (whole_corner(ref, corner, array, q, side) for side in range(2))
                 else:
-                    one = two = roll(part_corner(ref, array, q), 4, 0)
+                    one = two = roll(part_corner(ref, corner, array, q), 4, 0)
                 window[array, start + q * step, :mid_y] = one
                 window[array, start + q * step, 2 * mid_y :] = two
-    far = 3 * mid_x + first
-    fine_tiles = 4 * tiles_of(2 * mid_y, 2 * mid_z)
-    own_planes = fine_tiles + mid_x
-    for array in range(4):
-        for by in range(3):
-            rows = slice(by * mid_y, (by + 1) * mid_y)
-            window[array, first - 1, rows] = low_x2[own_planes + 3 * array + by]
-            window[array, far, rows] = high_x2[own_planes + 3 * array + by]
-    for by in range(3):
-        window[1, far + 1, by * mid_y : (by + 1) * mid_y] = high_x2[own_planes + 12 + by]
-
+        for place in range(extra):
+            array, plane = (place, end) if place < 4 else (1, end + 1)
+            window[array, plane, :mid_y] = ref[passed + place]
+            window[array, plane, 2 * mid_y :] = ref[passed + place]
+            window[array, plane, mid_y : 2 * mid_y] = ref[passed + extra + place]
     scale_coeffs(0.25, *(window.at[array] for array in range(4)), coeffs, (first - 1, far + 1), None, True)
 
 
@@ -553,24 +609,36 @@
     count = low_x_size * mid_y // 2
     summed = rest[pl.ds(0, count, 2), :] + rest[pl.ds(1, count, 2), :]
     coarse = dot(summed * 0.125, selector(mid_z, mid_z, lambda k, m: k // 2 == m))
-    low_tiles = (coarse + low[0], low[1], low[2])
-    iterates = [iterate[MID + plane, mid_y : 2 * mid_y] for plane in range(mid_x)]
+    tiles = (coarse + low[0], low[1], low[2])
+    x1 = [iterate[MID + plane, mid_y : 2 * mid_y] for plane in range(mid_x)]
     pairs = count_x // 2
-    following = lax.rem(place[0] // 2 + 1, pairs)
+    own, even = place[0] // 2, place[0] % 2 == 0
+    above, below = lax.rem(own + 1, pairs), lax.rem(own + pairs - 1, pairs)
 
     def fill(i, carry):
-        edge = jnp.where(i == following, mid_target[mid_x - 1], mid_target[0])
+        up, down = i == above, i == below
+        edge = jnp.where(up, mid_target[mid_x - 1], mid_target[0])
+        near_pair = up | down | (i == own)
+        far_side = (up & even) | (down & jnp.logical_not(even))
         for j in range(count_y):
-            for tile, value in enumerate(low_tiles + (edge,)):
-                slots[2 * i * count_y + j, tile] = value
-            for tile, value in enumerate(iterates):
-                slots[(2 * i + 1) * count_y + j, tile] = value
+            me = place[1]
+            beside = (j == me) | (j == lax.rem(me + 1, count_y)) | (j == lax.rem(me + count_y - 1, count_y))
+            near, side = near_pair & beside, far_side & beside
+            one, two = 2 * i * count_y + j, (2 * i + 1) * count_y + j
+            slots[one, 0] = tiles[0]
+            slots[one, 1] = jnp.where(near, edge, tiles[1])
+            slots[one, 2] = jnp.where(near, jnp.where(side & even, x1[2], x1[0]), tiles[2])
+            slots[two, 0] = jnp.where(near, jnp.where(side, tiles[1], x1[1]), tiles[0])
+            slots[two, 1] = jnp.where(near, jnp.where(side, tiles[2], x1[2]), tiles[1])
+            slots[two, 2] = jnp.where(
+                near, jnp.where(side & jnp.logical_not(even), x1[1], x1[3]), tiles[2]
+            )
         return carry
 
     each(0, pairs, fill)
 
 
-def solve_low(count_x, count_y, half, fields, coeffs, iterate, update):
+def solve_low(count_x, count_y, gathered, fields, coeffs, iterate, update):
     size_x, size_y, lanes = iterate.shape
     low_x, low_y = size_x // count_x, size_y // count_y
     low_z = lanes // 2
@@ -578,7 +646,7 @@
     def place(i, carry):
         for j in range(count_y):
             for kind in range(3):
-                tile = half(0, i * count_y + j, kind)
+                tile = gathered[i * count_y + j, kind]
                 for plane in range(low_x):
                     fields[kind, i * low_x + plane, j * low_y : (j + 1) * low_y] = tile[
                         plane * low_y : (plane + 1) * low_y
@@ -639,8 +707,16 @@
 def window_kernel(
     fields_own, low_x1, high_x1, low_y1, high_y1, low_c1, high_c1,
     own, low_x, high_x, low_y, high_y, low_c, high_c,
-    window, coeffs, own_windows, side_windows,
+    low, window, coeffs, near, own_windows, side_windows,
 ):
+    known = {(0, 0): (low[1], low[2]), (0, -1): low_tiles_of(low_y1), (0, 1): low_tiles_of(high_y1)}
+    for step, ref, distance in ((-1, low_c1, 1), (1, high_c1, 1), (-1, low_x, 2), (1, high_x, 2)):
+        start = ref.shape[0] - PASSED
+        for place, dy in enumerate((0, -1, 1)):
+            known[step * distance, dy] = (ref[start + 2 * place], ref[start + 2 * place + 1])
+    for (dx, dy), tiles in known.items():
+        for kind in range(2):
+            near[((dx + 2) * 3 + dy + 1) * 2 + kind] = tiles[kind]
     size_x, size_y, size_z = own.shape
     assemble_owns(own_windows, fields_own, low_y1, high_y1)
     assemble_sides(side_windows, (size_y, size_z), low_x1, high_x1, low_c1, high_c1)
@@ -656,9 +732,9 @@
 
 
 def last_kernel(
-    count_x, count_y, place, own_half, other_half, mid_coeffs, goal_in, fine_coeffs, window,
+    count_x, count_y, place, own_half, other_half, mid_coeffs, goal_in, fine_coeffs, window, near,
     out,
-    low_fields, low_coeffs, low_iterate, low_update,
+    gathered, low_fields, low_coeffs, low_iterate, low_update,
     goal, mid_iterate, mid_update, spread_mid,
     iterate, update, spread,
 ):
@@ -673,20 +749,41 @@
         one, two = own_half[device, tile], other_half[device, tile]
         return jnp.where(even, one, two) if which == 0 else jnp.where(even, two, one)
 
-    solve_low(count_x, count_y, half, low_fields, low_coeffs, low_iterate, low_update)
-
     def device(dx, dy):
         return lax.rem(me_x + dx + count_x, count_x) * count_y + lax.rem(me_y + dy + count_y, count_y)
+
+    def take(i, carry):
+        for kind in range(3):
+            gathered[i, kind] = half(0, i, kind)
+        return carry
+
+    each(0, count_x * count_y, take)
+    side = me_x % 2
+    for dy in (-1, 0, 1):
+        for source in (device(-2 - side, dy), device(3 - side, dy)):
+            for kind in range(2):
+                gathered[source, 1 + kind] = half(1, source, kind)
+    for dy in (-1, 0, 1):
+        for dx in range(-2, 3):
+            for kind in range(2):
+                gathered[device(dx, dy), 1 + kind] = near[((dx + 2) * 3 + dy + 1) * 2 + kind]
+    solve_low(count_x, count_y, gathered, low_fields, low_coeffs, low_iterate, low_update)
 
     first, far = MID - mid_x, MID + 2 * mid_x
     for dy in (-1, 0, 1):
         rows = slice((dy + 1) * mid_y, (dy + 2) * mid_y)
         for dx in (-1, 0, 1):
-            for plane in range(mid_x):
-                mid_iterate[MID + dx * mid_x + plane, rows] = half(1, device(dx, dy), plane)
-        for plane in range(first):
-            mid_iterate[plane, rows] = half(1, device(-2, dy), mid_x - first + plane)
-            mid_iterate[far + plane, rows] = half(1, device(2, dy), plane)
+            source = device(dx, dy)
+            start = MID + dx * mid_x
+            mid_iterate[start, rows] = half(0, source, 2)
+            for plane in range(1, mid_x):
+                mid_iterate[start + plane, rows] = half(1, source, plane - 1)
+        source = device(-2, dy)
+        mid_iterate[0, rows] = jnp.where(even, half(0, source, 2), half(1, source, 1))
+        mid_iterate[1, rows] = half(1, source, 2)
+        source = device(2, dy)
+        mid_iterate[far, rows] = half(0, source, 2)
+        mid_iterate[far + 1, rows] = jnp.where(even, half(1, source, 0), half(1, source, 2))
     low_size_x, low_size_y = low_iterate.shape[:2]
     low_planes, low_rows = (mid_x + 2 * MID) // 2, 16
     low_y = mid_y // 2
@@ -709,7 +806,7 @@
     for dy in (-1, 0, 1):
         rows = slice((dy + 1) * mid_y, (dy + 2) * mid_y)
         for plane, dx in ((first - 1, -2), (far, 2)):
-            goal[plane, rows] = half(0, device(dx, dy), 3) * mid_coeffs[6, plane, rows]
+            goal[plane, rows] = half(0, device(dx, dy), 1) * mid_coeffs[6, plane, rows]
     for sweep, pair in enumerate(chebyshev_weights(SWEEPS)):
         sweep_window(
             mid_iterate, mid_update, mid_coeffs, (first - 1 + sweep, far + 1 - sweep), pair, sweep == 0, goal
@@ -781,10 +878,10 @@
         pack_kernel,
         (initial, source, absorption, beta_x, beta_y, beta_z),
         [
-            tiles(sum(UP_PLANES) * plane + mids),
-            tiles(sum(DOWN_PLANES) * plane + mids),
-            tiles((6 * pairs + 1) * strip + mids),
-            tiles((6 * pairs + 2) * strip + mids),
+            tiles(sum(UP_PLANES) * plane),
+            tiles(sum(DOWN_PLANES) * plane),
+            tiles((6 * pairs + 1) * strip + 2 + 4 * STRIP),
+            tiles((6 * pairs + 2) * strip + 2 + 4 * STRIP),
             tiles(mids),
             tiles(3),
             (6,) + source.shape,
@@ -797,24 +894,26 @@
     low_y1, high_y1 = shifted(up_y, "gy", 1), shifted(down_y, "gy", -1)
     up_c, down_c = call(
         functools.partial(corner_kernel, size_x, size_z),
-        (low_y1, high_y1),
-        [tiles(sum(UP_CORNER) * strip + MID_CORNER), tiles(sum(DOWN_CORNER) * strip + MID_CORNER)],
+        (low_y1, high_y1, mid, low),
+        [tiles(corner_tiles(UP_CORNER) * strip + 14), tiles(corner_tiles(DOWN_CORNER) * strip + 16)],
     )
     low_c1, high_c1 = shifted(up_c, "gx", 1), shifted(down_c, "gx", -1)
 
     tall = (size_y + 2 * PAD, size_z)
     wide = (size_x + 2 * FINE,) + tall
-    own_windows, own_coeffs = call(
-        own_kernel, (own, low_y1, high_y1), [(6, size_x) + tall, (8, size_x - 1) + tall]
+    own_windows, own_coeffs, up_corner, down_corner = call(
+        own_kernel,
+        (own, low_y1, high_y1),
+        [(6, size_x) + tall, (8, size_x - 1) + tall, tiles(MID_CORNER), tiles(MID_CORNER)],
     )
     iterate, mid_target, up_x, down_x, up_y, down_y = call(
         fine_kernel,
-        (own_windows, own_coeffs, low_x1, high_x1, low_c1, high_c1),
+        (own_windows, own_coeffs, up_corner, down_corner, mid, low_x1, high_x1, low_c1, high_c1),
         [
             source.shape,
             (mid_x, mid_y, mid_z),
-            tiles(4 * plane + mid_x + 12),
-            tiles(4 * plane + mid_x + 15),
+            tiles(4 * plane + mid_x + MID_CORNER + mids + 8 + PASSED),
+            tiles(4 * plane + mid_x + MID_CORNER + mids + 10 + PASSED),
             tiles(pairs * strip + mid_x),
             tiles(pairs * strip + mid_x),
         ],
@@ -825,41 +924,41 @@
     up_c, down_c = call(
         functools.partial(corner_two_kernel, size_x, size_z),
         (low_y2, high_y2),
-        [tiles(3 * strip + 2 * mid_x)] * 2,
+        [tiles(2 * strip + 2 * mid_x)] * 2,
     )
     low_c2, high_c2 = shifted(up_c, "gx", 1), shifted(down_c, "gx", -1)
 
     mid_wide = (mid_x + 2 * MID, 3 * mid_y, mid_z)
     (mid_coeffs,) = call(
         mid_coeffs_kernel,
-        (mid, low_x1, high_x1, low_y1, high_y1, low_c1, high_c1, low_x2, high_x2),
+        (mid, low_y1, high_y1, low_x2, high_x2),
         [(8,) + mid_wide],
         [(4,) + mid_wide],
     )
     goal, slots = call(
         functools.partial(mid_kernel, count_x, count_y),
         (place, low, mid_target, mid_coeffs, low_x2, high_x2, low_y2, high_y2, low_c2, high_c2),
-        [mid_wide, (devices, 4) + TILE],
+        [mid_wide, (devices, 3) + TILE],
         [mid_wide] * 3 + [(low_x * mid_y, mid_z)],
         scalars=1,
     )
     own_half = lax.all_to_all(slots, ("gx", "gy"), 0, 0)
     other_half = lax.ppermute(own_half, "gx", [(i, i ^ 1) for i in range(count_x)])
 
-    window, coeffs = call(
+    window, coeffs, near = call(
         window_kernel,
         (own, low_x1, high_x1, low_y1, high_y1, low_c1, high_c1)
-        + (iterate, low_x2, high_x2, low_y2, high_y2, low_c2, high_c2),
-        [wide, (7, wide[0] - 4) + tall],
+        + (iterate, low_x2, high_x2, low_y2, high_y2, low_c2, high_c2, low),
+        [wide, (7, wide[0] - 4) + tall, tiles(30)],
         [(6, size_x) + tall, (6, 2 * FINE) + tall],
     )
     low_wide = (low_x * count_x, low_y * count_y, mid_z)
     low_planes = mid_wide[0] // 2
     (result,) = call(
         functools.partial(last_kernel, count_x, count_y),
-        (place, own_half, other_half, mid_coeffs, goal, coeffs, window),
+        (place, own_half, other_half, mid_coeffs, goal, coeffs, window, near),
         [source.shape],
-        [(3,) + low_wide, (7,) + low_wide, low_wide, low_wide]
+        [(devices, 3) + TILE, (3,) + low_wide, (7,) + low_wide, low_wide, low_wide]
         + [mid_wide, mid_wide, mid_wide, (low_planes * 32, mid_z)]
         + [wide, wide, (2, (mid_x + 4) * 2 * (mid_y + 8), mid_z)],
         scalars=1,

time: 71.3 us -> 67.5 us (0.947)
  blocking collectives: 19.9 us -> 17.2 us
  waiting for transfers between devices: 24.1 us -> 22.2 us
    all_to_all x1, blocking collectives: 19.9 us -> 17.2 us  [local(): own_half = lax.all_to_all(slots, ('gx', 'gy'), 0, 0)]
    ppermute x12, waiting for transfers between devices: 23.1 us -> 21.4 us  [shifted(): lax.ppermute(value, axis, [(i, (i + step) % count) for i in range(count)])]
  transfers between devices with their start and end apart: 13 -> 13, of which waited for: 8 -> 6; matrix products, arithmetic and copies ran while one was open for 0% -> 0% of each run, Pallas kernels for 1% -> 2%
where the time goes in v4:
time: 67.5 us; the launch traced here: 67.4 us
  waiting for transfers between devices  22.2 us (33%)
  blocking collectives  17.2 us (25%)
  starting transfers between devices  16.3 us (24%)
  Pallas kernels  11.4 us (17%)
    ppermute x12, waiting for transfers between devices, shifted(): lax.ppermute(value, axis, [(i, (i + step) % count) for i in range(count)])  21.4 us
    all_to_all x1, blocking collectives, local(): own_half = lax.all_to_all(slots, ('gx', 'gy'), 0, 0)  17.2 us
    ppermute x12, starting transfers between devices, shifted(): lax.ppermute(value, axis, [(i, (i + step) % count) for i in range(count)])  15.2 us
    pallas_call x9, Pallas kernels, call(): pl.pallas_call(kernel, out_shape=[pltpu.HBM(shape, F32) if i in far_out e...  11.4 us
  transfers between devices with their start and end apart: 13, of which 6 were waited for; matrix products, arithmetic and copies ran while one was open for 0% of the time, Pallas kernels for 2%

profile of v4, /device:TPU:0, one launch (start us, length us, event | category | flops | bytes accessed | tf_op | source)
XLA Modules:
  0.0 67.4 jit_solution(9099909296784189698)
XLA Ops:
  0.0 2.2 %shard_map.64 = (f32[100,8,128]{2,1,0:T(8,128)S(1)}, f32[104,8,128]{2,1,0:T(8,128)S(1)}, f32[64,8,128]{2,1,0:T(8,128)S(1)}, f32[66,8,128]{2,1,0:T(8,128)S(1)}, f...) custom-call(f32[8,16,256]{2,1,0:T(8,128)} %ini_in.1, f32[8,16,256]{2,1,0:T(8,128)} %src_in.1, ...), custom_call_target="tpu_custom_call" | custom-call | flops 1000 | bytes 1000 | tf_op jit(solution)/shard_map/pallas_call | solution.py:846
  2.2 5.1 %collective-permute-start.1 = (f32[66,8,128]{2,1,0:T(8,128)S(1)}, f32[66,8,128]{2,1,0:T(8,128)S(1)}, u32[]{:S(2)}, u32[]{:S(2)}) collective-permute-start(f32[66,8,128]{2,1,0:T(8,128)S(1)} %get-tuple-element.34), channel_id=1, source_target_pairs={{0,3},{1,0},{2,1},{3,2},{4,7},{5,4},{6,5},{7,6},{8,11},{9,8},{10,9... | collective-permute-start | bytes 811016 | tf_op jit(solution)/shard_map/ppermute | solution.py:113
  7.3 0.0 collective-permute-start
  7.3 1.6 %collective-permute-start.3 = (f32[104,8,128]{2,1,0:T(8,128)S(1)}, f32[104,8,128]{2,1,0:T(8,128)S(1)}, u32[]{:S(2)}, u32[]{:S(2)}) collective-permute-start(f32[104,8,128]{2,1,0:T(8,128)S(1)} %get-tuple-element.41), channel_id=1, source_target_pairs={{0,28},{4,0},{8,4},{12,8},{16,12},{20,16},{24,20},{28,24},{1,29},{... | collective-permute-start | bytes 1277960 | tf_op jit(solution)/shard_map/ppermute | solution.py:113
  8.9 0.0 collective-permute-start.2
  8.9 10.6 %collective-permute-done.low_y.low_y1 = f32[64,8,128]{2,1,0:T(8,128)S(1)} collective-permute-done((f32[64,8,128]{2,1,0:T(8,128)S(1)}, f32[64,8,128]{2,1,0:T(8,128)S(1)}, u32[]{:S(2)}, u32[]{:S(2)}) %collective-permute-start) | collective-permute-done | bytes 262176 | tf_op jit(solution)/shard_map/ppermute | solution.py:113
  19.6 0.0 collective-permute-done.1.high_y.high_y1
  19.6 1.1 %collective-permute-start.5 = (f32[46,8,128]{2,1,0:T(8,128)S(1)}, f32[46,8,128]{2,1,0:T(8,128)S(1)}, u32[]{:S(2)}, u32[]{:S(2)}) collective-permute-start(f32[46,8,128]{2,1,0:T(8,128)S(1)} %get-tuple-element.43), channel_id=1, source_target_pairs={{0,28},{4,0},{8,4},{12,8},{16,12},{20,16},{24,20},{28,24},{1,29},{... | collective-permute-start | bytes 565256 | tf_op jit(solution)/shard_map/ppermute | solution.py:113
  20.7 0.0 collective-permute-start.4
  20.7 0.3 shard_map.65
  21.0 0.0 collective-permute-done.2.low_x.low_x1
  21.0 0.0 collective-permute-done.3.high_x.high_x1
  21.0 6.5 %collective-permute-done.4.low_c.low_c1 = f32[42,8,128]{2,1,0:T(8,128)S(1)} collective-permute-done((f32[42,8,128]{2,1,0:T(8,128)S(1)}, f32[42,8,128]{2,1,0:T(8,128)S(1)}, u32[]{:S(2)}, u32[]{:S(2)}) %collective-permute-start.4) | collective-permute-done | bytes 172064 | tf_op jit(solution)/shard_map/ppermute | solution.py:113
  27.5 0.0 collective-permute-done.5.high_c.high_c1
  27.5 2.8 %shard_map.67 = (f32[8,16,256]{2,1,0:T(8,128)S(1)}, f32[4,8,128]{2,1,0:T(8,128)S(1)}, f32[74,8,128]{2,1,0:T(8,128)}, f32[76,8,128]{2,1,0:T(8,128)}, f32[12,8,128...) custom-call(f32[6,8,32,256]{3,2,1,0:T(8,128)S(1)} %get-tuple-element.35.own_windows, ...), custom_call_target="tpu_custom_call" | custom-call | flops 1000 | bytes 1000 | tf_op jit(solution)/shard_map/pallas_call | solution.py:846
  30.3 0.9 %collective-permute-start.7 = (f32[76,8,128]{2,1,0:T(8,128)}, f32[76,8,128]{2,1,0:T(8,128)S(1)}, u32[]{:S(2)}, u32[]{:S(2)}) collective-permute-start(f32[76,8,128]{2,1,0:T(8,128)} %get-tuple-element.46), channel_id=1, source_target_pairs={{0,28},{4,0},{8,4},{12,8},{16,12},{20,16},{24,20},{28,24},{1,29},{... | collective-permute-start | bytes 933896 | tf_op jit(solution)/shard_map/ppermute | solution.py:113
  31.2 0.0 collective-permute-start.6
  31.2 1.6 %collective-permute-start.8 = (f32[12,8,128]{2,1,0:T(8,128)S(1)}, f32[12,8,128]{2,1,0:T(8,128)S(1)}, u32[]{:S(2)}, u32[]{:S(2)}) collective-permute-start(f32[12,8,128]{2,1,0:T(8,128)S(1)} %get-tuple-element.47), channel_id=1, source_target_pairs={{0,1},{1,2},{2,3},{3,0},{4,5},{5,6},{6,7},{7,4},{8,9},{9,10},{10,1... | collective-permute-start | bytes 147464 | tf_op jit(solution)/shard_map/ppermute | solution.py:113
  32.8 2.2 %collective-permute-start.9 = (f32[12,8,128]{2,1,0:T(8,128)S(1)}, f32[12,8,128]{2,1,0:T(8,128)S(1)}, u32[]{:S(2)}, u32[]{:S(2)}) collective-permute-start(f32[12,8,128]{2,1,0:T(8,128)S(1)} %get-tuple-element.48), channel_id=1, source_target_pairs={{0,3},{1,0},{2,1},{3,2},{4,7},{5,4},{6,5},{7,6},{8,11},{9,8},{10,9... | collective-permute-start | bytes 147464 | tf_op jit(solution)/shard_map/ppermute | solution.py:113
  35.0 2.2 %collective-permute-done.8.low_y.low_y2 = f32[12,8,128]{2,1,0:T(8,128)S(1)} collective-permute-done((f32[12,8,128]{2,1,0:T(8,128)S(1)}, f32[12,8,128]{2,1,0:T(8,128)S(1)}, u32[]{:S(2)}, u32[]{:S(2)}) %collective-permute-start.8) | collective-permute-done | bytes 49184 | tf_op jit(solution)/shard_map/ppermute | solution.py:113
  37.2 0.2 collective-permute-done.9.high_y.high_y2
  37.5 0.1 collective-permute-start.10
  37.5 2.6 %collective-permute-start.11 = (f32[12,8,128]{2,1,0:T(8,128)S(1)}, f32[12,8,128]{2,1,0:T(8,128)S(1)}, u32[]{:S(2)}, u32[]{:S(2)}) collective-permute-start(f32[12,8,128]{2,1,0:T(8,128)S(1)} %get-tuple-element.50), channel_id=1, source_target_pairs={{0,28},{4,0},{8,4},{12,8},{16,12},{20,16},{24,20},{28,24},{1,29},{... | collective-permute-start | bytes 147464 | tf_op jit(solution)/shard_map/ppermute | solution.py:113
  40.2 0.1 pad_add_fusion.place
  40.2 0.0 collective-permute-done.6.low_x2.low_x
  40.2 0.0 collective-permute-done.7.high_x2.high_x
  40.2 0.2 shard_map.68.coeffs.mid_coeffs
  40.4 1.8 %collective-permute-done.10.low_c2.low_c = f32[12,8,128]{2,1,0:T(8,128)S(1)} collective-permute-done((f32[12,8,128]{2,1,0:T(8,128)S(1)}, f32[12,8,128]{2,1,0:T(8,128)S(1)}, u32[]{:S(2)}, u32[]{:S(2)}) %collective-permute-start.10) | collective-permute-done | bytes 49184 | tf_op jit(solution)/shard_map/ppermute | solution.py:113
  42.3 0.0 collective-permute-done.11.high_c2.high_c
  42.3 1.1 %shard_map.70 = (f32[16,24,128]{2,1,0:T(8,128)S(1)}, f32[32,3,8,128]{3,2,1,0:T(8,128)S(1)}) custom-call(s32[2]{0:T(128)S(1)} %pad_add_fusion.place, f32[3,8,128]{2,1,0:T(8,128)S(1)} %get-tuple-element.31.low_faces.low, f32[4,8,128]{2,1,0:T(8,128)S(1)} %get-tuple-element.44.mid_target, f32[8,16,24,128]{3,2,1,0:T(8,128)S(1)} %shard_map.68.coeffs.mid_coeffs, ...), custom_call_target="tpu_custom_call" | custom-call | flops 1000 | bytes 1000 | tf_op jit(solution)/shard_map/pallas_call | solution.py:846
  43.3 17.2 %all_to_all.5.own_half = f32[32,3,8,128]{3,2,1,0:T(8,128)S(1)} all-to-all(f32[32,3,8,128]{3,2,1,0:T(8,128)S(1)} %get-tuple-element.51), channel_id=1, replica_groups=mesh['gx'=8,'gy'=4] {'gx','gy'}, dimensions={0} | all-to-all | bytes 786432 | tf_op jit(solution)/shard_map/all_to_all | solution.py:945
  60.6 1.2 %collective-permute-start.12 = (f32[32,3,8,128]{3,2,1,0:T(8,128)S(1)}, f32[32,3,8,128]{3,2,1,0:T(8,128)S(1)}, u32[]{:S(2)}, u32[]{:S(2)}) collective-permute-start(f32[32,3,8,128]{3,2,1,0:T(8,128)S(1)} %all_to_all.5.own_half), channel_id=1, source_target_pairs={{0,4},{4,0},{8,12},{12,8},{16,20},{20,16},{24,28},{28,24},{1,5},{5... | collective-permute-start | bytes 1179656 | tf_op jit(solution)/shard_map/ppermute | solution.py:946
  61.7 0.5 shard_map.71
  62.2 0.8 %collective-permute-done.12.other_half = f32[32,3,8,128]{3,2,1,0:T(8,128)S(1)} collective-permute-done((f32[32,3,8,128]{3,2,1,0:T(8,128)S(1)}, f32[32,3,8,128]{3,2,1,0:T(8,128)S(1)}, u32[]{:S(2)}, u32[]{:S(2)}) %collective-permute-start.12) | collective-permute-done | bytes 393248 | tf_op jit(solution)/shard_map/ppermute | solution.py:946
  63.1 4.3 %shard_map.72 = f32[8,16,256]{2,1,0:T(8,128)} custom-call(s32[2]{0:T(128)S(1)} %pad_add_fusion.place, f32[32,3,8,128]{3,2,1,0:T(8,128)S(1)} %all_to_all.5.own_half, f32[32,3,8,128]{3,2,1,0:T(8,128)S(1)} %collective-permute-done.12.other_half, f32[8,16,24,128]{3,2,1,0:T(8,128)S(1)} %shard_map.68.coeffs.mid_coeffs, ...), custom_call_target="tpu_custom_call" | custom-call | flops 1000 | bytes 1000 | tf_op jit(solution)/shard_map/pallas_call | solution.py:846
  (2 shorter events, 0.0 us)
Async XLA Ops:
  2.2 17.4 %collective-permute-start.1 = (f32[66,8,128]{2,1,0:T(8,128)S(1)}, f32[66,8,128]{2,1,0:T(8,128)S(1)}, u32[]{:S(2)}, u32[]{:S(2)}) collective-permute-start(f32[66,8,128]{2,1,0:T(8,128)S(1)} %get-tuple-element.34), channel_id=1, source_target_pairs={{0,3},{1,0},{2,1},{3,2},{4,7},{5,4},{6,5},{7,6},{8,11},{9,8},{10,9... | collective-permute-start | bytes 811016 | tf_op jit(solution)/shard_map/ppermute | solution.py:113
  7.3 12.3 %collective-permute-start = (f32[64,8,128]{2,1,0:T(8,128)S(1)}, f32[64,8,128]{2,1,0:T(8,128)S(1)}, u32[]{:S(2)}, u32[]{:S(2)}) collective-permute-start(f32[64,8,128]{2,1,0:T(8,128)S(1)} %get-tuple-element.33), channel_id=1, source_target_pairs={{0,1},{1,2},{2,3},{3,0},{4,5},{5,6},{6,7},{7,4},{8,9},{9,10},{10,1... | collective-permute-start | bytes 786440 | tf_op jit(solution)/shard_map/ppermute | solution.py:113
  7.3 13.7 %collective-permute-start.3 = (f32[104,8,128]{2,1,0:T(8,128)S(1)}, f32[104,8,128]{2,1,0:T(8,128)S(1)}, u32[]{:S(2)}, u32[]{:S(2)}) collective-permute-start(f32[104,8,128]{2,1,0:T(8,128)S(1)} %get-tuple-element.41), channel_id=1, source_target_pairs={{0,28},{4,0},{8,4},{12,8},{16,12},{20,16},{24,20},{28,24},{1,29},{... | collective-permute-start | bytes 1277960 | tf_op jit(solution)/shard_map/ppermute | solution.py:113
  8.9 12.1 %collective-permute-start.2 = (f32[100,8,128]{2,1,0:T(8,128)S(1)}, f32[100,8,128]{2,1,0:T(8,128)S(1)}, u32[]{:S(2)}, u32[]{:S(2)}) collective-permute-start(f32[100,8,128]{2,1,0:T(8,128)S(1)} %get-tuple-element.40), channel_id=1, source_target_pairs={{0,4},{4,8},{8,12},{12,16},{16,20},{20,24},{24,28},{28,0},{1,5},{5... | collective-permute-start | bytes 1228808 | tf_op jit(solution)/shard_map/ppermute | solution.py:113
  19.6 7.9 %collective-permute-start.5 = (f32[46,8,128]{2,1,0:T(8,128)S(1)}, f32[46,8,128]{2,1,0:T(8,128)S(1)}, u32[]{:S(2)}, u32[]{:S(2)}) collective-permute-start(f32[46,8,128]{2,1,0:T(8,128)S(1)} %get-tuple-element.43), channel_id=1, source_target_pairs={{0,28},{4,0},{8,4},{12,8},{16,12},{20,16},{24,20},{28,24},{1,29},{... | collective-permute-start | bytes 565256 | tf_op jit(solution)/shard_map/ppermute | solution.py:113
  20.7 6.8 %collective-permute-start.4 = (f32[42,8,128]{2,1,0:T(8,128)S(1)}, f32[42,8,128]{2,1,0:T(8,128)S(1)}, u32[]{:S(2)}, u32[]{:S(2)}) collective-permute-start(f32[42,8,128]{2,1,0:T(8,128)S(1)} %get-tuple-element.42), channel_id=1, source_target_pairs={{0,4},{4,8},{8,12},{12,16},{16,20},{20,24},{24,28},{28,0},{1,5},{5... | collective-permute-start | bytes 516104 | tf_op jit(solution)/shard_map/ppermute | solution.py:113
  30.3 9.9 %collective-permute-start.7 = (f32[76,8,128]{2,1,0:T(8,128)}, f32[76,8,128]{2,1,0:T(8,128)S(1)}, u32[]{:S(2)}, u32[]{:S(2)}) collective-permute-start(f32[76,8,128]{2,1,0:T(8,128)} %get-tuple-element.46), channel_id=1, source_target_pairs={{0,28},{4,0},{8,4},{12,8},{16,12},{20,16},{24,20},{28,24},{1,29},{... | collective-permute-start | bytes 933896 | tf_op jit(solution)/shard_map/ppermute | solution.py:113
  31.2 9.0 %collective-permute-start.6 = (f32[74,8,128]{2,1,0:T(8,128)}, f32[74,8,128]{2,1,0:T(8,128)S(1)}, u32[]{:S(2)}, u32[]{:S(2)}) collective-permute-start(f32[74,8,128]{2,1,0:T(8,128)} %get-tuple-element.45), channel_id=1, source_target_pairs={{0,4},{4,8},{8,12},{12,16},{16,20},{20,24},{24,28},{28,0},{1,5},{5... | collective-permute-start | bytes 909320 | tf_op jit(solution)/shard_map/ppermute | solution.py:113
  31.2 6.0 %collective-permute-start.8 = (f32[12,8,128]{2,1,0:T(8,128)S(1)}, f32[12,8,128]{2,1,0:T(8,128)S(1)}, u32[]{:S(2)}, u32[]{:S(2)}) collective-permute-start(f32[12,8,128]{2,1,0:T(8,128)S(1)} %get-tuple-element.47), channel_id=1, source_target_pairs={{0,1},{1,2},{2,3},{3,0},{4,5},{5,6},{6,7},{7,4},{8,9},{9,10},{10,1... | collective-permute-start | bytes 147464 | tf_op jit(solution)/shard_map/ppermute | solution.py:113
  32.8 4.6 %collective-permute-start.9 = (f32[12,8,128]{2,1,0:T(8,128)S(1)}, f32[12,8,128]{2,1,0:T(8,128)S(1)}, u32[]{:S(2)}, u32[]{:S(2)}) collective-permute-start(f32[12,8,128]{2,1,0:T(8,128)S(1)} %get-tuple-element.48), channel_id=1, source_target_pairs={{0,3},{1,0},{2,1},{3,2},{4,7},{5,4},{6,5},{7,6},{8,11},{9,8},{10,9... | collective-permute-start | bytes 147464 | tf_op jit(solution)/shard_map/ppermute | solution.py:113
  37.5 4.8 %collective-permute-start.10 = (f32[12,8,128]{2,1,0:T(8,128)S(1)}, f32[12,8,128]{2,1,0:T(8,128)S(1)}, u32[]{:S(2)}, u32[]{:S(2)}) collective-permute-start(f32[12,8,128]{2,1,0:T(8,128)S(1)} %get-tuple-element.49), channel_id=1, source_target_pairs={{0,4},{4,8},{8,12},{12,16},{16,20},{20,24},{24,28},{28,0},{1,5},{5... | collective-permute-start | bytes 147464 | tf_op jit(solution)/shard_map/ppermute | solution.py:113
  37.5 4.7 %collective-permute-start.11 = (f32[12,8,128]{2,1,0:T(8,128)S(1)}, f32[12,8,128]{2,1,0:T(8,128)S(1)}, u32[]{:S(2)}, u32[]{:S(2)}) collective-permute-start(f32[12,8,128]{2,1,0:T(8,128)S(1)} %get-tuple-element.50), channel_id=1, source_target_pairs={{0,28},{4,0},{8,4},{12,8},{16,12},{20,16},{24,20},{28,24},{1,29},{... | collective-permute-start | bytes 147464 | tf_op jit(solution)/shard_map/ppermute | solution.py:113
  60.6 2.5 %collective-permute-start.12 = (f32[32,3,8,128]{3,2,1,0:T(8,128)S(1)}, f32[32,3,8,128]{3,2,1,0:T(8,128)S(1)}, u32[]{:S(2)}, u32[]{:S(2)}) collective-permute-start(f32[32,3,8,128]{3,2,1,0:T(8,128)S(1)} %all_to_all.5.own_half), channel_id=1, source_target_pairs={{0,4},{4,0},{8,12},{12,8},{16,20},{20,16},{24,28},{28,24},{1,5},{5... | collective-permute-start | bytes 1179656 | tf_op jit(solution)/shard_map/ppermute | solution.py:946

commit v5 on v4

--- a/solution.py
+++ b/solution.py
@@ -34,24 +34,44 @@
     return lax.broadcasted_iota(jnp.int32, shape, axis)
 
 
-def selector(rows, columns, hit):
-    return jnp.where(hit(iota((rows, columns), 0), iota((rows, columns), 1)), 1.0, 0.0).astype(F32)
-
-
-def pair_sum(size):
-    return selector(size, size // 2, lambda k, m: k // 2 == m)
-
-
-def pair_copy(size):
-    return selector(size, 2 * size, lambda k, m: k == m // 2)
-
-
-def dot(left, right):
-    return lax.dot(left, right, precision=lax.Precision.HIGHEST, preferred_element_type=F32)
-
-
 def roll(value, shift, axis):
     return pltpu.roll(value, shift % value.shape[axis], axis)
+
+
+def take(tile, index, axis):
+    return jnp.take_along_axis(tile, index, axis=axis, mode="promise_in_bounds")
+
+
+def rows_spread(tile, half):
+    return take(tile, iota(TILE, 0) // 2 + 4 * half, 0)
+
+
+def lanes_spread(tile, half):
+    return take(tile, iota(TILE, 1) // 2 + 64 * half, 1)
+
+
+def rows_merge(one, two, pairs=True):
+    row = iota(TILE, 0)
+    if pairs:
+        one, two = one + roll(one, -1, 0), two + roll(two, -1, 0)
+    index = (2 * row) % TILE[0]
+    return jnp.where(row < TILE[0] // 2, take(one, index, 0), take(two, index, 0))
+
+
+def lanes_merge(one, two, pairs=True):
+    lane = iota(TILE, 1)
+    if pairs:
+        one, two = one + roll(one, -1, 1), two + roll(two, -1, 1)
+    index = (2 * lane) % TILE[1]
+    return jnp.where(lane < TILE[1] // 2, take(one, index, 1), take(two, index, 1))
+
+
+def merge(plane, row_pairs=True, lane_pairs=True):
+    halves = []
+    for side in range(2):
+        lanes = slice(side * TILE[1], (side + 1) * TILE[1])
+        halves.append(rows_merge(plane[: TILE[0], lanes], plane[TILE[0] :, lanes], row_pairs))
+    return lanes_merge(*halves, lane_pairs)
 
 
 def each(start, stop, body, carry=0):
@@ -62,6 +82,10 @@
     return carry
 
 
+def here():
+    return lax.axis_index("gx"), lax.axis_index("gy")
+
+
 class Writer:
     def __init__(self, ref):
         self.ref, self.at = ref, 0
@@ -72,6 +96,36 @@
             for c in range(0, columns, TILE[1]):
                 self.ref[self.at] = value[r : r + TILE[0], c : c + TILE[1]]
                 self.at += 1
+
+
+class Tiles:
+    def __init__(self):
+        self.tiles = []
+
+    def put(self, value):
+        rows, columns = value.shape
+        for r in range(0, rows, TILE[0]):
+            for c in range(0, columns, TILE[1]):
+                self.tiles.append(value[r : r + TILE[0], c : c + TILE[1]])
+
+
+def send(first, second, even, up, down):
+    for at, (one, two) in enumerate(zip(up.tiles, down.tiles, strict=True)):
+        first[at] = jnp.where(even, one, two)
+        second[at] = jnp.where(even, two, one)
+
+
+class Got:
+    def __init__(self, first, second, even, low):
+        self.refs = (second, first) if low else (first, second)
+        self.even, self.shape = even, first.shape
+
+    def __getitem__(self, at):
+        return jnp.where(self.even, self.refs[0][at], self.refs[1][at])
+
+
+def got(first, second, even):
+    return Got(first, second, even, True), Got(first, second, even, False)
 
 
 class Reader:
@@ -108,6 +162,12 @@
     return iota((TILE[0], width), 0) < TILE[0] // 2
 
 
+def swapped(first, second, axis):
+    count = lax.axis_size(axis)
+    outer = [(i, (i + 1 if i % 2 else i - 1) % count) for i in range(count)]
+    return lax.ppermute(first, axis, [(i, i ^ 1) for i in range(count)]), lax.ppermute(second, axis, outer)
+
+
 def shifted(value, axis, step):
     count = lax.axis_size(axis)
     return lax.ppermute(value, axis, [(i, (i + step) % count) for i in range(count)])
@@ -115,7 +175,7 @@
 
 def pack_kernel(
     ini_in, src_in, absorb_in, face_x_in, face_y_in, face_z_in,
-    up_x, down_x, up_y, down_y, mid, low, own, rows_mid, sems,
+    up_x, down_x, up_y, down_y, mid, low, own, sems,
 ):
     copies = []
     for field, ref in enumerate((ini_in, src_in, absorb_in, face_x_in, face_y_in, face_z_in)):
@@ -126,52 +186,29 @@
     fields = tuple(own.at[field] for field in range(6))
     ini, src, absorb, face_x, face_y, face_z = fields
     size_x, size_y, size_z = ini.shape
-    half = size_y // 2
-    blocks = range(0, size_x, 2)
-
-    def both_planes(ref):
-        return [ref[plane] + ref[plane + 1] for plane in blocks]
-
-    stacked = both_planes(absorb) + [face_x[plane] for plane in blocks] + both_planes(face_y)
-    summed = dot(jnp.concatenate(stacked, axis=0), pair_sum(size_z))
-    picked = dot(
-        jnp.concatenate(both_planes(face_z), axis=0),
-        selector(size_z, size_z // 2, lambda k, m: k == 2 * m),
-    )
-    count = summed.shape[0]
-    rows_mid[:count] = summed
-    rows_mid[count:] = picked
-    out = Writer(mid)
-    for array, (factor, sides) in enumerate(((0.125, 2), (0.25, 2), (0.25, 1), (0.25, 2))):
-        lines = (size_x // 2) * half
-        start = 2 * array * lines
-        total = rows_mid[pl.ds(start, lines, 2), :]
-        if sides == 2:
-            total = total + rows_mid[pl.ds(start + 1, lines, 2), :]
-        out.put(total * factor)
-
-    mid_x, mid_z = size_x // 2, size_z // 2
-    both = (0, 1)
-    low_z = mid_z // 2
-
-    def coarser(array, planes, sides):
-        lines = []
-        for block in range(mid_x // 2):
+    mid_x = size_x // 2
+    for block in range(mid_x):
+        one, two = 2 * block, 2 * block + 1
+        mid[block] = merge(absorb[one] + absorb[two]) * 0.125
+        mid[mid_x + block] = merge(face_x[one]) * 0.25
+        mid[2 * mid_x + block] = merge(face_y[one] + face_y[two], row_pairs=False) * 0.25
+        mid[3 * mid_x + block] = merge(face_z[one] + face_z[two], lane_pairs=False) * 0.25
+
+    def coarser(array, planes, row_pairs=True, lane_pairs=True):
+        parts = []
+        for block in range(0, mid_x, 2):
             total = None
-            for plane in planes:
-                for side in sides:
-                    at = array * mid_x + 2 * block + plane
-                    part = mid[at, pl.ds(side, half // 2, 2), :]
-                    total = part if total is None else total + part
-            lines.append(total)
-        return jnp.concatenate(lines, axis=0)
-
-    left = selector(mid_z, mid_z, lambda k, m: k // 2 == m)
-    right = selector(mid_z, mid_z, lambda k, m: k // 2 == m - low_z)
-    evens = selector(mid_z, mid_z, lambda k, m: k == 2 * m)
-    low[0] = dot(coarser(0, both, both) * 0.125, right)
-    low[1] = dot(coarser(1, (0,), both) * 0.25, left) + dot(coarser(2, both, (0,)) * 0.25, right)
-    low[2] = dot(coarser(3, both, both) * 0.25, evens)
+            for plane in range(planes):
+                part = mid[array * mid_x + block + plane]
+                total = part if total is None else total + part
+            parts.append(total)
+        tile = rows_merge(*parts, row_pairs)
+        return lanes_merge(tile, tile, lane_pairs)
+
+    left = iota(TILE, 1) < TILE[1] // 2
+    low[0] = jnp.where(left, 0.0, coarser(0, 2) * 0.125)
+    low[1] = jnp.where(left, coarser(1, 1), coarser(2, 2, row_pairs=False)) * 0.25
+    low[2] = jnp.where(left, coarser(3, 2, lane_pairs=False) * 0.25, 0.0)
 
     tops, bottoms = Writer(up_x), Writer(down_x)
     for ref, count in zip(fields, UP_PLANES):
@@ -240,10 +277,11 @@
     return jnp.where(row >= 4, near, far) if low else jnp.where(row < 4, near, far)
 
 
-def corner_kernel(size_x, size_z, low_y, high_y, mid, low_faces, up, down):
+def corner_kernel(size_x, size_z, low_y, high_y, mid, low_faces, first, second):
+    place = here()
     upper = is_upper(size_z)
     per_field = (size_x // 2) * tiles_of(8, size_z)
-    tops, bottoms = Writer(up), Writer(down)
+    tops, bottoms = Tiles(), Tiles()
     for field in range(6):
         start = field * per_field
         planes = [size_x - 1 - plane for plane in range(UP_CORNER[field])]
@@ -251,10 +289,10 @@
         put_corners(bottoms, low_y, high_y, range(DOWN_CORNER[field]), upper, start)
     mid_x = size_x // 2
     upper = is_upper(TILE[1])
-    for writer, wanted in (
-        (tops, [(array, mid_x - 1) for array in range(4)]),
-        (bottoms, [(array, 0) for array in range(4)] + [(1, 1)]),
-    ):
+    for _ in range(len(bottoms.tiles) - len(tops.tiles)):
+        tops.put(low_faces[0])
+    for writer, near, next_plane in ((tops, mid_x - 1, mid_x - 2), (bottoms, 0, 1)):
+        wanted = [(array, near) for array in range(4)] + [(1, next_plane)]
         for array, plane in wanted:
             writer.put(
                 jnp.where(upper, mid_strip(high_y, array, plane, False), mid_strip(low_y, array, plane, True))
@@ -264,6 +302,7 @@
         for tiles in ((low_faces[1], low_faces[2]), low_tiles_of(low_y), low_tiles_of(high_y)):
             for tile in tiles:
                 writer.put(tile)
+    send(first, second, place[0] % 2 == 0, tops, bottoms)
 
 
 def low_tiles_of(ref):
@@ -332,10 +371,10 @@
 
 
 def scaled_remain(coeffs, i, below, here, above, goal=None):
-    total = (coeffs[6, i] if goal is None else goal[i]) - here
-    total = total + coeffs[0, i] * below + coeffs[1, i] * above
-    total = total + coeffs[2, i] * roll(here, 1, 0) + coeffs[3, i] * roll(here, -1, 0)
-    return total + coeffs[4, i] * roll(here, 1, 1) + coeffs[5, i] * roll(here, -1, 1)
+    along_z = coeffs[4, i] * roll(here, 1, 1) + coeffs[5, i] * roll(here, -1, 1)
+    along_y = coeffs[2, i] * roll(here, 1, 0) + coeffs[3, i] * roll(here, -1, 0)
+    along_x = coeffs[0, i] * below + coeffs[1, i] * above
+    return ((coeffs[6, i] if goal is None else goal[i]) - here + along_x) + (along_y + along_z)
 
 
 def sweep_window(iterate, update, coeffs, planes, pair, first, goal=None, source=None):
@@ -441,12 +480,15 @@
 
 
 def fine_kernel(
-    own_windows, own_coeffs, up_corner, down_corner, mid, low_x, high_x, low_c, high_c,
-    iterate_out, mid_target, up_x, down_x, up_y, down_y,
-    side_windows, side_coeffs, iterate, update, rest,
+    own_windows, own_coeffs, up_corner, down_corner, mid, low_x, high_x, first_c, second_c,
+    iterate_out, mid_target, first_x, second_x, first_y, second_y,
+    side_windows, side_coeffs, iterate, update,
 ):
     size_x, size_z = own_windows.shape[1], own_windows.shape[3]
     size_y = own_windows.shape[2] - 2 * PAD
+    place = here()
+    even = place[0] % 2 == 0
+    low_c, high_c = got(first_c, second_c, even)
     assemble_sides(side_windows, (size_y, size_z), low_x, high_x, low_c, high_c)
     end = FINE + size_x
     last = end + FINE - 1
@@ -465,45 +507,43 @@
             source=fields[0] if sweep == 0 else None,
         )
     mid_x, mid_y = size_x // 2, size_y // 2
-    lines = []
+    coarse = []
     for block in range(mid_x):
         total = None
         for plane in (FINE + 2 * block, FINE + 2 * block + 1):
             remain = scaled_remain(coeffs, plane, iterate[plane - 1], iterate[plane], iterate[plane + 1])
             remain = (remain * coeffs[7, plane])[PAD : PAD + size_y]
             total = remain if total is None else total + remain
-        lines.append(total)
-    rest[...] = dot(jnp.concatenate(lines, axis=0), pair_sum(size_z))
-    count = mid_x * mid_y
-    coarse = (rest[pl.ds(0, count, 2), :] + rest[pl.ds(1, count, 2), :]) * 0.125
-    for block in range(mid_x):
-        mid_target[block] = coarse[block * mid_y : (block + 1) * mid_y]
+        coarse.append(merge(total) * 0.125)
+        mid_target[block] = coarse[block]
     for plane in range(size_x):
         iterate_out[plane] = iterate[FINE + plane, PAD : PAD + size_y]
 
-    tops, bottoms = Writer(up_x), Writer(down_x)
+    tops, bottoms = Tiles(), Tiles()
     for plane in range(size_x - 4, size_x):
         tops.put(iterate_out[plane])
     for plane in range(4):
         bottoms.put(iterate_out[plane])
     upper = is_upper(size_z)
-    tops_y, bottoms_y = Writer(up_y), Writer(down_y)
+    tops_y, bottoms_y = Tiles(), Tiles()
     for pair in range(0, size_x, 2):
         one, two = iterate_out[pair], iterate_out[pair + 1]
         tops_y.put(jnp.where(upper, roll(one[size_y - 8 :], 4, 0), two[size_y - 8 :]))
         bottoms_y.put(jnp.where(upper, one[:8], roll(two[:8], 4, 0)))
     for writer in (tops, bottoms, tops_y, bottoms_y):
-        writer.put(coarse)
+        for tile in coarse:
+            writer.put(tile)
     for writer, ref in ((tops, up_corner), (bottoms, down_corner)):
         for tile in range(MID_CORNER):
             writer.put(ref[tile])
     for writer in (tops, bottoms):
         for tile in range(mid.shape[0]):
             writer.put(mid[tile])
-    for writer, corners, extra in ((tops, low_c, 4), (bottoms, high_c, 5)):
-        start = corners.shape[0] - PASSED - 2 * extra
-        for tile in range(start, corners.shape[0]):
+    for writer, corners in ((tops, low_c), (bottoms, high_c)):
+        for tile in range(corners.shape[0] - PASSED - 10, corners.shape[0]):
             writer.put(corners[tile])
+    send(first_x, second_x, even, tops, bottoms)
+    send(first_y, second_y, place[1] % 2 == 0, tops_y, bottoms_y)
 
 
 MID_CORNER = 24
@@ -518,18 +558,23 @@
     return ref[start + 16 + array * 2 + q - 2]
 
 
-def corner_two_kernel(size_x, size_z, low_y, high_y, up, down):
+def corner_two_kernel(size_x, size_z, first_y, second_y, first, second):
+    place = here()
     upper = is_upper(size_z)
-    tops, bottoms = Writer(up), Writer(down)
+    low_y, high_y = got(first_y, second_y, place[1] % 2 == 0)
+    tops, bottoms = Tiles(), Tiles()
     put_corners(tops, low_y, high_y, [size_x - 1, size_x - 2, size_x - 3], upper, 0)
     put_corners(bottoms, low_y, high_y, range(3), upper, 0)
     for writer in (tops, bottoms):
         for ref in (low_y, high_y):
             for tile in range(ref.shape[0] - size_x // 2, ref.shape[0]):
                 writer.put(ref[tile])
-
-
-def mid_coeffs_kernel(mid, low_y, high_y, low_x2, high_x2, coeffs, window):
+    send(first, second, place[0] % 2 == 0, tops, bottoms)
+
+
+def mid_coeffs_kernel(mid, low_y, high_y, first_x2, second_x2, coeffs, window):
+    place = here()
+    low_x2, high_x2 = got(first_x2, second_x2, place[0] % 2 == 0)
     mid_y, mid_z = mid.shape[1:]
     mid_x = mid.shape[0] // 4
     mids = 4 * mid_x
@@ -546,9 +591,7 @@
             window[array, MID + plane, 2 * mid_y :] = mid_strip(high_y, array, plane, False)
     passed += mids
     far = 3 * mid_x + first
-    for ref, start, step, end, extra in (
-        (low_x2, MID - 1, -1, first - 1, 4), (high_x2, MID + mid_x, 1, far, 5)
-    ):
+    for ref, start, step, end in ((low_x2, MID - 1, -1, first - 1), (high_x2, MID + mid_x, 1, far)):
         for array in range(4):
             for q in range(mid_x):
                 if q < 2:
@@ -557,22 +600,27 @@
                     one = two = roll(part_corner(ref, corner, array, q), 4, 0)
                 window[array, start + q * step, :mid_y] = one
                 window[array, start + q * step, 2 * mid_y :] = two
-        for place in range(extra):
-            array, plane = (place, end) if place < 4 else (1, end + 1)
-            window[array, plane, :mid_y] = ref[passed + place]
-            window[array, plane, 2 * mid_y :] = ref[passed + place]
-            window[array, plane, mid_y : 2 * mid_y] = ref[passed + extra + place]
+        for at in range(5):
+            array, plane = (at, end) if at < 4 else (1, end + step)
+            window[array, plane, :mid_y] = ref[passed + at]
+            window[array, plane, 2 * mid_y :] = ref[passed + at]
+            window[array, plane, mid_y : 2 * mid_y] = ref[passed + 5 + at]
     scale_coeffs(0.25, *(window.at[array] for array in range(4)), coeffs, (first - 1, far + 1), None, True)
 
 
 def mid_kernel(
-    count_x, count_y, place, low, mid_target, coeffs, low_x2, high_x2, low_y2, high_y2, low_c2, high_c2,
-    goal, slots, target, iterate, update, rest,
+    count_x, count_y, low, mid_target, coeffs, first_x2, second_x2, first_y2, second_y2, first_c2, second_c2,
+    goal, slots, target, iterate, update,
 ):
     mid_x, mid_y, mid_z = mid_target.shape
     first = MID - mid_x
     far = 3 * mid_x + first
     fine_tiles = 4 * tiles_of(2 * mid_y, 2 * mid_z)
+    place = here()
+    even = place[0] % 2 == 0
+    low_x2, high_x2 = got(first_x2, second_x2, even)
+    low_y2, high_y2 = got(first_y2, second_y2, place[1] % 2 == 0)
+    low_c2, high_c2 = got(first_c2, second_c2, even)
     blocks = {
         (0, 0): (low_c2, low_c2.shape[0] - 2 * mid_x), (0, 1): (low_x2, fine_tiles),
         (0, 2): (low_c2, low_c2.shape[0] - mid_x), (1, 0): (low_y2, low_y2.shape[0] - mid_x),
@@ -598,21 +646,20 @@
     each(first, far, start_sweep)
     for sweep in range(1, SWEEPS):
         sweep_window(iterate, update, coeffs, (first + sweep, far - sweep), weights[sweep], False, goal)
-    low_x_size = mid_x // 2
-    for block in range(low_x_size):
+    parts = []
+    for block in range(0, mid_x, 2):
         total = None
-        for plane in (MID + 2 * block, MID + 2 * block + 1):
+        for plane in (MID + block, MID + block + 1):
             remain = scaled_remain(coeffs, plane, iterate[plane - 1], iterate[plane], iterate[plane + 1], goal)
             remain = (remain * coeffs[7, plane])[mid_y : 2 * mid_y]
             total = remain if total is None else total + remain
-        rest[block * mid_y : (block + 1) * mid_y] = total
-    count = low_x_size * mid_y // 2
-    summed = rest[pl.ds(0, count, 2), :] + rest[pl.ds(1, count, 2), :]
-    coarse = dot(summed * 0.125, selector(mid_z, mid_z, lambda k, m: k // 2 == m))
-    tiles = (coarse + low[0], low[1], low[2])
+        parts.append(total)
+    coarse = rows_merge(*parts)
+    coarse = lanes_merge(coarse, coarse) * 0.125
+    tiles = (jnp.where(iota(TILE, 1) < TILE[1] // 2, coarse, low[0]), low[1], low[2])
     x1 = [iterate[MID + plane, mid_y : 2 * mid_y] for plane in range(mid_x)]
     pairs = count_x // 2
-    own, even = place[0] // 2, place[0] % 2 == 0
+    own = place[0] // 2
     above, below = lax.rem(own + 1, pairs), lax.rem(own + pairs - 1, pairs)
 
     def fill(i, carry):
@@ -705,15 +752,21 @@
 
 
 def window_kernel(
-    fields_own, low_x1, high_x1, low_y1, high_y1, low_c1, high_c1,
-    own, low_x, high_x, low_y, high_y, low_c, high_c,
+    fields_own, low_x1, high_x1, low_y1, high_y1, first_c1, second_c1,
+    own, first_x, second_x, first_y, second_y, first_c, second_c,
     low, window, coeffs, near, own_windows, side_windows,
 ):
+    place = here()
+    even = place[0] % 2 == 0
+    low_c1, high_c1 = got(first_c1, second_c1, even)
+    low_x, high_x = got(first_x, second_x, even)
+    low_y, high_y = got(first_y, second_y, place[1] % 2 == 0)
+    low_c, high_c = got(first_c, second_c, even)
     known = {(0, 0): (low[1], low[2]), (0, -1): low_tiles_of(low_y1), (0, 1): low_tiles_of(high_y1)}
     for step, ref, distance in ((-1, low_c1, 1), (1, high_c1, 1), (-1, low_x, 2), (1, high_x, 2)):
         start = ref.shape[0] - PASSED
-        for place, dy in enumerate((0, -1, 1)):
-            known[step * distance, dy] = (ref[start + 2 * place], ref[start + 2 * place + 1])
+        for at, dy in enumerate((0, -1, 1)):
+            known[step * distance, dy] = (ref[start + 2 * at], ref[start + 2 * at + 1])
     for (dx, dy), tiles in known.items():
         for kind in range(2):
             near[((dx + 2) * 3 + dy + 1) * 2 + kind] = tiles[kind]
@@ -732,17 +785,17 @@
 
 
 def last_kernel(
-    count_x, count_y, place, own_half, other_half, mid_coeffs, goal_in, fine_coeffs, window, near,
+    count_x, count_y, own_half, other_half, mid_coeffs, goal_in, fine_coeffs, window, near,
     out,
     gathered, low_fields, low_coeffs, low_iterate, low_update,
-    goal, mid_iterate, mid_update, spread_mid,
-    iterate, update, spread,
+    goal, mid_iterate, mid_update,
+    iterate, update,
 ):
     size_x, size_y, size_z = out.shape
     mid_x, mid_y, mid_z = size_x // 2, size_y // 2, size_z // 2
     last = size_x + 2 * FINE - 2
     coeffs = Stack((2, last, fine_coeffs, 0))
-    me_x, me_y = place[0], place[1]
+    me_x, me_y = here()
     even = me_x % 2 == 0
 
     def half(which, device, tile):
@@ -785,19 +838,13 @@
         mid_iterate[far, rows] = half(0, source, 2)
         mid_iterate[far + 1, rows] = jnp.where(even, half(1, source, 0), half(1, source, 2))
     low_size_x, low_size_y = low_iterate.shape[:2]
-    low_planes, low_rows = (mid_x + 2 * MID) // 2, 16
     low_y = mid_y // 2
     turn = lax.rem(low_size_y - me_y * low_y + low_y, low_size_y)
-    picked = []
-    for plane in range(low_planes):
+    for plane in range((mid_x + 2 * MID) // 2):
         at = lax.rem(me_x * (mid_x // 2) - MID // 2 + plane + low_size_x, low_size_x)
-        picked.append(pltpu.roll(low_iterate[at], turn, 0)[:low_rows])
-    wide = dot(jnp.concatenate(picked, axis=0), selector(mid_z, mid_z, lambda k, m: k == m // 2))
-    count = low_planes * low_rows
-    spread_mid[pl.ds(0, count, 2), :] = wide
-    spread_mid[pl.ds(1, count, 2), :] = wide
-    for plane in range(low_planes):
-        part = spread_mid[plane * 2 * low_rows : plane * 2 * low_rows + 3 * mid_y]
+        turned = pltpu.roll(low_iterate[at], turn, 0)
+        one, two = lanes_spread(turned[: TILE[0]], 0), lanes_spread(turned[TILE[0] : 2 * TILE[0]], 0)
+        part = jnp.concatenate([rows_spread(one, 0), rows_spread(one, 1), rows_spread(two, 0)], axis=0)
         mid_iterate[2 * plane] += part
         mid_iterate[2 * plane + 1] += part
 
@@ -813,18 +860,15 @@
         )
 
     fine_low = FINE - 4
-    planes = mid_x + 4
-    rows = mid_y + 8
-    picked = [roll(mid_iterate[MID - 2 + plane], -4, 0)[:rows] for plane in range(planes)]
-    wide = dot(jnp.concatenate(picked, axis=0), pair_copy(mid_z))
-    count = planes * rows
-    for side in range(2):
-        lanes = slice(side * mid_z, (side + 1) * mid_z)
-        spread[side, pl.ds(0, count, 2), :] = wide[:, lanes]
-        spread[side, pl.ds(1, count, 2), :] = wide[:, lanes]
-    for plane in range(planes):
-        lines = slice(plane * 2 * rows, (plane + 1) * 2 * rows)
-        part = jnp.concatenate([spread[0, lines], spread[1, lines]], axis=1)
+    for plane in range(mid_x + 4):
+        turned = roll(mid_iterate[MID - 2 + plane], -4, 0)
+        lines = []
+        for r in range(2):
+            tile = turned[r * TILE[0] : (r + 1) * TILE[0]]
+            for side in range(2):
+                line = rows_spread(tile, side)
+                lines.append(jnp.concatenate([lanes_spread(line, 0), lanes_spread(line, 1)], axis=1))
+        part = jnp.concatenate(lines, axis=0)
         for at in (fine_low + 2 * plane, fine_low + 2 * plane + 1):
             iterate[at] = window[at] + part
     for sweep, pair in enumerate(chebyshev_weights(SWEEPS)):
@@ -872,7 +916,6 @@
     def tiles(count):
         return (count,) + TILE
 
-    place = jnp.stack([lax.axis_index("gx"), lax.axis_index("gy")]).astype(jnp.int32)
     pairs = size_x // 2
     up_x, down_x, up_y, down_y, mid, low, own = call(
         pack_kernel,
@@ -886,18 +929,17 @@
             tiles(3),
             (6,) + source.shape,
         ],
-        [(4 * mid_x * size_y, mid_z)],
         far_in=range(6),
         sems=6,
     )
     low_x1, high_x1 = shifted(up_x, "gx", 1), shifted(down_x, "gx", -1)
     low_y1, high_y1 = shifted(up_y, "gy", 1), shifted(down_y, "gy", -1)
-    up_c, down_c = call(
+    first_c1, second_c1 = call(
         functools.partial(corner_kernel, size_x, size_z),
         (low_y1, high_y1, mid, low),
-        [tiles(corner_tiles(UP_CORNER) * strip + 14), tiles(corner_tiles(DOWN_CORNER) * strip + 16)],
-    )
-    low_c1, high_c1 = shifted(up_c, "gx", 1), shifted(down_c, "gx", -1)
+        [tiles(corner_tiles(DOWN_CORNER) * strip + 16)] * 2,
+    )
+    first_c1, second_c1 = swapped(first_c1, second_c1, "gx")
 
     tall = (size_y + 2 * PAD, size_z)
     wide = (size_x + 2 * FINE,) + tall
@@ -906,62 +948,59 @@
         (own, low_y1, high_y1),
         [(6, size_x) + tall, (8, size_x - 1) + tall, tiles(MID_CORNER), tiles(MID_CORNER)],
     )
-    iterate, mid_target, up_x, down_x, up_y, down_y = call(
+    iterate, mid_target, first_x2, second_x2, first_y2, second_y2 = call(
         fine_kernel,
-        (own_windows, own_coeffs, up_corner, down_corner, mid, low_x1, high_x1, low_c1, high_c1),
+        (own_windows, own_coeffs, up_corner, down_corner, mid, low_x1, high_x1, first_c1, second_c1),
         [
             source.shape,
             (mid_x, mid_y, mid_z),
-            tiles(4 * plane + mid_x + MID_CORNER + mids + 8 + PASSED),
+            tiles(4 * plane + mid_x + MID_CORNER + mids + 10 + PASSED),
             tiles(4 * plane + mid_x + MID_CORNER + mids + 10 + PASSED),
             tiles(pairs * strip + mid_x),
             tiles(pairs * strip + mid_x),
         ],
-        [(6, 2 * FINE) + tall, (8, 2 * FINE + 1) + tall, wide, wide, (mid_x * size_y, mid_z)],
-    )
-    low_x2, high_x2 = shifted(up_x, "gx", 1), shifted(down_x, "gx", -1)
-    low_y2, high_y2 = shifted(up_y, "gy", 1), shifted(down_y, "gy", -1)
-    up_c, down_c = call(
+        scratch=[(6, 2 * FINE) + tall, (8, 2 * FINE + 1) + tall, wide, wide],
+    )
+    first_x2, second_x2 = swapped(first_x2, second_x2, "gx")
+    first_y2, second_y2 = swapped(first_y2, second_y2, "gy")
+    first_c2, second_c2 = call(
         functools.partial(corner_two_kernel, size_x, size_z),
-        (low_y2, high_y2),
+        (first_y2, second_y2),
         [tiles(2 * strip + 2 * mid_x)] * 2,
     )
-    low_c2, high_c2 = shifted(up_c, "gx", 1), shifted(down_c, "gx", -1)
+    first_c2, second_c2 = swapped(first_c2, second_c2, "gx")
 
     mid_wide = (mid_x + 2 * MID, 3 * mid_y, mid_z)
     (mid_coeffs,) = call(
         mid_coeffs_kernel,
-        (mid, low_y1, high_y1, low_x2, high_x2),
+        (mid, low_y1, high_y1, first_x2, second_x2),
         [(8,) + mid_wide],
         [(4,) + mid_wide],
     )
     goal, slots = call(
         functools.partial(mid_kernel, count_x, count_y),
-        (place, low, mid_target, mid_coeffs, low_x2, high_x2, low_y2, high_y2, low_c2, high_c2),
+        (low, mid_target, mid_coeffs, first_x2, second_x2, first_y2, second_y2, first_c2, second_c2),
         [mid_wide, (devices, 3) + TILE],
-        [mid_wide] * 3 + [(low_x * mid_y, mid_z)],
-        scalars=1,
+        [mid_wide] * 3,
     )
     own_half = lax.all_to_all(slots, ("gx", "gy"), 0, 0)
     other_half = lax.ppermute(own_half, "gx", [(i, i ^ 1) for i in range(count_x)])
 
     window, coeffs, near = call(
         window_kernel,
-        (own, low_x1, high_x1, low_y1, high_y1, low_c1, high_c1)
-        + (iterate, low_x2, high_x2, low_y2, high_y2, low_c2, high_c2, low),
+        (own, low_x1, high_x1, low_y1, high_y1, first_c1, second_c1)
+        + (iterate, first_x2, second_x2, first_y2, second_y2, first_c2, second_c2, low),
         [wide, (7, wide[0] - 4) + tall, tiles(30)],
         [(6, size_x) + tall, (6, 2 * FINE) + tall],
     )
     low_wide = (low_x * count_x, low_y * count_y, mid_z)
-    low_planes = mid_wide[0] // 2
     (result,) = call(
         functools.partial(last_kernel, count_x, count_y),
-        (place, own_half, other_half, mid_coeffs, goal, coeffs, window, near),
+        (own_half, other_half, mid_coeffs, goal, coeffs, window, near),
         [source.shape],
         [(devices, 3) + TILE, (3,) + low_wide, (7,) + low_wide, low_wide, low_wide]
-        + [mid_wide, mid_wide, mid_wide, (low_planes * 32, mid_z)]
-        + [wide, wide, (2, (mid_x + 4) * 2 * (mid_y + 8), mid_z)],
-        scalars=1,
+        + [mid_wide, mid_wide, mid_wide]
+        + [wide, wide],
     )
     return result
 

time: 67.5 us -> 62.8 us (0.930)
  blocking collectives: 17.2 us -> 13.6 us
  Pallas kernels: 11.4 us -> 8.68 us
  waiting for transfers between devices: 22.2 us -> 23.9 us
    ppermute x0 -> x8, waiting for transfers between devices: none -> 12.5 us  [the longest x4 10.6 us: swapped(): lax.ppermute(second, axis, outer)]
    ppermute x12 -> x4, waiting for transfers between devices: 21.4 us -> 10.7 us  [shifted(): lax.ppermute(value, axis, [(i, (i + step) % count) for i in range(count)])]
    ppermute x12 -> x4, starting transfers between devices: 15.2 us -> 6.71 us  [shifted(): lax.ppermute(value, axis, [(i, (i + step) % count) for i in range(count)])]
    ppermute x0 -> x8, starting transfers between devices: none -> 8.4 us  [the longest x4 6.49 us: swapped(): lax.ppermute(second, axis, outer)]
    all_to_all x1, blocking collectives: 17.2 us -> 13.6 us  [local(): own_half = lax.all_to_all(slots, ('gx', 'gy'), 0, 0)]
    pallas_call x9, Pallas kernels: 11.4 us -> 8.68 us  [call(): pl.pallas_call(kernel, out_shape=[pltpu.HBM(shape, F32) if i in far_out e...]
where the time goes in v5:
time: 62.8 us; the launch traced here: 62.6 us
  waiting for transfers between devices  23.9 us (38%)
  starting transfers between devices  16.3 us (26%)
  blocking collectives  13.6 us (22%)
  Pallas kernels  8.68 us (14%)
    all_to_all x1, blocking collectives, local(): own_half = lax.all_to_all(slots, ('gx', 'gy'), 0, 0)  13.6 us
    ppermute x4, waiting for transfers between devices, shifted(): lax.ppermute(value, axis, [(i, (i + step) % count) for i in range(count)])  10.7 us
    ppermute x4, waiting for transfers between devices, swapped(): lax.ppermute(second, axis, outer)  10.6 us
    pallas_call x9, Pallas kernels, call(): pl.pallas_call(kernel, out_shape=[pltpu.HBM(shape, F32) if i in far_out e...  8.68 us
    ppermute x4, starting transfers between devices, shifted(): lax.ppermute(value, axis, [(i, (i + step) % count) for i in range(count)])  6.71 us
    ppermute x4, starting transfers between devices, swapped(): lax.ppermute(second, axis, outer)  6.49 us
    ppermute x4, starting transfers between devices, swapped(): lax.ppermute(first, axis, [(i, i ^ 1) for i in range(count)])  1.9 us
    ppermute x4, waiting for transfers between devices, swapped(): lax.ppermute(first, axis, [(i, i ^ 1) for i in range(count)])  1.9 us
  transfers between devices with their start and end apart: 13, of which 6 were waited for; matrix products, arithmetic and copies ran while one was open for 0% of the time, Pallas kernels for 2%

profile of v5, /device:TPU:0, one launch (start us, length us, event | category | flops | bytes accessed | tf_op | source)
XLA Modules:
  0.0 62.6 jit_solution(16761599144913374061)
XLA Ops:
  0.0 1.6 %shard_map.64 = (f32[100,8,128]{2,1,0:T(8,128)S(1)}, f32[104,8,128]{2,1,0:T(8,128)S(1)}, f32[64,8,128]{2,1,0:T(8,128)S(1)}, f32[66,8,128]{2,1,0:T(8,128)S(1)}, f...) custom-call(f32[8,16,256]{2,1,0:T(8,128)} %ini_in.1, f32[8,16,256]{2,1,0:T(8,128)} %src_in.1, ...), custom_call_target="tpu_custom_call" | custom-call | flops 1000 | bytes 1000 | tf_op jit(solution)/shard_map/pallas_call | solution.py:890
  1.7 5.1 %collective-permute-start.1 = (f32[66,8,128]{2,1,0:T(8,128)S(1)}, f32[66,8,128]{2,1,0:T(8,128)S(1)}, u32[]{:S(2)}, u32[]{:S(2)}) collective-permute-start(f32[66,8,128]{2,1,0:T(8,128)S(1)} %get-tuple-element.34), channel_id=1, source_target_pairs={{0,3},{1,0},{2,1},{3,2},{4,7},{5,4},{6,5},{7,6},{8,11},{9,8},{10,9... | collective-permute-start | bytes 811016 | tf_op jit(solution)/shard_map/ppermute | solution.py:173
  6.8 0.0 collective-permute-start
  6.8 1.6 %collective-permute-start.3 = (f32[104,8,128]{2,1,0:T(8,128)S(1)}, f32[104,8,128]{2,1,0:T(8,128)S(1)}, u32[]{:S(2)}, u32[]{:S(2)}) collective-permute-start(f32[104,8,128]{2,1,0:T(8,128)S(1)} %get-tuple-element.41), channel_id=1, source_target_pairs={{0,28},{4,0},{8,4},{12,8},{16,12},{20,16},{24,20},{28,24},{1,29},{... | collective-permute-start | bytes 1277960 | tf_op jit(solution)/shard_map/ppermute | solution.py:173
  8.4 0.0 collective-permute-start.2
  8.4 10.6 %collective-permute-done.low_y.low_y1 = f32[64,8,128]{2,1,0:T(8,128)S(1)} collective-permute-done((f32[64,8,128]{2,1,0:T(8,128)S(1)}, f32[64,8,128]{2,1,0:T(8,128)S(1)}, u32[]{:S(2)}, u32[]{:S(2)}) %collective-permute-start) | collective-permute-done | bytes 262176 | tf_op jit(solution)/shard_map/ppermute | solution.py:173
  19.0 0.0 collective-permute-done.1.high_y.high_y1
  19.0 0.1 shard_map.66
  19.1 0.1 collective-permute-start.4
  19.2 2.5 %collective-permute-start.5 = (f32[46,8,128]{2,1,0:T(8,128)S(1)}, f32[46,8,128]{2,1,0:T(8,128)S(1)}, u32[]{:S(2)}, u32[]{:S(2)}) collective-permute-start(f32[46,8,128]{2,1,0:T(8,128)S(1)} %get-tuple-element.43), channel_id=1, source_target_pairs={{0,28},{4,8},{8,4},{12,16},{16,12},{20,24},{24,20},{28,0},{1,29},{... | collective-permute-start | bytes 565256 | tf_op jit(solution)/shard_map/ppermute | solution.py:168
  21.7 0.3 shard_map.65
  22.1 0.0 collective-permute-done.2.low_x.low_x1
  22.1 0.0 collective-permute-done.3.high_x.high_x1
  22.1 0.0 collective-permute-done.4.first_c.first_c1
  22.1 4.4 %collective-permute-done.5.second_c.second_c1 = f32[46,8,128]{2,1,0:T(8,128)S(1)} collective-permute-done((f32[46,8,128]{2,1,0:T(8,128)S(1)}, f32[46,8,128]{2,1,0:T(8,128)S(1)}, u32[]{:S(2)}, u32[]{:S(2)}) %collective-permute-start.5) | collective-permute-done | bytes 188448 | tf_op jit(solution)/shard_map/ppermute | solution.py:168
  26.5 1.9 %shard_map.67 = (f32[8,16,256]{2,1,0:T(8,128)S(1)}, f32[4,8,128]{2,1,0:T(8,128)S(1)}, f32[76,8,128]{2,1,0:T(8,128)S(1)}, f32[76,8,128]{2,1,0:T(8,128)S(1)}, f32[...) custom-call(f32[6,8,32,256]{3,2,1,0:T(8,128)S(1)} %get-tuple-element.35.own_windows, ...), custom_call_target="tpu_custom_call" | custom-call | flops 1000 | bytes 1000 | tf_op jit(solution)/shard_map/pallas_call | solution.py:890
  28.4 0.1 collective-permute-start.6
  28.6 1.7 %collective-permute-start.7 = (f32[76,8,128]{2,1,0:T(8,128)S(1)}, f32[76,8,128]{2,1,0:T(8,128)S(1)}, u32[]{:S(2)}, u32[]{:S(2)}) collective-permute-start(f32[76,8,128]{2,1,0:T(8,128)S(1)} %get-tuple-element.46), channel_id=1, source_target_pairs={{0,28},{4,8},{8,4},{12,16},{16,12},{20,24},{24,20},{28,0},{1,29},{... | collective-permute-start | bytes 933896 | tf_op jit(solution)/shard_map/ppermute | solution.py:168
  30.3 1.6 %collective-permute-start.8 = (f32[12,8,128]{2,1,0:T(8,128)S(1)}, f32[12,8,128]{2,1,0:T(8,128)S(1)}, u32[]{:S(2)}, u32[]{:S(2)}) collective-permute-start(f32[12,8,128]{2,1,0:T(8,128)S(1)} %get-tuple-element.47), channel_id=1, source_target_pairs={{0,1},{1,0},{2,3},{3,2},{4,5},{5,4},{6,7},{7,6},{8,9},{9,8},{10,11... | collective-permute-start | bytes 147464 | tf_op jit(solution)/shard_map/ppermute | solution.py:168
  31.9 0.6 collective-permute-start.9
  32.5 1.9 %collective-permute-done.8.first_y.first_y2 = f32[12,8,128]{2,1,0:T(8,128)S(1)} collective-permute-done((f32[12,8,128]{2,1,0:T(8,128)S(1)}, f32[12,8,128]{2,1,0:T(8,128)S(1)}, u32[]{:S(2)}, u32[]{:S(2)}) %collective-permute-start.8) | collective-permute-done | bytes 49184 | tf_op jit(solution)/shard_map/ppermute | solution.py:168
  34.3 3.4 %collective-permute-done.9.second_y.second_y2 = f32[12,8,128]{2,1,0:T(8,128)S(1)} collective-permute-done((f32[12,8,128]{2,1,0:T(8,128)S(1)}, f32[12,8,128]{2,1,0:T(8,128)S(1)}, u32[]{:S(2)}, u32[]{:S(2)}) %collective-permute-start.9) | collective-permute-done | bytes 49184 | tf_op jit(solution)/shard_map/ppermute | solution.py:168
  37.8 0.1 collective-permute-start.10
  37.9 1.7 %collective-permute-start.11 = (f32[12,8,128]{2,1,0:T(8,128)S(1)}, f32[12,8,128]{2,1,0:T(8,128)S(1)}, u32[]{:S(2)}, u32[]{:S(2)}) collective-permute-start(f32[12,8,128]{2,1,0:T(8,128)S(1)} %get-tuple-element.50), channel_id=1, source_target_pairs={{0,28},{4,8},{8,4},{12,16},{16,12},{20,24},{24,20},{28,0},{1,29},{... | collective-permute-start | bytes 147464 | tf_op jit(solution)/shard_map/ppermute | solution.py:168
  39.5 0.0 collective-permute-done.6.first_x2.first_x
  39.5 0.0 collective-permute-done.7.second_x2.second_x
  39.6 0.2 shard_map.68.coeffs.mid_coeffs
  39.8 0.0 collective-permute-done.10.first_c2.first_c
  39.8 2.7 %collective-permute-done.11.second_c2.second_c = f32[12,8,128]{2,1,0:T(8,128)S(1)} collective-permute-done((f32[12,8,128]{2,1,0:T(8,128)S(1)}, f32[12,8,128]{2,1,0:T(8,128)S(1)}, u32[]{:S(2)}, u32[]{:S(2)}) %collective-permute-start.11) | collective-permute-done | bytes 49184 | tf_op jit(solution)/shard_map/ppermute | solution.py:168
  42.5 0.6 shard_map.70
  43.0 13.6 %all_to_all.5.own_half = f32[32,3,8,128]{3,2,1,0:T(8,128)S(1)} all-to-all(f32[32,3,8,128]{3,2,1,0:T(8,128)S(1)} %get-tuple-element.51), channel_id=1, replica_groups=mesh['gx'=8,'gy'=4] {'gx','gy'}, dimensions={0} | all-to-all | bytes 786432 | tf_op jit(solution)/shard_map/all_to_all | solution.py:986
  56.6 1.2 %collective-permute-start.12 = (f32[32,3,8,128]{3,2,1,0:T(8,128)S(1)}, f32[32,3,8,128]{3,2,1,0:T(8,128)S(1)}, u32[]{:S(2)}, u32[]{:S(2)}) collective-permute-start(f32[32,3,8,128]{3,2,1,0:T(8,128)S(1)} %all_to_all.5.own_half), channel_id=1, source_target_pairs={{0,4},{4,0},{8,12},{12,8},{16,20},{20,16},{24,28},{28,24},{1,5},{5... | collective-permute-start | bytes 1179656 | tf_op jit(solution)/shard_map/ppermute | solution.py:987
  57.8 0.5 shard_map.71
  58.3 0.8 %collective-permute-done.12.other_half = f32[32,3,8,128]{3,2,1,0:T(8,128)S(1)} collective-permute-done((f32[32,3,8,128]{3,2,1,0:T(8,128)S(1)}, f32[32,3,8,128]{3,2,1,0:T(8,128)S(1)}, u32[]{:S(2)}, u32[]{:S(2)}) %collective-permute-start.12) | collective-permute-done | bytes 393248 | tf_op jit(solution)/shard_map/ppermute | solution.py:987
  59.2 3.5 %shard_map.72 = f32[8,16,256]{2,1,0:T(8,128)} custom-call(f32[32,3,8,128]{3,2,1,0:T(8,128)S(1)} %all_to_all.5.own_half, f32[32,3,8,128]{3,2,1,0:T(8,128)S(1)} %collective-permute-done.12.other_half, f32[8,16,24,128]{3,2,1,0:T(8,128)S(1)} %shard_map.68.coeffs.mid_coeffs, f32[16,24,128]{2,1,0:T(8,128)S(1)} %get-tuple-element.52.goal_in, ...), custom_call_target="tpu_custom_call" | custom-call | flops 1000 | bytes 1000 | tf_op jit(solution)/shard_map/pallas_call | solution.py:890
  (1 shorter events, 0.0 us)
Async XLA Ops:
  1.7 17.4 %collective-permute-start.1 = (f32[66,8,128]{2,1,0:T(8,128)S(1)}, f32[66,8,128]{2,1,0:T(8,128)S(1)}, u32[]{:S(2)}, u32[]{:S(2)}) collective-permute-start(f32[66,8,128]{2,1,0:T(8,128)S(1)} %get-tuple-element.34), channel_id=1, source_target_pairs={{0,3},{1,0},{2,1},{3,2},{4,7},{5,4},{6,5},{7,6},{8,11},{9,8},{10,9... | collective-permute-start | bytes 811016 | tf_op jit(solution)/shard_map/ppermute | solution.py:173
  6.8 12.3 %collective-permute-start = (f32[64,8,128]{2,1,0:T(8,128)S(1)}, f32[64,8,128]{2,1,0:T(8,128)S(1)}, u32[]{:S(2)}, u32[]{:S(2)}) collective-permute-start(f32[64,8,128]{2,1,0:T(8,128)S(1)} %get-tuple-element.33), channel_id=1, source_target_pairs={{0,1},{1,2},{2,3},{3,0},{4,5},{5,6},{6,7},{7,4},{8,9},{9,10},{10,1... | collective-permute-start | bytes 786440 | tf_op jit(solution)/shard_map/ppermute | solution.py:173
  6.8 15.3 %collective-permute-start.3 = (f32[104,8,128]{2,1,0:T(8,128)S(1)}, f32[104,8,128]{2,1,0:T(8,128)S(1)}, u32[]{:S(2)}, u32[]{:S(2)}) collective-permute-start(f32[104,8,128]{2,1,0:T(8,128)S(1)} %get-tuple-element.41), channel_id=1, source_target_pairs={{0,28},{4,0},{8,4},{12,8},{16,12},{20,16},{24,20},{28,24},{1,29},{... | collective-permute-start | bytes 1277960 | tf_op jit(solution)/shard_map/ppermute | solution.py:173
  8.4 13.7 %collective-permute-start.2 = (f32[100,8,128]{2,1,0:T(8,128)S(1)}, f32[100,8,128]{2,1,0:T(8,128)S(1)}, u32[]{:S(2)}, u32[]{:S(2)}) collective-permute-start(f32[100,8,128]{2,1,0:T(8,128)S(1)} %get-tuple-element.40), channel_id=1, source_target_pairs={{0,4},{4,8},{8,12},{12,16},{16,20},{20,24},{24,28},{28,0},{1,5},{5... | collective-permute-start | bytes 1228808 | tf_op jit(solution)/shard_map/ppermute | solution.py:173
  19.1 3.0 %collective-permute-start.4 = (f32[46,8,128]{2,1,0:T(8,128)S(1)}, f32[46,8,128]{2,1,0:T(8,128)S(1)}, u32[]{:S(2)}, u32[]{:S(2)}) collective-permute-start(f32[46,8,128]{2,1,0:T(8,128)S(1)} %get-tuple-element.42), channel_id=1, source_target_pairs={{0,4},{4,0},{8,12},{12,8},{16,20},{20,16},{24,28},{28,24},{1,5},{5... | collective-permute-start | bytes 565256 | tf_op jit(solution)/shard_map/ppermute | solution.py:168
  19.2 7.4 %collective-permute-start.5 = (f32[46,8,128]{2,1,0:T(8,128)S(1)}, f32[46,8,128]{2,1,0:T(8,128)S(1)}, u32[]{:S(2)}, u32[]{:S(2)}) collective-permute-start(f32[46,8,128]{2,1,0:T(8,128)S(1)} %get-tuple-element.43), channel_id=1, source_target_pairs={{0,28},{4,8},{8,4},{12,16},{16,12},{20,24},{24,20},{28,0},{1,29},{... | collective-permute-start | bytes 565256 | tf_op jit(solution)/shard_map/ppermute | solution.py:168
  28.4 11.1 %collective-permute-start.6 = (f32[76,8,128]{2,1,0:T(8,128)S(1)}, f32[76,8,128]{2,1,0:T(8,128)S(1)}, u32[]{:S(2)}, u32[]{:S(2)}) collective-permute-start(f32[76,8,128]{2,1,0:T(8,128)S(1)} %get-tuple-element.45), channel_id=1, source_target_pairs={{0,4},{4,0},{8,12},{12,8},{16,20},{20,16},{24,28},{28,24},{1,5},{5... | collective-permute-start | bytes 933896 | tf_op jit(solution)/shard_map/ppermute | solution.py:168
  28.6 11.0 %collective-permute-start.7 = (f32[76,8,128]{2,1,0:T(8,128)S(1)}, f32[76,8,128]{2,1,0:T(8,128)S(1)}, u32[]{:S(2)}, u32[]{:S(2)}) collective-permute-start(f32[76,8,128]{2,1,0:T(8,128)S(1)} %get-tuple-element.46), channel_id=1, source_target_pairs={{0,28},{4,8},{8,4},{12,16},{16,12},{20,24},{24,20},{28,0},{1,29},{... | collective-permute-start | bytes 933896 | tf_op jit(solution)/shard_map/ppermute | solution.py:168
  30.3 4.1 %collective-permute-start.8 = (f32[12,8,128]{2,1,0:T(8,128)S(1)}, f32[12,8,128]{2,1,0:T(8,128)S(1)}, u32[]{:S(2)}, u32[]{:S(2)}) collective-permute-start(f32[12,8,128]{2,1,0:T(8,128)S(1)} %get-tuple-element.47), channel_id=1, source_target_pairs={{0,1},{1,0},{2,3},{3,2},{4,5},{5,4},{6,7},{7,6},{8,9},{9,8},{10,11... | collective-permute-start | bytes 147464 | tf_op jit(solution)/shard_map/ppermute | solution.py:168
  31.9 5.9 %collective-permute-start.9 = (f32[12,8,128]{2,1,0:T(8,128)S(1)}, f32[12,8,128]{2,1,0:T(8,128)S(1)}, u32[]{:S(2)}, u32[]{:S(2)}) collective-permute-start(f32[12,8,128]{2,1,0:T(8,128)S(1)} %get-tuple-element.48), channel_id=1, source_target_pairs={{0,3},{1,2},{2,1},{3,0},{4,7},{5,6},{6,5},{7,4},{8,11},{9,10},{10,... | collective-permute-start | bytes 147464 | tf_op jit(solution)/shard_map/ppermute | solution.py:168
  37.8 2.0 %collective-permute-start.10 = (f32[12,8,128]{2,1,0:T(8,128)S(1)}, f32[12,8,128]{2,1,0:T(8,128)S(1)}, u32[]{:S(2)}, u32[]{:S(2)}) collective-permute-start(f32[12,8,128]{2,1,0:T(8,128)S(1)} %get-tuple-element.49), channel_id=1, source_target_pairs={{0,4},{4,0},{8,12},{12,8},{16,20},{20,16},{24,28},{28,24},{1,5},{5... | collective-permute-start | bytes 147464 | tf_op jit(solution)/shard_map/ppermute | solution.py:168
  37.9 4.6 %collective-permute-start.11 = (f32[12,8,128]{2,1,0:T(8,128)S(1)}, f32[12,8,128]{2,1,0:T(8,128)S(1)}, u32[]{:S(2)}, u32[]{:S(2)}) collective-permute-start(f32[12,8,128]{2,1,0:T(8,128)S(1)} %get-tuple-element.50), channel_id=1, source_target_pairs={{0,28},{4,8},{8,4},{12,16},{16,12},{20,24},{24,20},{28,0},{1,29},{... | collective-permute-start | bytes 147464 | tf_op jit(solution)/shard_map/ppermute | solution.py:168
  56.6 2.5 %collective-permute-start.12 = (f32[32,3,8,128]{3,2,1,0:T(8,128)S(1)}, f32[32,3,8,128]{3,2,1,0:T(8,128)S(1)}, u32[]{:S(2)}, u32[]{:S(2)}) collective-permute-start(f32[32,3,8,128]{3,2,1,0:T(8,128)S(1)} %all_to_all.5.own_half), channel_id=1, source_target_pairs={{0,4},{4,0},{8,12},{12,8},{16,20},{20,16},{24,28},{28,24},{1,5},{5... | collective-permute-start | bytes 1179656 | tf_op jit(solution)/shard_map/ppermute | solution.py:987

commit v6 on v5

--- a/solution.py
+++ b/solution.py
@@ -165,7 +165,10 @@
 def swapped(first, second, axis):
     count = lax.axis_size(axis)
     outer = [(i, (i + 1 if i % 2 else i - 1) % count) for i in range(count)]
-    return lax.ppermute(first, axis, [(i, i ^ 1) for i in range(count)]), lax.ppermute(second, axis, outer)
+    inner = [(i, i ^ 1) for i in range(count)]
+    if axis == "gy":
+        inner, outer = outer, inner
+    return lax.ppermute(first, axis, inner), lax.ppermute(second, axis, outer)
 
 
 def shifted(value, axis, step):
@@ -206,9 +209,8 @@
         return lanes_merge(tile, tile, lane_pairs)
 
     left = iota(TILE, 1) < TILE[1] // 2
-    low[0] = jnp.where(left, 0.0, coarser(0, 2) * 0.125)
-    low[1] = jnp.where(left, coarser(1, 1), coarser(2, 2, row_pairs=False)) * 0.25
-    low[2] = jnp.where(left, coarser(3, 2, lane_pairs=False) * 0.25, 0.0)
+    low[0] = jnp.where(left, coarser(2, 2, row_pairs=False), coarser(3, 2, lane_pairs=False)) * 0.25
+    low[1] = jnp.where(left, coarser(0, 2) * 0.125, coarser(1, 1) * 0.25)
 
     tops, bottoms = Writer(up_x), Writer(down_x)
     for ref, count in zip(fields, UP_PLANES):
@@ -229,7 +231,7 @@
     bottoms_y.put(ini[:, 4, :])
     bottoms_y.put(face_y[:, 4, :])
     for writer in (tops_y, bottoms_y):
-        for tile in (1, 2):
+        for tile in range(2):
             writer.put(low[tile])
     row, upper = iota(TILE, 0), is_upper(TILE[1])
     for array in range(4):
@@ -299,7 +301,7 @@
             )
         for array, plane in wanted:
             writer.put(mid[array * mid_x + plane])
-        for tiles in ((low_faces[1], low_faces[2]), low_tiles_of(low_y), low_tiles_of(high_y)):
+        for tiles in ((low_faces[0], low_faces[1]), low_tiles_of(low_y), low_tiles_of(high_y)):
             for tile in tiles:
                 writer.put(tile)
     send(first, second, place[0] % 2 == 0, tops, bottoms)
@@ -543,7 +545,7 @@
         for tile in range(corners.shape[0] - PASSED - 10, corners.shape[0]):
             writer.put(corners[tile])
     send(first_x, second_x, even, tops, bottoms)
-    send(first_y, second_y, place[1] % 2 == 0, tops_y, bottoms_y)
+    send(first_y, second_y, place[1] % 2 == 1, tops_y, bottoms_y)
 
 
 MID_CORNER = 24
@@ -561,7 +563,7 @@
 def corner_two_kernel(size_x, size_z, first_y, second_y, first, second):
     place = here()
     upper = is_upper(size_z)
-    low_y, high_y = got(first_y, second_y, place[1] % 2 == 0)
+    low_y, high_y = got(first_y, second_y, place[1] % 2 == 1)
     tops, bottoms = Tiles(), Tiles()
     put_corners(tops, low_y, high_y, [size_x - 1, size_x - 2, size_x - 3], upper, 0)
     put_corners(bottoms, low_y, high_y, range(3), upper, 0)
@@ -572,9 +574,24 @@
     send(first, second, place[0] % 2 == 0, tops, bottoms)
 
 
-def mid_coeffs_kernel(mid, low_y, high_y, first_x2, second_x2, coeffs, window):
+def level_two_near(near, low, low_y, high_y, low_c, high_c, low_x2, high_x2):
+    known = {(0, 0): (low[0], low[1]), (0, -1): low_tiles_of(low_y), (0, 1): low_tiles_of(high_y)}
+    for step, ref, distance in ((-1, low_c, 1), (1, high_c, 1), (-1, low_x2, 2), (1, high_x2, 2)):
+        start = ref.shape[0] - PASSED
+        for at, dy in enumerate((0, -1, 1)):
+            known[step * distance, dy] = (ref[start + 2 * at], ref[start + 2 * at + 1])
+    for (dx, dy), tiles in known.items():
+        for kind in range(2):
+            near[((dx + 2) * 3 + dy + 1) * 2 + kind] = tiles[kind]
+
+
+def mid_coeffs_kernel(
+    mid, low, low_y, high_y, first_c, second_c, first_x2, second_x2, coeffs, near, window
+):
     place = here()
     low_x2, high_x2 = got(first_x2, second_x2, place[0] % 2 == 0)
+    low_c, high_c = got(first_c, second_c, place[0] % 2 == 0)
+    level_two_near(near, low, low_y, high_y, low_c, high_c, low_x2, high_x2)
     mid_y, mid_z = mid.shape[1:]
     mid_x = mid.shape[0] // 4
     mids = 4 * mid_x
@@ -619,7 +636,7 @@
     place = here()
     even = place[0] % 2 == 0
     low_x2, high_x2 = got(first_x2, second_x2, even)
-    low_y2, high_y2 = got(first_y2, second_y2, place[1] % 2 == 0)
+    low_y2, high_y2 = got(first_y2, second_y2, place[1] % 2 == 1)
     low_c2, high_c2 = got(first_c2, second_c2, even)
     blocks = {
         (0, 0): (low_c2, low_c2.shape[0] - 2 * mid_x), (0, 1): (low_x2, fine_tiles),
@@ -656,39 +673,51 @@
         parts.append(total)
     coarse = rows_merge(*parts)
     coarse = lanes_merge(coarse, coarse) * 0.125
-    tiles = (jnp.where(iota(TILE, 1) < TILE[1] // 2, coarse, low[0]), low[1], low[2])
+    left = iota(TILE, 1) < TILE[1] // 2
     x1 = [iterate[MID + plane, mid_y : 2 * mid_y] for plane in range(mid_x)]
+    low_one, low_two = low[0], low[1]
     pairs = count_x // 2
     own = place[0] // 2
     above, below = lax.rem(own + 1, pairs), lax.rem(own + pairs - 1, pairs)
+    odd = jnp.logical_not(even)
 
     def fill(i, carry):
         up, down = i == above, i == below
         edge = jnp.where(up, mid_target[mid_x - 1], mid_target[0])
+        edge_left, edge_right = jnp.where(left, coarse, roll(edge, TILE[1] // 2, 1)), jnp.where(left, coarse, edge)
         near_pair = up | down | (i == own)
-        far_side = (up & even) | (down & jnp.logical_not(even))
         for j in range(count_y):
             me = place[1]
             beside = (j == me) | (j == lax.rem(me + 1, count_y)) | (j == lax.rem(me + count_y - 1, count_y))
-            near, side = near_pair & beside, far_side & beside
+            far = jnp.logical_not(near_pair & beside)
             one, two = 2 * i * count_y + j, (2 * i + 1) * count_y + j
-            slots[one, 0] = tiles[0]
-            slots[one, 1] = jnp.where(near, edge, tiles[1])
-            slots[one, 2] = jnp.where(near, jnp.where(side & even, x1[2], x1[0]), tiles[2])
-            slots[two, 0] = jnp.where(near, jnp.where(side, tiles[1], x1[1]), tiles[0])
-            slots[two, 1] = jnp.where(near, jnp.where(side, tiles[2], x1[2]), tiles[1])
-            slots[two, 2] = jnp.where(
-                near, jnp.where(side & jnp.logical_not(even), x1[1], x1[3]), tiles[2]
-            )
+            slots[one, 0] = edge_left
+            slots[two, 0] = edge_right
+            for at, tile in ((1, low_one), (2, low_two)):
+                slots[one, at] = jnp.where(far | (down & odd), tile, jnp.where(up & even, x1[at + 1], x1[at - 1]))
+                slots[two, at] = jnp.where(far | (up & even), tile, jnp.where(down & odd, x1[at - 1], x1[at + 1]))
         return carry
 
     each(0, pairs, fill)
 
 
-def solve_low(count_x, count_y, gathered, fields, coeffs, iterate, update):
+def low_kernel(count_x, count_y, own_half, near, iterate, gathered, fields, coeffs, update):
     size_x, size_y, lanes = iterate.shape
     low_x, low_y = size_x // count_x, size_y // count_y
     low_z = lanes // 2
+    me_x, me_y = here()
+
+    def take_all(i, carry):
+        for kind in range(3):
+            gathered[i, kind] = own_half[i, kind]
+        return carry
+
+    each(0, count_x * count_y, take_all)
+    for dy in (-1, 0, 1):
+        for dx in range(-2, 3):
+            source = lax.rem(me_x + dx + count_x, count_x) * count_y + lax.rem(me_y + dy + count_y, count_y)
+            for kind in range(2):
+                gathered[source, 1 + kind] = near[((dx + 2) * 3 + dy + 1) * 2 + kind]
 
     def place(i, carry):
         for j in range(count_y):
@@ -712,13 +741,11 @@
         return jnp.where(i == size_x - 1, 0, i + 1)
 
     def prepare(i, carry):
-        first, second, third = fields[0, i], fields[1, i], fields[2, i]
-        xl, xh = second, fields[1, following(i)]
-        yl = roll(second, low_z, 1)
+        yl, xl = fields[1, i], roll(fields[2, i], low_z, 1)
+        zl, xh = roll(fields[1, i], low_z, 1), roll(fields[2, following(i)], low_z, 1)
         yh = roll(yl, -1, 0)
-        zl = third
-        zh = jnp.where(lane == low_z - 1, 0.0, roll(third, -1, 1))
-        diag = roll(first, low_z, 1) + scale * (xl + xh + yl + yh + zl + zh)
+        zh = jnp.where(lane == low_z - 1, 0.0, roll(zl, -1, 1))
+        diag = fields[2, i] + scale * (xl + xh + yl + yh + zl + zh)
         inverse = jnp.where(inside, 1.0 / diag, 0.0)
         scaled = scale * inverse
         coeffs[0, i] = scaled * xl
@@ -727,7 +754,7 @@
         coeffs[3, i] = scaled * yh
         coeffs[4, i] = jnp.where(lane == 0, 0.0, scaled * zl)
         coeffs[5, i] = scaled * zh
-        goal = first * inverse
+        goal = jnp.where(inside, fields[0, i], 0.0) * inverse
         coeffs[6, i] = goal
         update[i] = weights[0][1] * goal
         iterate[i] = weights[0][1] * goal
@@ -754,22 +781,14 @@
 def window_kernel(
     fields_own, low_x1, high_x1, low_y1, high_y1, first_c1, second_c1,
     own, first_x, second_x, first_y, second_y, first_c, second_c,
-    low, window, coeffs, near, own_windows, side_windows,
+    window, coeffs, own_windows, side_windows,
 ):
     place = here()
     even = place[0] % 2 == 0
     low_c1, high_c1 = got(first_c1, second_c1, even)
     low_x, high_x = got(first_x, second_x, even)
-    low_y, high_y = got(first_y, second_y, place[1] % 2 == 0)
+    low_y, high_y = got(first_y, second_y, place[1] % 2 == 1)
     low_c, high_c = got(first_c, second_c, even)
-    known = {(0, 0): (low[1], low[2]), (0, -1): low_tiles_of(low_y1), (0, 1): low_tiles_of(high_y1)}
-    for step, ref, distance in ((-1, low_c1, 1), (1, high_c1, 1), (-1, low_x, 2), (1, high_x, 2)):
-        start = ref.shape[0] - PASSED
-        for at, dy in enumerate((0, -1, 1)):
-            known[step * distance, dy] = (ref[start + 2 * at], ref[start + 2 * at + 1])
-    for (dx, dy), tiles in known.items():
-        for kind in range(2):
-            near[((dx + 2) * 3 + dy + 1) * 2 + kind] = tiles[kind]
     size_x, size_y, size_z = own.shape
     assemble_owns(own_windows, fields_own, low_y1, high_y1)
     assemble_sides(side_windows, (size_y, size_z), low_x1, high_x1, low_c1, high_c1)
@@ -785,9 +804,8 @@
 
 
 def last_kernel(
-    count_x, count_y, own_half, other_half, mid_coeffs, goal_in, fine_coeffs, window, near,
+    count_x, count_y, own_half, other_half, low_iterate, mid_coeffs, goal_in, fine_coeffs, window,
     out,
-    gathered, low_fields, low_coeffs, low_iterate, low_update,
     goal, mid_iterate, mid_update,
     iterate, update,
 ):
@@ -805,38 +823,17 @@
     def device(dx, dy):
         return lax.rem(me_x + dx + count_x, count_x) * count_y + lax.rem(me_y + dy + count_y, count_y)
 
-    def take(i, carry):
-        for kind in range(3):
-            gathered[i, kind] = half(0, i, kind)
-        return carry
-
-    each(0, count_x * count_y, take)
-    side = me_x % 2
-    for dy in (-1, 0, 1):
-        for source in (device(-2 - side, dy), device(3 - side, dy)):
-            for kind in range(2):
-                gathered[source, 1 + kind] = half(1, source, kind)
-    for dy in (-1, 0, 1):
-        for dx in range(-2, 3):
-            for kind in range(2):
-                gathered[device(dx, dy), 1 + kind] = near[((dx + 2) * 3 + dy + 1) * 2 + kind]
-    solve_low(count_x, count_y, gathered, low_fields, low_coeffs, low_iterate, low_update)
-
     first, far = MID - mid_x, MID + 2 * mid_x
     for dy in (-1, 0, 1):
         rows = slice((dy + 1) * mid_y, (dy + 2) * mid_y)
         for dx in (-1, 0, 1):
             source = device(dx, dy)
             start = MID + dx * mid_x
-            mid_iterate[start, rows] = half(0, source, 2)
-            for plane in range(1, mid_x):
-                mid_iterate[start + plane, rows] = half(1, source, plane - 1)
-        source = device(-2, dy)
-        mid_iterate[0, rows] = jnp.where(even, half(0, source, 2), half(1, source, 1))
-        mid_iterate[1, rows] = half(1, source, 2)
-        source = device(2, dy)
-        mid_iterate[far, rows] = half(0, source, 2)
-        mid_iterate[far + 1, rows] = jnp.where(even, half(1, source, 0), half(1, source, 2))
+            for plane in range(mid_x):
+                mid_iterate[start + plane, rows] = half(plane // 2, source, 1 + plane % 2)
+        for plane in range(2):
+            mid_iterate[plane, rows] = own_half[device(-2, dy), 1 + plane]
+            mid_iterate[far + plane, rows] = own_half[device(2, dy), 1 + plane]
     low_size_x, low_size_y = low_iterate.shape[:2]
     low_y = mid_y // 2
     turn = lax.rem(low_size_y - me_y * low_y + low_y, low_size_y)
@@ -848,12 +845,15 @@
         mid_iterate[2 * plane] += part
         mid_iterate[2 * plane + 1] += part
 
+    left = iota(TILE, 1) < TILE[1] // 2
     for plane in range(first, far):
         goal[plane] = goal_in[plane]
     for dy in (-1, 0, 1):
         rows = slice((dy + 1) * mid_y, (dy + 2) * mid_y)
         for plane, dx in ((first - 1, -2), (far, 2)):
-            goal[plane, rows] = half(0, device(dx, dy), 1) * mid_coeffs[6, plane, rows]
+            source = device(dx, dy)
+            edge = jnp.where(left, roll(half(0, source, 0), TILE[1] // 2, 1), half(1, source, 0))
+            goal[plane, rows] = edge * mid_coeffs[6, plane, rows]
     for sweep, pair in enumerate(chebyshev_weights(SWEEPS)):
         sweep_window(
             mid_iterate, mid_update, mid_coeffs, (first - 1 + sweep, far + 1 - sweep), pair, sweep == 0, goal
@@ -926,7 +926,7 @@
             tiles((6 * pairs + 1) * strip + 2 + 4 * STRIP),
             tiles((6 * pairs + 2) * strip + 2 + 4 * STRIP),
             tiles(mids),
-            tiles(3),
+            tiles(2),
             (6,) + source.shape,
         ],
         far_in=range(6),
@@ -971,10 +971,10 @@
     first_c2, second_c2 = swapped(first_c2, second_c2, "gx")
 
     mid_wide = (mid_x + 2 * MID, 3 * mid_y, mid_z)
-    (mid_coeffs,) = call(
+    mid_coeffs, near = call(
         mid_coeffs_kernel,
-        (mid, low_y1, high_y1, first_x2, second_x2),
-        [(8,) + mid_wide],
+        (mid, low, low_y1, high_y1, first_c1, second_c1, first_x2, second_x2),
+        [(8,) + mid_wide, tiles(30)],
         [(4,) + mid_wide],
     )
     goal, slots = call(
@@ -986,20 +986,25 @@
     own_half = lax.all_to_all(slots, ("gx", "gy"), 0, 0)
     other_half = lax.ppermute(own_half, "gx", [(i, i ^ 1) for i in range(count_x)])
 
-    window, coeffs, near = call(
+    window, coeffs = call(
         window_kernel,
         (own, low_x1, high_x1, low_y1, high_y1, first_c1, second_c1)
-        + (iterate, first_x2, second_x2, first_y2, second_y2, first_c2, second_c2, low),
-        [wide, (7, wide[0] - 4) + tall, tiles(30)],
+        + (iterate, first_x2, second_x2, first_y2, second_y2, first_c2, second_c2),
+        [wide, (7, wide[0] - 4) + tall],
         [(6, size_x) + tall, (6, 2 * FINE) + tall],
     )
     low_wide = (low_x * count_x, low_y * count_y, mid_z)
+    (low_iterate,) = call(
+        functools.partial(low_kernel, count_x, count_y),
+        (own_half, near),
+        [low_wide],
+        [(devices, 3) + TILE, (3,) + low_wide, (7,) + low_wide, low_wide],
+    )
     (result,) = call(
         functools.partial(last_kernel, count_x, count_y),
-        (own_half, other_half, mid_coeffs, goal, coeffs, window, near),
+        (own_half, other_half, low_iterate, mid_coeffs, goal, coeffs, window),
         [source.shape],
-        [(devices, 3) + TILE, (3,) + low_wide, (7,) + low_wide, low_wide, low_wide]
-        + [mid_wide, mid_wide, mid_wide]
+        [mid_wide, mid_wide, mid_wide]
         + [wide, wide],
     )
     return result

time: 62.8 us -> 62.1 us (0.989)
  waiting for transfers between devices: 23.9 us -> 22.8 us
  blocking collectives: 13.6 us -> 14.5 us
    all_to_all x1, blocking collectives: 13.6 us -> 14.5 us  [local(): own_half = lax.all_to_all(slots, ('gx', 'gy'), 0, 0)]
    ppermute x1, waiting for transfers between devices: 0.83 us -> 0.01 us  [local(): lax.ppermute(own_half, 'gx', [(i, i ^ 1) for i in range(count_x)])]
    pallas_call x9 -> x10, Pallas kernels: 8.68 us -> 8.8 us  [call(): pl.pallas_call(kernel, out_shape=[pltpu.HBM(shape, F32) if i in far_out e...]
  transfers between devices with their start and end apart: 13 -> 13, of which waited for: 6 -> 5; matrix products, arithmetic and copies ran while one was open for 0% -> 0% of each run, Pallas kernels for 2% -> 4%
where the time goes in v6:
time: 62.1 us; the launch traced here: 61.9 us
  waiting for transfers between devices  22.8 us (37%)
  starting transfers between devices  15.7 us (25%)
  blocking collectives  14.5 us (23%)
  Pallas kernels  8.8 us (14%)
    all_to_all x1, blocking collectives, local(): own_half = lax.all_to_all(slots, ('gx', 'gy'), 0, 0)  14.5 us
    ppermute x8, waiting for transfers between devices, swapped(): return (lax.ppermute(first, axis, inner), lax.ppermute(second, axis, outer))  12.1 us
    ppermute x4, waiting for transfers between devices, shifted(): lax.ppermute(value, axis, [(i, (i + step) % count) for i in range(count)])  10.7 us
    pallas_call x10, Pallas kernels, call(): pl.pallas_call(kernel, out_shape=[pltpu.HBM(shape, F32) if i in far_out e...  8.8 us
    ppermute x8, starting transfers between devices, swapped(): return (lax.ppermute(first, axis, inner), lax.ppermute(second, axis, outer))  7.84 us
    ppermute x4, starting transfers between devices, shifted(): lax.ppermute(value, axis, [(i, (i + step) % count) for i in range(count)])  6.71 us
  transfers between devices with their start and end apart: 13, of which 5 were waited for; matrix products, arithmetic and copies ran while one was open for 0% of the time, Pallas kernels for 4%

profile of v6, /device:TPU:0, one launch (start us, length us, event | category | flops | bytes accessed | tf_op | source)
XLA Modules:
  0.0 61.9 jit_solution(13655294733165638456)
XLA Ops:
  0.0 1.6 %shard_map.64 = (f32[100,8,128]{2,1,0:T(8,128)S(1)}, f32[104,8,128]{2,1,0:T(8,128)S(1)}, f32[64,8,128]{2,1,0:T(8,128)S(1)}, f32[66,8,128]{2,1,0:T(8,128)S(1)}, f...) custom-call(f32[8,16,256]{2,1,0:T(8,128)} %ini_in.1, f32[8,16,256]{2,1,0:T(8,128)} %src_in.1, ...), custom_call_target="tpu_custom_call" | custom-call | flops 1000 | bytes 1000 | tf_op jit(solution)/shard_map/pallas_call | solution.py:890
  1.7 5.1 %collective-permute-start.1 = (f32[66,8,128]{2,1,0:T(8,128)S(1)}, f32[66,8,128]{2,1,0:T(8,128)S(1)}, u32[]{:S(2)}, u32[]{:S(2)}) collective-permute-start(f32[66,8,128]{2,1,0:T(8,128)S(1)} %get-tuple-element.35), channel_id=1, source_target_pairs={{0,3},{1,0},{2,1},{3,2},{4,7},{5,4},{6,5},{7,6},{8,11},{9,8},{10,9... | collective-permute-start | bytes 811016 | tf_op jit(solution)/shard_map/ppermute | solution.py:176
  6.8 0.0 collective-permute-start
  6.8 1.6 %collective-permute-start.3 = (f32[104,8,128]{2,1,0:T(8,128)S(1)}, f32[104,8,128]{2,1,0:T(8,128)S(1)}, u32[]{:S(2)}, u32[]{:S(2)}) collective-permute-start(f32[104,8,128]{2,1,0:T(8,128)S(1)} %get-tuple-element.42), channel_id=1, source_target_pairs={{0,28},{4,0},{8,4},{12,8},{16,12},{20,16},{24,20},{28,24},{1,29},{... | collective-permute-start | bytes 1277960 | tf_op jit(solution)/shard_map/ppermute | solution.py:176
  8.4 0.0 collective-permute-start.2
  8.4 10.6 %collective-permute-done.low_y.low_y1 = f32[64,8,128]{2,1,0:T(8,128)S(1)} collective-permute-done((f32[64,8,128]{2,1,0:T(8,128)S(1)}, f32[64,8,128]{2,1,0:T(8,128)S(1)}, u32[]{:S(2)}, u32[]{:S(2)}) %collective-permute-start) | collective-permute-done | bytes 262176 | tf_op jit(solution)/shard_map/ppermute | solution.py:176
  19.0 0.0 collective-permute-done.1.high_y.high_y1
  19.0 0.1 shard_map.66
  19.1 0.1 collective-permute-start.4
  19.2 2.5 %collective-permute-start.5 = (f32[46,8,128]{2,1,0:T(8,128)S(1)}, f32[46,8,128]{2,1,0:T(8,128)S(1)}, u32[]{:S(2)}, u32[]{:S(2)}) collective-permute-start(f32[46,8,128]{2,1,0:T(8,128)S(1)} %get-tuple-element.44), channel_id=1, source_target_pairs={{0,28},{4,8},{8,4},{12,16},{16,12},{20,24},{24,20},{28,0},{1,29},{... | collective-permute-start | bytes 565256 | tf_op jit(solution)/shard_map/ppermute | solution.py:171
  21.7 0.3 shard_map.65
  22.0 0.0 collective-permute-done.2.low_x.low_x1
  22.1 0.0 collective-permute-done.3.high_x.high_x1
  22.1 0.0 collective-permute-done.4.first_c.first_c1
  22.1 4.5 %collective-permute-done.5.second_c.second_c1 = f32[46,8,128]{2,1,0:T(8,128)S(1)} collective-permute-done((f32[46,8,128]{2,1,0:T(8,128)S(1)}, f32[46,8,128]{2,1,0:T(8,128)S(1)}, u32[]{:S(2)}, u32[]{:S(2)}) %collective-permute-start.5) | collective-permute-done | bytes 188448 | tf_op jit(solution)/shard_map/ppermute | solution.py:171
  26.5 1.9 %shard_map.67 = (f32[8,16,256]{2,1,0:T(8,128)S(1)}, f32[4,8,128]{2,1,0:T(8,128)S(1)}, f32[76,8,128]{2,1,0:T(8,128)S(1)}, f32[76,8,128]{2,1,0:T(8,128)S(1)}, f32[...) custom-call(f32[6,8,32,256]{3,2,1,0:T(8,128)S(1)} %get-tuple-element.36.own_windows, ...), custom_call_target="tpu_custom_call" | custom-call | flops 1000 | bytes 1000 | tf_op jit(solution)/shard_map/pallas_call | solution.py:890
  28.4 0.1 collective-permute-start.6
  28.6 1.7 %collective-permute-start.7 = (f32[76,8,128]{2,1,0:T(8,128)S(1)}, f32[76,8,128]{2,1,0:T(8,128)S(1)}, u32[]{:S(2)}, u32[]{:S(2)}) collective-permute-start(f32[76,8,128]{2,1,0:T(8,128)S(1)} %get-tuple-element.47), channel_id=1, source_target_pairs={{0,28},{4,8},{8,4},{12,16},{16,12},{20,24},{24,20},{28,0},{1,29},{... | collective-permute-start | bytes 933896 | tf_op jit(solution)/shard_map/ppermute | solution.py:171
  30.3 1.7 %collective-permute-start.8 = (f32[12,8,128]{2,1,0:T(8,128)S(1)}, f32[12,8,128]{2,1,0:T(8,128)S(1)}, u32[]{:S(2)}, u32[]{:S(2)}) collective-permute-start(f32[12,8,128]{2,1,0:T(8,128)S(1)} %get-tuple-element.49), channel_id=1, source_target_pairs={{0,3},{1,2},{2,1},{3,0},{4,7},{5,6},{6,5},{7,4},{8,11},{9,10},{10,... | collective-permute-start | bytes 147464 | tf_op jit(solution)/shard_map/ppermute | solution.py:171
  32.0 0.0 collective-permute-start.9
  32.0 4.5 %collective-permute-done.8.first_y.first_y2 = f32[12,8,128]{2,1,0:T(8,128)S(1)} collective-permute-done((f32[12,8,128]{2,1,0:T(8,128)S(1)}, f32[12,8,128]{2,1,0:T(8,128)S(1)}, u32[]{:S(2)}, u32[]{:S(2)}) %collective-permute-start.8) | collective-permute-done | bytes 49184 | tf_op jit(solution)/shard_map/ppermute | solution.py:171
  36.5 0.2 collective-permute-done.9.second_y.second_y2
  36.7 0.1 collective-permute-start.10
  36.8 1.6 %collective-permute-start.11 = (f32[12,8,128]{2,1,0:T(8,128)S(1)}, f32[12,8,128]{2,1,0:T(8,128)S(1)}, u32[]{:S(2)}, u32[]{:S(2)}) collective-permute-start(f32[12,8,128]{2,1,0:T(8,128)S(1)} %get-tuple-element.52), channel_id=1, source_target_pairs={{0,28},{4,8},{8,4},{12,16},{16,12},{20,24},{24,20},{28,0},{1,29},{... | collective-permute-start | bytes 147464 | tf_op jit(solution)/shard_map/ppermute | solution.py:171
  38.4 0.0 collective-permute-done.6.first_x2.first_x
  38.4 0.0 collective-permute-done.7.second_x2.second_x
  38.4 0.2 shard_map.68
  38.6 0.0 collective-permute-done.10.first_c2.first_c
  38.6 2.9 %collective-permute-done.11.second_c2.second_c = f32[12,8,128]{2,1,0:T(8,128)S(1)} collective-permute-done((f32[12,8,128]{2,1,0:T(8,128)S(1)}, f32[12,8,128]{2,1,0:T(8,128)S(1)}, u32[]{:S(2)}, u32[]{:S(2)}) %collective-permute-start.11) | collective-permute-done | bytes 49184 | tf_op jit(solution)/shard_map/ppermute | solution.py:171
  41.5 0.5 shard_map.70
  42.0 14.5 %all_to_all.5.own_half = f32[32,3,8,128]{3,2,1,0:T(8,128)S(1)} all-to-all(f32[32,3,8,128]{3,2,1,0:T(8,128)S(1)} %get-tuple-element.53), channel_id=1, replica_groups=mesh['gx'=8,'gy'=4] {'gx','gy'}, dimensions={0} | all-to-all | bytes 786432 | tf_op jit(solution)/shard_map/all_to_all | solution.py:986
  56.6 1.2 %collective-permute-start.12 = (f32[32,3,8,128]{3,2,1,0:T(8,128)S(1)}, f32[32,3,8,128]{3,2,1,0:T(8,128)S(1)}, u32[]{:S(2)}, u32[]{:S(2)}) collective-permute-start(f32[32,3,8,128]{3,2,1,0:T(8,128)S(1)} %all_to_all.5.own_half), channel_id=1, source_target_pairs={{0,4},{4,0},{8,12},{12,8},{16,20},{20,16},{24,28},{28,24},{1,5},{5... | collective-permute-start | bytes 1179656 | tf_op jit(solution)/shard_map/ppermute | solution.py:987
  57.7 0.5 shard_map.72
  58.2 1.3 %shard_map.71.low_iterate = f32[16,16,128]{2,1,0:T(8,128)S(1)} custom-call(f32[32,3,8,128]{3,2,1,0:T(8,128)S(1)} %all_to_all.5.own_half, f32[30,8,128]{2,1,0:T(8,128)S(1)} %get-tuple-element.54.near), custom_call_target="tpu_custom_call" | custom-call | flops 1000 | bytes 1000 | tf_op jit(solution)/shard_map/pallas_call | solution.py:890
  59.6 0.0 collective-permute-done.12.other_half
  59.6 2.4 %shard_map.73 = f32[8,16,256]{2,1,0:T(8,128)} custom-call(f32[32,3,8,128]{3,2,1,0:T(8,128)S(1)} %all_to_all.5.own_half, f32[32,3,8,128]{3,2,1,0:T(8,128)S(1)} %collective-permute-done.12.other_half, f32[16,16,128]{2,1,0:T(8,128)S(1)} %shard_map.71.low_iterate, f32[8,16,24,128]{3,2,1,0:T(8,128)S(1)} %get-tuple-element.48.coeffs.mid_coeffs, ...), custom_call_target="tpu_custom_call" | custom-call | flops 1000 | bytes 1000 | tf_op jit(solution)/shard_map/pallas_call | solution.py:890
  (1 shorter events, 0.0 us)
Async XLA Ops:
  1.7 17.4 %collective-permute-start.1 = (f32[66,8,128]{2,1,0:T(8,128)S(1)}, f32[66,8,128]{2,1,0:T(8,128)S(1)}, u32[]{:S(2)}, u32[]{:S(2)}) collective-permute-start(f32[66,8,128]{2,1,0:T(8,128)S(1)} %get-tuple-element.35), channel_id=1, source_target_pairs={{0,3},{1,0},{2,1},{3,2},{4,7},{5,4},{6,5},{7,6},{8,11},{9,8},{10,9... | collective-permute-start | bytes 811016 | tf_op jit(solution)/shard_map/ppermute | solution.py:176
  6.8 12.3 %collective-permute-start = (f32[64,8,128]{2,1,0:T(8,128)S(1)}, f32[64,8,128]{2,1,0:T(8,128)S(1)}, u32[]{:S(2)}, u32[]{:S(2)}) collective-permute-start(f32[64,8,128]{2,1,0:T(8,128)S(1)} %get-tuple-element.34), channel_id=1, source_target_pairs={{0,1},{1,2},{2,3},{3,0},{4,5},{5,6},{6,7},{7,4},{8,9},{9,10},{10,1... | collective-permute-start | bytes 786440 | tf_op jit(solution)/shard_map/ppermute | solution.py:176
  6.8 15.3 %collective-permute-start.3 = (f32[104,8,128]{2,1,0:T(8,128)S(1)}, f32[104,8,128]{2,1,0:T(8,128)S(1)}, u32[]{:S(2)}, u32[]{:S(2)}) collective-permute-start(f32[104,8,128]{2,1,0:T(8,128)S(1)} %get-tuple-element.42), channel_id=1, source_target_pairs={{0,28},{4,0},{8,4},{12,8},{16,12},{20,16},{24,20},{28,24},{1,29},{... | collective-permute-start | bytes 1277960 | tf_op jit(solution)/shard_map/ppermute | solution.py:176
  8.4 13.7 %collective-permute-start.2 = (f32[100,8,128]{2,1,0:T(8,128)S(1)}, f32[100,8,128]{2,1,0:T(8,128)S(1)}, u32[]{:S(2)}, u32[]{:S(2)}) collective-permute-start(f32[100,8,128]{2,1,0:T(8,128)S(1)} %get-tuple-element.41), channel_id=1, source_target_pairs={{0,4},{4,8},{8,12},{12,16},{16,20},{20,24},{24,28},{28,0},{1,5},{5... | collective-permute-start | bytes 1228808 | tf_op jit(solution)/shard_map/ppermute | solution.py:176
  19.1 3.0 %collective-permute-start.4 = (f32[46,8,128]{2,1,0:T(8,128)S(1)}, f32[46,8,128]{2,1,0:T(8,128)S(1)}, u32[]{:S(2)}, u32[]{:S(2)}) collective-permute-start(f32[46,8,128]{2,1,0:T(8,128)S(1)} %get-tuple-element.43), channel_id=1, source_target_pairs={{0,4},{4,0},{8,12},{12,8},{16,20},{20,16},{24,28},{28,24},{1,5},{5... | collective-permute-start | bytes 565256 | tf_op jit(solution)/shard_map/ppermute | solution.py:171
  19.2 7.4 %collective-permute-start.5 = (f32[46,8,128]{2,1,0:T(8,128)S(1)}, f32[46,8,128]{2,1,0:T(8,128)S(1)}, u32[]{:S(2)}, u32[]{:S(2)}) collective-permute-start(f32[46,8,128]{2,1,0:T(8,128)S(1)} %get-tuple-element.44), channel_id=1, source_target_pairs={{0,28},{4,8},{8,4},{12,16},{16,12},{20,24},{24,20},{28,0},{1,29},{... | collective-permute-start | bytes 565256 | tf_op jit(solution)/shard_map/ppermute | solution.py:171
  28.4 10.0 %collective-permute-start.6 = (f32[76,8,128]{2,1,0:T(8,128)S(1)}, f32[76,8,128]{2,1,0:T(8,128)S(1)}, u32[]{:S(2)}, u32[]{:S(2)}) collective-permute-start(f32[76,8,128]{2,1,0:T(8,128)S(1)} %get-tuple-element.46), channel_id=1, source_target_pairs={{0,4},{4,0},{8,12},{12,8},{16,20},{20,16},{24,28},{28,24},{1,5},{5... | collective-permute-start | bytes 933896 | tf_op jit(solution)/shard_map/ppermute | solution.py:171
  28.6 9.8 %collective-permute-start.7 = (f32[76,8,128]{2,1,0:T(8,128)S(1)}, f32[76,8,128]{2,1,0:T(8,128)S(1)}, u32[]{:S(2)}, u32[]{:S(2)}) collective-permute-start(f32[76,8,128]{2,1,0:T(8,128)S(1)} %get-tuple-element.47), channel_id=1, source_target_pairs={{0,28},{4,8},{8,4},{12,16},{16,12},{20,24},{24,20},{28,0},{1,29},{... | collective-permute-start | bytes 933896 | tf_op jit(solution)/shard_map/ppermute | solution.py:171
  30.3 6.3 %collective-permute-start.8 = (f32[12,8,128]{2,1,0:T(8,128)S(1)}, f32[12,8,128]{2,1,0:T(8,128)S(1)}, u32[]{:S(2)}, u32[]{:S(2)}) collective-permute-start(f32[12,8,128]{2,1,0:T(8,128)S(1)} %get-tuple-element.49), channel_id=1, source_target_pairs={{0,3},{1,2},{2,1},{3,0},{4,7},{5,6},{6,5},{7,4},{8,11},{9,10},{10,... | collective-permute-start | bytes 147464 | tf_op jit(solution)/shard_map/ppermute | solution.py:171
  32.0 4.7 %collective-permute-start.9 = (f32[12,8,128]{2,1,0:T(8,128)S(1)}, f32[12,8,128]{2,1,0:T(8,128)S(1)}, u32[]{:S(2)}, u32[]{:S(2)}) collective-permute-start(f32[12,8,128]{2,1,0:T(8,128)S(1)} %get-tuple-element.50), channel_id=1, source_target_pairs={{0,1},{1,0},{2,3},{3,2},{4,5},{5,4},{6,7},{7,6},{8,9},{9,8},{10,11... | collective-permute-start | bytes 147464 | tf_op jit(solution)/shard_map/ppermute | solution.py:171
  36.7 1.9 %collective-permute-start.10 = (f32[12,8,128]{2,1,0:T(8,128)S(1)}, f32[12,8,128]{2,1,0:T(8,128)S(1)}, u32[]{:S(2)}, u32[]{:S(2)}) collective-permute-start(f32[12,8,128]{2,1,0:T(8,128)S(1)} %get-tuple-element.51), channel_id=1, source_target_pairs={{0,4},{4,0},{8,12},{12,8},{16,20},{20,16},{24,28},{28,24},{1,5},{5... | collective-permute-start | bytes 147464 | tf_op jit(solution)/shard_map/ppermute | solution.py:171
  36.8 4.7 %collective-permute-start.11 = (f32[12,8,128]{2,1,0:T(8,128)S(1)}, f32[12,8,128]{2,1,0:T(8,128)S(1)}, u32[]{:S(2)}, u32[]{:S(2)}) collective-permute-start(f32[12,8,128]{2,1,0:T(8,128)S(1)} %get-tuple-element.52), channel_id=1, source_target_pairs={{0,28},{4,8},{8,4},{12,16},{16,12},{20,24},{24,20},{28,0},{1,29},{... | collective-permute-start | bytes 147464 | tf_op jit(solution)/shard_map/ppermute | solution.py:171
  56.6 3.0 %collective-permute-start.12 = (f32[32,3,8,128]{3,2,1,0:T(8,128)S(1)}, f32[32,3,8,128]{3,2,1,0:T(8,128)S(1)}, u32[]{:S(2)}, u32[]{:S(2)}) collective-permute-start(f32[32,3,8,128]{3,2,1,0:T(8,128)S(1)} %all_to_all.5.own_half), channel_id=1, source_target_pairs={{0,4},{4,0},{8,12},{12,8},{16,20},{20,16},{24,28},{28,24},{1,5},{5... | collective-permute-start | bytes 1179656 | tf_op jit(solution)/shard_map/ppermute | solution.py:987

commit v7 on v6

--- a/solution.py
+++ b/solution.py
@@ -147,7 +147,7 @@
 DOWN_PLANES = (5, 4, 4, 5, 4, 4)
 UP_CORNER = (4, 3, 3, 3, 4, 3)
 DOWN_CORNER = (4, 3, 3, 4, 4, 3)
-STRIP = 3
+STRIP = 2
 
 
 def corner_tiles(counts):
@@ -233,19 +233,12 @@
     for writer in (tops_y, bottoms_y):
         for tile in range(2):
             writer.put(low[tile])
-    row, upper = iota(TILE, 0), is_upper(TILE[1])
+    upper = is_upper(TILE[1])
     for array in range(4):
-        parts = [mid[array * mid_x + plane] for plane in range(mid_x)]
         for pair in range(0, mid_x, 2):
-            one, two = parts[pair], parts[pair + 1]
-            tops_y.put(jnp.where(upper, roll(one, 4, 0), two))
-            bottoms_y.put(jnp.where(upper, one, roll(two, 4, 0)))
-        far_low, far_high = roll(parts[0], -2, 0), roll(parts[0], -4, 0)
-        for plane in range(1, mid_x):
-            far_low = jnp.where(row < 2 * plane, far_low, roll(parts[plane], 2 * plane - 2, 0))
-            far_high = jnp.where(row < 2 * plane, far_high, roll(parts[plane], 2 * plane - 4, 0))
-        tops_y.put(far_low)
-        bottoms_y.put(far_high)
+            one, two = mid[array * mid_x + pair], mid[array * mid_x + pair + 1]
+            for writer in (tops_y, bottoms_y):
+                writer.put(jnp.where(upper, roll(one, -2, 0), roll(two, 2, 0)))
 
 
 def corner_of(low_y, high_y, plane, upper, first_tile=0):
@@ -270,13 +263,24 @@
     writer.put(mix(*parts[-2:]))
 
 
+def mid_beside(ref, array, plane, low):
+    pairs = (ref.shape[0] - 4 * STRIP - 2) // 12
+    at = ((2 + array) * pairs + plane) * 2
+    halves = []
+    for side in range(2):
+        total = ref[at + side]
+        if array != 1:
+            total = total + roll(total, 4, 0)
+        if array != 2:
+            total = total + roll(total, -1, 0)
+        halves.append(take(total, (2 * iota(TILE, 0) + (4 if low else 0)) % TILE[0], 0))
+    return lanes_merge(*halves, array != 3) * (0.125 if array == 0 else 0.25)
+
+
 def mid_strip(ref, array, plane, low):
-    start = ref.shape[0] - 4 * STRIP + array * STRIP
-    near, far, row = ref[start + plane // 2], ref[start + 2], iota(TILE, 0)
-    if (plane % 2 == 0) == low:
-        near = roll(near, 4, 0)
-    far = roll(far, (2 if low else 4) - 2 * plane, 0)
-    return jnp.where(row >= 4, near, far) if low else jnp.where(row < 4, near, far)
+    far = roll(ref[ref.shape[0] - 4 * STRIP + array * STRIP + plane // 2], 2 if plane % 2 == 0 else -2, 0)
+    row = iota(TILE, 0)
+    return jnp.where((row >= 2) & (row < 6), far, mid_beside(ref, array, plane, low))
 
 
 def corner_kernel(size_x, size_z, low_y, high_y, mid, low_faces, first, second):
@@ -297,7 +301,7 @@
         wanted = [(array, near) for array in range(4)] + [(1, next_plane)]
         for array, plane in wanted:
             writer.put(
-                jnp.where(upper, mid_strip(high_y, array, plane, False), mid_strip(low_y, array, plane, True))
+                jnp.where(upper, mid_beside(high_y, array, plane, False), mid_beside(low_y, array, plane, True))
             )
         for array, plane in wanted:
             writer.put(mid[array * mid_x + plane])
@@ -462,22 +466,25 @@
         starts[3] += (down_c - 1) * strip_tiles
 
 
-def own_kernel(own, low_y, high_y, windows, coeffs, up_corner, down_corner):
+def own_kernel(own, low_y, high_y, windows, coeffs, up_corner, down_corner, strips):
     assemble_owns(windows, own, low_y, high_y)
     fields = [windows.at[field] for field in range(6)]
     scale_coeffs(1.0, *fields[2:], coeffs, (0, own.shape[1] - 1), fields[1], True)
     mid_x = own.shape[1] // 2
     tops, bottoms = Writer(up_corner), Writer(down_corner)
     upper = is_upper(TILE[1])
-    sides = ((low_y, True), (high_y, False))
+    for side, (ref, low) in enumerate(((low_y, True), (high_y, False))):
+        for array in range(4):
+            for plane in range(mid_x):
+                strips[(side * 4 + array) * mid_x + plane] = mid_strip(ref, array, plane, low)
     for writer, first, step in ((tops, mid_x - 1, -1), (bottoms, 0, 1)):
         for array in range(4):
             for q in range(2):
-                for ref, low in sides:
-                    writer.put(mid_strip(ref, array, first + q * step, low))
+                for side in range(2):
+                    writer.put(strips[(side * 4 + array) * mid_x + first + q * step])
         for array in range(4):
             for q in range(2, 4):
-                one, two = (roll(mid_strip(ref, array, first + q * step, low), 4, 0) for ref, low in sides)
+                one, two = (roll(strips[(side * 4 + array) * mid_x + first + q * step], 4, 0) for side in range(2))
                 writer.put(jnp.where(upper, one, two))
 
 
@@ -586,7 +593,7 @@
 
 
 def mid_coeffs_kernel(
-    mid, low, low_y, high_y, first_c, second_c, first_x2, second_x2, coeffs, near, window
+    mid, low, strips, low_y, high_y, first_c, second_c, first_x2, second_x2, coeffs, near, window
 ):
     place = here()
     low_x2, high_x2 = got(first_x2, second_x2, place[0] % 2 == 0)
@@ -604,8 +611,8 @@
                 window[array, first + block * mid_x + plane, mid_y : 2 * mid_y] = ref[start + array * mid_x + plane]
     for array in range(4):
         for plane in range(mid_x):
-            window[array, MID + plane, :mid_y] = mid_strip(low_y, array, plane, True)
-            window[array, MID + plane, 2 * mid_y :] = mid_strip(high_y, array, plane, False)
+            window[array, MID + plane, :mid_y] = strips[array * mid_x + plane]
+            window[array, MID + plane, 2 * mid_y :] = strips[(4 + array) * mid_x + plane]
     passed += mids
     far = 3 * mid_x + first
     for ref, start, step, end in ((low_x2, MID - 1, -1, first - 1), (high_x2, MID + mid_x, 1, far)):
@@ -626,7 +633,7 @@
 
 
 def mid_kernel(
-    count_x, count_y, low, mid_target, coeffs, first_x2, second_x2, first_y2, second_y2, first_c2, second_c2,
+    count_x, count_y, low, mid_target, coeffs, first_x2, second_x2, first_y2, second_y2, first_c2, second_c2, unused,
     goal, slots, target, iterate, update,
 ):
     mid_x, mid_y, mid_z = mid_target.shape
@@ -702,8 +709,8 @@
 
 
 def low_kernel(count_x, count_y, own_half, near, iterate, gathered, fields, coeffs, update):
-    size_x, size_y, lanes = iterate.shape
-    low_x, low_y = size_x // count_x, size_y // count_y
+    planes, size_y, lanes = iterate.shape
+    low_x, low_y = 2 * planes // count_x, size_y // count_y
     low_z = lanes // 2
     me_x, me_y = here()
 
@@ -719,34 +726,37 @@
             for kind in range(2):
                 gathered[source, 1 + kind] = near[((dx + 2) * 3 + dy + 1) * 2 + kind]
 
+    left = iota(TILE, 1) < low_z
+
     def place(i, carry):
         for j in range(count_y):
-            for kind in range(3):
-                tile = gathered[i * count_y + j, kind]
+            one = [gathered[i * count_y + j, kind] for kind in range(3)]
+            two = [gathered[(i + count_x // 2) * count_y + j, kind] for kind in range(3)]
+            parts = [jnp.where(left, low, roll(high, low_z, 1)) for low, high in zip(one, two)]
+            parts += [jnp.where(left, roll(low, low_z, 1), high) for low, high in zip(one[1:], two[1:])]
+            for kind, tile in enumerate(parts):
                 for plane in range(low_x):
                     fields[kind, i * low_x + plane, j * low_y : (j + 1) * low_y] = tile[
                         plane * low_y : (plane + 1) * low_y
                     ]
         return carry
 
-    each(0, count_x, place)
-    lane = iota((size_y, lanes), 1)
-    inside = lane < low_z
+    each(0, count_x // 2, place)
+    lane = iota((size_y, lanes), 1) % low_z
     scale = 0.0625
     weights = chebyshev_weights(COARSE_SWEEPS)
 
-    def following(i):
+    def next_plane(ref, i, first):
         if isinstance(i, int):
-            return (i + 1) % size_x
-        return jnp.where(i == size_x - 1, 0, i + 1)
+            return roll(first, low_z, 1) if i == planes - 1 else ref[i + 1]
+        return jnp.where(i == planes - 1, roll(first, low_z, 1), ref[jnp.minimum(i + 1, planes - 1)])
 
     def prepare(i, carry):
-        yl, xl = fields[1, i], roll(fields[2, i], low_z, 1)
-        zl, xh = roll(fields[1, i], low_z, 1), roll(fields[2, following(i)], low_z, 1)
+        goal, yl, diag, zl, xl = (fields[kind, i] for kind in range(5))
+        xh = next_plane(fields.at[4], i, fields[4, 0])
         yh = roll(yl, -1, 0)
         zh = jnp.where(lane == low_z - 1, 0.0, roll(zl, -1, 1))
-        diag = fields[2, i] + scale * (xl + xh + yl + yh + zl + zh)
-        inverse = jnp.where(inside, 1.0 / diag, 0.0)
+        inverse = 1.0 / (diag + scale * (xl + xh + yl + yh + zl + zh))
         scaled = scale * inverse
         coeffs[0, i] = scaled * xl
         coeffs[1, i] = scaled * xh
@@ -754,50 +764,47 @@
         coeffs[3, i] = scaled * yh
         coeffs[4, i] = jnp.where(lane == 0, 0.0, scaled * zl)
         coeffs[5, i] = scaled * zh
-        goal = jnp.where(inside, fields[0, i], 0.0) * inverse
+        goal = goal * inverse
         coeffs[6, i] = goal
         update[i] = weights[0][1] * goal
         iterate[i] = weights[0][1] * goal
         return carry
 
-    each(0, size_x, prepare)
+    each(0, planes, prepare)
     for pair in weights[1:]:
         start = iterate[0]
 
         def body(i, carry, pair=pair, start=start):
             below, here = carry
-            if isinstance(i, int):
-                above = start if i == size_x - 1 else iterate[i + 1]
-            else:
-                above = jnp.where(i == size_x - 1, start, iterate[following(i)])
+            above = next_plane(iterate, i, start)
             step = pair[1] * scaled_remain(coeffs, i, below, here, above) + pair[0] * update[i]
             update[i] = step
             iterate[i] = here + step
             return here, above
 
-        each(0, size_x, body, (iterate[size_x - 1], start))
-
-
-def window_kernel(
-    fields_own, low_x1, high_x1, low_y1, high_y1, first_c1, second_c1,
-    own, first_x, second_x, first_y, second_y, first_c, second_c,
-    window, coeffs, own_windows, side_windows,
-):
+        each(0, planes, body, (roll(iterate[planes - 1], low_z, 1), start))
+
+
+def fine_coeffs_kernel(fields_own, low_x, high_x, low_y, high_y, first_c, second_c, coeffs, own_windows, side_windows):
+    size_x, size_y, size_z = fields_own.shape[1:]
+    low_c, high_c = got(first_c, second_c, here()[0] % 2 == 0)
+    assemble_owns(own_windows, fields_own, low_y, high_y)
+    assemble_sides(side_windows, (size_y, size_z), low_x, high_x, low_c, high_c)
+    end = FINE + size_x
+    windows = Stack(
+        (0, FINE, side_windows, 0), (FINE, end, own_windows, 0), (end, end + FINE, side_windows, FINE)
+    )
+    fields = [windows.of(field) for field in range(6)]
+    scale_coeffs(1.0, *fields[2:], Stack((2, end + 3, coeffs, 0)), (2, end + 3), fields[1])
+
+
+def window_kernel(own, first_x, second_x, first_y, second_y, first_c, second_c, window):
+    size_x, size_y, size_z = own.shape
     place = here()
     even = place[0] % 2 == 0
-    low_c1, high_c1 = got(first_c1, second_c1, even)
     low_x, high_x = got(first_x, second_x, even)
     low_y, high_y = got(first_y, second_y, place[1] % 2 == 1)
     low_c, high_c = got(first_c, second_c, even)
-    size_x, size_y, size_z = own.shape
-    assemble_owns(own_windows, fields_own, low_y1, high_y1)
-    assemble_sides(side_windows, (size_y, size_z), low_x1, high_x1, low_c1, high_c1)
-    end = FINE + size_x
-    windows = Stack(
-        (0, FINE, side_windows, 0), (FINE, end, own_windows, 0), (end, end + FINE, side_windows, FINE)
-    )
-    fields = [windows.of(field) for field in range(6)]
-    scale_coeffs(1.0, *fields[2:], Stack((2, end + 3, coeffs, 0)), (2, end + 3), fields[1])
     assemble_own(window.at[FINE : FINE + size_x], own, low_y, high_y, 0, 0)
     assemble_side(window, FINE - 4, 4, (size_y, size_z), low_x, 0, low_c, 0, 3, True)
     assemble_side(window, FINE + size_x, 4, (size_y, size_z), high_x, 0, high_c, 0, 3, False)
@@ -834,13 +841,15 @@
         for plane in range(2):
             mid_iterate[plane, rows] = own_half[device(-2, dy), 1 + plane]
             mid_iterate[far + plane, rows] = own_half[device(2, dy), 1 + plane]
-    low_size_x, low_size_y = low_iterate.shape[:2]
+    low_planes, low_size_y = low_iterate.shape[:2]
+    low_size_x = 2 * low_planes
     low_y = mid_y // 2
     turn = lax.rem(low_size_y - me_y * low_y + low_y, low_size_y)
     for plane in range((mid_x + 2 * MID) // 2):
         at = lax.rem(me_x * (mid_x // 2) - MID // 2 + plane + low_size_x, low_size_x)
-        turned = pltpu.roll(low_iterate[at], turn, 0)
-        one, two = lanes_spread(turned[: TILE[0]], 0), lanes_spread(turned[TILE[0] : 2 * TILE[0]], 0)
+        turned = pltpu.roll(low_iterate[lax.rem(at, low_planes)], turn, 0)
+        side = at // low_planes
+        one, two = lanes_spread(turned[: TILE[0]], side), lanes_spread(turned[TILE[0] : 2 * TILE[0]], side)
         part = jnp.concatenate([rows_spread(one, 0), rows_spread(one, 1), rows_spread(two, 0)], axis=0)
         mid_iterate[2 * plane] += part
         mid_iterate[2 * plane + 1] += part
@@ -943,10 +952,10 @@
 
     tall = (size_y + 2 * PAD, size_z)
     wide = (size_x + 2 * FINE,) + tall
-    own_windows, own_coeffs, up_corner, down_corner = call(
+    own_windows, own_coeffs, up_corner, down_corner, strips = call(
         own_kernel,
         (own, low_y1, high_y1),
-        [(6, size_x) + tall, (8, size_x - 1) + tall, tiles(MID_CORNER), tiles(MID_CORNER)],
+        [(6, size_x) + tall, (8, size_x - 1) + tall, tiles(MID_CORNER), tiles(MID_CORNER), tiles(2 * mids)],
     )
     iterate, mid_target, first_x2, second_x2, first_y2, second_y2 = call(
         fine_kernel,
@@ -973,32 +982,34 @@
     mid_wide = (mid_x + 2 * MID, 3 * mid_y, mid_z)
     mid_coeffs, near = call(
         mid_coeffs_kernel,
-        (mid, low, low_y1, high_y1, first_c1, second_c1, first_x2, second_x2),
+        (mid, low, strips, low_y1, high_y1, first_c1, second_c1, first_x2, second_x2),
         [(8,) + mid_wide, tiles(30)],
         [(4,) + mid_wide],
     )
+    (coeffs,) = call(
+        fine_coeffs_kernel,
+        (own, low_x1, high_x1, low_y1, high_y1, first_c1, second_c1),
+        [(7, wide[0] - 4) + tall],
+        [(6, size_x) + tall, (6, 2 * FINE) + tall],
+    )
     goal, slots = call(
         functools.partial(mid_kernel, count_x, count_y),
-        (low, mid_target, mid_coeffs, first_x2, second_x2, first_y2, second_y2, first_c2, second_c2),
+        (low, mid_target, mid_coeffs, first_x2, second_x2, first_y2, second_y2, first_c2, second_c2, coeffs),
         [mid_wide, (devices, 3) + TILE],
         [mid_wide] * 3,
     )
     own_half = lax.all_to_all(slots, ("gx", "gy"), 0, 0)
     other_half = lax.ppermute(own_half, "gx", [(i, i ^ 1) for i in range(count_x)])
 
-    window, coeffs = call(
-        window_kernel,
-        (own, low_x1, high_x1, low_y1, high_y1, first_c1, second_c1)
-        + (iterate, first_x2, second_x2, first_y2, second_y2, first_c2, second_c2),
-        [wide, (7, wide[0] - 4) + tall],
-        [(6, size_x) + tall, (6, 2 * FINE) + tall],
-    )
-    low_wide = (low_x * count_x, low_y * count_y, mid_z)
+    (window,) = call(
+        window_kernel, (iterate, first_x2, second_x2, first_y2, second_y2, first_c2, second_c2), [wide]
+    )
+    low_wide = (low_x * count_x // 2, low_y * count_y, mid_z)
     (low_iterate,) = call(
         functools.partial(low_kernel, count_x, count_y),
         (own_half, near),
         [low_wide],
-        [(devices, 3) + TILE, (3,) + low_wide, (7,) + low_wide, low_wide],
+        [(devices, 3) + TILE, (5,) + low_wide, (7,) + low_wide, low_wide],
     )
     (result,) = call(
         functools.partial(last_kernel, count_x, count_y),

time: 62.1 us -> 60.9 us (0.981)
  waiting for transfers between devices: 22.8 us -> 21.1 us
    ppermute x8, waiting for transfers between devices: 12.1 us -> 10.8 us  [swapped(): return (lax.ppermute(first, axis, inner), lax.ppermute(second, axis, outer))]
    ppermute x4, waiting for transfers between devices: 10.7 us -> 9.95 us  [shifted(): lax.ppermute(value, axis, [(i, (i + step) % count) for i in range(count)])]
    pallas_call x10 -> x11, Pallas kernels: 8.8 us -> 9.23 us  [call(): pl.pallas_call(kernel, out_shape=[pltpu.HBM(shape, F32) if i in far_out e...]
  transfers between devices with their start and end apart: 13 -> 13, of which waited for: 5 -> 6; matrix products, arithmetic and copies ran while one was open for 0% -> 0% of each run, Pallas kernels for 4% -> 5%
where the time goes in v7:
time: 60.9 us; the launch traced here: 60.7 us
  waiting for transfers between devices  21.1 us (35%)
  starting transfers between devices  15.7 us (26%)
  blocking collectives  14.5 us (24%)
  Pallas kernels  9.23 us (15%)
    all_to_all x1, blocking collectives, local(): own_half = lax.all_to_all(slots, ('gx', 'gy'), 0, 0)  14.5 us
    ppermute x8, waiting for transfers between devices, swapped(): return (lax.ppermute(first, axis, inner), lax.ppermute(second, axis, outer))  10.8 us
    ppermute x4, waiting for transfers between devices, shifted(): lax.ppermute(value, axis, [(i, (i + step) % count) for i in range(count)])  9.95 us
    pallas_call x11, Pallas kernels, call(): pl.pallas_call(kernel, out_shape=[pltpu.HBM(shape, F32) if i in far_out e...  9.23 us
    ppermute x8, starting transfers between devices, swapped(): return (lax.ppermute(first, axis, inner), lax.ppermute(second, axis, outer))  7.83 us
    ppermute x4, starting transfers between devices, shifted(): lax.ppermute(value, axis, [(i, (i + step) % count) for i in range(count)])  6.71 us
  transfers between devices with their start and end apart: 13, of which 6 were waited for; matrix products, arithmetic and copies ran while one was open for 0% of the time, Pallas kernels for 5%

profile of v7, /device:TPU:0, one launch (start us, length us, event | category | flops | bytes accessed | tf_op | source)
XLA Modules:
  0.0 60.7 jit_solution(6002835093858615939)
XLA Ops:
  0.0 1.6 %shard_map.64 = (f32[100,8,128]{2,1,0:T(8,128)S(1)}, f32[104,8,128]{2,1,0:T(8,128)S(1)}, f32[60,8,128]{2,1,0:T(8,128)S(1)}, f32[62,8,128]{2,1,0:T(8,128)S(1)}, f...) custom-call(f32[8,16,256]{2,1,0:T(8,128)} %ini_in.1, f32[8,16,256]{2,1,0:T(8,128)} %src_in.1, ...), custom_call_target="tpu_custom_call" | custom-call | flops 1000 | bytes 1000 | tf_op jit(solution)/shard_map/pallas_call | solution.py:899
  1.7 5.1 %collective-permute-start.1 = (f32[62,8,128]{2,1,0:T(8,128)S(1)}, f32[62,8,128]{2,1,0:T(8,128)S(1)}, u32[]{:S(2)}, u32[]{:S(2)}) collective-permute-start(f32[62,8,128]{2,1,0:T(8,128)S(1)} %get-tuple-element.34), channel_id=1, source_target_pairs={{0,3},{1,0},{2,1},{3,2},{4,7},{5,4},{6,5},{7,6},{8,11},{9,8},{10,9... | collective-permute-start | bytes 761864 | tf_op jit(solution)/shard_map/ppermute | solution.py:176
  6.8 0.0 collective-permute-start
  6.8 1.6 %collective-permute-start.3 = (f32[104,8,128]{2,1,0:T(8,128)S(1)}, f32[104,8,128]{2,1,0:T(8,128)S(1)}, u32[]{:S(2)}, u32[]{:S(2)}) collective-permute-start(f32[104,8,128]{2,1,0:T(8,128)S(1)} %get-tuple-element.41), channel_id=1, source_target_pairs={{0,28},{4,0},{8,4},{12,8},{16,12},{20,16},{24,20},{28,24},{1,29},{... | collective-permute-start | bytes 1277960 | tf_op jit(solution)/shard_map/ppermute | solution.py:176
  8.4 0.0 collective-permute-start.2
  8.4 9.9 %collective-permute-done.low_y = f32[60,8,128]{2,1,0:T(8,128)S(1)} collective-permute-done((f32[60,8,128]{2,1,0:T(8,128)S(1)}, f32[60,8,128]{2,1,0:T(8,128)S(1)}, u32[]{:S(2)}, u32[]{:S(2)}) %collective-permute-start) | collective-permute-done | bytes 245792 | tf_op jit(solution)/shard_map/ppermute | solution.py:176
  18.3 0.0 collective-permute-done.1.high_y
  18.3 0.2 shard_map.66
  18.5 0.1 collective-permute-start.4
  18.6 2.5 %collective-permute-start.5 = (f32[46,8,128]{2,1,0:T(8,128)S(1)}, f32[46,8,128]{2,1,0:T(8,128)S(1)}, u32[]{:S(2)}, u32[]{:S(2)}) collective-permute-start(f32[46,8,128]{2,1,0:T(8,128)S(1)} %get-tuple-element.43), channel_id=1, source_target_pairs={{0,28},{4,8},{8,4},{12,16},{16,12},{20,24},{24,20},{28,0},{1,29},{... | collective-permute-start | bytes 565256 | tf_op jit(solution)/shard_map/ppermute | solution.py:171
  21.2 1.1 %shard_map.65 = (f32[6,8,32,256]{3,2,1,0:T(8,128)S(1)}, f32[8,7,32,256]{3,2,1,0:T(8,128)S(1)}, f32[24,8,128]{2,1,0:T(8,128)S(1)}, f32[24,8,128]{2,1,0:T(8,128)S(1)}, f32[32,8,128]{2,1,0:T(8,128)S(1)}) custom-call(f32[6,8,16,256]{3,2,1,0:T(8,128)S(1)} %get-tuple-element.32.own.fields_own, f32[60,8,128]{2,1,0:T(8,128)S(1)} %collective-permute-done.low_y, ...), custom_call_target="tpu_custom_call" | custom-call | flops 1000 | bytes 1000 | tf_op jit(solution)/shard_map/pallas_call | solution.py:899
  22.3 0.0 collective-permute-done.2.low_x
  22.3 0.0 collective-permute-done.3.high_x
  22.3 0.0 collective-permute-done.4.first_c
  22.3 3.7 %collective-permute-done.5.second_c = f32[46,8,128]{2,1,0:T(8,128)S(1)} collective-permute-done((f32[46,8,128]{2,1,0:T(8,128)S(1)}, f32[46,8,128]{2,1,0:T(8,128)S(1)}, u32[]{:S(2)}, u32[]{:S(2)}) %collective-permute-start.5) | collective-permute-done | bytes 188448 | tf_op jit(solution)/shard_map/ppermute | solution.py:171
  26.0 1.9 %shard_map.67 = (f32[8,16,256]{2,1,0:T(8,128)S(1)}, f32[4,8,128]{2,1,0:T(8,128)S(1)}, f32[76,8,128]{2,1,0:T(8,128)S(1)}, f32[76,8,128]{2,1,0:T(8,128)S(1)}, f32[...) custom-call(f32[6,8,32,256]{3,2,1,0:T(8,128)S(1)} %get-tuple-element.35.own_windows, ...), custom_call_target="tpu_custom_call" | custom-call | flops 1000 | bytes 1000 | tf_op jit(solution)/shard_map/pallas_call | solution.py:899
  27.9 0.1 collective-permute-start.6
  28.0 1.7 %collective-permute-start.7 = (f32[76,8,128]{2,1,0:T(8,128)S(1)}, f32[76,8,128]{2,1,0:T(8,128)S(1)}, u32[]{:S(2)}, u32[]{:S(2)}) collective-permute-start(f32[76,8,128]{2,1,0:T(8,128)S(1)} %get-tuple-element.47), channel_id=1, source_target_pairs={{0,28},{4,8},{8,4},{12,16},{16,12},{20,24},{24,20},{28,0},{1,29},{... | collective-permute-start | bytes 933896 | tf_op jit(solution)/shard_map/ppermute | solution.py:171
  29.7 1.7 %collective-permute-start.8 = (f32[12,8,128]{2,1,0:T(8,128)S(1)}, f32[12,8,128]{2,1,0:T(8,128)S(1)}, u32[]{:S(2)}, u32[]{:S(2)}) collective-permute-start(f32[12,8,128]{2,1,0:T(8,128)S(1)} %get-tuple-element.49), channel_id=1, source_target_pairs={{0,3},{1,2},{2,1},{3,0},{4,7},{5,6},{6,5},{7,4},{8,11},{9,10},{10,... | collective-permute-start | bytes 147464 | tf_op jit(solution)/shard_map/ppermute | solution.py:171
  31.5 0.0 collective-permute-start.9
  31.5 4.5 %collective-permute-done.8.first_y.first_y2 = f32[12,8,128]{2,1,0:T(8,128)S(1)} collective-permute-done((f32[12,8,128]{2,1,0:T(8,128)S(1)}, f32[12,8,128]{2,1,0:T(8,128)S(1)}, u32[]{:S(2)}, u32[]{:S(2)}) %collective-permute-start.8) | collective-permute-done | bytes 49184 | tf_op jit(solution)/shard_map/ppermute | solution.py:171
  36.0 0.2 collective-permute-done.9.second_y.second_y2
  36.2 0.1 collective-permute-start.10
  36.3 1.6 %collective-permute-start.11 = (f32[12,8,128]{2,1,0:T(8,128)S(1)}, f32[12,8,128]{2,1,0:T(8,128)S(1)}, u32[]{:S(2)}, u32[]{:S(2)}) collective-permute-start(f32[12,8,128]{2,1,0:T(8,128)S(1)} %get-tuple-element.52), channel_id=1, source_target_pairs={{0,28},{4,8},{8,4},{12,16},{16,12},{20,24},{24,20},{28,0},{1,29},{... | collective-permute-start | bytes 147464 | tf_op jit(solution)/shard_map/ppermute | solution.py:171
  37.9 0.5 shard_map.70.unused.fine_coeffs
  38.4 0.0 collective-permute-done.6.first_x2.first_x
  38.4 0.0 collective-permute-done.7.second_x2.second_x
  38.4 0.2 shard_map.68
  38.6 0.0 collective-permute-done.10.first_c2.first_c
  38.6 2.4 %collective-permute-done.11.second_c2.second_c = f32[12,8,128]{2,1,0:T(8,128)S(1)} collective-permute-done((f32[12,8,128]{2,1,0:T(8,128)S(1)}, f32[12,8,128]{2,1,0:T(8,128)S(1)}, u32[]{:S(2)}, u32[]{:S(2)}) %collective-permute-start.11) | collective-permute-done | bytes 49184 | tf_op jit(solution)/shard_map/ppermute | solution.py:171
  41.0 0.5 shard_map.71
  41.5 14.5 %all_to_all.5.own_half = f32[32,3,8,128]{3,2,1,0:T(8,128)S(1)} all-to-all(f32[32,3,8,128]{3,2,1,0:T(8,128)S(1)} %get-tuple-element.53), channel_id=1, replica_groups=mesh['gx'=8,'gy'=4] {'gx','gy'}, dimensions={0} | all-to-all | bytes 786432 | tf_op jit(solution)/shard_map/all_to_all | solution.py:1001
  56.0 1.2 %collective-permute-start.12 = (f32[32,3,8,128]{3,2,1,0:T(8,128)S(1)}, f32[32,3,8,128]{3,2,1,0:T(8,128)S(1)}, u32[]{:S(2)}, u32[]{:S(2)}) collective-permute-start(f32[32,3,8,128]{3,2,1,0:T(8,128)S(1)} %all_to_all.5.own_half), channel_id=1, source_target_pairs={{0,4},{4,0},{8,12},{12,8},{16,20},{20,16},{24,28},{28,24},{1,5},{5... | collective-permute-start | bytes 1179656 | tf_op jit(solution)/shard_map/ppermute | solution.py:1002
  57.2 0.9 %shard_map.72.low_iterate = f32[8,16,128]{2,1,0:T(8,128)S(1)} custom-call(f32[32,3,8,128]{3,2,1,0:T(8,128)S(1)} %all_to_all.5.own_half, f32[30,8,128]{2,1,0:T(8,128)S(1)} %get-tuple-element.54.near), custom_call_target="tpu_custom_call" | custom-call | flops 1000 | bytes 1000 | tf_op jit(solution)/shard_map/pallas_call | solution.py:899
  58.2 0.4 collective-permute-done.12.other_half
  58.5 2.2 %shard_map.74 = f32[8,16,256]{2,1,0:T(8,128)} custom-call(f32[32,3,8,128]{3,2,1,0:T(8,128)S(1)} %all_to_all.5.own_half, f32[32,3,8,128]{3,2,1,0:T(8,128)S(1)} %collective-permute-done.12.other_half, f32[8,16,128]{2,1,0:T(8,128)S(1)} %shard_map.72.low_iterate, f32[8,16,24,128]{3,2,1,0:T(8,128)S(1)} %get-tuple-element.48.coeffs.mid_coeffs, ...), custom_call_target="tpu_custom_call" | custom-call | flops 1000 | bytes 1000 | tf_op jit(solution)/shard_map/pallas_call | solution.py:899
  (2 shorter events, 0.1 us)
Async XLA Ops:
  1.7 16.7 %collective-permute-start.1 = (f32[62,8,128]{2,1,0:T(8,128)S(1)}, f32[62,8,128]{2,1,0:T(8,128)S(1)}, u32[]{:S(2)}, u32[]{:S(2)}) collective-permute-start(f32[62,8,128]{2,1,0:T(8,128)S(1)} %get-tuple-element.34), channel_id=1, source_target_pairs={{0,3},{1,0},{2,1},{3,2},{4,7},{5,4},{6,5},{7,6},{8,11},{9,8},{10,9... | collective-permute-start | bytes 761864 | tf_op jit(solution)/shard_map/ppermute | solution.py:176
  6.8 11.6 %collective-permute-start = (f32[60,8,128]{2,1,0:T(8,128)S(1)}, f32[60,8,128]{2,1,0:T(8,128)S(1)}, u32[]{:S(2)}, u32[]{:S(2)}) collective-permute-start(f32[60,8,128]{2,1,0:T(8,128)S(1)} %get-tuple-element.33), channel_id=1, source_target_pairs={{0,1},{1,2},{2,3},{3,0},{4,5},{5,6},{6,7},{7,4},{8,9},{9,10},{10,1... | collective-permute-start | bytes 737288 | tf_op jit(solution)/shard_map/ppermute | solution.py:176
  6.8 15.5 %collective-permute-start.3 = (f32[104,8,128]{2,1,0:T(8,128)S(1)}, f32[104,8,128]{2,1,0:T(8,128)S(1)}, u32[]{:S(2)}, u32[]{:S(2)}) collective-permute-start(f32[104,8,128]{2,1,0:T(8,128)S(1)} %get-tuple-element.41), channel_id=1, source_target_pairs={{0,28},{4,0},{8,4},{12,8},{16,12},{20,16},{24,20},{28,24},{1,29},{... | collective-permute-start | bytes 1277960 | tf_op jit(solution)/shard_map/ppermute | solution.py:176
  8.4 13.9 %collective-permute-start.2 = (f32[100,8,128]{2,1,0:T(8,128)S(1)}, f32[100,8,128]{2,1,0:T(8,128)S(1)}, u32[]{:S(2)}, u32[]{:S(2)}) collective-permute-start(f32[100,8,128]{2,1,0:T(8,128)S(1)} %get-tuple-element.40), channel_id=1, source_target_pairs={{0,4},{4,8},{8,12},{12,16},{16,20},{20,24},{24,28},{28,0},{1,5},{5... | collective-permute-start | bytes 1228808 | tf_op jit(solution)/shard_map/ppermute | solution.py:176
  18.5 3.8 %collective-permute-start.4 = (f32[46,8,128]{2,1,0:T(8,128)S(1)}, f32[46,8,128]{2,1,0:T(8,128)S(1)}, u32[]{:S(2)}, u32[]{:S(2)}) collective-permute-start(f32[46,8,128]{2,1,0:T(8,128)S(1)} %get-tuple-element.42), channel_id=1, source_target_pairs={{0,4},{4,0},{8,12},{12,8},{16,20},{20,16},{24,28},{28,24},{1,5},{5... | collective-permute-start | bytes 565256 | tf_op jit(solution)/shard_map/ppermute | solution.py:171
  18.6 7.4 %collective-permute-start.5 = (f32[46,8,128]{2,1,0:T(8,128)S(1)}, f32[46,8,128]{2,1,0:T(8,128)S(1)}, u32[]{:S(2)}, u32[]{:S(2)}) collective-permute-start(f32[46,8,128]{2,1,0:T(8,128)S(1)} %get-tuple-element.43), channel_id=1, source_target_pairs={{0,28},{4,8},{8,4},{12,16},{16,12},{20,24},{24,20},{28,0},{1,29},{... | collective-permute-start | bytes 565256 | tf_op jit(solution)/shard_map/ppermute | solution.py:171
  27.9 10.5 %collective-permute-start.6 = (f32[76,8,128]{2,1,0:T(8,128)S(1)}, f32[76,8,128]{2,1,0:T(8,128)S(1)}, u32[]{:S(2)}, u32[]{:S(2)}) collective-permute-start(f32[76,8,128]{2,1,0:T(8,128)S(1)} %get-tuple-element.46), channel_id=1, source_target_pairs={{0,4},{4,0},{8,12},{12,8},{16,20},{20,16},{24,28},{28,24},{1,5},{5... | collective-permute-start | bytes 933896 | tf_op jit(solution)/shard_map/ppermute | solution.py:171
  28.0 10.3 %collective-permute-start.7 = (f32[76,8,128]{2,1,0:T(8,128)S(1)}, f32[76,8,128]{2,1,0:T(8,128)S(1)}, u32[]{:S(2)}, u32[]{:S(2)}) collective-permute-start(f32[76,8,128]{2,1,0:T(8,128)S(1)} %get-tuple-element.47), channel_id=1, source_target_pairs={{0,28},{4,8},{8,4},{12,16},{16,12},{20,24},{24,20},{28,0},{1,29},{... | collective-permute-start | bytes 933896 | tf_op jit(solution)/shard_map/ppermute | solution.py:171
  29.7 6.3 %collective-permute-start.8 = (f32[12,8,128]{2,1,0:T(8,128)S(1)}, f32[12,8,128]{2,1,0:T(8,128)S(1)}, u32[]{:S(2)}, u32[]{:S(2)}) collective-permute-start(f32[12,8,128]{2,1,0:T(8,128)S(1)} %get-tuple-element.49), channel_id=1, source_target_pairs={{0,3},{1,2},{2,1},{3,0},{4,7},{5,6},{6,5},{7,4},{8,11},{9,10},{10,... | collective-permute-start | bytes 147464 | tf_op jit(solution)/shard_map/ppermute | solution.py:171
  31.5 4.7 %collective-permute-start.9 = (f32[12,8,128]{2,1,0:T(8,128)S(1)}, f32[12,8,128]{2,1,0:T(8,128)S(1)}, u32[]{:S(2)}, u32[]{:S(2)}) collective-permute-start(f32[12,8,128]{2,1,0:T(8,128)S(1)} %get-tuple-element.50), channel_id=1, source_target_pairs={{0,1},{1,0},{2,3},{3,2},{4,5},{5,4},{6,7},{7,6},{8,9},{9,8},{10,11... | collective-permute-start | bytes 147464 | tf_op jit(solution)/shard_map/ppermute | solution.py:171
  36.2 2.4 %collective-permute-start.10 = (f32[12,8,128]{2,1,0:T(8,128)S(1)}, f32[12,8,128]{2,1,0:T(8,128)S(1)}, u32[]{:S(2)}, u32[]{:S(2)}) collective-permute-start(f32[12,8,128]{2,1,0:T(8,128)S(1)} %get-tuple-element.51), channel_id=1, source_target_pairs={{0,4},{4,0},{8,12},{12,8},{16,20},{20,16},{24,28},{28,24},{1,5},{5... | collective-permute-start | bytes 147464 | tf_op jit(solution)/shard_map/ppermute | solution.py:171
  36.3 4.7 %collective-permute-start.11 = (f32[12,8,128]{2,1,0:T(8,128)S(1)}, f32[12,8,128]{2,1,0:T(8,128)S(1)}, u32[]{:S(2)}, u32[]{:S(2)}) collective-permute-start(f32[12,8,128]{2,1,0:T(8,128)S(1)} %get-tuple-element.52), channel_id=1, source_target_pairs={{0,28},{4,8},{8,4},{12,16},{16,12},{20,24},{24,20},{28,0},{1,29},{... | collective-permute-start | bytes 147464 | tf_op jit(solution)/shard_map/ppermute | solution.py:171
  56.0 2.5 %collective-permute-start.12 = (f32[32,3,8,128]{3,2,1,0:T(8,128)S(1)}, f32[32,3,8,128]{3,2,1,0:T(8,128)S(1)}, u32[]{:S(2)}, u32[]{:S(2)}) collective-permute-start(f32[32,3,8,128]{3,2,1,0:T(8,128)S(1)} %all_to_all.5.own_half), channel_id=1, source_target_pairs={{0,4},{4,0},{8,12},{12,8},{16,20},{20,16},{24,28},{28,24},{1,5},{5... | collective-permute-start | bytes 1179656 | tf_op jit(solution)/shard_map/ppermute | solution.py:1002

commit v8 on v7

--- a/solution.py
+++ b/solution.py
@@ -109,10 +109,10 @@
                 self.tiles.append(value[r : r + TILE[0], c : c + TILE[1]])
 
 
-def send(first, second, even, up, down):
+def send(first, second, odd, up, down):
     for at, (one, two) in enumerate(zip(up.tiles, down.tiles, strict=True)):
-        first[at] = jnp.where(even, one, two)
-        second[at] = jnp.where(even, two, one)
+        first[at] = jnp.where(odd, one, two)
+        second[at] = jnp.where(odd, two, one)
 
 
 class Got:
@@ -166,9 +166,7 @@
     count = lax.axis_size(axis)
     outer = [(i, (i + 1 if i % 2 else i - 1) % count) for i in range(count)]
     inner = [(i, i ^ 1) for i in range(count)]
-    if axis == "gy":
-        inner, outer = outer, inner
-    return lax.ppermute(first, axis, inner), lax.ppermute(second, axis, outer)
+    return lax.ppermute(first, axis, outer), lax.ppermute(second, axis, inner)
 
 
 def shifted(value, axis, step):
@@ -308,7 +306,7 @@
         for tiles in ((low_faces[0], low_faces[1]), low_tiles_of(low_y), low_tiles_of(high_y)):
             for tile in tiles:
                 writer.put(tile)
-    send(first, second, place[0] % 2 == 0, tops, bottoms)
+    send(first, second, place[0] % 2 == 1, tops, bottoms)
 
 
 def low_tiles_of(ref):
@@ -496,8 +494,8 @@
     size_x, size_z = own_windows.shape[1], own_windows.shape[3]
     size_y = own_windows.shape[2] - 2 * PAD
     place = here()
-    even = place[0] % 2 == 0
-    low_c, high_c = got(first_c, second_c, even)
+    odd = place[0] % 2 == 1
+    low_c, high_c = got(first_c, second_c, odd)
     assemble_sides(side_windows, (size_y, size_z), low_x, high_x, low_c, high_c)
     end = FINE + size_x
     last = end + FINE - 1
@@ -551,7 +549,7 @@
     for writer, corners in ((tops, low_c), (bottoms, high_c)):
         for tile in range(corners.shape[0] - PASSED - 10, corners.shape[0]):
             writer.put(corners[tile])
-    send(first_x, second_x, even, tops, bottoms)
+    send(first_x, second_x, odd, tops, bottoms)
     send(first_y, second_y, place[1] % 2 == 1, tops_y, bottoms_y)
 
 
@@ -578,7 +576,7 @@
         for ref in (low_y, high_y):
             for tile in range(ref.shape[0] - size_x // 2, ref.shape[0]):
                 writer.put(ref[tile])
-    send(first, second, place[0] % 2 == 0, tops, bottoms)
+    send(first, second, place[0] % 2 == 1, tops, bottoms)
 
 
 def level_two_near(near, low, low_y, high_y, low_c, high_c, low_x2, high_x2):
@@ -596,8 +594,8 @@
     mid, low, strips, low_y, high_y, first_c, second_c, first_x2, second_x2, coeffs, near, window
 ):
     place = here()
-    low_x2, high_x2 = got(first_x2, second_x2, place[0] % 2 == 0)
-    low_c, high_c = got(first_c, second_c, place[0] % 2 == 0)
+    low_x2, high_x2 = got(first_x2, second_x2, place[0] % 2 == 1)
+    low_c, high_c = got(first_c, second_c, place[0] % 2 == 1)
     level_two_near(near, low, low_y, high_y, low_c, high_c, low_x2, high_x2)
     mid_y, mid_z = mid.shape[1:]
     mid_x = mid.shape[0] // 4
@@ -642,9 +640,10 @@
     fine_tiles = 4 * tiles_of(2 * mid_y, 2 * mid_z)
     place = here()
     even = place[0] % 2 == 0
-    low_x2, high_x2 = got(first_x2, second_x2, even)
+    odd = place[0] % 2 == 1
+    low_x2, high_x2 = got(first_x2, second_x2, odd)
     low_y2, high_y2 = got(first_y2, second_y2, place[1] % 2 == 1)
-    low_c2, high_c2 = got(first_c2, second_c2, even)
+    low_c2, high_c2 = got(first_c2, second_c2, odd)
     blocks = {
         (0, 0): (low_c2, low_c2.shape[0] - 2 * mid_x), (0, 1): (low_x2, fine_tiles),
         (0, 2): (low_c2, low_c2.shape[0] - mid_x), (1, 0): (low_y2, low_y2.shape[0] - mid_x),
@@ -686,7 +685,6 @@
     pairs = count_x // 2
     own = place[0] // 2
     above, below = lax.rem(own + 1, pairs), lax.rem(own + pairs - 1, pairs)
-    odd = jnp.logical_not(even)
 
     def fill(i, carry):
         up, down = i == above, i == below
@@ -787,7 +785,7 @@
 
 def fine_coeffs_kernel(fields_own, low_x, high_x, low_y, high_y, first_c, second_c, coeffs, own_windows, side_windows):
     size_x, size_y, size_z = fields_own.shape[1:]
-    low_c, high_c = got(first_c, second_c, here()[0] % 2 == 0)
+    low_c, high_c = got(first_c, second_c, here()[0] % 2 == 1)
     assemble_owns(own_windows, fields_own, low_y, high_y)
     assemble_sides(side_windows, (size_y, size_z), low_x, high_x, low_c, high_c)
     end = FINE + size_x
@@ -801,10 +799,10 @@
 def window_kernel(own, first_x, second_x, first_y, second_y, first_c, second_c, window):
     size_x, size_y, size_z = own.shape
     place = here()
-    even = place[0] % 2 == 0
-    low_x, high_x = got(first_x, second_x, even)
+    odd = place[0] % 2 == 1
+    low_x, high_x = got(first_x, second_x, odd)
     low_y, high_y = got(first_y, second_y, place[1] % 2 == 1)
-    low_c, high_c = got(first_c, second_c, even)
+    low_c, high_c = got(first_c, second_c, odd)
     assemble_own(window.at[FINE : FINE + size_x], own, low_y, high_y, 0, 0)
     assemble_side(window, FINE - 4, 4, (size_y, size_z), low_x, 0, low_c, 0, 3, True)
     assemble_side(window, FINE + size_x, 4, (size_y, size_z), high_x, 0, high_c, 0, 3, False)

time: 60.9 us -> 60.2 us (0.989)
  starting transfers between devices: 15.7 us -> 13.6 us
  waiting for transfers between devices: 21.1 us -> 22.8 us
    ppermute x8, starting transfers between devices: 7.83 us -> 5.71 us  [swapped(): return (lax.ppermute(first, axis, outer), lax.ppermute(second, axis, inner))]
    ppermute x8, waiting for transfers between devices: 10.8 us -> 12.4 us  [swapped(): return (lax.ppermute(first, axis, outer), lax.ppermute(second, axis, inner))]
  transfers between devices with their start and end apart: 13 -> 13, of which waited for: 6 -> 7; matrix products, arithmetic and copies ran while one was open for 0% -> 0% of each run, Pallas kernels for 5% -> 5%
where the time goes in v8:
time: 60.2 us; the launch traced here: 60 us
  waiting for transfers between devices  22.8 us (38%)
  blocking collectives  14.3 us (24%)
  starting transfers between devices  13.6 us (23%)
  Pallas kernels  9.23 us (15%)
    all_to_all x1, blocking collectives, local(): own_half = lax.all_to_all(slots, ('gx', 'gy'), 0, 0)  14.3 us
    ppermute x8, waiting for transfers between devices, swapped(): return (lax.ppermute(first, axis, outer), lax.ppermute(second, axis, inner))  12.4 us
    ppermute x4, waiting for transfers between devices, shifted(): lax.ppermute(value, axis, [(i, (i + step) % count) for i in range(count)])  9.95 us
    pallas_call x11, Pallas kernels, call(): pl.pallas_call(kernel, out_shape=[pltpu.HBM(shape, F32) if i in far_out e...  9.23 us
    ppermute x4, starting transfers between devices, shifted(): lax.ppermute(value, axis, [(i, (i + step) % count) for i in range(count)])  6.71 us
    ppermute x8, starting transfers between devices, swapped(): return (lax.ppermute(first, axis, outer), lax.ppermute(second, axis, inner))  5.71 us
  transfers between devices with their start and end apart: 13, of which 7 were waited for; matrix products, arithmetic and copies ran while one was open for 0% of the time, Pallas kernels for 5%

profile of v8, /device:TPU:0, one launch (start us, length us, event | category | flops | bytes accessed | tf_op | source)
XLA Modules:
  0.0 60.0 jit_solution(17678992921217109882)
XLA Ops:
  0.0 1.6 %shard_map.64 = (f32[100,8,128]{2,1,0:T(8,128)S(1)}, f32[104,8,128]{2,1,0:T(8,128)S(1)}, f32[60,8,128]{2,1,0:T(8,128)S(1)}, f32[62,8,128]{2,1,0:T(8,128)S(1)}, f...) custom-call(f32[8,16,256]{2,1,0:T(8,128)} %ini_in.1, f32[8,16,256]{2,1,0:T(8,128)} %src_in.1, ...), custom_call_target="tpu_custom_call" | custom-call | flops 1000 | bytes 1000 | tf_op jit(solution)/shard_map/pallas_call | solution.py:897
  1.7 5.1 %collective-permute-start.1 = (f32[62,8,128]{2,1,0:T(8,128)S(1)}, f32[62,8,128]{2,1,0:T(8,128)S(1)}, u32[]{:S(2)}, u32[]{:S(2)}) collective-permute-start(f32[62,8,128]{2,1,0:T(8,128)S(1)} %get-tuple-element.34), channel_id=1, source_target_pairs={{0,3},{1,0},{2,1},{3,2},{4,7},{5,4},{6,5},{7,6},{8,11},{9,8},{10,9... | collective-permute-start | bytes 761864 | tf_op jit(solution)/shard_map/ppermute | solution.py:174
  6.8 0.0 collective-permute-start
  6.8 1.6 %collective-permute-start.3 = (f32[104,8,128]{2,1,0:T(8,128)S(1)}, f32[104,8,128]{2,1,0:T(8,128)S(1)}, u32[]{:S(2)}, u32[]{:S(2)}) collective-permute-start(f32[104,8,128]{2,1,0:T(8,128)S(1)} %get-tuple-element.41), channel_id=1, source_target_pairs={{0,28},{4,0},{8,4},{12,8},{16,12},{20,16},{24,20},{28,24},{1,29},{... | collective-permute-start | bytes 1277960 | tf_op jit(solution)/shard_map/ppermute | solution.py:174
  8.4 0.0 collective-permute-start.2
  8.4 9.9 %collective-permute-done.low_y = f32[60,8,128]{2,1,0:T(8,128)S(1)} collective-permute-done((f32[60,8,128]{2,1,0:T(8,128)S(1)}, f32[60,8,128]{2,1,0:T(8,128)S(1)}, u32[]{:S(2)}, u32[]{:S(2)}) %collective-permute-start) | collective-permute-done | bytes 245792 | tf_op jit(solution)/shard_map/ppermute | solution.py:174
  18.3 0.0 collective-permute-done.1.high_y
  18.3 0.2 shard_map.66
  18.5 1.1 %collective-permute-start.4 = (f32[46,8,128]{2,1,0:T(8,128)S(1)}, f32[46,8,128]{2,1,0:T(8,128)S(1)}, u32[]{:S(2)}, u32[]{:S(2)}) collective-permute-start(f32[46,8,128]{2,1,0:T(8,128)S(1)} %get-tuple-element.42), channel_id=1, source_target_pairs={{0,28},{4,8},{8,4},{12,16},{16,12},{20,24},{24,20},{28,0},{1,29},{... | collective-permute-start | bytes 565256 | tf_op jit(solution)/shard_map/ppermute | solution.py:169
  19.6 0.6 collective-permute-start.5
  20.2 1.1 %shard_map.65 = (f32[6,8,32,256]{3,2,1,0:T(8,128)S(1)}, f32[8,7,32,256]{3,2,1,0:T(8,128)S(1)}, f32[24,8,128]{2,1,0:T(8,128)S(1)}, f32[24,8,128]{2,1,0:T(8,128)S(1)}, f32[32,8,128]{2,1,0:T(8,128)S(1)}) custom-call(f32[6,8,16,256]{3,2,1,0:T(8,128)S(1)} %get-tuple-element.32.own.fields_own, f32[60,8,128]{2,1,0:T(8,128)S(1)} %collective-permute-done.low_y, ...), custom_call_target="tpu_custom_call" | custom-call | flops 1000 | bytes 1000 | tf_op jit(solution)/shard_map/pallas_call | solution.py:897
  21.3 0.0 collective-permute-done.2.low_x
  21.4 0.0 collective-permute-done.3.high_x
  21.4 5.1 %collective-permute-done.4.first_c = f32[46,8,128]{2,1,0:T(8,128)S(1)} collective-permute-done((f32[46,8,128]{2,1,0:T(8,128)S(1)}, f32[46,8,128]{2,1,0:T(8,128)S(1)}, u32[]{:S(2)}, u32[]{:S(2)}) %collective-permute-start.4) | collective-permute-done | bytes 188448 | tf_op jit(solution)/shard_map/ppermute | solution.py:169
  26.4 0.0 collective-permute-done.5.second_c
  26.4 1.9 %shard_map.67 = (f32[8,16,256]{2,1,0:T(8,128)S(1)}, f32[4,8,128]{2,1,0:T(8,128)S(1)}, f32[76,8,128]{2,1,0:T(8,128)S(1)}, f32[76,8,128]{2,1,0:T(8,128)S(1)}, f32[...) custom-call(f32[6,8,32,256]{3,2,1,0:T(8,128)S(1)} %get-tuple-element.35.own_windows, ...), custom_call_target="tpu_custom_call" | custom-call | flops 1000 | bytes 1000 | tf_op jit(solution)/shard_map/pallas_call | solution.py:897
  28.3 1.1 %collective-permute-start.6 = (f32[76,8,128]{2,1,0:T(8,128)S(1)}, f32[76,8,128]{2,1,0:T(8,128)S(1)}, u32[]{:S(2)}, u32[]{:S(2)}) collective-permute-start(f32[76,8,128]{2,1,0:T(8,128)S(1)} %get-tuple-element.46), channel_id=1, source_target_pairs={{0,28},{4,8},{8,4},{12,16},{16,12},{20,24},{24,20},{28,0},{1,29},{... | collective-permute-start | bytes 933896 | tf_op jit(solution)/shard_map/ppermute | solution.py:169
  29.4 0.0 collective-permute-start.7
  29.4 1.3 %collective-permute-start.8 = (f32[12,8,128]{2,1,0:T(8,128)S(1)}, f32[12,8,128]{2,1,0:T(8,128)S(1)}, u32[]{:S(2)}, u32[]{:S(2)}) collective-permute-start(f32[12,8,128]{2,1,0:T(8,128)S(1)} %get-tuple-element.49), channel_id=1, source_target_pairs={{0,3},{1,2},{2,1},{3,0},{4,7},{5,6},{6,5},{7,4},{8,11},{9,10},{10,... | collective-permute-start | bytes 147464 | tf_op jit(solution)/shard_map/ppermute | solution.py:169
  30.7 0.3 collective-permute-start.9
  31.0 4.7 %collective-permute-done.8.first_y.first_y2 = f32[12,8,128]{2,1,0:T(8,128)S(1)} collective-permute-done((f32[12,8,128]{2,1,0:T(8,128)S(1)}, f32[12,8,128]{2,1,0:T(8,128)S(1)}, u32[]{:S(2)}, u32[]{:S(2)}) %collective-permute-start.8) | collective-permute-done | bytes 49184 | tf_op jit(solution)/shard_map/ppermute | solution.py:169
  35.7 0.1 collective-permute-done.9.second_y.second_y2
  35.9 0.5 collective-permute-start.10
  36.3 0.9 %collective-permute-start.11 = (f32[12,8,128]{2,1,0:T(8,128)S(1)}, f32[12,8,128]{2,1,0:T(8,128)S(1)}, u32[]{:S(2)}, u32[]{:S(2)}) collective-permute-start(f32[12,8,128]{2,1,0:T(8,128)S(1)} %get-tuple-element.52), channel_id=1, source_target_pairs={{0,4},{4,0},{8,12},{12,8},{16,20},{20,16},{24,28},{28,24},{1,5},{5... | collective-permute-start | bytes 147464 | tf_op jit(solution)/shard_map/ppermute | solution.py:169
  37.2 0.5 shard_map.70.unused.fine_coeffs
  37.7 0.7 %collective-permute-done.6.first_x2.first_x = f32[76,8,128]{2,1,0:T(8,128)S(1)} collective-permute-done((f32[76,8,128]{2,1,0:T(8,128)S(1)}, f32[76,8,128]{2,1,0:T(8,128)S(1)}, u32[]{:S(2)}, u32[]{:S(2)}) %collective-permute-start.6) | collective-permute-done | bytes 311328 | tf_op jit(solution)/shard_map/ppermute | solution.py:169
  38.4 0.0 collective-permute-done.7.second_x2.second_x
  38.4 0.2 shard_map.68
  38.6 1.8 %collective-permute-done.10.first_c2.first_c = f32[12,8,128]{2,1,0:T(8,128)S(1)} collective-permute-done((f32[12,8,128]{2,1,0:T(8,128)S(1)}, f32[12,8,128]{2,1,0:T(8,128)S(1)}, u32[]{:S(2)}, u32[]{:S(2)}) %collective-permute-start.10) | collective-permute-done | bytes 49184 | tf_op jit(solution)/shard_map/ppermute | solution.py:169
  40.5 0.0 collective-permute-done.11.second_c2.second_c
  40.5 0.5 shard_map.71
  41.0 14.3 %all_to_all.5.own_half = f32[32,3,8,128]{3,2,1,0:T(8,128)S(1)} all-to-all(f32[32,3,8,128]{3,2,1,0:T(8,128)S(1)} %get-tuple-element.53), channel_id=1, replica_groups=mesh['gx'=8,'gy'=4] {'gx','gy'}, dimensions={0} | all-to-all | bytes 786432 | tf_op jit(solution)/shard_map/all_to_all | solution.py:999
  55.3 1.2 %collective-permute-start.12 = (f32[32,3,8,128]{3,2,1,0:T(8,128)S(1)}, f32[32,3,8,128]{3,2,1,0:T(8,128)S(1)}, u32[]{:S(2)}, u32[]{:S(2)}) collective-permute-start(f32[32,3,8,128]{3,2,1,0:T(8,128)S(1)} %all_to_all.5.own_half), channel_id=1, source_target_pairs={{0,4},{4,0},{8,12},{12,8},{16,20},{20,16},{24,28},{28,24},{1,5},{5... | collective-permute-start | bytes 1179656 | tf_op jit(solution)/shard_map/ppermute | solution.py:1000
  56.5 0.9 %shard_map.72.low_iterate = f32[8,16,128]{2,1,0:T(8,128)S(1)} custom-call(f32[32,3,8,128]{3,2,1,0:T(8,128)S(1)} %all_to_all.5.own_half, f32[30,8,128]{2,1,0:T(8,128)S(1)} %get-tuple-element.54.near), custom_call_target="tpu_custom_call" | custom-call | flops 1000 | bytes 1000 | tf_op jit(solution)/shard_map/pallas_call | solution.py:897
  57.4 0.4 collective-permute-done.12.other_half
  57.8 2.2 %shard_map.74 = f32[8,16,256]{2,1,0:T(8,128)} custom-call(f32[32,3,8,128]{3,2,1,0:T(8,128)S(1)} %all_to_all.5.own_half, f32[32,3,8,128]{3,2,1,0:T(8,128)S(1)} %collective-permute-done.12.other_half, f32[8,16,128]{2,1,0:T(8,128)S(1)} %shard_map.72.low_iterate, f32[8,16,24,128]{3,2,1,0:T(8,128)S(1)} %get-tuple-element.48.coeffs.mid_coeffs, ...), custom_call_target="tpu_custom_call" | custom-call | flops 1000 | bytes 1000 | tf_op jit(solution)/shard_map/pallas_call | solution.py:897
  (2 shorter events, 0.1 us)
Async XLA Ops:
  1.7 16.7 %collective-permute-start.1 = (f32[62,8,128]{2,1,0:T(8,128)S(1)}, f32[62,8,128]{2,1,0:T(8,128)S(1)}, u32[]{:S(2)}, u32[]{:S(2)}) collective-permute-start(f32[62,8,128]{2,1,0:T(8,128)S(1)} %get-tuple-element.34), channel_id=1, source_target_pairs={{0,3},{1,0},{2,1},{3,2},{4,7},{5,4},{6,5},{7,6},{8,11},{9,8},{10,9... | collective-permute-start | bytes 761864 | tf_op jit(solution)/shard_map/ppermute | solution.py:174
  6.8 11.6 %collective-permute-start = (f32[60,8,128]{2,1,0:T(8,128)S(1)}, f32[60,8,128]{2,1,0:T(8,128)S(1)}, u32[]{:S(2)}, u32[]{:S(2)}) collective-permute-start(f32[60,8,128]{2,1,0:T(8,128)S(1)} %get-tuple-element.33), channel_id=1, source_target_pairs={{0,1},{1,2},{2,3},{3,0},{4,5},{5,6},{6,7},{7,4},{8,9},{9,10},{10,1... | collective-permute-start | bytes 737288 | tf_op jit(solution)/shard_map/ppermute | solution.py:174
  6.8 14.6 %collective-permute-start.3 = (f32[104,8,128]{2,1,0:T(8,128)S(1)}, f32[104,8,128]{2,1,0:T(8,128)S(1)}, u32[]{:S(2)}, u32[]{:S(2)}) collective-permute-start(f32[104,8,128]{2,1,0:T(8,128)S(1)} %get-tuple-element.41), channel_id=1, source_target_pairs={{0,28},{4,0},{8,4},{12,8},{16,12},{20,16},{24,20},{28,24},{1,29},{... | collective-permute-start | bytes 1277960 | tf_op jit(solution)/shard_map/ppermute | solution.py:174
  8.4 13.0 %collective-permute-start.2 = (f32[100,8,128]{2,1,0:T(8,128)S(1)}, f32[100,8,128]{2,1,0:T(8,128)S(1)}, u32[]{:S(2)}, u32[]{:S(2)}) collective-permute-start(f32[100,8,128]{2,1,0:T(8,128)S(1)} %get-tuple-element.40), channel_id=1, source_target_pairs={{0,4},{4,8},{8,12},{12,16},{16,20},{20,24},{24,28},{28,0},{1,5},{5... | collective-permute-start | bytes 1228808 | tf_op jit(solution)/shard_map/ppermute | solution.py:174
  18.5 7.9 %collective-permute-start.4 = (f32[46,8,128]{2,1,0:T(8,128)S(1)}, f32[46,8,128]{2,1,0:T(8,128)S(1)}, u32[]{:S(2)}, u32[]{:S(2)}) collective-permute-start(f32[46,8,128]{2,1,0:T(8,128)S(1)} %get-tuple-element.42), channel_id=1, source_target_pairs={{0,28},{4,8},{8,4},{12,16},{16,12},{20,24},{24,20},{28,0},{1,29},{... | collective-permute-start | bytes 565256 | tf_op jit(solution)/shard_map/ppermute | solution.py:169
  19.6 6.8 %collective-permute-start.5 = (f32[46,8,128]{2,1,0:T(8,128)S(1)}, f32[46,8,128]{2,1,0:T(8,128)S(1)}, u32[]{:S(2)}, u32[]{:S(2)}) collective-permute-start(f32[46,8,128]{2,1,0:T(8,128)S(1)} %get-tuple-element.43), channel_id=1, source_target_pairs={{0,4},{4,0},{8,12},{12,8},{16,20},{20,16},{24,28},{28,24},{1,5},{5... | collective-permute-start | bytes 565256 | tf_op jit(solution)/shard_map/ppermute | solution.py:169
  28.3 10.1 %collective-permute-start.6 = (f32[76,8,128]{2,1,0:T(8,128)S(1)}, f32[76,8,128]{2,1,0:T(8,128)S(1)}, u32[]{:S(2)}, u32[]{:S(2)}) collective-permute-start(f32[76,8,128]{2,1,0:T(8,128)S(1)} %get-tuple-element.46), channel_id=1, source_target_pairs={{0,28},{4,8},{8,4},{12,16},{16,12},{20,24},{24,20},{28,0},{1,29},{... | collective-permute-start | bytes 933896 | tf_op jit(solution)/shard_map/ppermute | solution.py:169
  29.4 9.0 %collective-permute-start.7 = (f32[76,8,128]{2,1,0:T(8,128)S(1)}, f32[76,8,128]{2,1,0:T(8,128)S(1)}, u32[]{:S(2)}, u32[]{:S(2)}) collective-permute-start(f32[76,8,128]{2,1,0:T(8,128)S(1)} %get-tuple-element.47), channel_id=1, source_target_pairs={{0,4},{4,0},{8,12},{12,8},{16,20},{20,16},{24,28},{28,24},{1,5},{5... | collective-permute-start | bytes 933896 | tf_op jit(solution)/shard_map/ppermute | solution.py:169
  29.4 6.3 %collective-permute-start.8 = (f32[12,8,128]{2,1,0:T(8,128)S(1)}, f32[12,8,128]{2,1,0:T(8,128)S(1)}, u32[]{:S(2)}, u32[]{:S(2)}) collective-permute-start(f32[12,8,128]{2,1,0:T(8,128)S(1)} %get-tuple-element.49), channel_id=1, source_target_pairs={{0,3},{1,2},{2,1},{3,0},{4,7},{5,6},{6,5},{7,4},{8,11},{9,10},{10,... | collective-permute-start | bytes 147464 | tf_op jit(solution)/shard_map/ppermute | solution.py:169
  30.7 5.1 %collective-permute-start.9 = (f32[12,8,128]{2,1,0:T(8,128)S(1)}, f32[12,8,128]{2,1,0:T(8,128)S(1)}, u32[]{:S(2)}, u32[]{:S(2)}) collective-permute-start(f32[12,8,128]{2,1,0:T(8,128)S(1)} %get-tuple-element.50), channel_id=1, source_target_pairs={{0,1},{1,0},{2,3},{3,2},{4,5},{5,4},{6,7},{7,6},{8,9},{9,8},{10,11... | collective-permute-start | bytes 147464 | tf_op jit(solution)/shard_map/ppermute | solution.py:169
  35.9 4.6 %collective-permute-start.10 = (f32[12,8,128]{2,1,0:T(8,128)S(1)}, f32[12,8,128]{2,1,0:T(8,128)S(1)}, u32[]{:S(2)}, u32[]{:S(2)}) collective-permute-start(f32[12,8,128]{2,1,0:T(8,128)S(1)} %get-tuple-element.51), channel_id=1, source_target_pairs={{0,28},{4,8},{8,4},{12,16},{16,12},{20,24},{24,20},{28,0},{1,29},{... | collective-permute-start | bytes 147464 | tf_op jit(solution)/shard_map/ppermute | solution.py:169
  36.3 4.1 %collective-permute-start.11 = (f32[12,8,128]{2,1,0:T(8,128)S(1)}, f32[12,8,128]{2,1,0:T(8,128)S(1)}, u32[]{:S(2)}, u32[]{:S(2)}) collective-permute-start(f32[12,8,128]{2,1,0:T(8,128)S(1)} %get-tuple-element.52), channel_id=1, source_target_pairs={{0,4},{4,0},{8,12},{12,8},{16,20},{20,16},{24,28},{28,24},{1,5},{5... | collective-permute-start | bytes 147464 | tf_op jit(solution)/shard_map/ppermute | solution.py:169
  55.3 2.5 %collective-permute-start.12 = (f32[32,3,8,128]{3,2,1,0:T(8,128)S(1)}, f32[32,3,8,128]{3,2,1,0:T(8,128)S(1)}, u32[]{:S(2)}, u32[]{:S(2)}) collective-permute-start(f32[32,3,8,128]{3,2,1,0:T(8,128)S(1)} %all_to_all.5.own_half), channel_id=1, source_target_pairs={{0,4},{4,0},{8,12},{12,8},{16,20},{20,16},{24,28},{28,24},{1,5},{5... | collective-permute-start | bytes 1179656 | tf_op jit(solution)/shard_map/ppermute | solution.py:1000

commit v9 on v8

--- a/solution.py
+++ b/solution.py
@@ -572,10 +572,15 @@
     tops, bottoms = Tiles(), Tiles()
     put_corners(tops, low_y, high_y, [size_x - 1, size_x - 2, size_x - 3], upper, 0)
     put_corners(bottoms, low_y, high_y, range(3), upper, 0)
-    for writer in (tops, bottoms):
-        for ref in (low_y, high_y):
-            for tile in range(ref.shape[0] - size_x // 2, ref.shape[0]):
-                writer.put(ref[tile])
+    mid_x = size_x // 2
+    upper = is_upper(TILE[1])
+    start = low_y.shape[0] - mid_x
+    for writer, near, step in ((tops, mid_x - 1, -1), (bottoms, 0, 1)):
+        writer.put(low_y[start + near])
+        writer.put(high_y[start + near])
+        for q in range(1, mid_x):
+            at = start + near + q * step
+            writer.put(jnp.where(upper, roll(low_y[at], 4, 0), roll(high_y[at], 4, 0)))
     send(first, second, place[0] % 2 == 1, tops, bottoms)
 
 
@@ -645,11 +650,10 @@
     low_y2, high_y2 = got(first_y2, second_y2, place[1] % 2 == 1)
     low_c2, high_c2 = got(first_c2, second_c2, odd)
     blocks = {
-        (0, 0): (low_c2, low_c2.shape[0] - 2 * mid_x), (0, 1): (low_x2, fine_tiles),
-        (0, 2): (low_c2, low_c2.shape[0] - mid_x), (1, 0): (low_y2, low_y2.shape[0] - mid_x),
+        (0, 1): (low_x2, fine_tiles),
+        (1, 0): (low_y2, low_y2.shape[0] - mid_x),
         (1, 2): (high_y2, high_y2.shape[0] - mid_x),
-        (2, 0): (high_c2, high_c2.shape[0] - 2 * mid_x), (2, 1): (high_x2, fine_tiles),
-        (2, 2): (high_c2, high_c2.shape[0] - mid_x),
+        (2, 1): (high_x2, fine_tiles),
     }
     for plane in range(mid_x):
         target[MID + plane, mid_y : 2 * mid_y] = mid_target[plane]
@@ -657,6 +661,12 @@
         for plane in range(mid_x):
             target[first + bx * mid_x + plane, by * mid_y : (by + 1) * mid_y] = ref[start + plane]
 
+    for ref, near, step in ((low_c2, MID - 1, -1), (high_c2, MID + mid_x, 1)):
+        start = ref.shape[0] - mid_x - 1
+        for q in range(mid_x):
+            one, two = (ref[start], ref[start + 1]) if q == 0 else [roll(ref[start + 1 + q], 4, 0)] * 2
+            target[near + q * step, :mid_y] = one
+            target[near + q * step, 2 * mid_y :] = two
     weights = chebyshev_weights(SWEEPS)
 
     def start_sweep(i, carry):
@@ -973,7 +983,7 @@
     first_c2, second_c2 = call(
         functools.partial(corner_two_kernel, size_x, size_z),
         (first_y2, second_y2),
-        [tiles(2 * strip + 2 * mid_x)] * 2,
+        [tiles(2 * strip + mid_x + 1)] * 2,
     )
     first_c2, second_c2 = swapped(first_c2, second_c2, "gx")
 

time: 60.2 us -> 59.9 us (level)
  no operation moved by 1% of the time
where the time goes in v9:
time: 59.9 us; the launch traced here: 59.8 us
  waiting for transfers between devices  22.5 us (38%)
  blocking collectives  14.4 us (24%)
  starting transfers between devices  13.6 us (23%)
  Pallas kernels  9.23 us (15%)
    all_to_all x1, blocking collectives, local(): own_half = lax.all_to_all(slots, ('gx', 'gy'), 0, 0)  14.4 us
    ppermute x8, waiting for transfers between devices, swapped(): return (lax.ppermute(first, axis, outer), lax.ppermute(second, axis, inner))  12.2 us
    ppermute x4, waiting for transfers between devices, shifted(): lax.ppermute(value, axis, [(i, (i + step) % count) for i in range(count)])  9.95 us
    pallas_call x11, Pallas kernels, call(): pl.pallas_call(kernel, out_shape=[pltpu.HBM(shape, F32) if i in far_out e...  9.23 us
    ppermute x4, starting transfers between devices, shifted(): lax.ppermute(value, axis, [(i, (i + step) % count) for i in range(count)])  6.71 us
    ppermute x8, starting transfers between devices, swapped(): return (lax.ppermute(first, axis, outer), lax.ppermute(second, axis, inner))  5.71 us
  transfers between devices with their start and end apart: 13, of which 7 were waited for; matrix products, arithmetic and copies ran while one was open for 0% of the time, Pallas kernels for 5%

profile of v9, /device:TPU:0, one launch (start us, length us, event | category | flops | bytes accessed | tf_op | source)
XLA Modules:
  0.0 59.8 jit_solution(17668158383658427281)
XLA Ops:
  0.0 1.6 %shard_map.64 = (f32[100,8,128]{2,1,0:T(8,128)S(1)}, f32[104,8,128]{2,1,0:T(8,128)S(1)}, f32[60,8,128]{2,1,0:T(8,128)S(1)}, f32[62,8,128]{2,1,0:T(8,128)S(1)}, f...) custom-call(f32[8,16,256]{2,1,0:T(8,128)} %ini_in.1, f32[8,16,256]{2,1,0:T(8,128)} %src_in.1, ...), custom_call_target="tpu_custom_call" | custom-call | flops 1000 | bytes 1000 | tf_op jit(solution)/shard_map/pallas_call | solution.py:907
  1.7 5.1 %collective-permute-start.1 = (f32[62,8,128]{2,1,0:T(8,128)S(1)}, f32[62,8,128]{2,1,0:T(8,128)S(1)}, u32[]{:S(2)}, u32[]{:S(2)}) collective-permute-start(f32[62,8,128]{2,1,0:T(8,128)S(1)} %get-tuple-element.34), channel_id=1, source_target_pairs={{0,3},{1,0},{2,1},{3,2},{4,7},{5,4},{6,5},{7,6},{8,11},{9,8},{10,9... | collective-permute-start | bytes 761864 | tf_op jit(solution)/shard_map/ppermute | solution.py:174
  6.8 0.0 collective-permute-start
  6.8 1.6 %collective-permute-start.3 = (f32[104,8,128]{2,1,0:T(8,128)S(1)}, f32[104,8,128]{2,1,0:T(8,128)S(1)}, u32[]{:S(2)}, u32[]{:S(2)}) collective-permute-start(f32[104,8,128]{2,1,0:T(8,128)S(1)} %get-tuple-element.41), channel_id=1, source_target_pairs={{0,28},{4,0},{8,4},{12,8},{16,12},{20,16},{24,20},{28,24},{1,29},{... | collective-permute-start | bytes 1277960 | tf_op jit(solution)/shard_map/ppermute | solution.py:174
  8.4 0.0 collective-permute-start.2
  8.4 9.9 %collective-permute-done.low_y = f32[60,8,128]{2,1,0:T(8,128)S(1)} collective-permute-done((f32[60,8,128]{2,1,0:T(8,128)S(1)}, f32[60,8,128]{2,1,0:T(8,128)S(1)}, u32[]{:S(2)}, u32[]{:S(2)}) %collective-permute-start) | collective-permute-done | bytes 245792 | tf_op jit(solution)/shard_map/ppermute | solution.py:174
  18.3 0.0 collective-permute-done.1.high_y
  18.3 0.2 shard_map.66
  18.5 1.1 %collective-permute-start.4 = (f32[46,8,128]{2,1,0:T(8,128)S(1)}, f32[46,8,128]{2,1,0:T(8,128)S(1)}, u32[]{:S(2)}, u32[]{:S(2)}) collective-permute-start(f32[46,8,128]{2,1,0:T(8,128)S(1)} %get-tuple-element.42), channel_id=1, source_target_pairs={{0,28},{4,8},{8,4},{12,16},{16,12},{20,24},{24,20},{28,0},{1,29},{... | collective-permute-start | bytes 565256 | tf_op jit(solution)/shard_map/ppermute | solution.py:169
  19.6 0.6 collective-permute-start.5
  20.2 1.1 %shard_map.65 = (f32[6,8,32,256]{3,2,1,0:T(8,128)S(1)}, f32[8,7,32,256]{3,2,1,0:T(8,128)S(1)}, f32[24,8,128]{2,1,0:T(8,128)S(1)}, f32[24,8,128]{2,1,0:T(8,128)S(1)}, f32[32,8,128]{2,1,0:T(8,128)S(1)}) custom-call(f32[6,8,16,256]{3,2,1,0:T(8,128)S(1)} %get-tuple-element.32.own.fields_own, f32[60,8,128]{2,1,0:T(8,128)S(1)} %collective-permute-done.low_y, ...), custom_call_target="tpu_custom_call" | custom-call | flops 1000 | bytes 1000 | tf_op jit(solution)/shard_map/pallas_call | solution.py:907
  21.3 0.0 collective-permute-done.2.low_x
  21.4 0.0 collective-permute-done.3.high_x
  21.4 5.1 %collective-permute-done.4.first_c = f32[46,8,128]{2,1,0:T(8,128)S(1)} collective-permute-done((f32[46,8,128]{2,1,0:T(8,128)S(1)}, f32[46,8,128]{2,1,0:T(8,128)S(1)}, u32[]{:S(2)}, u32[]{:S(2)}) %collective-permute-start.4) | collective-permute-done | bytes 188448 | tf_op jit(solution)/shard_map/ppermute | solution.py:169
  26.4 0.0 collective-permute-done.5.second_c
  26.4 1.9 %shard_map.67 = (f32[8,16,256]{2,1,0:T(8,128)S(1)}, f32[4,8,128]{2,1,0:T(8,128)S(1)}, f32[76,8,128]{2,1,0:T(8,128)S(1)}, f32[76,8,128]{2,1,0:T(8,128)S(1)}, f32[...) custom-call(f32[6,8,32,256]{3,2,1,0:T(8,128)S(1)} %get-tuple-element.35.own_windows, ...), custom_call_target="tpu_custom_call" | custom-call | flops 1000 | bytes 1000 | tf_op jit(solution)/shard_map/pallas_call | solution.py:907
  28.3 1.1 %collective-permute-start.6 = (f32[76,8,128]{2,1,0:T(8,128)S(1)}, f32[76,8,128]{2,1,0:T(8,128)S(1)}, u32[]{:S(2)}, u32[]{:S(2)}) collective-permute-start(f32[76,8,128]{2,1,0:T(8,128)S(1)} %get-tuple-element.46), channel_id=1, source_target_pairs={{0,28},{4,8},{8,4},{12,16},{16,12},{20,24},{24,20},{28,0},{1,29},{... | collective-permute-start | bytes 933896 | tf_op jit(solution)/shard_map/ppermute | solution.py:169
  29.4 0.0 collective-permute-start.7
  29.4 1.3 %collective-permute-start.8 = (f32[12,8,128]{2,1,0:T(8,128)S(1)}, f32[12,8,128]{2,1,0:T(8,128)S(1)}, u32[]{:S(2)}, u32[]{:S(2)}) collective-permute-start(f32[12,8,128]{2,1,0:T(8,128)S(1)} %get-tuple-element.49), channel_id=1, source_target_pairs={{0,3},{1,2},{2,1},{3,0},{4,7},{5,6},{6,5},{7,4},{8,11},{9,10},{10,... | collective-permute-start | bytes 147464 | tf_op jit(solution)/shard_map/ppermute | solution.py:169
  30.7 0.3 collective-permute-start.9
  31.0 4.7 %collective-permute-done.8.first_y.first_y2 = f32[12,8,128]{2,1,0:T(8,128)S(1)} collective-permute-done((f32[12,8,128]{2,1,0:T(8,128)S(1)}, f32[12,8,128]{2,1,0:T(8,128)S(1)}, u32[]{:S(2)}, u32[]{:S(2)}) %collective-permute-start.8) | collective-permute-done | bytes 49184 | tf_op jit(solution)/shard_map/ppermute | solution.py:169
  35.7 0.1 collective-permute-done.9.second_y.second_y2
  35.9 0.5 collective-permute-start.10
  36.3 0.9 %collective-permute-start.11 = (f32[9,8,128]{2,1,0:T(8,128)S(1)}, f32[9,8,128]{2,1,0:T(8,128)S(1)}, u32[]{:S(2)}, u32[]{:S(2)}) collective-permute-start(f32[9,8,128]{2,1,0:T(8,128)S(1)} %get-tuple-element.52), channel_id=1, source_target_pairs={{0,4},{4,0},{8,12},{12,8},{16,20},{20,16},{24,28},{28,24},{1,5},{5... | collective-permute-start | bytes 110600 | tf_op jit(solution)/shard_map/ppermute | solution.py:169
  37.2 0.5 shard_map.70.unused.fine_coeffs
  37.7 0.7 %collective-permute-done.6.first_x2.first_x = f32[76,8,128]{2,1,0:T(8,128)S(1)} collective-permute-done((f32[76,8,128]{2,1,0:T(8,128)S(1)}, f32[76,8,128]{2,1,0:T(8,128)S(1)}, u32[]{:S(2)}, u32[]{:S(2)}) %collective-permute-start.6) | collective-permute-done | bytes 311328 | tf_op jit(solution)/shard_map/ppermute | solution.py:169
  38.4 0.0 collective-permute-done.7.second_x2.second_x
  38.4 0.2 shard_map.68
  38.6 1.6 %collective-permute-done.10.first_c2.first_c = f32[9,8,128]{2,1,0:T(8,128)S(1)} collective-permute-done((f32[9,8,128]{2,1,0:T(8,128)S(1)}, f32[9,8,128]{2,1,0:T(8,128)S(1)}, u32[]{:S(2)}, u32[]{:S(2)}) %collective-permute-start.10) | collective-permute-done | bytes 36896 | tf_op jit(solution)/shard_map/ppermute | solution.py:169
  40.2 0.0 collective-permute-done.11.second_c2.second_c
  40.2 0.5 shard_map.71
  40.7 14.4 %all_to_all.5.own_half = f32[32,3,8,128]{3,2,1,0:T(8,128)S(1)} all-to-all(f32[32,3,8,128]{3,2,1,0:T(8,128)S(1)} %get-tuple-element.53), channel_id=1, replica_groups=mesh['gx'=8,'gy'=4] {'gx','gy'}, dimensions={0} | all-to-all | bytes 786432 | tf_op jit(solution)/shard_map/all_to_all | solution.py:1009
  55.1 1.2 %collective-permute-start.12 = (f32[32,3,8,128]{3,2,1,0:T(8,128)S(1)}, f32[32,3,8,128]{3,2,1,0:T(8,128)S(1)}, u32[]{:S(2)}, u32[]{:S(2)}) collective-permute-start(f32[32,3,8,128]{3,2,1,0:T(8,128)S(1)} %all_to_all.5.own_half), channel_id=1, source_target_pairs={{0,4},{4,0},{8,12},{12,8},{16,20},{20,16},{24,28},{28,24},{1,5},{5... | collective-permute-start | bytes 1179656 | tf_op jit(solution)/shard_map/ppermute | solution.py:1010
  56.3 0.9 %shard_map.72.low_iterate = f32[8,16,128]{2,1,0:T(8,128)S(1)} custom-call(f32[32,3,8,128]{3,2,1,0:T(8,128)S(1)} %all_to_all.5.own_half, f32[30,8,128]{2,1,0:T(8,128)S(1)} %get-tuple-element.54.near), custom_call_target="tpu_custom_call" | custom-call | flops 1000 | bytes 1000 | tf_op jit(solution)/shard_map/pallas_call | solution.py:907
  57.2 0.4 collective-permute-done.12.other_half
  57.6 2.2 %shard_map.74 = f32[8,16,256]{2,1,0:T(8,128)} custom-call(f32[32,3,8,128]{3,2,1,0:T(8,128)S(1)} %all_to_all.5.own_half, f32[32,3,8,128]{3,2,1,0:T(8,128)S(1)} %collective-permute-done.12.other_half, f32[8,16,128]{2,1,0:T(8,128)S(1)} %shard_map.72.low_iterate, f32[8,16,24,128]{3,2,1,0:T(8,128)S(1)} %get-tuple-element.48.coeffs.mid_coeffs, ...), custom_call_target="tpu_custom_call" | custom-call | flops 1000 | bytes 1000 | tf_op jit(solution)/shard_map/pallas_call | solution.py:907
  (2 shorter events, 0.1 us)
Async XLA Ops:
  1.7 16.7 %collective-permute-start.1 = (f32[62,8,128]{2,1,0:T(8,128)S(1)}, f32[62,8,128]{2,1,0:T(8,128)S(1)}, u32[]{:S(2)}, u32[]{:S(2)}) collective-permute-start(f32[62,8,128]{2,1,0:T(8,128)S(1)} %get-tuple-element.34), channel_id=1, source_target_pairs={{0,3},{1,0},{2,1},{3,2},{4,7},{5,4},{6,5},{7,6},{8,11},{9,8},{10,9... | collective-permute-start | bytes 761864 | tf_op jit(solution)/shard_map/ppermute | solution.py:174
  6.8 11.6 %collective-permute-start = (f32[60,8,128]{2,1,0:T(8,128)S(1)}, f32[60,8,128]{2,1,0:T(8,128)S(1)}, u32[]{:S(2)}, u32[]{:S(2)}) collective-permute-start(f32[60,8,128]{2,1,0:T(8,128)S(1)} %get-tuple-element.33), channel_id=1, source_target_pairs={{0,1},{1,2},{2,3},{3,0},{4,5},{5,6},{6,7},{7,4},{8,9},{9,10},{10,1... | collective-permute-start | bytes 737288 | tf_op jit(solution)/shard_map/ppermute | solution.py:174
  6.8 14.6 %collective-permute-start.3 = (f32[104,8,128]{2,1,0:T(8,128)S(1)}, f32[104,8,128]{2,1,0:T(8,128)S(1)}, u32[]{:S(2)}, u32[]{:S(2)}) collective-permute-start(f32[104,8,128]{2,1,0:T(8,128)S(1)} %get-tuple-element.41), channel_id=1, source_target_pairs={{0,28},{4,0},{8,4},{12,8},{16,12},{20,16},{24,20},{28,24},{1,29},{... | collective-permute-start | bytes 1277960 | tf_op jit(solution)/shard_map/ppermute | solution.py:174
  8.4 13.0 %collective-permute-start.2 = (f32[100,8,128]{2,1,0:T(8,128)S(1)}, f32[100,8,128]{2,1,0:T(8,128)S(1)}, u32[]{:S(2)}, u32[]{:S(2)}) collective-permute-start(f32[100,8,128]{2,1,0:T(8,128)S(1)} %get-tuple-element.40), channel_id=1, source_target_pairs={{0,4},{4,8},{8,12},{12,16},{16,20},{20,24},{24,28},{28,0},{1,5},{5... | collective-permute-start | bytes 1228808 | tf_op jit(solution)/shard_map/ppermute | solution.py:174
  18.5 7.9 %collective-permute-start.4 = (f32[46,8,128]{2,1,0:T(8,128)S(1)}, f32[46,8,128]{2,1,0:T(8,128)S(1)}, u32[]{:S(2)}, u32[]{:S(2)}) collective-permute-start(f32[46,8,128]{2,1,0:T(8,128)S(1)} %get-tuple-element.42), channel_id=1, source_target_pairs={{0,28},{4,8},{8,4},{12,16},{16,12},{20,24},{24,20},{28,0},{1,29},{... | collective-permute-start | bytes 565256 | tf_op jit(solution)/shard_map/ppermute | solution.py:169
  19.6 6.8 %collective-permute-start.5 = (f32[46,8,128]{2,1,0:T(8,128)S(1)}, f32[46,8,128]{2,1,0:T(8,128)S(1)}, u32[]{:S(2)}, u32[]{:S(2)}) collective-permute-start(f32[46,8,128]{2,1,0:T(8,128)S(1)} %get-tuple-element.43), channel_id=1, source_target_pairs={{0,4},{4,0},{8,12},{12,8},{16,20},{20,16},{24,28},{28,24},{1,5},{5... | collective-permute-start | bytes 565256 | tf_op jit(solution)/shard_map/ppermute | solution.py:169
  28.3 10.1 %collective-permute-start.6 = (f32[76,8,128]{2,1,0:T(8,128)S(1)}, f32[76,8,128]{2,1,0:T(8,128)S(1)}, u32[]{:S(2)}, u32[]{:S(2)}) collective-permute-start(f32[76,8,128]{2,1,0:T(8,128)S(1)} %get-tuple-element.46), channel_id=1, source_target_pairs={{0,28},{4,8},{8,4},{12,16},{16,12},{20,24},{24,20},{28,0},{1,29},{... | collective-permute-start | bytes 933896 | tf_op jit(solution)/shard_map/ppermute | solution.py:169
  29.4 9.0 %collective-permute-start.7 = (f32[76,8,128]{2,1,0:T(8,128)S(1)}, f32[76,8,128]{2,1,0:T(8,128)S(1)}, u32[]{:S(2)}, u32[]{:S(2)}) collective-permute-start(f32[76,8,128]{2,1,0:T(8,128)S(1)} %get-tuple-element.47), channel_id=1, source_target_pairs={{0,4},{4,0},{8,12},{12,8},{16,20},{20,16},{24,28},{28,24},{1,5},{5... | collective-permute-start | bytes 933896 | tf_op jit(solution)/shard_map/ppermute | solution.py:169
  29.4 6.3 %collective-permute-start.8 = (f32[12,8,128]{2,1,0:T(8,128)S(1)}, f32[12,8,128]{2,1,0:T(8,128)S(1)}, u32[]{:S(2)}, u32[]{:S(2)}) collective-permute-start(f32[12,8,128]{2,1,0:T(8,128)S(1)} %get-tuple-element.49), channel_id=1, source_target_pairs={{0,3},{1,2},{2,1},{3,0},{4,7},{5,6},{6,5},{7,4},{8,11},{9,10},{10,... | collective-permute-start | bytes 147464 | tf_op jit(solution)/shard_map/ppermute | solution.py:169
  30.7 5.1 %collective-permute-start.9 = (f32[12,8,128]{2,1,0:T(8,128)S(1)}, f32[12,8,128]{2,1,0:T(8,128)S(1)}, u32[]{:S(2)}, u32[]{:S(2)}) collective-permute-start(f32[12,8,128]{2,1,0:T(8,128)S(1)} %get-tuple-element.50), channel_id=1, source_target_pairs={{0,1},{1,0},{2,3},{3,2},{4,5},{5,4},{6,7},{7,6},{8,9},{9,8},{10,11... | collective-permute-start | bytes 147464 | tf_op jit(solution)/shard_map/ppermute | solution.py:169
  35.9 4.3 %collective-permute-start.10 = (f32[9,8,128]{2,1,0:T(8,128)S(1)}, f32[9,8,128]{2,1,0:T(8,128)S(1)}, u32[]{:S(2)}, u32[]{:S(2)}) collective-permute-start(f32[9,8,128]{2,1,0:T(8,128)S(1)} %get-tuple-element.51), channel_id=1, source_target_pairs={{0,28},{4,8},{8,4},{12,16},{16,12},{20,24},{24,20},{28,0},{1,29},{... | collective-permute-start | bytes 110600 | tf_op jit(solution)/shard_map/ppermute | solution.py:169
  36.3 3.9 %collective-permute-start.11 = (f32[9,8,128]{2,1,0:T(8,128)S(1)}, f32[9,8,128]{2,1,0:T(8,128)S(1)}, u32[]{:S(2)}, u32[]{:S(2)}) collective-permute-start(f32[9,8,128]{2,1,0:T(8,128)S(1)} %get-tuple-element.52), channel_id=1, source_target_pairs={{0,4},{4,0},{8,12},{12,8},{16,20},{20,16},{24,28},{28,24},{1,5},{5... | collective-permute-start | bytes 110600 | tf_op jit(solution)/shard_map/ppermute | solution.py:169
  55.1 2.5 %collective-permute-start.12 = (f32[32,3,8,128]{3,2,1,0:T(8,128)S(1)}, f32[32,3,8,128]{3,2,1,0:T(8,128)S(1)}, u32[]{:S(2)}, u32[]{:S(2)}) collective-permute-start(f32[32,3,8,128]{3,2,1,0:T(8,128)S(1)} %all_to_all.5.own_half), channel_id=1, source_target_pairs={{0,4},{4,0},{8,12},{12,8},{16,20},{20,16},{24,28},{28,24},{1,5},{5... | collective-permute-start | bytes 1179656 | tf_op jit(solution)/shard_map/ppermute | solution.py:1010
